TPU v7x, 32 devices: a whole 2x2x4 slice. The times are simulated.
32 devices in a mesh: clip: 8 (over z, y), row: 4 (over x, core).
Axes of the slice: x: 2, y: 2, z: 4, core: 2. Of those that a mesh axis runs over, the one named last changes fastest.
Arguments:
- frames: bfloat16 [8, 12, 3, 256, 256], P('clip', None, None, 'row'), may hold values from -6 to 6
- frame_start: int32 [8, 8], P('clip'), may hold values from 0 to 7
- boundary_mask: int32 [8, 8], P('clip'), may hold values from 0 to 1, as said below
- stem_weight: bfloat16 [64, 735], P('clip'), may hold values from -0.21875 to 0.21875
- stem_gain: float32 [64], replicated, may hold values from 0.5 to 1.5
- stem_bias: float32 [64], replicated, may hold values from -3 to 3
- block_input: bfloat16 [64, 8, 8, 2048], P('clip', 'row'), may hold values from -6 to 6
- w_one: bfloat16 [2048, 512], P('clip'), may hold values from -0.125 to 0.125
- w_reduce: bfloat16 [512, 128], P('clip'), may hold values from -0.25 to 0.25
- k_fine: bfloat16 [1152, 128], P('clip'), may hold values from -0.1875 to 0.1875
- k_half: bfloat16 [1152, 128], P('clip'), may hold values from -0.1875 to 0.1875
- k_quarter: bfloat16 [1152, 128], P('clip'), may hold values from -0.1875 to 0.1875
- w_expand: bfloat16 [128, 512], P('clip'), may hold values from -0.5 to 0.5
- w_two: bfloat16 [4608, 512], P('clip'), may hold values from -0.09375 to 0.09375
- w_three: bfloat16 [512, 2048], P('clip'), may hold values from -0.25 to 0.25
- gain_one: float32 [512], replicated, may hold values from 0.5 to 1.5
- bias_one: float32 [512], replicated, may hold values from -3 to 3
- gain_two: float32 [512], replicated, may hold values from 0.5 to 1.5
- bias_two: float32 [512], replicated, may hold values from -3 to 3
- gain_three: float32 [2048], replicated, may hold values from 0.5 to 1.5
- bias_three: float32 [2048], replicated, may hold values from -3 to 3
- stem_cot: bfloat16 [64, 64, 128, 128], P('clip', None, 'row'), may hold values from -6 to 6
- block_cot: bfloat16 [64, 8, 8, 2048], P('clip', 'row'), may hold values from -6 to 6
Outputs:
- block_out: bfloat16 [64, 8, 8, 2048], P('clip', 'row')
- input_grad: float32 [64, 8, 8, 2048], P('clip', 'row')
- stem_weight_grad: float32 [64, 735], P('clip')
- stem_gain_grad: float32 [64], replicated
- stem_bias_grad: float32 [64], replicated
- w_one_grad: float32 [2048, 512], P('clip')
- w_reduce_grad: float32 [512, 128], P('clip')
- k_fine_grad: float32 [1152, 128], P('clip')
- k_half_grad: float32 [1152, 128], P('clip')
- k_quarter_grad: float32 [1152, 128], P('clip')
- w_expand_grad: float32 [128, 512], P('clip')
- w_two_grad: float32 [4608, 512], P('clip')
- w_three_grad: float32 [512, 2048], P('clip')
- gain_one_grad: float32 [512], replicated
- bias_one_grad: float32 [512], replicated
- gain_two_grad: float32 [512], replicated
- bias_two_grad: float32 [512], replicated
- gain_three_grad: float32 [2048], replicated
- bias_three_grad: float32 [2048], replicated
Inputs may be any that keep to these rules, and one draw needn't show every extreme that they name: `frame_start`: the 5 frames from this one form the segment's window. `boundary_mask`: each clip slot holds one or two videos; exactly one segment of a slot is 0, the last segment of its first video (7 where the slot holds one video).
All inputs are finite; a program needn't handle non-finite values.
Results may differ from a plain program's by a relative error of at most 0.02.
Values may be sent and summed in bfloat16 or wider, within the bound.
No kernel may reach another device: no remote copies, remote signals or barrier semaphores. Data moves between devices by JAX's collectives and lax.ppermute only.
A program may use at most 192 MiB of HBM per device.

v0:
```python
import jax
import jax.numpy as jnp
from jax import lax
from jax.sharding import PartitionSpec as P

STEM = 64
SEG = 8
WIN = 5


epsilon = 1e-05
highest = lax.Precision.HIGHEST


def with_halo(x, sides, width):
    for axis, dim in sides:
        size, length = (lax.axis_size(axis), x.shape[dim])
        up = [(i, (i + 1) % size) for i in range(size - 1)]
        down = [(j, i) for i, j in up]
        last = lax.slice_in_dim(x, length - width, length, axis=dim)
        leading = lax.slice_in_dim(x, 0, width, axis=dim)
        before = lax.ppermute(last, axis, up)
        after = lax.ppermute(leading, axis, down)
        x = jnp.concatenate([before, x, after], axis=dim)
    return x


def silu_slope(values):
    sigmoid_val = jax.nn.sigmoid(values)
    return sigmoid_val * (1.0 + values * (1.0 - sigmoid_val))


def norm_forward(pre_act, norm_gain, norm_bias, sum_axes, gain_shape):
    totals = lax.psum(
        (jnp.sum(pre_act, sum_axes), jnp.sum(pre_act * pre_act, sum_axes)), ("clip", "row")
    )
    count_all = pre_act.size // norm_gain.shape[0] * lax.axis_size("clip") * lax.axis_size("row")
    mean_vec = totals[0] / count_all
    variance = totals[1] / count_all - mean_vec * mean_vec
    inverse = lax.rsqrt(variance + epsilon)
    normed = (pre_act - mean_vec.reshape(gain_shape)) * inverse.reshape(gain_shape)
    return (normed, normed * norm_gain.reshape(gain_shape) + norm_bias.reshape(gain_shape), inverse)


def norm_backward(cotangent, normed, norm_gain, inverse, sum_axes, gain_shape):
    totals = lax.psum(
        (jnp.sum(cotangent, sum_axes), jnp.sum(cotangent * normed, sum_axes)), ("clip", "row")
    )
    count_all = cotangent.size // norm_gain.shape[0] * lax.axis_size("clip") * lax.axis_size("row")
    factor = (norm_gain * inverse).reshape(gain_shape)
    result = factor * (
        cotangent
        - (totals[0] / count_all).reshape(gain_shape)
        - normed * (totals[1] / count_all).reshape(gain_shape)
    )
    return (result, totals[1], totals[0])


def project(tensor, weight):
    flat_rows = tensor.reshape(-1, tensor.shape[-1])
    return jnp.dot(flat_rows, weight, preferred_element_type=jnp.float32).reshape(
        tensor.shape[:-1] + (weight.shape[1],)
    )


def project_back(cotangent, weight):
    flat_rows = cotangent.reshape(-1, cotangent.shape[-1])
    result = lax.dot_general(
        flat_rows, weight, (((1,), (1,)), ((), ())), preferred_element_type=jnp.float32
    )
    return result.reshape(cotangent.shape[:-1] + (weight.shape[0],))


def outer_sum(tensor, cotangent):
    return lax.dot_general(
        tensor.reshape(-1, tensor.shape[-1]),
        cotangent.reshape(-1, cotangent.shape[-1]),
        (((0,), (0,)), ((), ())),
        preferred_element_type=jnp.float32,
    )


def conv_rows(padded, kernel, precision=None):
    channels = padded.shape[-1]
    kernel_taps = kernel.reshape(3, 3, channels, -1)
    return lax.conv_general_dilated(
        padded,
        kernel_taps,
        (1, 1),
        ((0, 0), (1, 1)),
        dimension_numbers=("NHWC", "HWIO", "NHWC"),
        preferred_element_type=jnp.float32,
        precision=precision,
    )


def flipped(kernel, channels):
    kernel_taps = kernel.reshape(3, 3, channels, -1)
    return jnp.flip(kernel_taps, (0, 1)).transpose(0, 1, 3, 2).reshape(-1, channels)


def kernel_grad(padded, cotangent, precision=None):
    widened = jnp.pad(padded, ((0, 0), (0, 0), (1, 1), (0, 0)))
    result = lax.conv_general_dilated(
        widened,
        cotangent,
        (1, 1),
        "VALID",
        dimension_numbers=("CHWN", "IHWO", "HWNC"),
        preferred_element_type=jnp.float32,
        precision=precision,
    )
    return result.reshape(-1, cotangent.shape[-1])


def pad_rows(tensor):
    return jnp.pad(tensor, ((0, 0), (1, 1), (0, 0), (0, 0)))


def pool_sum(tensor):
    images, height, breadth, channels = tensor.shape
    return tensor.reshape(images, height // 2, 2, breadth // 2, 2, channels).sum(axis=(2, 4))


def spread(tensor, factor):
    return jnp.repeat(jnp.repeat(tensor, factor, axis=1), factor, axis=2)


def fine_halo(tensor):
    return with_halo(tensor, (("row", 1),), 1)


def back_halo(tensor):
    return with_halo(tensor, (("row", 1),), 1)


def per_device(
    frames,
    frame_start,
    boundary_mask,
    stem_weight,
    stem_gain,
    stem_bias,
    block_input,
    w_one,
    w_reduce,
    k_fine,
    k_half,
    k_quarter,
    w_expand,
    w_two,
    w_three,
    gain_one,
    bias_one,
    gain_two,
    bias_two,
    gain_three,
    bias_three,
    stem_cot,
    block_cot,
):
    gathered = (
        lax.all_gather(stem_weight, "clip", axis=0, tiled=True),
        lax.all_gather(w_one, "clip", axis=0, tiled=True),
        lax.all_gather(w_reduce, "clip", axis=0, tiled=True),
        lax.all_gather(k_fine, "clip", axis=0, tiled=True),
        lax.all_gather(k_half, "clip", axis=0, tiled=True),
        lax.all_gather(k_quarter, "clip", axis=0, tiled=True),
        lax.all_gather(w_expand, "clip", axis=0, tiled=True),
        lax.all_gather(w_two, "clip", axis=0, tiled=True),
        lax.all_gather(w_three, "clip", axis=0, tiled=True),
    )
    (
        full_stem,
        full_one,
        full_reduce,
        full_fine,
        full_half,
        full_quarter,
        full_expand,
        full_two,
        full_three,
    ) = gathered
    clip_count = frames.shape[0]
    frame_rows = frames.shape[3]
    columns = frames.shape[4]
    offsets = frame_start[:, :, None] + jnp.arange(WIN, dtype=jnp.int32)
    window = jax.vmap(lambda clip_frames, frame_picks: clip_frames[frame_picks])(frames, offsets)
    window_float = window.astype(jnp.float32)
    center = window_float[:, :, (WIN - 1) // 2]
    differences = window_float[:, :, 1:] - window_float[:, :, :-1]
    stacked = jnp.concatenate([center[:, :, None], differences], axis=2)
    stacked = stacked.reshape(clip_count * SEG, 3 * WIN, frame_rows, columns).astype(jnp.bfloat16)
    padded_stem = with_halo(stacked, (("row", 2),), 3)
    padded_stem = jnp.pad(padded_stem, ((0, 0), (0, 0), (0, 0), (3, 3)))
    stem_kernel = full_stem.reshape(STEM, 3 * WIN, 7, 7)
    stem_pre = lax.conv_general_dilated(
        padded_stem,
        stem_kernel,
        (2, 2),
        "VALID",
        dimension_numbers=("NCHW", "OIHW", "NCHW"),
        preferred_element_type=jnp.float32,
    )
    channel_shape = (1, -1, 1, 1)
    stem_normed, stem_level, stem_inverse = norm_forward(
        stem_pre, stem_gain, stem_bias, (0, 2, 3), channel_shape
    )
    stem_outer = stem_cot.astype(jnp.float32) * silu_slope(stem_level)
    stem_grad, stem_gain_grad, stem_bias_grad = norm_backward(
        stem_outer, stem_normed, stem_gain, stem_inverse, (0, 2, 3), channel_shape
    )
    stem_kernel_grad = lax.conv_general_dilated(
        padded_stem,
        stem_grad.astype(jnp.bfloat16),
        (1, 1),
        "VALID",
        rhs_dilation=(2, 2),
        dimension_numbers=("CNHW", "IOHW", "CNHW"),
        preferred_element_type=jnp.float32,
    )[:, :, :7, :7]
    count_local, block_rows, block_cols, in_channels = block_input.shape
    last_shape = (-1,)
    map_axes = (0, 1, 2)
    first_pre = project(block_input, full_one)
    normed_one, level_one, inverse_one = norm_forward(
        first_pre, gain_one, bias_one, map_axes, last_shape
    )
    hidden_one = jax.nn.silu(level_one).astype(jnp.bfloat16)
    reduced = project(hidden_one, full_reduce)
    red_channels = reduced.shape[-1]
    shaped = reduced.reshape(clip_count, SEG, block_rows, block_cols, red_channels)
    following = jnp.concatenate([shaped[:, 1:], shaped[:, -1:]], axis=1)
    mask_float = boundary_mask.astype(jnp.float32)[:, :, None, None, None]
    change = (
        (mask_float * (following - shaped))
        .reshape(count_local, block_rows, block_cols, red_channels)
        .astype(jnp.bfloat16)
    )
    change_padded = fine_halo(change)
    fine_out = conv_rows(change_padded, full_fine)
    half_map = (pool_sum(change.astype(jnp.float32)) * 0.25).astype(jnp.bfloat16)
    gathered_half = lax.all_gather(half_map, "row", axis=1, tiled=True)
    quarter = pool_sum(gathered_half.astype(jnp.float32)) * 0.25
    quarter_kernel = full_quarter.astype(jnp.float32)
    quarter_padded = pad_rows(quarter)
    coarsest = conv_rows(quarter_padded, quarter_kernel, highest)
    row_start = lax.axis_index("row") * block_rows
    up_quarter = lax.dynamic_slice_in_dim(spread(coarsest, 4), row_start, block_rows, 1)
    half_padded = with_halo(half_map, (("row", 1),), 1)
    coarse = conv_rows(half_padded, full_half)
    up_half = spread(coarse, 2)
    merged = (fine_out + up_half + up_quarter).astype(jnp.bfloat16)
    gate_pre = project(merged, full_expand)
    sigmoid_gate = jax.nn.sigmoid(gate_pre)
    hidden_float = hidden_one.astype(jnp.float32)
    gated_map = (hidden_float * (1.0 + sigmoid_gate)).astype(jnp.bfloat16)
    gated_padded = fine_halo(gated_map)
    second = conv_rows(gated_padded, full_two)
    normed_two, level_two, inverse_two = norm_forward(
        second, gain_two, bias_two, map_axes, last_shape
    )
    hidden_two = jax.nn.silu(level_two).astype(jnp.bfloat16)
    third_pre = project(hidden_two, full_three)
    normed_three, level_three, inverse_three = norm_forward(
        third_pre, gain_three, bias_three, map_axes, last_shape
    )
    summed = level_three + block_input.astype(jnp.float32)
    block_out = jax.nn.silu(summed).astype(jnp.bfloat16)
    grad_summed = block_cot.astype(jnp.float32) * silu_slope(summed)
    grad_third, gain_three_grad, bias_three_grad = norm_backward(
        grad_summed, normed_three, gain_three, inverse_three, map_axes, last_shape
    )
    grad_third = grad_third.astype(jnp.bfloat16)
    three_grad = outer_sum(hidden_two, grad_third)
    grad_level_two = project_back(grad_third, full_three) * silu_slope(level_two)
    grad_second, gain_two_grad, bias_two_grad = norm_backward(
        grad_level_two, normed_two, gain_two, inverse_two, map_axes, last_shape
    )
    grad_second = grad_second.astype(jnp.bfloat16)
    two_grad = kernel_grad(gated_padded, grad_second)
    grad_gated = conv_rows(back_halo(grad_second), flipped(full_two, gated_map.shape[-1]))
    grad_gate = (grad_gated * hidden_float * sigmoid_gate * (1.0 - sigmoid_gate)).astype(
        jnp.bfloat16
    )
    grad_hidden_gate = grad_gated * (1.0 + sigmoid_gate)
    expand_grad = outer_sum(merged, grad_gate)
    grad_merged = project_back(grad_gate, full_expand)
    grad_fine = grad_merged.astype(jnp.bfloat16)
    fine_grad = kernel_grad(change_padded, grad_fine)
    grad_change = conv_rows(back_halo(grad_fine), flipped(full_fine, red_channels))
    canvas = jnp.zeros(
        (count_local, gathered_half.shape[1] * 2, block_cols, red_channels), jnp.float32
    )
    canvas = lax.dynamic_update_slice_in_dim(canvas, grad_merged, row_start, 1)
    canvas_half = pool_sum(canvas)
    grad_coarsest = pool_sum(canvas_half)
    quarter_grad = kernel_grad(quarter_padded, grad_coarsest, highest)
    grad_quarter = conv_rows(
        pad_rows(grad_coarsest), flipped(quarter_kernel, red_channels), highest
    )
    spread_back = spread(grad_quarter, 2) * 0.25
    grad_coarse = pool_sum(grad_merged).astype(jnp.bfloat16)
    half_grad = kernel_grad(half_padded, grad_coarse)
    coarse_padded = with_halo(grad_coarse, (("row", 1),), 1)
    local_half = conv_rows(coarse_padded, flipped(full_half, red_channels))
    grad_half = (
        lax.psum_scatter(
            spread_back.astype(jnp.bfloat16), "row", scatter_dimension=1, tiled=True
        ).astype(jnp.float32)
        + local_half
    )
    grad_change = grad_change + spread(grad_half, 2) * 0.25
    keep_mask = (
        mask_float * (jnp.arange(SEG) < SEG - 1).astype(jnp.float32)[None, :, None, None, None]
    )
    carried = keep_mask * grad_change.reshape(clip_count, SEG, block_rows, block_cols, red_channels)
    grad_reduced = (
        jnp.concatenate([jnp.zeros_like(carried[:, :1]), carried[:, :-1]], axis=1) - carried
    )
    grad_reduced = grad_reduced.reshape(count_local, block_rows, block_cols, red_channels).astype(
        jnp.bfloat16
    )
    reduce_grad = outer_sum(hidden_one, grad_reduced)
    grad_hidden = grad_hidden_gate + project_back(grad_reduced, full_reduce)
    grad_level_one = grad_hidden * silu_slope(level_one)
    grad_first, gain_one_grad, bias_one_grad = norm_backward(
        grad_level_one, normed_one, gain_one, inverse_one, map_axes, last_shape
    )
    grad_first = grad_first.astype(jnp.bfloat16)
    one_grad = outer_sum(block_input, grad_first)
    input_grad = grad_summed + project_back(grad_first, full_one)
    partial_grads = (
        stem_kernel_grad.reshape(STEM, -1),
        one_grad,
        reduce_grad,
        fine_grad,
        half_grad,
        quarter_grad,
        expand_grad,
        two_grad,
        three_grad,
    )
    row_totals = (
        lax.psum(partial_grads[0].astype(jnp.bfloat16), "row").astype(jnp.float32),
        lax.psum(partial_grads[1].astype(jnp.bfloat16), "row").astype(jnp.float32),
        lax.psum(partial_grads[2].astype(jnp.bfloat16), "row").astype(jnp.float32),
        lax.psum(partial_grads[3].astype(jnp.bfloat16), "row").astype(jnp.float32),
        lax.psum(partial_grads[4].astype(jnp.bfloat16), "row").astype(jnp.float32),
        lax.psum(partial_grads[5].astype(jnp.bfloat16), "row").astype(jnp.float32),
        lax.psum(partial_grads[6].astype(jnp.bfloat16), "row").astype(jnp.float32),
        lax.psum(partial_grads[7].astype(jnp.bfloat16), "row").astype(jnp.float32),
        lax.psum(partial_grads[8].astype(jnp.bfloat16), "row").astype(jnp.float32),
    )
    shares = (
        lax.psum_scatter(row_totals[0], "clip", scatter_dimension=0, tiled=True),
        lax.psum_scatter(row_totals[1], "clip", scatter_dimension=0, tiled=True),
        lax.psum_scatter(row_totals[2], "clip", scatter_dimension=0, tiled=True),
        lax.psum_scatter(row_totals[3], "clip", scatter_dimension=0, tiled=True),
        lax.psum_scatter(row_totals[4], "clip", scatter_dimension=0, tiled=True),
        lax.psum_scatter(row_totals[5], "clip", scatter_dimension=0, tiled=True),
        lax.psum_scatter(row_totals[6], "clip", scatter_dimension=0, tiled=True),
        lax.psum_scatter(row_totals[7], "clip", scatter_dimension=0, tiled=True),
        lax.psum_scatter(row_totals[8], "clip", scatter_dimension=0, tiled=True),
    )
    return (
        block_out,
        input_grad,
        shares[0],
        stem_gain_grad,
        stem_bias_grad,
        shares[1],
        shares[2],
        shares[3],
        shares[4],
        shares[5],
        shares[6],
        shares[7],
        shares[8],
        gain_one_grad,
        bias_one_grad,
        gain_two_grad,
        bias_two_grad,
        gain_three_grad,
        bias_three_grad,
    )


def solution(mesh):
    in_specs = (
        P("clip", None, None, "row", None),
        P("clip", None),
        P("clip", None),
        P("clip", None),
        P(),
        P(),
        P("clip", "row", None, None),
        P("clip", None),
        P("clip", None),
        P("clip", None),
        P("clip", None),
        P("clip", None),
        P("clip", None),
        P("clip", None),
        P("clip", None),
        P(),
        P(),
        P(),
        P(),
        P(),
        P(),
        P("clip", None, "row", None),
        P("clip", "row", None, None),
    )
    out_specs = (
        P("clip", "row", None, None),
        P("clip", "row", None, None),
        P("clip", None),
        P(),
        P(),
        P("clip", None),
        P("clip", None),
        P("clip", None),
        P("clip", None),
        P("clip", None),
        P("clip", None),
        P("clip", None),
        P("clip", None),
        P(),
        P(),
        P(),
        P(),
        P(),
        P(),
    )
    return jax.shard_map(
        per_device, mesh=mesh, in_specs=in_specs, out_specs=out_specs, check_vma=False
    )
```

profile of v0, /device:TPU:0, one launch (start us, length us, event | category | flops | bytes accessed | tf_op | source)
XLA Modules:
  0.0 1704.1 jit_solution(8273070794320087949)
XLA Ops:
  9.6 2.8 gather_fusion
  12.4 3.1 convert_element_type.251
  22.4 3.7 collective-permute-start.12
  26.3 21.1 %copy.193 = bf16[8,15,64,256]{1,0,3,2:T(8,128)(2,1)} copy(bf16[8,15,64,256]{3,2,1,0:T(8,128)(2,1)} %bitcast.155) | data formatting | bytes 7864320 | tf_op jit(solution)/shard_map/convert_element_type | solution.py:193
  47.5 33.0 %all_gather.36 = bf16[128,512]{1,0:T(8,128)(2,1)S(1)} all-gather(bf16[16,512]{1,0:T(8,128)(2,1)S(1)} %copy-done.56), channel_id=1, replica_groups=mesh['clip'=8,'row'=4] {'clip'}, dimensions={0}, use_global_device_ids=true | all-gather | bytes 147456 | tf_op jit(solution)/shard_map/all_gather | solution.py:169
  80.4 31.9 %all_gather.32 = bf16[1152,128]{1,0:T(8,128)(2,1)S(1)} all-gather(bf16[144,128]{1,0:T(8,128)(2,1)S(1)} %copy-done.42), channel_id=1, replica_groups=mesh['clip'=8,'row'=4] {'clip'}, dimensions={0}, use_global_device_ids=true | all-gather | bytes 331776 | tf_op jit(solution)/shard_map/all_gather | solution.py:166
  112.3 31.9 %all_gather.34 = bf16[1152,128]{1,0:T(8,128)(2,1)S(1)} all-gather(bf16[144,128]{1,0:T(8,128)(2,1)S(1)} %copy-done.43), channel_id=1, replica_groups=mesh['clip'=8,'row'=4] {'clip'}, dimensions={0}, use_global_device_ids=true | all-gather | bytes 331776 | tf_op jit(solution)/shard_map/all_gather | solution.py:168
  144.2 30.7 %all_gather.31 = bf16[512,128]{1,0:T(8,128)(2,1)S(1)} all-gather(bf16[64,128]{1,0:T(8,128)(2,1)S(1)} %copy-done.57), channel_id=1, replica_groups=mesh['clip'=8,'row'=4] {'clip'}, dimensions={0}, use_global_device_ids=true | all-gather | bytes 147456 | tf_op jit(solution)/shard_map/all_gather | solution.py:165
  174.9 31.9 %all_gather.33 = bf16[1152,128]{1,0:T(8,128)(2,1)S(1)} all-gather(bf16[144,128]{1,0:T(8,128)(2,1)S(1)} %copy-done.44), channel_id=1, replica_groups=mesh['clip'=8,'row'=4] {'clip'}, dimensions={0}, use_global_device_ids=true | all-gather | bytes 331776 | tf_op jit(solution)/shard_map/all_gather | solution.py:167
  206.9 30.5 %all_gather.39 = bf16[64,735]{1,0:T(8,128)(2,1)S(1)} all-gather(bf16[8,735]{1,0:T(8,128)(2,1)S(1)} %copy-done.62), channel_id=1, replica_groups=mesh['clip'=8,'row'=4] {'clip'}, dimensions={0}, use_global_device_ids=true | all-gather | bytes 105840 | tf_op jit(solution)/shard_map/all_gather | solution.py:163
  239.9 2.8 copy.192
  245.0 38.8 %all-reduce.8 = (f32[512]{0:T(512)S(1)}, f32[512]{0:T(512)S(1)}) all-reduce(f32[512]{0:T(512)S(1)} %get-tuple-element.148, f32[512]{0:T(512)S(1)} %get-tuple-element.147), channel_id=1, replica_groups=mesh['clip'=8,'row'=4] {'clip','row'}, use_global_device_ids=true, to_apply=%region_3.4 | all-reduce | flops 1024 | bytes 8192 | tf_op jit(solution)/shard_map/psum | solution.py:34
  286.4 3.0 collective-permute-start.2
  289.5 5.8 all-gather
  297.2 3.0 collective-permute-start
  303.7 4.2 collective-permute-start.4
  308.0 38.1 %fusion.83 = (f32[64]{0:T(128)S(1)}, f32[64]{0:T(128)S(1)}, f32[8,64,32,128]{1,0,3,2:T(8,128)}) fusion(bf16[64,15,7,7]{0,3,2,1:T(8,128)(2,1)} %reshape.377, bf16[8,15,3,256]{1,0,3,2:T(8,128)(2,1)S(1)} %copy.194, bf16[8,15,64,256]{1,0,3,2:T(8,128)(2,1)} %copy.193, bf16[8,15,3,256]{1,0,3,2:T(8,128)(2,1)} %copy.192), kind=kOutput, calls=%fused_computation.167 | convolution fusion | flops 3081363456 | bytes 12784000 | tf_op jit(solution)/shard_map/conv_general_dilated | solution.py:197
  346.1 10.9 copy.197
  357.1 3.3 fusion.89
  360.4 42.4 %all-reduce.7 = (f32[512]{0:T(512)S(1)}, f32[512]{0:T(512)S(1)}) all-reduce(f32[512]{0:T(512)S(1)} %get-tuple-element.146, f32[512]{0:T(512)S(1)} %get-tuple-element.145), channel_id=1, replica_groups=mesh['clip'=8,'row'=4] {'clip','row'}, use_global_device_ids=true, to_apply=%region_9.10 | all-reduce | flops 1024 | bytes 8192 | tf_op jit(solution)/shard_map/psum | solution.py:34
  405.1 50.0 %all-reduce.6 = (f32[2048]{0:T(1024)S(1)}, f32[2048]{0:T(1024)S(1)}) all-reduce(f32[2048]{0:T(1024)S(1)} %get-tuple-element.140, f32[2048]{0:T(1024)S(1)} %get-tuple-element.139), channel_id=1, replica_groups=mesh['clip'=8,'row'=4] {'clip','row'}, use_global_device_ids=true, to_apply=%region_13.14 | all-reduce | flops 4096 | bytes 32768 | tf_op jit(solution)/shard_map/psum | solution.py:34
  455.1 2.6 fusion.85
  457.7 42.0 %all-reduce.5 = (f32[2048]{0:T(1024)S(1)}, f32[2048]{0:T(1024)S(1)}) all-reduce(f32[2048]{0:T(1024)S(1)} %get-tuple-element.138, f32[2048]{0:T(1024)S(1)} %get-tuple-element.137), channel_id=1, replica_groups=mesh['clip'=8,'row'=4] {'clip','row'}, use_global_device_ids=true, to_apply=%region_17.18 | all-reduce | flops 4096 | bytes 32768 | tf_op jit(solution)/shard_map/psum | solution.py:46
  500.0 2.5 fusion.88
  502.5 38.5 %all-reduce.4 = (f32[64]{0:T(128)S(1)}, f32[64]{0:T(128)S(1)}, f32[512]{0:T(512)S(1)}, f32[512]{0:T(512)S(1)}) all-reduce(f32[64]{0:T(128)S(1)} %get-tuple-element.134, f32[64]{0:T(128)S(1)} %get-tuple-element.133, f32[512]{0:T(512)S(1)} %get-tuple-element.144, ...), channel_id=1, replica_groups=mesh['clip'=8,'row'=4] {'clip','row'}, use_global_device_ids=true, to_apply=%region_31.32 | all-reduce | flops 1152 | bytes 9216 | tf_op jit(solution)/shard_map/psum | solution.py:34
  541.8 3.9 convolution_convert_fusion
  547.3 3.0 collective-permute-start.6
  550.4 7.0 fusion.84
  563.9 4.4 collective-permute-start.10
  576.2 4.3 collective-permute-start.8
  580.5 12.9 reduce-scatter.13.cloned.1.call-done
  596.6 39.4 %all-reduce.3 = (f32[64]{0:T(128)S(1)}, f32[64]{0:T(128)S(1)}, f32[512]{0:T(512)S(1)}, f32[512]{0:T(512)S(1)}) all-reduce(f32[64]{0:T(128)S(1)} %get-tuple-element.136, f32[64]{0:T(128)S(1)} %get-tuple-element.135, f32[512]{0:T(512)S(1)} %get-tuple-element.142, ...), channel_id=1, replica_groups=mesh['clip'=8,'row'=4] {'clip','row'}, use_global_device_ids=true, to_apply=%region_37.38 | all-reduce | flops 1152 | bytes 9216 | tf_op jit(solution)/shard_map/psum | solution.py:46
  637.1 8.6 multiply_convert_fusion
  645.7 8.8 copy.198
  654.6 110.7 %fusion.11 = bf16[64,15,7,7]{0,1,3,2:T(8,128)(2,1)S(1)} fusion(bf16[8,64,32,128]{1,0,3,2:T(8,128)(2,1)} %copy.198, bf16[8,15,3,256]{1,0,3,2:T(8,128)(2,1)S(1)} %copy-done.17, bf16[8,15,64,256]{1,0,3,2:T(8,128)(2,1)} %copy.193, bf16[8,15,3,256]{1,0,3,2:T(8,128)(2,1)} %copy.192), kind=kOutput, calls=%fused_computation.27 | convolution fusion | flops 3075119104 | bytes 8589184 | tf_op jit(solution)/shard_map/slice | solution.py:213
  768.4 187.1 %all-reduce.12.cloned.1.call-done = (bf16[64,735]{0,1:T(8,128)(2,1)}, bf16[2048,512]{0,1:T(8,128)(2,1)}, bf16[512,128]{1,0:T(8,128)(2,1)}, bf16[1152,128]{1,0:T(...) async-done(((bf16[64,735]{0,1:T(8,128)(2,1)}, ...) | async-done | bytes 10153872 | tf_op jit(solution)/shard_map/psum | solution.py:345
  955.6 4.2 convert_element_type.260
  967.9 7.4 convert_element_type.276
  975.4 3.5 convolution_add_fusion
  978.9 69.6 %reduce-scatter.15.cloned.1.call-done = f32[256,512]{0,1:T(8,128)} async-done(((f32[2048,512]{0,1:T(8,128)}), f32[256,512]{0,1:T(8,128)}) %reduce-scatter.15.cloned.1.call-update) | async-done | bytes 524304 | tf_op jit(solution)/shard_map/reduce_scatter | solution.py:357
  1050.5 63.1 %reduce-scatter.31.cloned.1.call-done = f32[8,735]{1,0:T(8,128)} async-done(((f32[64,735]{1,0:T(8,128)}), f32[8,735]{1,0:T(8,128)}) %reduce-scatter.31.cloned.1.call-update) | async-done | bytes 23536
  1113.6 64.6 %reduce-scatter.17.cloned.1.call-done = f32[64,128]{1,0:T(8,128)} async-done(((f32[512,128]{1,0:T(8,128)}), f32[64,128]{1,0:T(8,128)}) %reduce-scatter.17.cloned.1.call-update) | async-done | bytes 32784 | tf_op jit(solution)/shard_map/reduce_scatter | solution.py:358
  1178.2 64.5 %reduce-scatter.25.cloned.1.call-done = f32[16,512]{1,0:T(8,128)} async-done(((f32[128,512]{1,0:T(8,128)}), f32[16,512]{1,0:T(8,128)}) %reduce-scatter.25.cloned.1.call-update) | async-done | bytes 32784 | tf_op jit(solution)/shard_map/reduce_scatter | solution.py:362
  1242.7 65.2 %reduce-scatter.19.cloned.1.call-done = f32[144,128]{1,0:T(8,128)} async-done(((f32[1152,128]{1,0:T(8,128)}), f32[144,128]{1,0:T(8,128)}) %reduce-scatter.19.cloned.1.call-update) | async-done | bytes 73744 | tf_op jit(solution)/shard_map/reduce_scatter | solution.py:359
  1307.9 65.1 %reduce-scatter.21.cloned.1.call-done = f32[144,128]{1,0:T(8,128)} async-done(((f32[1152,128]{1,0:T(8,128)}), f32[144,128]{1,0:T(8,128)}) %reduce-scatter.21.cloned.1.call-update) | async-done | bytes 73744 | tf_op jit(solution)/shard_map/reduce_scatter | solution.py:360
  1373.0 65.2 %reduce-scatter.23.cloned.1.call-done = f32[144,128]{1,0:T(8,128)} async-done(((f32[1152,128]{1,0:T(8,128)}), f32[144,128]{1,0:T(8,128)}) %reduce-scatter.23.cloned.1.call-update) | async-done | bytes 73744 | tf_op jit(solution)/shard_map/reduce_scatter | solution.py:361
  1438.2 91.3 %reduce-scatter.29.cloned.1.call-done = f32[64,2048]{1,0:T(8,128)} async-done(((f32[512,2048]{1,0:T(8,128)}), f32[64,2048]{1,0:T(8,128)}) %reduce-scatter.29.cloned.1.call-update) | async-done | bytes 524304 | tf_op jit(solution)/shard_map/reduce_scatter | solution.py:364
  1529.5 167.7 %reduce-scatter.27.cloned.1.call-done = f32[576,512]{1,0:T(8,128)} async-done(((f32[4608,512]{1,0:T(8,128)}), f32[576,512]{1,0:T(8,128)}) %reduce-scatter.27.cloned.1.call-update) | async-done | bytes 1179664 | tf_op jit(solution)/shard_map/reduce_scatter | solution.py:363
  (329 shorter events, 58.3 us)
Async XLA Ops:
  7.2 235.5 %all-gather.5.cloned.1.call-start = ((), (), s32[]{:S(2)}) async-start(), calls=%async_computation.10 | async-start | bytes 2359296 | tf_op jit(solution)/shard_map/all_gather | solution.py:164
  7.9 349.2 %all-gather.7.cloned.1.call-start = ((), (), s32[]{:S(2)}) async-start(), calls=%async_computation.11 | async-start | bytes 5308416 | tf_op jit(solution)/shard_map/all_gather | solution.py:170
  8.7 394.2 %all-gather.9.cloned.1.call-start = ((), (), s32[]{:S(2)}) async-start(), calls=%async_computation.12 | async-start | bytes 2359296 | tf_op jit(solution)/shard_map/all_gather | solution.py:171
  20.5 218.4 %collective-permute-start.13 = (bf16[8,15,3,256]{3,0,2,1:T(8,128)(2,1)S(1)}, bf16[8,15,3,256]{3,0,2,1:T(8,128)(2,1)S(1)}, u32[]{:S(2)}, u32[]{:S(2)}) collective-permute-start(bf16[8,15,3,256]{3,0,2,1:T(8,128)(2,1)S(1)} %copy.191), channel_id=1, source_target_pairs={{1,0},{2,1},{3,2},{5,4},{6,5},{7,6},{9,8},{10,9},{11,10},{13,12},{... | collective-permute-start | bytes 552968 | tf_op jit(solution)/shard_map/ppermute | solution.py:23
  22.4 217.4 %collective-permute-start.12 = (bf16[8,15,3,256]{3,0,2,1:T(8,128)(2,1)}, bf16[8,15,3,256]{3,0,2,1:T(8,128)(2,1)}, u32[]{:S(2)}, u32[]{:S(2)}) collective-permute-start(bf16[8,15,3,256]{3,0,2,1:T(8,128)(2,1)} %copy.190), channel_id=1, source_target_pairs={{0,1},{1,2},{2,3},{4,5},{5,6},{6,7},{8,9},{9,10},{10,11},{12,13},{... | collective-permute-start | bytes 552968 | tf_op jit(solution)/shard_map/ppermute | solution.py:22
  26.2 567.2 %reduce-scatter.13.cloned.1.call-start = ((), (), s32[]{:S(2)}) async-start(), calls=%async_computation.13 | async-start | bytes 40960 | tf_op jit(solution)/shard_map/reduce_scatter | solution.py:308
  26.3 117.9 %copy-start.57 = (bf16[64,128]{1,0:T(8,128)(2,1)S(1)}, bf16[64,128]{1,0:T(8,128)(2,1)}, u32[]{:S(2)}) copy-start(bf16[64,128]{1,0:T(8,128)(2,1)} %param.31) | copy-start | bytes 49156
  26.3 148.6 %copy-start.84 = (s32[1,8]{1,0:T(1,128)S(1)}, s32[1,8]{1,0:T(1,128)}, u32[]{:S(2)}) copy-start(s32[1,8]{1,0:T(1,128)} %param.25) | copy-start | bytes 100
  26.3 148.6 %copy-start.44 = (bf16[144,128]{1,0:T(8,128)(2,1)S(1)}, bf16[144,128]{1,0:T(8,128)(2,1)}, u32[]{:S(2)}) copy-start(bf16[144,128]{1,0:T(8,128)(2,1)} %param.33) | copy-start | bytes 110596
  26.3 180.5 %copy-start.62 = (bf16[8,735]{1,0:T(8,128)(2,1)S(1)}, bf16[8,735]{1,0:T(8,128)(2,1)}, u32[]{:S(2)}) copy-start(bf16[8,735]{1,0:T(8,128)(2,1)} %param.26) | copy-start | bytes 35284
  47.4 236.3 %copy-start.54 = (f32[512]{0:T(512)S(1)}, f32[512]{0:T(512)}, u32[]{:S(2)}) copy-start(f32[512]{0:T(512)} %param.38) | copy-start | bytes 6148
  47.4 236.9 %copy-start.64 = (f32[512]{0:T(512)S(1)}, f32[512]{0:T(512)}, u32[]{:S(2)}) copy-start(f32[512]{0:T(512)} %param.39) | copy-start | bytes 6148
  80.4 221.0 %copy-start.24 = (bf16[128,512]{1,0:T(8,128)(2,1)}, bf16[128,512]{1,0:T(8,128)(2,1)S(1)}, u32[]{:S(2)}) copy-start(bf16[128,512]{1,0:T(8,128)(2,1)S(1)} %all_gather.36) | copy-start | bytes 393220
  112.3 189.1 %copy-start.6 = (bf16[1152,128]{1,0:T(8,128)(2,1)}, bf16[1152,128]{1,0:T(8,128)(2,1)S(1)}, u32[]{:S(2)}) copy-start(bf16[1152,128]{1,0:T(8,128)(2,1)S(1)} %all_gather.32) | copy-start | bytes 884740
  144.1 158.2 %copy-start.8 = (bf16[1152,128]{1,0:T(8,128)(2,1)}, bf16[1152,128]{1,0:T(8,128)(2,1)S(1)}, u32[]{:S(2)}) copy-start(bf16[1152,128]{1,0:T(8,128)(2,1)S(1)} %all_gather.34) | copy-start | bytes 884740
  174.9 127.4 %copy-start.22 = (bf16[512,128]{1,0:T(8,128)(2,1)}, bf16[512,128]{1,0:T(8,128)(2,1)S(1)}, u32[]{:S(2)}) copy-start(bf16[512,128]{1,0:T(8,128)(2,1)S(1)} %all_gather.31) | copy-start | bytes 393220
  239.9 106.2 %copy-start.16 = (bf16[8,15,3,256]{1,0,3,2:T(8,128)(2,1)}, bf16[8,15,3,256]{1,0,3,2:T(8,128)(2,1)S(1)}, u32[]{:S(2)}) copy-start(bf16[8,15,3,256]{1,0,3,2:T(8,128)(2,1)S(1)} %copy.194) | copy-start | bytes 552964
  285.1 15.6 collective-permute-start.3
  286.4 14.3 collective-permute-start.2
  295.9 5.0 collective-permute-start.1
  297.2 3.9 collective-permute-start
  302.4 54.7 %collective-permute-start.5 = (bf16[8,1,8,512]{3,2,1,0:T(8,128)(2,1)S(1)}, bf16[8,1,8,512]{3,2,1,0:T(8,128)(2,1)S(1)}, u32[]{:S(2)}, u32[]{:S(2)}) collective-permute-start(bf16[8,1,8,512]{3,2,1,0:T(8,128)(2,1)S(1)} %get-tuple-element.184), channel_id=1, source_target_pairs={{1,0},{2,1},{3,2},{5,4},{6,5},{7,6},{9,8},{10,9},{11,10},{13,12},{... | collective-permute-start | bytes 196616 | tf_op jit(solution)/shard_map/ppermute | solution.py:23
  303.7 53.3 %collective-permute-start.4 = (bf16[8,1,8,512]{3,2,1,0:T(8,128)(2,1)S(1)}, bf16[8,1,8,512]{3,2,1,0:T(8,128)(2,1)S(1)}, u32[]{:S(2)}, u32[]{:S(2)}) collective-permute-start(bf16[8,1,8,512]{3,2,1,0:T(8,128)(2,1)S(1)} %get-tuple-element.183), channel_id=1, source_target_pairs={{0,1},{1,2},{2,3},{4,5},{5,6},{6,7},{8,9},{9,10},{10,11},{12,13},{... | collective-permute-start | bytes 196616 | tf_op jit(solution)/shard_map/ppermute | solution.py:22
  545.7 14.0 collective-permute-start.7
  547.3 12.5 collective-permute-start.6
  562.6 17.9 %collective-permute-start.11 = (bf16[8,1,4,128]{3,0,2,1:T(8,128)(2,1)S(1)}, bf16[8,1,4,128]{3,0,2,1:T(8,128)(2,1)S(1)}, u32[]{:S(2)}, u32[]{:S(2)}) collective-permute-start(bf16[8,1,4,128]{3,0,2,1:T(8,128)(2,1)S(1)} %bitcast.188), channel_id=1, source_target_pairs={{1,0},{2,1},{3,2},{5,4},{6,5},{7,6},{9,8},{10,9},{11,10},{13,12},{... | collective-permute-start | bytes 24584 | tf_op jit(solution)/shard_map/ppermute | solution.py:23
  563.9 16.6 collective-permute-start.10
  572.8 382.8 %all-reduce.12.cloned.1.call-start = ((), (), s32[]{:S(2)}) async-start(), calls=%async_computation.23 | async-start | bytes 20496384 | tf_op jit(solution)/shard_map/psum | solution.py:345
  574.9 19.4 %collective-permute-start.9 = (bf16[8,1,8,128]{3,0,2,1:T(8,128)(2,1)S(1)}, bf16[8,1,8,128]{3,0,2,1:T(8,128)(2,1)S(1)}, u32[]{:S(2)}, u32[]{:S(2)}) collective-permute-start(bf16[8,1,8,128]{3,0,2,1:T(8,128)(2,1)S(1)} %get-tuple-element.188), channel_id=1, source_target_pairs={{1,0},{2,1},{3,2},{5,4},{6,5},{7,6},{9,8},{10,9},{11,10},{13,12},{... | collective-permute-start | bytes 49160 | tf_op jit(solution)/shard_map/ppermute | solution.py:23
  576.2 18.1 %collective-permute-start.8 = (bf16[8,1,8,128]{3,0,2,1:T(8,128)(2,1)S(1)}, bf16[8,1,8,128]{3,0,2,1:T(8,128)(2,1)S(1)}, u32[]{:S(2)}, u32[]{:S(2)}) collective-permute-start(bf16[8,1,8,128]{3,0,2,1:T(8,128)(2,1)S(1)} %get-tuple-element.187), channel_id=1, source_target_pairs={{0,1},{1,2},{2,3},{4,5},{5,6},{6,7},{8,9},{9,10},{10,11},{12,13},{... | collective-permute-start | bytes 49160 | tf_op jit(solution)/shard_map/ppermute | solution.py:22
  654.5 111.6 %copy-start.14 = (f32[8,2,8,512]{3,2,1,0:T(8,128)S(1)}, f32[8,2,8,512]{3,2,1,0:T(8,128)}, u32[]{:S(2)}) copy-start(f32[8,2,8,512]{3,2,1,0:T(8,128)} %copy-done.12) | copy-start | bytes 786436
  654.5 111.6 %copy-start.32 = (f32[8,2,8,512]{3,2,1,0:T(8,128)S(1)}, f32[8,2,8,512]{3,2,1,0:T(8,128)}, u32[]{:S(2)}) copy-start(f32[8,2,8,512]{3,2,1,0:T(8,128)} %get-tuple-element.208) | copy-start | bytes 786436
  654.5 111.6 %copy-start.47 = (f32[512]{0:T(512)S(1)}, f32[512]{0:T(512)}, u32[]{:S(2)}) copy-start(f32[512]{0:T(512)} %copy-done.45) | copy-start | bytes 6148
  654.5 111.6 %copy-start.50 = (f32[512]{0:T(512)S(1)}, f32[512]{0:T(512)}, u32[]{:S(2)}) copy-start(f32[512]{0:T(512)} %copy-done.48) | copy-start | bytes 6148
  654.5 111.6 %copy-start.66 = (f32[512]{0:T(512)S(1)}, f32[512]{0:T(512)}, u32[]{:S(2)}) copy-start(f32[512]{0:T(512)} %broadcast_multiply_fusion.4) | copy-start | bytes 6148
  654.5 111.6 %copy-start.67 = (f32[512]{0:T(512)S(1)}, f32[512]{0:T(512)}, u32[]{:S(2)}) copy-start(f32[512]{0:T(512)} %broadcast_multiply_fusion.5) | copy-start | bytes 6148
  654.5 111.6 %copy-start.68 = (f32[512]{0:T(512)S(1)}, f32[512]{0:T(512)}, u32[]{:S(2)}) copy-start(f32[512]{0:T(512)} %get-tuple-element.194) | copy-start | bytes 6148
  654.6 111.7 %copy-start.19 = (bf16[8,2,8,2048]{3,2,1,0:T(8,128)(2,1)S(1)}, bf16[8,2,8,2048]{3,2,1,0:T(8,128)(2,1)}, u32[]{:S(2)}) copy-start(bf16[8,2,8,2048]{3,2,1,0:T(8,128)(2,1)} %param.29) | copy-start | bytes 1572868
  768.4 280.1 %reduce-scatter.15.cloned.1.call-start = ((), (), s32[]{:S(2)}) async-start(), calls=%async_computation.14 | async-start | bytes 4718592 | tf_op jit(solution)/shard_map/reduce_scatter | solution.py:357
  959.8 153.7 %reduce-scatter.31.cloned.1.call-start = ((), (), s32[]{:S(2)}) async-start(), calls=%async_computation.22 | async-start | bytes 221184
  960.7 217.4 %reduce-scatter.17.cloned.1.call-start = ((), (), s32[]{:S(2)}) async-start(), calls=%async_computation.15 | async-start | bytes 294912 | tf_op jit(solution)/shard_map/reduce_scatter | solution.py:358
  961.6 281.1 %reduce-scatter.25.cloned.1.call-start = ((), (), s32[]{:S(2)}) async-start(), calls=%async_computation.19 | async-start | bytes 294912 | tf_op jit(solution)/shard_map/reduce_scatter | solution.py:362
  962.4 345.5 %reduce-scatter.19.cloned.1.call-start = ((), (), s32[]{:S(2)}) async-start(), calls=%async_computation.16 | async-start | bytes 663552 | tf_op jit(solution)/shard_map/reduce_scatter | solution.py:359
  963.3 409.6 %reduce-scatter.21.cloned.1.call-start = ((), (), s32[]{:S(2)}) async-start(), calls=%async_computation.17 | async-start | bytes 663552 | tf_op jit(solution)/shard_map/reduce_scatter | solution.py:360
  964.3 473.9 %reduce-scatter.23.cloned.1.call-start = ((), (), s32[]{:S(2)}) async-start(), calls=%async_computation.18 | async-start | bytes 663552 | tf_op jit(solution)/shard_map/reduce_scatter | solution.py:361
  965.3 564.3 %reduce-scatter.29.cloned.1.call-start = ((), (), s32[]{:S(2)}) async-start(), calls=%async_computation.21 | async-start | bytes 4718592 | tf_op jit(solution)/shard_map/reduce_scatter | solution.py:364
  967.9 729.3 %reduce-scatter.27.cloned.1.call-start = ((), (), s32[]{:S(2)}) async-start(), calls=%async_computation.20 | async-start | bytes 10616832 | tf_op jit(solution)/shard_map/reduce_scatter | solution.py:363
  975.4 721.8 %copy-start.1 = (bf16[1,12,3,64,256]{4,3,2,1,0:T(8,128)(2,1)S(1)}, bf16[1,12,3,64,256]{4,3,2,1,0:T(8,128)(2,1)}, u32[]{:S(2)}) copy-start(bf16[1,12,3,64,256]{4,3,2,1,0:T(8,128)(2,1)} %param.23) | copy-start | bytes 3538948
  (71 other events, 1556.3 us)
Sparse Core Ops, SparseCore 0:
  10.2 52.3 all-gather.4
  64.7 86.7 all-gather.6
  153.6 50.8 all-gather.8
  572.9 20.4 reduce-scatter.12
  768.5 186.9 all-reduce.11
  960.0 88.4 reduce-scatter.14
  1052.6 60.8 reduce-scatter.30
  1117.8 60.2 reduce-scatter.16
  1182.4 60.2 reduce-scatter.24
  1246.7 61.1 reduce-scatter.18
  1311.8 61.1 reduce-scatter.20
  1377.0 61.1 reduce-scatter.22
  1442.4 87.0 reduce-scatter.28
  1534.0 163.1 reduce-scatter.26
where the time goes:
time: 1710 us; the launch traced here: 1700 us
  waiting for transfers between devices  918 us (54%)
  blocking collectives  447 us (26%)
  matrix products  183 us (11%)
  local copies, waits for them, and re-layouts  59.5 us (3%)
  other arithmetic  45.5 us (3%)
  starting transfers between devices  35.6 us (2%)
    psum x1, waiting for transfers between devices, per_device(): lax.psum(partial_grads[0].astype(jnp.bfloat16), 'row').astype(jnp.float32)  187 us
    psum x4, blocking collectives, norm_forward(): lax.psum((jnp.sum(pre_act, sum_axes), jnp.sum(pre_act * pre_act, sum_axes...  170 us
    reduce_scatter x1, waiting for transfers between devices, per_device(): lax.psum_scatter(row_totals[7], 'clip', scatter_dimension=0, tiled=True)  168 us
    slice x1, matrix products, per_device(): lax.conv_general_dilated(padded_stem, stem_grad.astype(jnp.bfloat16), (1,...  111 us
    reduce_scatter x1, waiting for transfers between devices, per_device(): lax.psum_scatter(row_totals[8], 'clip', scatter_dimension=0, tiled=True)  91.3 us
    psum x2, blocking collectives, norm_backward(): lax.psum((jnp.sum(cotangent, sum_axes), jnp.sum(cotangent * normed, sum_a...  81.4 us
    reduce_scatter x1, waiting for transfers between devices, per_device(): lax.psum_scatter(row_totals[1], 'clip', scatter_dimension=0, tiled=True)  69.6 us
    reduce_scatter x1, waiting for transfers between devices, per_device(): lax.psum_scatter(row_totals[5], 'clip', scatter_dimension=0, tiled=True)  65.2 us
  transfers between devices with their start and end apart: 28, of which 12 were waited for; matrix products, arithmetic and copies ran while one was open for 8% of the time, Pallas kernels for 0%

commit v1 on v0

v1 whole, which is shorter than its diff:
```python
import jax
import jax.numpy as jnp
from jax import lax
from jax.sharding import PartitionSpec as P

STEM = 64
SEG = 8
WIN = 5


epsilon = 1e-05
highest = lax.Precision.HIGHEST


def with_halo(x, sides, width):
    for axis, dim in sides:
        size, length = (lax.axis_size(axis), x.shape[dim])
        up = [(i, (i + 1) % size) for i in range(size - 1)]
        down = [(j, i) for i, j in up]
        last = lax.slice_in_dim(x, length - width, length, axis=dim)
        leading = lax.slice_in_dim(x, 0, width, axis=dim)
        before = lax.ppermute(last, axis, up)
        after = lax.ppermute(leading, axis, down)
        x = jnp.concatenate([before, x, after], axis=dim)
    return x


def silu_slope(values):
    sigmoid_val = jax.nn.sigmoid(values)
    return sigmoid_val * (1.0 + values * (1.0 - sigmoid_val))


def project(tensor, weight):
    flat_rows = tensor.reshape(-1, tensor.shape[-1])
    return jnp.dot(flat_rows, weight, preferred_element_type=jnp.float32).reshape(
        tensor.shape[:-1] + (weight.shape[1],)
    )


def project_back(cotangent, weight):
    flat_rows = cotangent.reshape(-1, cotangent.shape[-1])
    result = lax.dot_general(
        flat_rows, weight, (((1,), (1,)), ((), ())), preferred_element_type=jnp.float32
    )
    return result.reshape(cotangent.shape[:-1] + (weight.shape[0],))


def outer_sum(tensor, cotangent):
    return lax.dot_general(
        tensor.reshape(-1, tensor.shape[-1]),
        cotangent.reshape(-1, cotangent.shape[-1]),
        (((0,), (0,)), ((), ())),
        preferred_element_type=jnp.float32,
    )


def conv_same(padded, kernel, precision=None):
    channels = padded.shape[-1]
    kernel_taps = kernel.reshape(3, 3, channels, -1)
    return lax.conv_general_dilated(
        padded,
        kernel_taps,
        (1, 1),
        ((1, 1), (1, 1)),
        dimension_numbers=("NHWC", "HWIO", "NHWC"),
        preferred_element_type=jnp.float32,
        precision=precision,
    )


def flipped(kernel, channels):
    kernel_taps = kernel.reshape(3, 3, channels, -1)
    return jnp.flip(kernel_taps, (0, 1)).transpose(0, 1, 3, 2).reshape(-1, channels)


def kernel_grad(padded, cotangent, precision=None):
    widened = jnp.pad(padded, ((0, 0), (1, 1), (1, 1), (0, 0)))
    result = lax.conv_general_dilated(
        widened,
        cotangent,
        (1, 1),
        "VALID",
        dimension_numbers=("CHWN", "IHWO", "HWNC"),
        preferred_element_type=jnp.float32,
        precision=precision,
    )
    return result.reshape(-1, cotangent.shape[-1])


def pool_sum(tensor):
    images, height, breadth, channels = tensor.shape
    return tensor.reshape(images, height // 2, 2, breadth // 2, 2, channels).sum(axis=(2, 4))


def spread(tensor, factor):
    return jnp.repeat(jnp.repeat(tensor, factor, axis=1), factor, axis=2)


def exchange(blocks, axis):
    return lax.all_to_all(blocks, axis, 0, 0)


def to_all(part, axis):
    size = lax.axis_size(axis)
    return exchange(jnp.broadcast_to(part[None], (size,) + part.shape), axis)


def total(sums, axis):
    flat = jnp.concatenate([entry.reshape(-1) for entry in sums])
    rows = jnp.pad(flat, (0, -flat.size % 1024)).reshape(-1, 128)
    flat = jnp.sum(to_all(rows, axis), 0).reshape(-1)
    results, start = [], 0
    for entry in sums:
        results.append(flat[start : start + entry.size].reshape(entry.shape))
        start += entry.size
    return results


def moments(values, axes):
    return (jnp.sum(values, axes), jnp.sum(values * values, axes))


def statistics(totals, count):
    mean = totals[0] / count
    return mean, lax.rsqrt(totals[1] / count - mean * mean + epsilon)


def gather_pair(shard):
    side = lax.rem(lax.axis_index("row"), 2)
    half = shard.shape[0] // 2
    mine = to_all(lax.dynamic_slice_in_dim(shard, side * half, half, 0), "clip")
    size = lax.axis_size("row")
    other = lax.ppermute(mine, "row", [(i, i ^ 1) for i in range(size)])
    lower = jnp.where(side == 0, mine, other)
    upper = jnp.where(side == 0, other, mine)
    return jnp.stack([lower, upper], 1).reshape((mine.shape[0], 2 * half) + mine.shape[2:])


def strided(vector, clips, rows, place):
    return lax.dynamic_index_in_dim(
        vector.reshape(clips, rows, -1), place, 1, keepdims=False
    ).reshape(-1)


def per_device(
    frames,
    frame_start,
    boundary_mask,
    stem_weight,
    stem_gain,
    stem_bias,
    block_input,
    w_one,
    w_reduce,
    k_fine,
    k_half,
    k_quarter,
    w_expand,
    w_two,
    w_three,
    gain_one,
    bias_one,
    gain_two,
    bias_two,
    gain_three,
    bias_three,
    stem_cot,
    block_cot,
):
    bf16, f32 = jnp.bfloat16, jnp.float32
    nc, nr = lax.axis_size("clip"), lax.axis_size("row")
    place = lax.axis_index("row")
    both = ("clip", "row")
    clip_count = frames.shape[0]
    images, block_rows, cols, c_in = block_input.shape
    mid = gain_one.shape[0]
    red = w_reduce.shape[1]
    height = block_rows * nr
    mid_r, in_r = mid // nr, c_in // nr
    step = c_in // (nc * nr)
    pixels = images * height * cols
    own = images * block_rows * cols
    map_count = pixels * nc

    full_stem = to_all(stem_weight, "clip").reshape(STEM, -1)
    full_one = gather_pair(w_one).reshape(c_in, mid)
    parts = (w_reduce, k_fine, k_half, k_quarter, w_expand.reshape(-1, red))
    packed = gather_pair(jnp.concatenate(parts, 0))
    full_small, start = [], 0
    for part in parts:
        full_small.append(packed[:, start : start + part.shape[0]].reshape(-1, red))
        start += part.shape[0]
    full_reduce, full_fine, full_half, full_quarter, full_expand = full_small
    full_expand = full_expand.reshape(red, mid)
    two_r = to_all(
        lax.dynamic_slice_in_dim(w_two, place * mid_r, mid_r, 1), "clip"
    ).reshape(-1, mid_r)
    three_r = to_all(
        lax.dynamic_index_in_dim(
            w_three.reshape(-1, nc, nr, step), place, 2, keepdims=False
        ).reshape(-1, in_r),
        "clip",
    ).reshape(mid, in_r)

    def to_channels(tensor):
        return tensor.reshape(images, block_rows, cols, nc, nr, step).transpose(4, 0, 1, 2, 3, 5)

    def from_pixels(blocks):
        return blocks.swapaxes(0, 1).reshape(images, height, cols, -1)

    swapped = exchange(
        jnp.stack([to_channels(block_input), to_channels(block_cot)], 1), "row"
    ).reshape(nr, 2, images, block_rows, cols, in_r)
    input_r = from_pixels(swapped[:, 0])
    cot_r = from_pixels(swapped[:, 1])

    frame_rows = frames.shape[3]
    columns = frames.shape[4]
    offsets = frame_start[:, :, None] + jnp.arange(WIN, dtype=jnp.int32)
    window = jax.vmap(lambda clip_frames, frame_picks: clip_frames[frame_picks])(frames, offsets)
    window_float = window.astype(f32)
    center = window_float[:, :, (WIN - 1) // 2]
    differences = window_float[:, :, 1:] - window_float[:, :, :-1]
    stacked = jnp.concatenate([center[:, :, None], differences], axis=2)
    stacked = stacked.reshape(clip_count * SEG, 3 * WIN, frame_rows, columns).astype(bf16)
    padded_stem = with_halo(stacked, (("row", 2),), 3)
    padded_stem = jnp.pad(padded_stem, ((0, 0), (0, 0), (0, 0), (3, 3)))
    stem_kernel = full_stem.reshape(STEM, 3 * WIN, 7, 7)
    stem_pre = lax.conv_general_dilated(
        padded_stem,
        stem_kernel,
        (2, 2),
        "VALID",
        dimension_numbers=("NCHW", "OIHW", "NCHW"),
        preferred_element_type=f32,
    )
    column = (1, -1, 1, 1)
    stem_count = stem_pre.size // STEM * nc * nr
    stem_mean, stem_inverse = statistics(total(moments(stem_pre, (0, 2, 3)), both), stem_count)
    stem_normed = (stem_pre - stem_mean.reshape(column)) * stem_inverse.reshape(column)
    stem_level = stem_normed * stem_gain.reshape(column) + stem_bias.reshape(column)
    stem_outer = stem_cot.astype(f32) * silu_slope(stem_level)
    stem_bias_grad, stem_gain_grad = total(
        (jnp.sum(stem_outer, (0, 2, 3)), jnp.sum(stem_outer * stem_normed, (0, 2, 3))), both
    )
    stem_grad = (stem_gain * stem_inverse).reshape(column) * (
        stem_outer
        - (stem_bias_grad / stem_count).reshape(column)
        - stem_normed * (stem_gain_grad / stem_count).reshape(column)
    )
    stem_kernel_grad = lax.conv_general_dilated(
        padded_stem,
        stem_grad.astype(bf16),
        (1, 1),
        "VALID",
        rhs_dilation=(2, 2),
        dimension_numbers=("CNHW", "IOHW", "CNHW"),
        preferred_element_type=f32,
    )[:, :, :7, :7]

    first_pre = project(block_input, full_one)
    mean_one, inverse_one = statistics(total(moments(first_pre, (0, 1, 2)), both), map_count)
    normed_one = (first_pre - mean_one) * inverse_one
    level_one = normed_one * gain_one + bias_one
    hidden_one = jax.nn.silu(level_one).astype(bf16)
    shaped = project(hidden_one, full_reduce).reshape(clip_count, SEG, block_rows, cols, red)
    following = jnp.concatenate([shaped[:, 1:], shaped[:, -1:]], axis=1)
    mask_float = boundary_mask.astype(f32)[:, :, None, None, None]
    change = (mask_float * (following - shaped)).reshape(images, block_rows, cols, red)
    change = from_pixels(lax.all_gather(change.astype(bf16), "row"))
    row_start = place * block_rows

    def own_rows(tensor):
        return lax.dynamic_slice_in_dim(tensor, row_start, block_rows, 1)

    half_map = (pool_sum(change.astype(f32)) * 0.25).astype(bf16)
    quarter = pool_sum(half_map.astype(f32)) * 0.25
    quarter_kernel = full_quarter.astype(f32)
    fine_out = conv_same(change, full_fine)
    coarse = conv_same(half_map, full_half)
    coarsest = conv_same(quarter, quarter_kernel, highest)
    merged = own_rows(fine_out + spread(coarse, 2) + spread(coarsest, 4)).astype(bf16)
    sigmoid_gate = jax.nn.sigmoid(project(merged, full_expand))
    hidden_float = hidden_one.astype(f32)
    gated = (hidden_float * (1.0 + sigmoid_gate)).astype(bf16)
    gated = from_pixels(lax.all_gather(gated, "row"))
    second = conv_same(gated, two_r)

    def mid_slice(vector):
        return lax.dynamic_slice_in_dim(vector, place * mid_r, mid_r, 0)

    gain_two_r = mid_slice(gain_two)
    mean_two, inverse_two = statistics(total(moments(second, (0, 1, 2)), "clip"), map_count)
    normed_two = (second - mean_two) * inverse_two
    level_two = normed_two * gain_two_r + mid_slice(bias_two)
    hidden_two = jax.nn.silu(level_two).astype(bf16).reshape(pixels, mid_r)
    hidden_two = lax.all_gather(hidden_two, "row").swapaxes(0, 1).reshape(pixels, mid)
    third = jnp.dot(hidden_two, three_r, preferred_element_type=f32)
    gain_three_r = strided(gain_three, nc, nr, place)
    bias_three_r = strided(bias_three, nc, nr, place)
    mean_three, inverse_three = statistics(total(moments(third, 0), "clip"), map_count)
    normed_three = (third - mean_three) * inverse_three
    summed = normed_three * gain_three_r + bias_three_r + input_r.reshape(pixels, in_r).astype(f32)
    block_out_r = jax.nn.silu(summed).astype(bf16)
    grad_summed = cot_r.reshape(pixels, in_r).astype(f32) * silu_slope(summed)
    bias_three_grad, gain_three_grad = total(
        (jnp.sum(grad_summed, 0), jnp.sum(grad_summed * normed_three, 0)), "clip"
    )

    def to_pixels(tensor):
        return tensor.reshape(images, nr, block_rows, cols, in_r).swapaxes(0, 1)

    returned = exchange(
        jnp.stack([to_pixels(block_out_r), to_pixels(grad_summed.astype(bf16))], 1), "row"
    )
    returned = returned.reshape(nr, 2, images, block_rows, cols, nc, step)
    returned = returned.transpose(1, 2, 3, 4, 5, 0, 6).reshape(2, images, block_rows, cols, c_in)
    block_out = returned[0]

    grad_third = (
        gain_three_r
        * inverse_three
        * (
            grad_summed
            - bias_three_grad / map_count
            - normed_three * (gain_three_grad / map_count)
        )
    ).astype(bf16)
    three_grad = jnp.sum(
        exchange(outer_sum(hidden_two, grad_third).astype(bf16).reshape(nc, -1, in_r), "clip"),
        0,
        dtype=f32,
    )
    back_two = project_back(grad_third, three_r).astype(bf16)
    back_two = jnp.sum(
        exchange(back_two.reshape(pixels, nr, mid_r).swapaxes(0, 1), "row"), 0, dtype=f32
    ).reshape(level_two.shape)
    grad_two = back_two * silu_slope(level_two)
    bias_two_grad, gain_two_grad = total(
        (jnp.sum(grad_two, (0, 1, 2)), jnp.sum(grad_two * normed_two, (0, 1, 2))), "clip"
    )
    grad_second = (
        gain_two_r
        * inverse_two
        * (grad_two - bias_two_grad / map_count - normed_two * (gain_two_grad / map_count))
    ).astype(bf16)
    two_grad = jnp.sum(
        exchange(kernel_grad(gated, grad_second).astype(bf16).reshape(nc, -1, mid_r), "clip"),
        0,
        dtype=f32,
    )
    grad_gated = conv_same(grad_second, flipped(two_r, mid)).astype(bf16)
    grad_gated = grad_gated.reshape(images, nr, block_rows, cols, mid).swapaxes(0, 1)
    grad_gated = jnp.sum(exchange(grad_gated, "row"), 0, dtype=f32)
    grad_gate = (grad_gated * hidden_float * sigmoid_gate * (1.0 - sigmoid_gate)).astype(bf16)
    expand_grad = outer_sum(merged, grad_gate)
    grad_fine = project_back(grad_gate, full_expand).astype(bf16)
    grad_fine = from_pixels(lax.all_gather(grad_fine, "row"))
    grad_coarse = pool_sum(grad_fine.astype(f32))
    grad_coarsest = pool_sum(grad_coarse)
    grad_coarse = grad_coarse.astype(bf16)
    grad_half = conv_same(grad_coarse, flipped(full_half, red)) + 0.25 * spread(
        conv_same(grad_coarsest, flipped(quarter_kernel, red), highest), 2
    )
    grad_change = own_rows(
        conv_same(grad_fine, flipped(full_fine, red)) + 0.25 * spread(grad_half, 2)
    )
    keep_mask = mask_float * (jnp.arange(SEG) < SEG - 1).astype(f32)[None, :, None, None, None]
    carried = keep_mask * grad_change.reshape(shaped.shape)
    grad_reduced = (
        jnp.concatenate([jnp.zeros_like(carried[:, :1]), carried[:, :-1]], axis=1) - carried
    )
    grad_reduced = grad_reduced.reshape(images, block_rows, cols, red).astype(bf16)
    reduce_grad = outer_sum(hidden_one, grad_reduced)
    grad_hidden = grad_gated * (1.0 + sigmoid_gate) + project_back(grad_reduced, full_reduce)
    grad_one = grad_hidden * silu_slope(level_one)
    bias_one_grad, gain_one_grad = total(
        (jnp.sum(grad_one, (0, 1, 2)), jnp.sum(grad_one * normed_one, (0, 1, 2))), both
    )
    grad_first = (
        gain_one
        * inverse_one
        * (grad_one - bias_one_grad / map_count - normed_one * (gain_one_grad / map_count))
    ).astype(bf16)
    input_grad = returned[1].astype(f32) + project_back(grad_first, full_one)
    grad_first = from_pixels(lax.all_gather(grad_first, "row"))
    one_grad = outer_sum(input_r, grad_first).astype(bf16).reshape(nc, -1, mid)

    def padded_parts(gradient):
        shares = gradient.reshape(nc, -1)
        shares = jnp.pad(shares, ((0, 0), (0, -shares.shape[1] % (nr * 8 * red))))
        return shares.reshape(nc, nr, -1, red)

    def quarter_of(gradient):
        return lax.dynamic_index_in_dim(padded_parts(gradient), place, 1, keepdims=False)

    def share_of(blocks, like):
        return blocks.reshape(-1)[: like.size].reshape(like.shape)

    clip_parts = [
        one_grad.reshape(nc, -1, red),
        quarter_of(kernel_grad(change, grad_fine)).astype(bf16),
        quarter_of(kernel_grad(half_map, grad_coarse)).astype(bf16),
        quarter_of(kernel_grad(quarter, grad_coarsest, highest)).astype(bf16),
    ]
    clip_sizes = [part.shape[1] for part in clip_parts]
    clip_sum = jnp.sum(exchange(jnp.concatenate(clip_parts, 1), "clip"), 0, dtype=f32)
    both_parts = [
        padded_parts(part).reshape(nc * nr, -1, red)
        for part in (reduce_grad, expand_grad, stem_kernel_grad)
    ]
    both_sizes = [part.shape[1] for part in both_parts]
    both_sum = jnp.sum(
        exchange(jnp.concatenate(both_parts, 1).astype(bf16), both), 0, dtype=f32
    )
    shares_a = lax.all_gather(
        jnp.concatenate([two_grad.reshape(-1, red), three_grad.reshape(-1, red)], 0).astype(bf16),
        "row",
    ).astype(f32)
    two_rows = two_grad.size // red
    two_share = shares_a[:, :two_rows].reshape(nr, -1, mid_r).swapaxes(0, 1).reshape(-1, mid)
    three_share = shares_a[:, two_rows:].reshape(nr, -1, nc, step)
    three_share = three_share.transpose(1, 2, 0, 3).reshape(-1, c_in)
    shares_b = lax.all_gather(
        jnp.concatenate([clip_sum, both_sum], 0).astype(bf16), "row"
    ).astype(f32)
    cut = []
    start = 0
    for size in clip_sizes + both_sizes:
        cut.append(shares_b[:, start : start + size])
        start += size
    one_share = cut[0].reshape(-1, mid)
    fine_share, half_share, quarter_share, reduce_share, expand_share, stem_share = (
        share_of(blocks, like)
        for blocks, like in zip(
            cut[1:], (k_fine, k_half, k_quarter, w_reduce, w_expand, stem_weight)
        )
    )
    vectors = jnp.concatenate([gain_two_grad, bias_two_grad, gain_three_grad, bias_three_grad])
    vectors = lax.all_gather(vectors.reshape(-1, red), "row").reshape(nr, -1)
    gain_two_full = vectors[:, :mid_r].reshape(-1)
    bias_two_full = vectors[:, mid_r : 2 * mid_r].reshape(-1)
    gain_three_full = vectors[:, 2 * mid_r : 2 * mid_r + in_r].reshape(nr, nc, step)
    bias_three_full = vectors[:, 2 * mid_r + in_r :].reshape(nr, nc, step)
    return (
        block_out,
        input_grad,
        stem_share,
        stem_gain_grad,
        stem_bias_grad,
        one_share,
        reduce_share,
        fine_share,
        half_share,
        quarter_share,
        expand_share,
        two_share,
        three_share,
        gain_one_grad,
        bias_one_grad,
        gain_two_full,
        bias_two_full,
        gain_three_full.swapaxes(0, 1).reshape(-1),
        bias_three_full.swapaxes(0, 1).reshape(-1),
    )


def solution(mesh):
    in_specs = (
        P("clip", None, None, "row", None),
        P("clip", None),
        P("clip", None),
        P("clip", None),
        P(),
        P(),
        P("clip", "row", None, None),
        P("clip", None),
        P("clip", None),
        P("clip", None),
        P("clip", None),
        P("clip", None),
        P("clip", None),
        P("clip", None),
        P("clip", None),
        P(),
        P(),
        P(),
        P(),
        P(),
        P(),
        P("clip", None, "row", None),
        P("clip", "row", None, None),
    )
    out_specs = (
        P("clip", "row", None, None),
        P("clip", "row", None, None),
        P("clip", None),
        P(),
        P(),
        P("clip", None),
        P("clip", None),
        P("clip", None),
        P("clip", None),
        P("clip", None),
        P("clip", None),
        P("clip", None),
        P("clip", None),
        P(),
        P(),
        P(),
        P(),
        P(),
        P(),
    )
    return jax.shard_map(
        per_device, mesh=mesh, in_specs=in_specs, out_specs=out_specs, check_vma=False
    )
```

time: 1710 us -> 652 us (0.38)
  waiting for transfers between devices: 918 us -> 105 us
  blocking collectives: 447 us -> 71.6 us
  local copies, waits for them, and re-layouts: 59.5 us -> 138 us
  starting transfers between devices: 35.6 us -> 93.9 us
    reduce_scatter x9 -> x0, waiting for transfers between devices: 666 us -> none  [the longest x1 168 us: per_device(): lax.psum_scatter(row_totals[7], 'clip', scatter_dimension=0, tiled=True)]
    psum x6 -> x0, blocking collectives: 251 us -> none  [the longest x4 170 us: norm_forward(): lax.psum((jnp.sum(pre_act, sum_axes), jnp.sum(pre_act * pre_act, sum_axes...]
    psum x1 -> x0, waiting for transfers between devices: 187 us -> none  [per_device(): lax.psum(partial_grads[0].astype(jnp.bfloat16), 'row').astype(jnp.float32)]
    all_gather x7 -> x8, blocking collectives: 196 us -> 71.6 us  [the longest x1 16.5 us: per_device(): gated = from_pixels(lax.all_gather(gated, 'row'))]
    all_to_all x0 -> x21, waiting for transfers between devices: none -> 105 us  [exchange(): return lax.all_to_all(blocks, axis, 0, 0)]
    all_to_all x0 -> x21, starting transfers between devices: none -> 89.4 us  [exchange(): return lax.all_to_all(blocks, axis, 0, 0)]
    unnamed x15 -> x0, waiting for transfers between devices: 64.6 us -> none
    reshape x2 -> x24, local copies, waits for them, and re-layouts: 0.8 us -> 26.2 us  [the longest x2 6.42 us: per_device(): returned = returned.reshape(nr, 2, images, block_rows, cols, nc, step)]
  transfers between devices with their start and end apart: 28 -> 25, of which waited for: 12 -> 13; matrix products, arithmetic and copies ran while one was open for 8% -> 46% of each run, Pallas kernels for 0% -> 0%
where the time goes in v1:
time: 652 us; the launch traced here: 645 us
  matrix products  177 us (27%)
  local copies, waits for them, and re-layouts  138 us (21%)
  waiting for transfers between devices  105 us (16%)
  starting transfers between devices  93.9 us (14%)
  blocking collectives  71.6 us (11%)
  other arithmetic  58.2 us (9%)
    slice x1, matrix products, per_device(): lax.conv_general_dilated(padded_stem, stem_grad.astype(bf16), (1, 1), 'VA...  111 us
    all_to_all x21, waiting for transfers between devices, exchange(): return lax.all_to_all(blocks, axis, 0, 0)  105 us
    all_to_all x21, starting transfers between devices, exchange(): return lax.all_to_all(blocks, axis, 0, 0)  89.4 us
    conv_general_dilated x1, matrix products, per_device(): lax.conv_general_dilated(padded_stem, stem_kernel, (2, 2), 'VALID', dimen...  40 us
    convert_element_type x1, local copies, waits for them, and re-layouts, per_device(): stacked.reshape(clip_count * SEG, 3 * WIN, frame_rows, columns).astype(bf16)  20.9 us
    all_gather x1, blocking collectives, per_device(): gated = from_pixels(lax.all_gather(gated, 'row'))  16.5 us
    all_gather x1, blocking collectives, per_device(): grad_fine = from_pixels(lax.all_gather(grad_fine, 'row'))  14.4 us
    unnamed x206, local copies, waits for them, and re-layouts  14 us
  transfers between devices with their start and end apart: 25, of which 13 were waited for; matrix products, arithmetic and copies ran while one was open for 46% of the time, Pallas kernels for 0%

profile of v1, /device:TPU:0, one launch (start us, length us, event | category | flops | bytes accessed | tf_op | source)
XLA Modules:
  0.0 645.4 jit_solution(9231464022677437465)
XLA Ops:
  2.1 7.3 %all-to-all-start.15 = ((bf16[8,8,735]{2,1,0:T(8,128)(2,1)}), bf16[8,8,735]{2,1,0:T(8,128)(2,1)S(1)}, u32[]{:S(2)}, u32[]{:S(2)}) async-start(bf16[8,8,735]{2,1,0:T(8,128)(2,1)} %broadcast_in_dim.73), calls=%async_computation.15 | async-start | bytes 196608 | tf_op jit(solution)/shard_map/all_to_all | solution.py:100
  25.7 20.9 %copy.345 = bf16[8,15,64,256]{1,0,3,2:T(8,128)(2,1)} copy(bf16[8,15,64,256]{3,2,1,0:T(8,128)(2,1)} %bitcast.359) | data formatting | bytes 7864320 | tf_op jit(solution)/shard_map/convert_element_type | solution.py:225
  52.2 40.0 %fusion.72 = (f32[64]{0:T(128)S(1)}, f32[64]{0:T(128)S(1)}, f32[8,64,32,128]{1,0,3,2:T(8,128)}) fusion(bf16[64,15,7,7]{0,3,2,1:T(8,128)(2,1)S(1)} %reshape_reshape.66, bf16[8,15,3,256]{1,0,3,2:T(8,128)(2,1)} %copy.346, bf16[8,15,64,256]{1,0,3,2:T(8,128)(2,1)} %copy.345, bf16[8,15,3,256]{1,0,3,2:T(8,128)(2,1)S(1)} %copy.344), kind=kOutput, calls=%fused_computation.216 | convolution fusion | flops 3081363456 | bytes 12784000 | tf_op jit(solution)/shard_map/conv_general_dilated | solution.py:229
  93.0 6.0 all-to-all-start.16
  99.2 8.1 %all-to-all-done.16 = f32[32,8,128]{2,1,0:T(8,128)S(1)} async-done(((f32[32,8,128]{2,1,0:T(8,128)}), f32[32,8,128]{2,1,0:T(8,128)S(1)}, u32[]{:S(2)}, u32[]{:S(2)}) %all-to-all-start.16) | async-done | bytes 131104 | tf_op jit(solution)/shard_map/all_to_all | solution.py:100
  108.2 4.4 all-to-all-start.2
  119.3 10.9 %copy.349 = f32[8,64,32,128]{3,2,1,0:T(8,128)} copy(f32[8,64,32,128]{1,0,3,2:T(8,128)} %get-tuple-element.101) | data formatting | bytes 16777216 | tf_op jit(solution)/shard_map/conv_general_dilated | solution.py:229
  132.0 6.0 all-to-all-start
  138.0 10.1 %fusion.73 = (f32[64]{0:T(128)S(1)}, f32[64]{0:T(128)S(1)}, f32[8,64,32,128]{3,2,1,0:T(8,128)}) fusion(f32[64]{0:T(128)S(1)} %get-tuple-element.34, f32[8,64,32,128]{3,2,1,0:T(8,128)} %copy.349, f32[64]{0:T(128)S(1)} %get-tuple-element.82, f32[64]{0:T(128)S(1)} %copy-done.92, f32[64]{0:T(128)S(1)} %copy-done.90, bf16[8,64,32,128]{3,2,1,0:T(8,128)(2,1)} %param.44), kind=kLoop, calls=%fused_computation.217 | loop fusion | flops 33554304 | bytes 20973056 | tf_op jit(solution)/shard_map/reduce_sum | solution.py:244
  148.2 15.7 %all-to-all-done = bf16[8,128,512]{2,1,0:T(8,128)(2,1)S(1)} async-done(((bf16[8,128,512]{2,1,0:T(8,128)(2,1)}), bf16[8,128,512]{2,1,0:T(8,128)(2,1)S(1)}, u32[]{:S(2)}, u32[]{:S(2)}) %all-to-all-start) | async-done | bytes 1048608 | tf_op jit(solution)/shard_map/all_to_all | solution.py:100
  178.0 4.4 reshape.734
  188.8 5.8 all-to-all-start.1
  194.8 8.1 %all-to-all-done.1 = f32[32,8,128]{2,1,0:T(8,128)S(1)} async-done(((f32[32,8,128]{2,1,0:T(8,128)}), f32[32,8,128]{2,1,0:T(8,128)S(1)}, u32[]{:S(2)}, u32[]{:S(2)}) %all-to-all-start.1) | async-done | bytes 131104 | tf_op jit(solution)/shard_map/all_to_all | solution.py:100
  204.0 3.6 all-to-all-start.3
  208.6 5.4 all_gather.36
  215.5 21.2 %all-to-all-done.3 = bf16[8,576,128]{2,1,0:T(8,128)(2,1)S(1)} async-done(((bf16[8,576,128]{2,1,0:T(8,128)(2,1)}), bf16[8,576,128]{2,1,0:T(8,128)(2,1)S(1)}, u32[]{:S(2)}, u32[]{:S(2)}) %all-to-all-start.3) | async-done | bytes 1179680 | tf_op jit(solution)/shard_map/all_to_all | solution.py:100
  236.8 3.5 all-to-all-start.7
  241.9 16.5 %all-gather = bf16[32,2,8,512]{3,2,1,0:T(8,128)(2,1)S(1)} all-gather(bf16[8,2,8,512]{3,2,1,0:T(8,128)(2,1)S(1)} %get-tuple-element.96), channel_id=2, replica_groups=mesh['clip'=8,'row'=4] {'row'}, dimensions={0}, use_global_device_ids=true | all-gather | bytes 655360 | tf_op jit(solution)/shard_map/all_gather | solution.py:286
  260.8 3.6 all-to-all-start.4
  271.9 5.8 all-to-all-start.5
  281.3 6.5 %all_gather.39 = bf16[4,512,128]{2,1,0:T(8,128)(2,1)S(1)} all-gather(bf16[1,512,128]{2,1,0:T(8,128)(2,1)S(1)} %bitcast.400), channel_id=1, replica_groups=mesh['clip'=8,'row'=4] {'row'}, dimensions={0}, use_global_device_ids=true | all-gather | bytes 655360 | tf_op jit(solution)/shard_map/all_gather | solution.py:297
  288.1 4.2 all-to-all-done.5
  293.4 3.6 all-to-all-start.6
  299.0 4.7 all-to-all-done.6
  306.9 3.3 all-to-all-start.9
  310.3 8.6 %multiply_convert_fusion = bf16[8,64,32,128]{3,2,1,0:T(8,128)(2,1)} fusion(f32[8,64,32,128]{3,2,1,0:T(8,128)} %get-tuple-element.39, f32[8,64,32,128]{3,2,1,0:T(8,128)} %copy.349, f32[64]{0:T(128)S(1)} %get-tuple-element.80, f32[64]{0:T(128)S(1)} %get-tuple-element.35, f32[64]{0:T(128)S(1)} %copy-done.80, f32[64]{0:T(128)S(1)} %copy-done.82, f32[64]{0:T(128)S(1)} %copy-done.87), kind=kLoop, calls=%fused_computation.5 | loop fusion | flops 14680064 | bytes 20972800 | tf_op jit(solution)/shard_map/convert_element_type | solution.py:253
  318.9 8.7 %copy.350 = bf16[8,64,32,128]{1,0,3,2:T(8,128)(2,1)} copy(bf16[8,64,32,128]{3,2,1,0:T(8,128)(2,1)} %multiply_convert_fusion) | data formatting | bytes 8388608 | tf_op jit(solution)/shard_map/convert_element_type | solution.py:253
  330.0 4.3 all-to-all-start.10
  334.3 110.6 %fusion.4 = bf16[64,15,7,7]{0,1,3,2:T(8,128)(2,1)S(1)} fusion(bf16[8,64,32,128]{1,0,3,2:T(8,128)(2,1)} %copy.350, bf16[8,15,3,256]{1,0,3,2:T(8,128)(2,1)} %copy.346, bf16[8,15,64,256]{1,0,3,2:T(8,128)(2,1)} %copy.345, bf16[8,15,3,256]{1,0,3,2:T(8,128)(2,1)} %copy-done.35), kind=kOutput, calls=%fused_computation.22 | convolution fusion | flops 3075119104 | bytes 8589184 | tf_op jit(solution)/shard_map/slice | solution.py:251
  445.1 4.1 copy.351
  454.6 5.9 all-to-all-start.11
  463.1 4.1 all-to-all-done.11
  469.9 3.5 all-to-all-start.12
  477.0 5.2 all-to-all-done.12
  482.2 3.5 all-to-all-start.8
  487.3 14.4 %all-gather.1 = bf16[32,2,8,128]{3,2,1,0:T(8,128)(2,1)S(1)} all-gather(bf16[8,2,8,128]{3,2,1,0:T(8,128)(2,1)S(1)} %convolution_convert_fusion.5), channel_id=3, replica_groups=mesh['clip'=8,'row'=4] {'row'}, dimensions={0}, use_global_device_ids=true | all-gather | bytes 163840 | tf_op jit(solution)/shard_map/all_gather | solution.py:358
  518.5 5.4 all-to-all-done.13
  523.9 3.5 all-to-all-start.20
  532.2 7.6 %all-gather.2 = bf16[32,2,8,512]{3,2,1,0:T(8,128)(2,1)} all-gather(bf16[8,2,8,512]{3,2,1,0:T(8,128)(2,1)S(1)} %multiply_convert_fusion.4), channel_id=4, replica_groups=mesh['clip'=8,'row'=4] {'row'}, dimensions={0}, use_global_device_ids=true | all-gather | bytes 655360 | tf_op jit(solution)/shard_map/all_gather | solution.py:386
  550.0 8.4 %all-to-all-done.18 = bf16[32,48,128]{2,1,0:T(8,128)(2,1)S(1)} async-done(((bf16[32,48,128]{2,1,0:T(8,128)(2,1)}), bf16[32,48,128]{2,1,0:T(8,128)(2,1)S(1)}, u32[]{:S(2)}, u32[]{:S(2)}) %all-to-all-start.18) | async-done | bytes 393248 | tf_op jit(solution)/shard_map/all_to_all | solution.py:100
  558.4 4.0 all-to-all-start.14
  565.4 16.7 %all-to-all-done.14 = bf16[8,376,128]{2,1,0:T(8,128)(2,1)S(1)} async-done(((bf16[8,376,128]{2,1,0:T(8,128)(2,1)}), bf16[8,376,128]{2,1,0:T(8,128)(2,1)S(1)}, u32[]{:S(2)}, u32[]{:S(2)}) %all-to-all-start.14) | async-done | bytes 770080 | tf_op jit(solution)/shard_map/all_to_all | solution.py:100
  582.1 3.6 all-to-all-start.19
  586.4 5.2 all_gather.46
  596.5 3.6 copy.417
  602.7 3.7 reshape.698
  615.9 6.9 %all_gather.44 = bf16[4,424,128]{2,1,0:T(8,128)(2,1)S(1)} all-gather(bf16[1,424,128]{2,1,0:T(8,128)(2,1)S(1)} %pad_maximum_fusion.13), channel_id=1, replica_groups=mesh['clip'=8,'row'=4] {'row'}, dimensions={0}, use_global_device_ids=true | all-gather | bytes 542720 | tf_op jit(solution)/shard_map/all_gather | solution.py:424
  627.9 9.1 %all_gather.45 = bf16[4,832,128]{2,1,0:T(8,128)(2,1)S(1)} all-gather(bf16[1,832,128]{2,1,0:T(8,128)(2,1)S(1)} %pad_maximum_fusion.12), channel_id=1, replica_groups=mesh['clip'=8,'row'=4] {'row'}, dimensions={0}, use_global_device_ids=true | all-gather | bytes 1064960 | tf_op jit(solution)/shard_map/all_gather | solution.py:416
  (432 shorter events, 162.2 us)
Async XLA Ops:
  2.1 44.6 %all-to-all-start.15 = ((bf16[8,8,735]{2,1,0:T(8,128)(2,1)}), bf16[8,8,735]{2,1,0:T(8,128)(2,1)S(1)}, u32[]{:S(2)}, u32[]{:S(2)}) async-start(bf16[8,8,735]{2,1,0:T(8,128)(2,1)} %broadcast_in_dim.73), calls=%async_computation.15 | async-start | bytes 196608 | tf_op jit(solution)/shard_map/all_to_all | solution.py:100
  21.1 29.3 %collective-permute-start.3 = (bf16[8,15,3,256]{3,0,2,1:T(8,128)(2,1)S(1)}, bf16[8,15,3,256]{3,0,2,1:T(8,128)(2,1)S(1)}, u32[]{:S(2)}, u32[]{:S(2)}) collective-permute-start(bf16[8,15,3,256]{3,0,2,1:T(8,128)(2,1)S(1)} %copy.343), channel_id=1, source_target_pairs={{1,0},{2,1},{3,2},{5,4},{6,5},{7,6},{9,8},{10,9},{11,10},{13,12},{... | collective-permute-start | bytes 552968 | tf_op jit(solution)/shard_map/ppermute | solution.py:23
  22.5 26.9 %collective-permute-start.2 = (bf16[8,15,3,256]{3,0,2,1:T(8,128)(2,1)S(1)}, bf16[8,15,3,256]{3,0,2,1:T(8,128)(2,1)S(1)}, u32[]{:S(2)}, u32[]{:S(2)}) collective-permute-start(bf16[8,15,3,256]{3,0,2,1:T(8,128)(2,1)S(1)} %copy.342), channel_id=1, source_target_pairs={{0,1},{1,2},{2,3},{4,5},{5,6},{6,7},{8,9},{9,10},{10,11},{12,13},{... | collective-permute-start | bytes 552968 | tf_op jit(solution)/shard_map/ppermute | solution.py:22
  52.2 46.8 %copy-start.61 = (bf16[144,128]{1,0:T(8,128)(2,1)S(1)}, bf16[144,128]{1,0:T(8,128)(2,1)}, u32[]{:S(2)}) copy-start(bf16[144,128]{1,0:T(8,128)(2,1)} %param.34) | copy-start | bytes 110596
  52.2 46.9 %copy-start.70 = (bf16[16,512]{1,0:T(8,128)(2,1)S(1)}, bf16[16,512]{1,0:T(8,128)(2,1)}, u32[]{:S(2)}) copy-start(bf16[16,512]{1,0:T(8,128)(2,1)} %param.35) | copy-start | bytes 49156
  52.2 60.4 %copy-start.38 = (bf16[8,2,8,2048]{3,2,1,0:T(8,128)(2,1)S(1)}, bf16[8,2,8,2048]{3,2,1,0:T(8,128)(2,1)}, u32[]{:S(2)}) copy-start(bf16[8,2,8,2048]{3,2,1,0:T(8,128)(2,1)} %param.45) | copy-start | bytes 1572868
  92.3 23.5 %copy-start.56 = (bf16[256,512]{1,0:T(8,128)(2,1)S(1)}, bf16[256,512]{1,0:T(8,128)(2,1)}, u32[]{:S(2)}) copy-start(bf16[256,512]{1,0:T(8,128)(2,1)} %param.30) | copy-start | bytes 786436
  93.0 14.3 %all-to-all-start.16 = ((f32[32,8,128]{2,1,0:T(8,128)}), f32[32,8,128]{2,1,0:T(8,128)S(1)}, u32[]{:S(2)}, u32[]{:S(2)}) async-start(f32[32,8,128]{2,1,0:T(8,128)} %broadcast_in_dim.75), calls=%async_computation.16 | async-start | bytes 262144 | tf_op jit(solution)/shard_map/all_to_all | solution.py:100
  108.2 22.8 %all-to-all-start.2 = ((bf16[8,280,128]{2,1,0:T(8,128)(2,1)}), bf16[8,280,128]{2,1,0:T(8,128)(2,1)}, u32[]{:S(2)}, u32[]{:S(2)}) async-start(bf16[8,280,128]{2,1,0:T(8,128)(2,1)} %broadcast_in_dim.54), calls=%async_computation.2 | async-start | bytes 1146880 | tf_op jit(solution)/shard_map/all_to_all | solution.py:100
  132.0 31.8 %all-to-all-start = ((bf16[8,128,512]{2,1,0:T(8,128)(2,1)}), bf16[8,128,512]{2,1,0:T(8,128)(2,1)S(1)}, u32[]{:S(2)}, u32[]{:S(2)}) async-start(bf16[8,128,512]{2,1,0:T(8,128)(2,1)} %broadcast_in_dim.52), calls=%async_computation | async-start | bytes 2097152 | tf_op jit(solution)/shard_map/all_to_all | solution.py:100
  138.0 45.0 %collective-permute-start.1 = (bf16[8,280,128]{2,1,0:T(8,128)(2,1)}, bf16[8,280,128]{2,1,0:T(8,128)(2,1)}, u32[]{:S(2)}, u32[]{:S(2)}) collective-permute-start(bf16[8,280,128]{2,1,0:T(8,128)(2,1)} %all-to-all-done.2), channel_id=1, source_target_pairs={{0,1},{1,0},{2,3},{3,2},{4,5},{5,4},{6,7},{7,6},{8,9},{9,8},{10,11... | collective-permute-start | bytes 1720328 | tf_op jit(solution)/shard_map/ppermute | solution.py:133
  138.0 31.6 %copy-start.75 = (f32[2048]{0:T(1024)S(1)}, f32[2048]{0:T(1024)}, u32[]{:S(2)}) copy-start(f32[2048]{0:T(1024)} %param.42) | copy-start | bytes 24580
  138.0 31.7 %copy-start.76 = (f32[2048]{0:T(1024)S(1)}, f32[2048]{0:T(1024)}, u32[]{:S(2)}) copy-start(f32[2048]{0:T(1024)} %param.43) | copy-start | bytes 24580
  163.9 20.8 %collective-permute-start = (bf16[8,128,512]{2,1,0:T(8,128)(2,1)S(1)}, bf16[8,128,512]{2,1,0:T(8,128)(2,1)}, u32[]{:S(2)}, u32[]{:S(2)}) collective-permute-start(bf16[8,128,512]{2,1,0:T(8,128)(2,1)S(1)} %all-to-all-done), channel_id=1, source_target_pairs={{0,1},{1,0},{2,3},{3,2},{4,5},{5,4},{6,7},{7,6},{8,9},{9,8},{10,11... | collective-permute-start | bytes 3145736 | tf_op jit(solution)/shard_map/ppermute | solution.py:133
  164.6 17.8 %all-to-all-start.17 = ((f32[32,8,128]{2,1,0:T(8,128)}), f32[32,8,128]{2,1,0:T(8,128)S(1)}, u32[]{:S(2)}, u32[]{:S(2)}) async-start(f32[32,8,128]{2,1,0:T(8,128)} %broadcast_in_dim.153), calls=%async_computation.17 | async-start | bytes 262144 | tf_op jit(solution)/shard_map/all_to_all | solution.py:100
  184.5 23.8 %copy-start.53 = (bf16[8,64,128]{2,1,0:T(8,128)(2,1)}, bf16[8,64,128]{2,1,0:T(8,128)(2,1)S(1)}, u32[]{:S(2)}) copy-start(bf16[8,64,128]{2,1,0:T(8,128)(2,1)S(1)} %get-tuple-element.58) | copy-start | bytes 393220
  184.6 55.7 %copy-start.39 = (bf16[128,512,1,1]{1,0,2,3:T(8,128)(2,1)}, bf16[128,512,1,1]{1,0,2,3:T(8,128)(2,1)S(1)}, u32[]{:S(2)}) copy-start(bf16[128,512,1,1]{1,0,2,3:T(8,128)(2,1)S(1)} %reshape.712) | copy-start | bytes 393220
  188.0 52.3 %copy-start.7 = (f32[512,128]{0,1:T(8,128)}, f32[512,128]{0,1:T(8,128)S(1)}, u32[]{:S(2)}) copy-start(f32[512,128]{0,1:T(8,128)S(1)} %get-tuple-element.95) | copy-start | bytes 786436
  188.8 14.1 %all-to-all-start.1 = ((f32[32,8,128]{2,1,0:T(8,128)}), f32[32,8,128]{2,1,0:T(8,128)S(1)}, u32[]{:S(2)}, u32[]{:S(2)}) async-start(f32[32,8,128]{2,1,0:T(8,128)} %broadcast_in_dim.53), calls=%async_computation.1 | async-start | bytes 262144 | tf_op jit(solution)/shard_map/all_to_all | solution.py:100
  204.0 32.7 %all-to-all-start.3 = ((bf16[8,576,128]{2,1,0:T(8,128)(2,1)}), bf16[8,576,128]{2,1,0:T(8,128)(2,1)S(1)}, u32[]{:S(2)}, u32[]{:S(2)}) async-start(bf16[8,576,128]{2,1,0:T(8,128)(2,1)} %broadcast_in_dim.59), calls=%async_computation.3 | async-start | bytes 2359296 | tf_op jit(solution)/shard_map/all_to_all | solution.py:100
  207.7 34.3 %copy-start.64 = (f32[512]{0:T(512)}, f32[512]{0:T(512)S(1)}, u32[]{:S(2)}) copy-start(f32[512]{0:T(512)S(1)} %multiply_bitcast_fusion.1) | copy-start | bytes 6148
  208.3 33.7 %copy-start.62 = (f32[512]{0:T(512)}, f32[512]{0:T(512)S(1)}, u32[]{:S(2)}) copy-start(f32[512]{0:T(512)S(1)} %get-tuple-element.84) | copy-start | bytes 6148
  214.1 22.7 %copy-start.43 = (bf16[8,4,2,8,128]{4,0,3,2,1:T(8,128)(2,1)}, bf16[8,4,2,8,128]{4,0,3,2,1:T(8,128)(2,1)S(1)}, u32[]{:S(2)}) copy-start(bf16[8,4,2,8,128]{4,0,3,2,1:T(8,128)(2,1)S(1)} %copy.315) | copy-start | bytes 393220
  214.3 44.1 %copy-start.41 = (bf16[8,4,4,128]{3,0,2,1:T(8,128)(2,1)}, bf16[8,4,4,128]{3,0,2,1:T(8,128)(2,1)S(1)}, u32[]{:S(2)}) copy-start(bf16[8,4,4,128]{3,0,2,1:T(8,128)(2,1)S(1)} %fusion.36) | copy-start | bytes 98308
  215.5 26.4 %copy-start.50 = (bf16[8,2,8,128]{3,0,2,1:T(8,128)(2,1)}, bf16[8,2,8,128]{3,0,2,1:T(8,128)(2,1)S(1)}, u32[]{:S(2)}) copy-start(bf16[8,2,8,128]{3,0,2,1:T(8,128)(2,1)S(1)} %fusion.33) | copy-start | bytes 98308
  236.8 23.4 %copy-start.11 = (bf16[8,576,128]{2,1,0:T(8,128)(2,1)}, bf16[8,576,128]{2,1,0:T(8,128)(2,1)S(1)}, u32[]{:S(2)}) copy-start(bf16[8,576,128]{2,1,0:T(8,128)(2,1)S(1)} %all-to-all-done.3) | copy-start | bytes 3538948
  236.8 23.4 %all-to-all-start.7 = ((bf16[4,2,65536]{2,1,0:T(2,128)(2,1)}), bf16[4,2,65536]{2,1,0:T(2,128)(2,1)S(1)}, u32[]{:S(2)}, u32[]{:S(2)}) async-start(bf16[4,2,65536]{2,1,0:T(2,128)(2,1)} %reshape.734), calls=%async_computation.7 | async-start | bytes 2097152 | tf_op jit(solution)/shard_map/all_to_all | solution.py:100
  260.1 36.9 %copy-start.15 = (f32[8,8,8,128]{3,0,2,1:T(8,128)}, f32[8,8,8,128]{3,0,2,1:T(8,128)S(1)}, u32[]{:S(2)}) copy-start(f32[8,8,8,128]{3,0,2,1:T(8,128)S(1)} %get-tuple-element.98) | copy-start | bytes 786436
  260.8 10.3 %all-to-all-start.4 = ((f32[8,8,128]{2,1,0:T(8,128)}), f32[8,8,128]{2,1,0:T(8,128)S(1)}, u32[]{:S(2)}, u32[]{:S(2)}) async-start(f32[8,8,128]{2,1,0:T(8,128)} %broadcast_in_dim.61), calls=%async_computation.4 | async-start | bytes 65536 | tf_op jit(solution)/shard_map/all_to_all | solution.py:100
  271.9 20.3 %all-to-all-start.5 = ((bf16[8,64,512]{2,1,0:T(8,128)(2,1)}), bf16[8,64,512]{2,1,0:T(8,128)(2,1)S(1)}, u32[]{:S(2)}, u32[]{:S(2)}) async-start(bf16[8,64,512]{2,1,0:T(8,128)(2,1)} %broadcast_in_dim.63), calls=%async_computation.5 | async-start | bytes 1048576 | tf_op jit(solution)/shard_map/all_to_all | solution.py:100
  279.9 23.8 %copy-start.66 = (f32[512]{0:T(512)S(1)}, f32[512]{0:T(512)}, u32[]{:S(2)}) copy-start(f32[512]{0:T(512)} %mul.405) | copy-start | bytes 6148
  279.9 23.9 %copy-start.72 = (f32[512]{0:T(512)S(1)}, f32[512]{0:T(512)}, u32[]{:S(2)}) copy-start(f32[512]{0:T(512)} %add.244) | copy-start | bytes 6148
  293.4 10.3 %all-to-all-start.6 = ((f32[8,8,128]{2,1,0:T(8,128)}), f32[8,8,128]{2,1,0:T(8,128)S(1)}, u32[]{:S(2)}, u32[]{:S(2)}) async-start(f32[8,8,128]{2,1,0:T(8,128)} %broadcast_in_dim.64), calls=%async_computation.6 | async-start | bytes 65536 | tf_op jit(solution)/shard_map/all_to_all | solution.py:100
  306.9 20.7 %all-to-all-start.9 = ((f32[8,8,128]{2,1,0:T(8,128)}), f32[8,8,128]{2,1,0:T(8,128)S(1)}, u32[]{:S(2)}, u32[]{:S(2)}) async-start(f32[8,8,128]{2,1,0:T(8,128)} %broadcast_in_dim.65), calls=%async_computation.9 | async-start | bytes 65536 | tf_op jit(solution)/shard_map/all_to_all | solution.py:100
  327.6 117.3 %copy-start.57 = (f32[8,128]{1,0:T(8,128)}, f32[8,128]{1,0:T(8,128)S(1)}, u32[]{:S(2)}) copy-start(f32[8,128]{1,0:T(8,128)S(1)} %reduce_sum.335) | copy-start | bytes 12292
  330.0 121.7 %all-to-all-start.10 = ((bf16[4,512,128]{1,2,0:T(8,128)(2,1)}), bf16[4,512,128]{1,2,0:T(8,128)(2,1)}, u32[]{:S(2)}, u32[]{:S(2)}) async-start(bf16[4,512,128]{1,2,0:T(8,128)(2,1)} %bitcast.67), calls=%async_computation.10 | async-start | bytes 1048576 | tf_op jit(solution)/shard_map/all_to_all | solution.py:100
  454.6 12.6 %all-to-all-start.11 = ((f32[8,8,128]{2,1,0:T(8,128)}), f32[8,8,128]{2,1,0:T(8,128)S(1)}, u32[]{:S(2)}, u32[]{:S(2)}) async-start(f32[8,8,128]{2,1,0:T(8,128)} %broadcast_in_dim.67), calls=%async_computation.11 | async-start | bytes 65536 | tf_op jit(solution)/shard_map/all_to_all | solution.py:100
  469.9 12.3 %all-to-all-start.12 = ((bf16[4,8,2,8,512]{4,1,3,2,0:T(8,128)(2,1)}), bf16[4,8,2,8,512]{4,1,3,2,0:T(8,128)(2,1)S(1)}, u32[]{:S(2)}, u32[]{:S(2)}) async-start(bf16[4,8,2,8,512]{4,1,3,2,0:T(8,128)(2,1)} %bitcast.402), calls=%async_computation.12 | async-start | bytes 1048576 | tf_op jit(solution)/shard_map/all_to_all | solution.py:100
  473.4 28.3 %copy-start.23 = (bf16[8,144,128]{2,1,0:T(8,128)(2,1)S(1)}, bf16[8,144,128]{2,1,0:T(8,128)(2,1)}, u32[]{:S(2)}) copy-start(bf16[8,144,128]{2,1,0:T(8,128)(2,1)} %copy-done.22) | copy-start | bytes 884740
  475.8 27.2 %copy-start.44 = (bf16[8,4,2,8,128]{4,0,3,2,1:T(8,128)(2,1)S(1)}, bf16[8,4,2,8,128]{4,0,3,2,1:T(8,128)(2,1)}, u32[]{:S(2)}) copy-start(bf16[8,4,2,8,128]{4,0,3,2,1:T(8,128)(2,1)} %copy-done.43) | copy-start | bytes 393220
  482.2 30.2 %all-to-all-start.8 = ((bf16[4,2,8,2,8,512]{5,4,3,2,1,0:T(8,128)(2,1)}), bf16[4,2,8,2,8,512]{5,4,3,2,1,0:T(8,128)(2,1)S(1)}, u32[]{:S(2)}, u32[]{:S(2)}) async-start(bf16[4,2,8,2,8,512]{5,4,3,2,1,0:T(8,128)(2,1)} %pad_maximum_fusion.9), calls=%async_computation.8 | async-start | bytes 2097152 | tf_op jit(solution)/shard_map/all_to_all | solution.py:100
  512.1 33.1 %copy-start.32 = (bf16[4,1,8,2,8,512]{5,4,3,2,1,0:T(8,128)(2,1)S(1)}, bf16[4,1,8,2,8,512]{5,4,3,2,1,0:T(8,128)(2,1)}, u32[]{:S(2)}) copy-start(bf16[4,1,8,2,8,512]{5,4,3,2,1,0:T(8,128)(2,1)} %get-tuple-element.65) | copy-start | bytes 1572868
  512.4 35.2 %copy-start.13 = (bf16[4,2,8,2,8,512]{5,4,3,2,1,0:T(8,128)(2,1)}, bf16[4,2,8,2,8,512]{5,4,3,2,1,0:T(8,128)(2,1)S(1)}, u32[]{:S(2)}) copy-start(bf16[4,2,8,2,8,512]{5,4,3,2,1,0:T(8,128)(2,1)S(1)} %all-to-all-done.8) | copy-start | bytes 3145732
  513.1 10.8 %all-to-all-start.13 = ((f32[32,8,128]{2,1,0:T(8,128)}), f32[32,8,128]{2,1,0:T(8,128)S(1)}, u32[]{:S(2)}, u32[]{:S(2)}) async-start(f32[32,8,128]{2,1,0:T(8,128)} %broadcast_in_dim.72), calls=%async_computation.13 | async-start | bytes 262144 | tf_op jit(solution)/shard_map/all_to_all | solution.py:100
  523.9 18.6 %all-to-all-start.20 = ((bf16[8,64,512]{2,1,0:T(8,128)(2,1)}), bf16[8,64,512]{2,1,0:T(8,128)(2,1)S(1)}, u32[]{:S(2)}, u32[]{:S(2)}) async-start(bf16[8,64,512]{2,1,0:T(8,128)(2,1)} %bitcast.126), calls=%async_computation.20 | async-start | bytes 1048576 | tf_op jit(solution)/shard_map/all_to_all | solution.py:100
  542.5 15.9 %all-to-all-start.18 = ((bf16[32,48,128]{2,1,0:T(8,128)(2,1)}), bf16[32,48,128]{2,1,0:T(8,128)(2,1)S(1)}, u32[]{:S(2)}, u32[]{:S(2)}) async-start(bf16[32,48,128]{2,1,0:T(8,128)(2,1)} %pad_maximum_fusion.11), calls=%async_computation.18 | async-start | bytes 786432 | tf_op jit(solution)/shard_map/all_to_all | solution.py:100
  558.4 23.7 %all-to-all-start.14 = ((bf16[8,376,128]{2,1,0:T(8,128)(2,1)}), bf16[8,376,128]{2,1,0:T(8,128)(2,1)S(1)}, u32[]{:S(2)}, u32[]{:S(2)}) async-start(bf16[8,376,128]{2,1,0:T(8,128)(2,1)} %pad_maximum_fusion.10), calls=%async_computation.14 | async-start | bytes 1540096 | tf_op jit(solution)/shard_map/all_to_all | solution.py:100
  582.1 45.6 %all-to-all-start.19 = ((bf16[8,576,128]{2,1,0:T(8,128)(2,1)}), bf16[8,576,128]{2,1,0:T(8,128)(2,1)S(1)}, u32[]{:S(2)}, u32[]{:S(2)}) async-start(bf16[8,576,128]{2,1,0:T(8,128)(2,1)} %bitcast.393), calls=%async_computation.19 | async-start | bytes 2359296 | tf_op jit(solution)/shard_map/all_to_all | solution.py:100
  (73 other events, 790.1 us)

commit v2 on v0

v2 whole, which is shorter than its diff:
```python
import functools

import jax
import jax.numpy as jnp
from jax import lax
from jax.experimental import pallas as pl
from jax.experimental.pallas import tpu as pltpu
from jax.sharding import PartitionSpec as P

STEM = 64
SEG = 8
WIN = 5


epsilon = 1e-05


def silu_slope(values):
    sigmoid_val = jax.nn.sigmoid(values)
    return sigmoid_val * (1.0 + values * (1.0 - sigmoid_val))


def statistics(totals, count):
    mean = totals[0] / count
    return mean, lax.rsqrt(totals[1] / count - mean * mean + epsilon)


def stack_index(shape, dim):
    return lax.broadcasted_iota(jnp.int32, shape, dim)


def stem_planes_kernel(
    start_ref, local_ref, above_ref, below_ref, planes_ref, pick_ref, shift_ref
):
    pair = pl.program_id(0)

    @pl.when(pair == 0)
    def _():
        dims = (256, 240)
        out, inner = stack_index(dims, 0), stack_index(dims, 1)
        channel, plane = out % 16, inner // 16
        plus = plane == jnp.where(channel < 3, channel + 6, channel)
        minus = (channel >= 3) & (plane == channel - 3)
        value = jnp.where(plus, 1.0, 0.0) - jnp.where(minus, 1.0, 0.0)
        keep = (out // 16 == inner % 16) & (channel < 15)
        pick_ref[...] = jnp.where(keep, value, 0.0).astype(jnp.bfloat16)
        dims = (256, 896)
        source, target = stack_index(dims, 0), stack_index(dims, 1)
        wanted = 2 * (target % 128) + target // 128 - 3
        shift_ref[...] = jnp.where(source == wanted, 1.0, 0.0).astype(jnp.bfloat16)

    for side in range(2):
        first = start_ref[2 * pair + side]
        lanes = slice(128 * side, 128 * side + 128)
        for block in range(6):
            if block == 0:
                window = above_ref[pl.ds(first, WIN)]
            elif block == 5:
                window = below_ref[pl.ds(first, WIN)]
            else:
                window = local_ref[pl.ds(first, WIN), :, 16 * block - 16 : 16 * block, :]
            window = window.reshape(240, 256)
            stacked = jnp.dot(pick_ref[...], window, preferred_element_type=jnp.float32)
            shifted = jnp.dot(
                stacked.astype(jnp.bfloat16), shift_ref[...], preferred_element_type=jnp.float32
            ).astype(jnp.bfloat16)
            low, high = (8 if block == 0 else 0), (8 if block == 5 else 16)
            for kx in range(7):
                piece = shifted[:, 128 * kx : 128 * kx + 128].reshape(16, 16, 128)
                planes_ref[
                    0, 16 * block - 8 + low : 16 * block - 8 + high, 16 * kx : 16 * kx + 16, lanes
                ] = piece[low:high]


def stem_conv_kernel(planes_ref, weight_ref, pre_ref, sums_ref):
    @pl.when(pl.program_id(0) == 0)
    def _():
        sums_ref[...] = jnp.zeros_like(sums_ref)

    @pl.loop(0, 8)
    def _(group):
        patches = planes_ref[0, pl.ds(5 + 8 * group, 13)].reshape(13 * 112, 256)
        out = jnp.dot(weight_ref[...], patches, preferred_element_type=jnp.float32)
        out = out.reshape(4, 64, 256)
        for side in range(2):
            half = out[:, :, 128 * side : 128 * side + 128]
            pre_ref[side, pl.ds(4 * group, 4)] = half
            sums_ref[0] += jnp.sum(half, 0)
            sums_ref[1] += jnp.sum(half * half, 0)


def stem_slope_kernel(pre_ref, cot_ref, vectors_ref, outer_ref, sums_ref, swap_ref):
    @pl.when(pl.program_id(0) == 0)
    def _():
        out, inner = stack_index((256, 256), 0), stack_index((256, 256), 1)
        hit = (out // 16 == inner % 16) & (out % 16 == inner // 16)
        swap_ref[...] = jnp.where(hit, 1.0, 0.0).astype(jnp.bfloat16)
        sums_ref[...] = jnp.zeros_like(sums_ref)

    for part in range(4):
        channels = slice(16 * part, 16 * part + 16)
        mean, inverse = vectors_ref[0, channels], vectors_ref[1, channels]
        gain, bias = vectors_ref[2, channels], vectors_ref[3, channels]
        block = jnp.concatenate(
            [cot_ref[0, channels, 16 * k : 16 * k + 16, :].reshape(256, 128) for k in range(2)], 1
        )
        turned = jnp.dot(swap_ref[...], block, preferred_element_type=jnp.float32)
        total_bias, total_gain = jnp.zeros((16, 128)), jnp.zeros((16, 128))
        for k in range(2):
            rows = slice(16 * k, 16 * k + 16)
            cot = turned[:, 128 * k : 128 * k + 128].reshape(16, 16, 128)
            normed = (pre_ref[0, rows, channels, :] - mean) * inverse
            outer = cot * silu_slope(normed * gain + bias)
            outer_ref[0, rows, channels, :] = outer.astype(jnp.bfloat16)
            total_bias += jnp.sum(outer, 0)
            total_gain += jnp.sum(outer * normed, 0)
        sums_ref[0, channels] += total_bias
        sums_ref[1, channels] += total_gain


def stem_grad_kernel(planes_ref, pre_ref, outer_ref, vectors_ref, out_ref, acc_ref):
    pair, last = pl.program_id(0), pl.num_programs(0) - 1

    @pl.when(pair == 0)
    def _():
        acc_ref[...] = jnp.zeros_like(acc_ref)

    @pl.loop(0, 8)
    def _(group):
        rows = pl.ds(4 * group, 4)
        sides = []
        for side in range(2):
            normed = (pre_ref[side, rows] - vectors_ref[0]) * vectors_ref[1]
            outer = outer_ref[side, rows].astype(jnp.float32)
            grad = vectors_ref[2] * (outer - vectors_ref[3] - normed * vectors_ref[4])
            sides.append(grad.astype(jnp.bfloat16).reshape(256, 128))
        patches = planes_ref[0, pl.ds(5 + 8 * group, 13)].reshape(13 * 112, 256)
        acc_ref[...] += lax.dot_general(
            jnp.concatenate(sides, 1),
            patches,
            (((1,), (1,)), ((), ())),
            preferred_element_type=jnp.float32,
        )

    @pl.when(pair == last)
    def _():
        total = acc_ref[0:64, 0:784]
        for y in range(1, 4):
            total += acc_ref[64 * y : 64 * y + 64, 224 * y : 224 * y + 784]
        total = jnp.concatenate([total, jnp.zeros((64, 240), jnp.float32)], 1)
        for part in range(8):
            out_ref[part] = total[:, 128 * part : 128 * part + 128]


stem_limit = 24 * 1024 * 1024
block_limit = 40 * 1024 * 1024
planes_shape, map_shape = (80, 112, 256), (32, 64, 128)


def whole(shape):
    return pl.BlockSpec(shape, lambda *_: (0,) * len(shape))


def by_step(shape):
    return pl.BlockSpec(shape, lambda i: (i,) + (0,) * (len(shape) - 1))


def in_hbm(array):
    return pltpu.with_memory_space_constraint(array, pltpu.HBM)


def stem_call(kernel, steps, in_specs, out_specs, outs, scratch, flops, moved, args, waits=()):
    used = len(args)

    def body(*refs):
        kernel(*refs[:used], *refs[used + len(waits) :])

    return pl.pallas_call(
        body,
        grid=(steps,),
        in_specs=in_specs + [pl.BlockSpec(memory_space=pl.ANY)] * len(waits),
        out_specs=out_specs,
        out_shape=[
            (pltpu.HBM if len(shape) == 4 else jax.ShapeDtypeStruct)(shape, dtype)
            for shape, dtype in outs
        ],
        scratch_shapes=[pltpu.VMEM(shape, dtype) for shape, dtype in scratch],
        compiler_params=pltpu.CompilerParams(vmem_limit_bytes=stem_limit),
        cost_estimate=pl.CostEstimate(flops=flops, bytes_accessed=moved, transcendentals=0),
    )(*(in_hbm(entry) if entry.ndim > 1 else entry for entry in args), *waits)


def stem_planes(starts, local, above, below):
    pairs = starts.shape[0] // 2
    return stem_call(
        stem_planes_kernel,
        pairs,
        [pl.BlockSpec(memory_space=pltpu.SMEM)]
        + [whole(entry.shape) for entry in (local, above, below)],
        [by_step((1,) + planes_shape)],
        [((pairs,) + planes_shape, jnp.bfloat16)],
        [((256, 240), jnp.bfloat16), ((256, 896), jnp.bfloat16)],
        4 * 10**9 * pairs,
        5 * 10**6 * pairs,
        (starts, local, above, below),
    )[0]


def stem_conv(planes, weight, *waits):
    pairs = planes.shape[0]
    return stem_call(
        stem_conv_kernel,
        pairs,
        [
            by_step((1,) + planes_shape),
            whole(weight.shape),
        ],
        [by_step((2,) + map_shape), whole((2, 64, 128))],
        [((2 * pairs,) + map_shape, jnp.float32), ((2, 64, 128), jnp.float32)],
        [],
        4 * 10**9 * pairs,
        7 * 10**6 * pairs,
        (planes, weight),
        waits,
    )


def stem_slope(pre, cot, first, vectors, *waits):
    images = pre.shape[0] // 2
    return stem_call(
        stem_slope_kernel,
        images,
        [
            pl.BlockSpec((1,) + map_shape, lambda i: (i + first, 0, 0, 0)),
            pl.BlockSpec((1, 64, 32, 128), lambda i: (i + first, 0, 0, 0)),
            whole(vectors.shape),
        ],
        [by_step((1,) + map_shape), whole((2, 64, 128))],
        [((images,) + map_shape, jnp.bfloat16), ((2, 64, 128), jnp.float32)],
        [((256, 256), jnp.bfloat16)],
        10**9 * images,
        2 * 10**6 * images,
        (pre, cot, vectors),
        waits,
    )


def stem_grad(planes, pre, outer, first, vectors, *waits):
    pairs = planes.shape[0] // 2

    def later(shape):
        return pl.BlockSpec(shape, lambda i: (i + first, 0, 0, 0))

    return stem_call(
        stem_grad_kernel,
        pairs,
        [
            later((1,) + planes_shape), later((2,) + map_shape), by_step((2,) + map_shape),
            whole(vectors.shape),
        ],
        [whole((8, 64, 128))],
        [((8, 64, 128), jnp.float32)],
        [((256, 13 * 112), jnp.float32)],
        4 * 10**9 * pairs,
        8 * 10**6 * pairs,
        (planes, pre, outer, vectors),
        waits,
    )[0]


def filters_inside(weight):
    taps = weight.reshape(-1, 3 * WIN, 49).swapaxes(1, 2)
    return jnp.pad(taps, ((0, 0), (0, 0), (0, 1))).reshape(weight.shape[0], -1)


def filters_outside(weight):
    return weight.reshape(-1, 49, 16)[:, :, : 3 * WIN].swapaxes(1, 2).reshape(weight.shape[0], -1)


def lanes(*entries):
    return jnp.broadcast_to(jnp.stack(entries)[:, :, None], (len(entries), entries[0].size, 128))


taps = [(ky, kx) for ky in range(3) for kx in range(3)]
f32, bf16 = jnp.float32, jnp.bfloat16


def dot(left, right, sides="NN", precision=None):
    contract = ((0 if sides[0] == "T" else 1,), (1 if sides[1] == "T" else 0,))
    return lax.dot_general(
        left, right, (contract, ((), ())), preferred_element_type=f32, precision=precision
    )


def split_dot(matrix, values):
    upper = values.astype(bf16)
    lower = (values - upper.astype(f32)).astype(bf16)
    return dot(matrix, upper) + dot(matrix, lower)


def shift_columns(pad_ref, values, width):
    rows = values.shape[0]
    band = (pad_ref.shape[1] - rows) // 2
    column = stack_index(values.shape, 0) % width
    wide = values.astype(f32)
    for kx in range(3):
        moved = wide
        if kx == 0:
            moved = jnp.where(column == 0, 0.0, pltpu.roll(wide, 1, 0))
        if kx == 2:
            moved = jnp.where(column == width - 1, 0.0, pltpu.roll(wide, rows - 1, 0))
        zeros = jnp.zeros((band, values.shape[1]), pad_ref.dtype)
        pad_ref[kx, 0:band] = zeros
        pad_ref[kx, band : band + rows] = moved.astype(pad_ref.dtype)
        pad_ref[kx, band + rows :] = zeros
    return band


def conv_taps(pad_ref, band, first, rows, weight_ref, back=False, precision=None):
    channels = weight_ref.shape[0] // 9
    result = None
    for ky, kx in taps:
        part = pad_ref[kx, pl.ds(first + ky * band, rows)]
        tap = 8 - (3 * ky + kx) if back else 3 * ky + kx
        weight = weight_ref[tap * channels : (tap + 1) * channels, :].astype(pad_ref.dtype)
        term = dot(part, weight, "NT" if back else "NN", precision)
        result = term if result is None else result + term
    return result


def pool_matrix(out_rows, rows, factor, width, value, dtype=bf16):
    out, inner = stack_index((out_rows, rows), 0), stack_index((out_rows, rows), 1)
    band, small = SEG * width, width // factor
    out_band = SEG * small
    hit = (
        (out // out_band == inner // band // factor)
        & (out % out_band // small == inner % band // width)
        & (out % small == inner % width // factor)
    )
    return jnp.where(hit, value, 0.0).astype(dtype)


def spread_matrix(rows, factor, width):
    small = width // factor
    dims = (rows, SEG * small)
    out, inner = stack_index(dims, 0), stack_index(dims, 1)
    image, column = out % (SEG * width) // width, out % width
    hit = (inner // small == image) & (inner % small == column // factor)
    return jnp.where(hit, 1.0, 0.0).astype(bf16)


def as_row(block):
    return jnp.concatenate([block[j : j + 1] for j in range(block.shape[0])], 1)


def as_block(row):
    lanes_of = row.shape[1] // 128
    return jnp.concatenate([row[:, 128 * j : 128 * j + 128] for j in range(lanes_of)], 0)


def put_sums(out_ref, first, second, extra=None):
    block = jnp.concatenate([as_block(first), as_block(second)], 0)
    rows = out_ref.shape[1]
    if extra is not None:
        block = jnp.concatenate([block, extra], 0)
    if block.shape[0] < rows:
        block = jnp.concatenate([block, jnp.zeros((rows - block.shape[0], 128), f32)], 0)
    out_ref[...] = jnp.broadcast_to(block[None], out_ref.shape)


def get_sums(sums_ref, rows):
    block = jnp.sum(sums_ref[...], 0)
    return as_row(block[:rows]), as_row(block[rows : 2 * rows])


def norm_of(sums_ref, rows, count):
    first, second = get_sums(sums_ref, rows)
    mean = first / count
    return mean, lax.rsqrt(second / count - mean * mean + epsilon)


def silu(values):
    return values * jax.nn.sigmoid(values)


def column_sum(values):
    return jnp.sum(values, 0, keepdims=True)


def padded(rows, unit=16):
    return (rows + unit - 1) // unit * unit


def pack_kernel(place_ref, side_ref, one_ref, fine_ref, half_w_ref, quarter_w_ref, expand_ref,
                reduce_ref, two_ref, three_ref, sent_ref, parts_ref, early_ref):
    place, side = place_ref[0], side_ref[0]
    half = one_ref.shape[0] // 2
    quarter = early_ref.shape[0] // 4
    start = 0
    for part_ref in (fine_ref, half_w_ref, quarter_w_ref):
        early_ref[start : start + part_ref.shape[0]] = part_ref[...]
        start += padded(part_ref.shape[0])
    for block in range(expand_ref.shape[1] // 128):
        lanes_of = slice(128 * block, 128 * block + 128)
        early_ref[start : start + expand_ref.shape[0]] = expand_ref[:, lanes_of]
        start += padded(expand_ref.shape[0])

    def put(start, value):
        shape = (sent_ref.shape[0],) + value.shape
        sent_ref[:, start : start + value.shape[0]] = jnp.broadcast_to(value[None], shape)
        return start + padded(value.shape[0])

    start = 0
    rows = pl.ds(pl.multiple_of(side * half, half), half)
    for block in range(one_ref.shape[1] // 128):
        start = put(start, one_ref[rows, 128 * block : 128 * block + 128])
    start = put(start, early_ref[pl.ds(pl.multiple_of(place * quarter, quarter), quarter)])
    put(start, reduce_ref[...])
    wide = three_ref.shape[1] // 4
    columns = pl.ds(pl.multiple_of(place * 128, 128), 128)
    parts_ref[0 : two_ref.shape[0]] = two_ref[:, columns]
    start = padded(two_ref.shape[0])
    for block in range(wide // 128):
        columns = pl.ds(pl.multiple_of(place * wide + 128 * block, 128), 128)
        parts_ref[start : start + three_ref.shape[0]] = three_ref[:, columns]
        start += padded(three_ref.shape[0])


def own_lanes(place_ref, *refs):
    wide = refs[0].shape[1] // 4
    return [ref[:, pl.ds(pl.multiple_of(place_ref[0] * wide, wide), wide)] for ref in refs]


def first_kernel(side_ref, x_ref, mine_ref, other_ref, stem_ref,
                 full_ref, first_ref, sums_ref):
    side = side_ref[0]
    half = full_ref.shape[2]
    for part in range(full_ref.shape[3] // 128):
        rows, lanes_of = slice(half * part, half * part + half), slice(128 * part, 128 * part + 128)
        full_ref[:, pl.ds(side, 1), :, lanes_of] = mine_ref[:, rows][:, None]
        full_ref[:, pl.ds(1 - side, 1), :, lanes_of] = other_ref[:, rows][:, None]
    weight = full_ref[...].reshape(x_ref.shape[1], -1)
    first = dot(x_ref[...], weight)
    first_ref[...] = first
    put_sums(sums_ref, column_sum(first), column_sum(first * first), stem_row(stem_ref))


def stem_row(*refs):
    stem = sum(ref[...] for ref in refs).reshape(128, 128)
    return dot(jnp.ones((8, 128), f32), stem, "NT", lax.Precision.HIGHEST)


def hidden_kernel(count, mask_ref, sums_ref, first_ref, gain_ref, bias_ref, reduce_ref,
                  hidden_ref, change_ref, norm_ref):
    mean, inverse = norm_of(sums_ref, 4, count)
    norm_ref[...] = jnp.concatenate([mean, inverse], 0)
    level = (first_ref[...] - mean) * inverse * gain_ref[...] + bias_ref[...]
    hidden = silu(level).astype(bf16)
    hidden_ref[...] = hidden
    reduced = dot(hidden, reduce_ref[...])
    reduced = reduced.reshape(-1, SEG, 8, reduced.shape[1])
    steps = [
        mask_ref[0, t].astype(f32) * (reduced[:, t + 1] - reduced[:, t]) for t in range(SEG - 1)
    ]
    steps.append(jnp.zeros_like(steps[0]))
    change_ref[...] = jnp.stack(steps, 1).reshape(change_ref.shape).astype(bf16)


def gate_kernel(place_ref, change_ref, hidden_ref, fine_ref, half_w_ref, quarter_w_ref, expand_ref,
                gated_ref, sigmoid_ref, merged_ref, half_ref, quarter_ref,
                pad_ref, pad_half_ref, pad_quarter_ref):
    place = place_ref[0]
    change = change_ref[...]
    own = gated_ref.shape[0]
    band = shift_columns(pad_ref, change, 8)
    first = pl.multiple_of(place * own, own)
    fine = conv_taps(pad_ref, band, first, own, fine_ref)
    half = dot(pool_matrix(own, 4 * own, 2, 8, 0.25), change).astype(bf16)
    half_ref[...] = half
    band = shift_columns(pad_half_ref, half, 4)
    coarse = conv_taps(pad_half_ref, band, pl.multiple_of(place * 32, 32), 32, half_w_ref)
    quarter = dot(pool_matrix(own // 4, own, 2, 4, 0.25), half)
    quarter_ref[...] = quarter
    band = shift_columns(pad_quarter_ref, quarter, 2)
    coarsest = conv_taps(
        pad_quarter_ref, band, pl.multiple_of(place // 2 * 16, 16), 16, quarter_w_ref,
        precision=lax.Precision.HIGHEST,
    )
    merged = (
        fine
        + split_dot(spread_matrix(own, 2, 8), coarse)
        + split_dot(spread_matrix(own, 4, 8), coarsest)
    ).astype(bf16)
    merged_ref[...] = merged
    sigmoid = jax.nn.sigmoid(dot(merged, expand_ref[...]))
    sigmoid_ref[...] = sigmoid
    gated_ref[...] = (hidden_ref[...].astype(f32) * (1.0 + sigmoid)).astype(bf16)


def second_kernel(two_rows, gated_ref, packed_ref, second_ref, weight_ref, sums_ref, pad_ref):
    for clip in range(packed_ref.shape[0]):
        weight_ref[two_rows * clip : two_rows * clip + two_rows] = packed_ref[clip, :two_rows]
    band = shift_columns(pad_ref, gated_ref[...], 8)
    second = conv_taps(pad_ref, band, 0, second_ref.shape[0], weight_ref)
    second_ref[...] = second
    put_sums(sums_ref, column_sum(second), column_sum(second * second))


def hidden_two_kernel(count, place_ref, sums_ref, second_ref, gain_ref, bias_ref, hidden_ref, norm_ref):
    mean, inverse = norm_of(sums_ref, 1, count)
    norm_ref[...] = jnp.concatenate([mean, inverse], 0)
    gain, bias = own_lanes(place_ref, gain_ref, bias_ref)
    level = (second_ref[...] - mean) * inverse * gain + bias
    hidden_ref[...] = silu(level).astype(bf16)


def third_kernel(two_rows, three_rows, hidden_ref, packed_ref, third_ref, weight_ref, sums_ref):
    start = padded(two_rows)
    for block in range(weight_ref.shape[1] // 128):
        for clip in range(packed_ref.shape[0]):
            weight_ref[
                three_rows * clip : three_rows * clip + three_rows, 128 * block : 128 * block + 128
            ] = packed_ref[clip, start : start + three_rows]
        start += padded(three_rows)
    third = None
    for part in range(hidden_ref.shape[0]):
        term = dot(hidden_ref[part], weight_ref[128 * part : 128 * part + 128, :])
        third = term if third is None else third + term
    third_ref[...] = third
    put_sums(sums_ref, column_sum(third), column_sum(third * third))


def sources(place, size):
    return [place ^ s for s in range(size)]


def output_kernel(count, place_ref, sums_ref, third_ref, gain_ref, bias_ref,
                  x0_ref, x1_ref, x2_ref, x3_ref, c0_ref, c1_ref, c2_ref, c3_ref,
                  low_ref, high_ref, send_ref, slope_ref, norm_ref, out_sums_ref):
    place = place_ref[0]
    mean, inverse = norm_of(sums_ref, 4, count)
    norm_ref[...] = jnp.concatenate([mean, inverse], 0)
    gain, bias = own_lanes(place_ref, gain_ref, bias_ref)
    own, wide = x0_ref.shape[0], third_ref.shape[1]
    lanes_r = pl.ds(pl.multiple_of(place * wide, wide), wide)
    total_bias, total_gain = jnp.zeros((1, wide), f32), jnp.zeros((1, wide), f32)
    pieces = zip(
        sources(place, 4), (x0_ref, x1_ref, x2_ref, x3_ref), (c0_ref, c1_ref, c2_ref, c3_ref)
    )
    for source, x_ref, c_ref in pieces:
        rows = pl.ds(pl.multiple_of(source * own, own), own)
        normed = (third_ref[rows] - mean) * inverse
        summed = normed * gain + bias + x_ref[:, lanes_r].astype(f32)
        sigmoid = jax.nn.sigmoid(summed)
        send_ref[pl.ds(source, 1), 0] = (summed * sigmoid).astype(bf16)[None]
        slope = c_ref[...].astype(f32) * (sigmoid * (1.0 + summed * (1.0 - sigmoid)))
        slope_ref[rows] = slope
        send_ref[pl.ds(source, 1), 1] = slope.astype(bf16)[None]
        total_bias += column_sum(slope)
        total_gain += column_sum(slope * normed)
    put_sums(out_sums_ref, total_bias, total_gain, stem_row(low_ref, high_ref))


def third_back_kernel(count, place_ref, sums_ref, third_ref, slope_ref, norm_ref, gain_ref, weight_ref,
                      grad_ref, part_ref, vectors_ref):
    total_bias, total_gain = get_sums(sums_ref, 4)
    vectors_ref[...] = jnp.concatenate([as_block(total_bias), as_block(total_gain)], 0)
    mean, inverse = norm_ref[0:1], norm_ref[1:2]
    normed = (third_ref[...] - mean) * inverse
    grad = own_lanes(place_ref, gain_ref)[0] * inverse * (
        slope_ref[...] - total_bias / count - normed * (total_gain / count)
    )
    grad = grad.astype(bf16)
    grad_ref[...] = grad
    back = dot(grad, weight_ref[...], "NT").astype(bf16)
    rest, stem = jnp.sum(sums_ref[:, 8:16], 0), []
    for _ in range(2):
        stem.append(rest.astype(bf16).astype(f32))
        rest = rest - stem[-1]
    order = stack_index((16, 128), 0)
    stem = jnp.where(
        order == 0, stem[0][0:1], jnp.where(order == 1, stem[1][0:1], rest[0:1])
    ).astype(bf16)
    rows = grad.shape[0]
    for part in range(part_ref.shape[0]):
        part_ref[part, :rows] = back[:, 128 * part : 128 * part + 128]
        part_ref[part, rows:] = stem


def second_slope_kernel(place_ref, part_ref, second_ref, norm_ref, gain_ref, bias_ref,
                        grad_ref, stem_ref, sums_ref):
    rows = second_ref.shape[0]
    back = jnp.sum(part_ref[:, :rows].astype(f32), 0)
    stem = jnp.sum(part_ref[:, rows:].astype(f32), 0)
    stem_ref[...] = jnp.broadcast_to(stem[0:1] + stem[1:2] + stem[2:3], stem_ref.shape)
    normed = (second_ref[...] - norm_ref[0:1]) * norm_ref[1:2]
    gain, bias = own_lanes(place_ref, gain_ref, bias_ref)
    grad = back * silu_slope(normed * gain + bias)
    grad_ref[...] = grad
    put_sums(sums_ref, column_sum(grad), column_sum(grad * normed))


def second_back_kernel(count, place_ref, sums_ref, slope_ref, second_ref, norm_ref, gain_ref, weight_ref,
                       grad_ref, part_ref, vectors_ref, pad_ref):
    total_bias, total_gain = get_sums(sums_ref, 1)
    vectors_ref[...] = jnp.concatenate([total_bias, total_gain], 0)
    inverse = norm_ref[1:2]
    normed = (second_ref[...] - norm_ref[0:1]) * inverse
    grad = own_lanes(place_ref, gain_ref)[0] * inverse * (
        slope_ref[...] - total_bias / count - normed * (total_gain / count)
    )
    grad = grad.astype(bf16)
    grad_ref[...] = grad
    band = shift_columns(pad_ref, grad, 8)
    own = part_ref.shape[1]
    for part in range(part_ref.shape[0]):
        back = conv_taps(pad_ref, band, part * own, own, weight_ref, True)
        part_ref[part] = back.astype(bf16)


def split_blocks(side, first_ref, second_ref, put):
    for index in range(2 * first_ref.shape[0]):
        own, rest = (first_ref, second_ref) if index % 2 == 0 else (second_ref, first_ref)

        @pl.when(side == 0)
        def _():
            put(index, own, index // 2)

        @pl.when(side == 1)
        def _():
            put(index, rest, index // 2)


def wide_grads_kernel(side_ref, gated_ref, grad_ref, hidden_ref, third_ref,
                      keep_ref, send_ref, pad_ref, all_ref):
    band = shift_columns(pad_ref, gated_ref[...], 8)
    rows, channels = gated_ref.shape
    clips = 2 * keep_ref.shape[0]
    two_rows = 9 * channels // clips
    for ky, kx in taps:
        tap = 3 * ky + kx
        all_ref[tap * channels : (tap + 1) * channels, :] = dot(
            pad_ref[kx, ky * band : ky * band + rows], grad_ref[...], "TN"
        ).astype(bf16)
    start = 9 * channels
    for part in range(hidden_ref.shape[0]):
        value = dot(hidden_ref[part], third_ref[...], "TN").astype(bf16)
        for block in range(value.shape[1] // 128):
            first = start + channels * block + 128 * part
            all_ref[first : first + 128] = value[:, 128 * block : 128 * block + 128]
    three_rows = channels // clips

    def put(clip, out_ref, index):
        out_ref[index, 0:two_rows] = all_ref[two_rows * clip : two_rows * clip + two_rows]
        at = padded(two_rows)
        for block in range(third_ref.shape[1] // 128):
            first = start + channels * block + three_rows * clip
            out_ref[index, at : at + three_rows] = all_ref[first : first + three_rows]
            at += padded(three_rows)

    split_blocks(side_ref[0], keep_ref, send_ref, put)


def halve_kernel(side_ref, held_ref, arrived_ref, keep_ref, send_ref):
    def put(source, out_ref, index):
        total = held_ref[source].astype(f32) + arrived_ref[source].astype(f32)
        out_ref[index] = total.astype(bf16)

    split_blocks(side_ref[0], keep_ref, send_ref, put)


def last_kernel(held_ref, arrived_ref, three_ref, two_ref, out_ref):
    rows = held_ref.shape[1]
    total = held_ref[0].astype(f32) + arrived_ref[0].astype(f32)
    out_ref[0:rows] = total.astype(bf16)
    vectors = jnp.concatenate([three_ref[...], two_ref[...], jnp.zeros((6, 128), f32)], 0)
    upper = vectors.astype(bf16)
    out_ref[rows : rows + 16] = upper
    out_ref[rows + 16 : rows + 32] = (vectors - upper.astype(f32)).astype(bf16)


def gate_back_kernel(part_ref, hidden_ref, sigmoid_ref, expand_ref,
                     fine_ref, gate_ref, hidden_grad_ref):
    gated = jnp.sum(part_ref[...].astype(f32), 0)
    sigmoid = sigmoid_ref[...]
    gate = (gated * hidden_ref[...].astype(f32) * sigmoid * (1.0 - sigmoid)).astype(bf16)
    gate_ref[...] = gate
    hidden_grad_ref[...] = gated * (1.0 + sigmoid)
    fine_ref[...] = dot(gate, expand_ref[...], "NT").astype(bf16)


def reduce_back_kernel(place_ref, mask_ref, grad_ref, fine_ref, half_w_ref, quarter_w_ref,
                       reduce_ref, hidden_grad_ref, first_ref, norm_ref, gain_ref, bias_ref,
                       reduced_ref, slope_ref, coarse_ref, coarsest_ref, sums_ref,
                       pad_ref, pad_half_ref, pad_quarter_ref):
    place = place_ref[0]
    own = reduced_ref.shape[0]
    grad_fine = grad_ref[...]
    coarse = dot(pool_matrix(own, 4 * own, 2, 8, 1.0), grad_fine).astype(bf16)
    coarse_ref[...] = coarse
    coarsest = dot(pool_matrix(own // 4, 4 * own, 4, 8, 1.0), grad_fine)
    coarsest_ref[...] = coarsest
    band = shift_columns(pad_quarter_ref, coarsest, 2)
    low = conv_taps(
        pad_quarter_ref, band, pl.multiple_of(place // 2 * 16, 16), 16, quarter_w_ref, True,
        lax.Precision.HIGHEST,
    )
    band = shift_columns(pad_half_ref, coarse, 4)
    middle = conv_taps(pad_half_ref, band, pl.multiple_of(place * 32, 32), 32, half_w_ref, True)
    middle = middle + 0.25 * split_dot(spread_matrix(32, 2, 4), low)
    band = shift_columns(pad_ref, grad_fine, 8)
    change = conv_taps(pad_ref, band, pl.multiple_of(place * own, own), own, fine_ref, True)
    change = change + 0.25 * split_dot(spread_matrix(own, 2, 8), middle)
    change = change.reshape(-1, SEG, 8, change.shape[1])
    carried = [mask_ref[0, t].astype(f32) * change[:, t] for t in range(SEG - 1)]
    zero = jnp.zeros_like(carried[0])
    before, here = [zero] + carried, carried + [zero]
    reduced = jnp.stack([b - h for b, h in zip(before, here)], 1)
    reduced = reduced.reshape(reduced_ref.shape).astype(bf16)
    reduced_ref[...] = reduced
    grad_hidden = hidden_grad_ref[...] + dot(reduced, reduce_ref[...], "NT")
    normed = (first_ref[...] - norm_ref[0:1]) * norm_ref[1:2]
    slope = grad_hidden * silu_slope(normed * gain_ref[...] + bias_ref[...])
    slope_ref[...] = slope
    put_sums(sums_ref, column_sum(slope), column_sum(slope * normed))


def first_back_kernel(count, sums_ref, slope_ref, first_ref, norm_ref, gain_ref,
                      grad_ref, vectors_ref):
    total_bias, total_gain = get_sums(sums_ref, 4)
    vectors_ref[...] = jnp.concatenate([total_bias, total_gain], 0)
    inverse = norm_ref[1:2]
    normed = (first_ref[...] - norm_ref[0:1]) * inverse
    grad = gain_ref[...] * inverse * (
        slope_ref[...] - total_bias / count - normed * (total_gain / count)
    )
    grad_ref[...] = grad.astype(bf16)


def one_grad_kernel(place_ref, grad_ref, x0_ref, x1_ref, x2_ref, x3_ref, out_ref):
    place = place_ref[0]
    wide = out_ref.shape[1]
    lanes_r = pl.ds(pl.multiple_of(place * wide, wide), wide)
    total = None
    for source, x_ref in zip(sources(place, 4), (x0_ref, x1_ref, x2_ref, x3_ref)):
        grad = grad_ref[pl.ds(source, 1), :, lanes_r][0]
        term = dot(x_ref[...], grad, "TN")
        total = term if total is None else total + term
    out_ref[...] = total.astype(bf16)


def small_grads_kernel(change_ref, half_ref, quarter_ref, grad_ref, coarse_ref, coarsest_ref,
                       hidden_ref, reduced_ref, merged_ref, gate_ref,
                       fine_ref, half_w_ref, quarter_w_ref, reduce_ref, expand_ref,
                       pad_ref, pad_half_ref, pad_quarter_ref):
    scales = (
        (change_ref, grad_ref, fine_ref, pad_ref, 8, None),
        (half_ref, coarse_ref, half_w_ref, pad_half_ref, 4, None),
        (quarter_ref, coarsest_ref, quarter_w_ref, pad_quarter_ref, 2, lax.Precision.HIGHEST),
    )
    for map_ref, cot_ref, out_ref, padded_ref, width, precision in scales:
        rows, channels = map_ref.shape
        band = shift_columns(padded_ref, map_ref[...], width)
        for ky, kx in taps:
            tap = 3 * ky + kx
            out_ref[tap * channels : (tap + 1) * channels, :] = dot(
                padded_ref[kx, ky * band : ky * band + rows], cot_ref[...], "TN", precision
            ).astype(bf16)
    reduce_ref[...] = dot(hidden_ref[...], reduced_ref[...], "TN").astype(bf16)
    value = dot(merged_ref[...], gate_ref[...], "TN").astype(bf16)
    for block in range(expand_ref.shape[0]):
        expand_ref[block] = value[:, 128 * block : 128 * block + 128]


def input_grad_kernel(place_ref, grad_ref, weight_ref, r0_ref, r1_ref, r2_ref, r3_ref,
                      input_ref, out_ref):
    place = place_ref[0]
    wide = r0_ref.shape[2]
    for source, r_ref in zip(sources(place, 4), (r0_ref, r1_ref, r2_ref, r3_ref)):
        lanes_r = pl.ds(pl.multiple_of(source * wide, wide), wide)
        weight = weight_ref[pl.ds(pl.multiple_of(source * wide, wide), wide), :]
        value = dot(grad_ref[...], weight, "NT") + r_ref[1].astype(f32)
        shape = (input_ref.shape[1], input_ref.shape[0], input_ref.shape[2], wide)
        value, result = value.reshape(shape), r_ref[0].astype(f32).reshape(shape)
        for row in range(shape[0]):
            input_ref[:, row, :, lanes_r] = value[row]
            out_ref[:, row, :, lanes_r] = result[row].astype(bf16)


class Fresh:
    def __init__(self, array):
        self.array = array


def call(kernel, scalars, arrays, outs, scratch=(), waits=(), flops=10**9, moved=2 * 10**6):
    used = len(scalars) + len(arrays)

    def body(*refs):
        kernel(*refs[:used], *refs[used + len(waits) :])

    shapes = [(entry.array if isinstance(entry, Fresh) else entry).shape for entry in arrays]
    return pl.pallas_call(
        body,
        grid=(1,),
        in_specs=[pl.BlockSpec(memory_space=pltpu.SMEM)] * len(scalars)
        + [whole(shape) for shape in shapes]
        + [pl.BlockSpec(memory_space=pl.ANY)] * len(waits),
        out_specs=[whole(shape) for shape, _ in outs],
        out_shape=[pltpu.HBM(shape, dtype) for shape, dtype in outs],
        scratch_shapes=[pltpu.VMEM(shape, dtype) for shape, dtype in scratch],
        compiler_params=pltpu.CompilerParams(vmem_limit_bytes=block_limit),
        cost_estimate=pl.CostEstimate(flops=flops, bytes_accessed=moved, transcendentals=0),
    )(
        *scalars,
        *(entry.array if isinstance(entry, Fresh) else in_hbm(entry) for entry in arrays),
        *waits,
    )


def together(*values):
    return lax.optimization_barrier(values)


def exchange(blocks, axis):
    return lax.all_to_all(blocks, axis, 0, 0)


def to_all(part, axis):
    size = lax.axis_size(axis)
    return exchange(jnp.broadcast_to(part[None], (size,) + part.shape), axis)


def swap(piece, axis, step):
    return lax.ppermute(piece, axis, [(i, i ^ step) for i in range(lax.axis_size(axis))])


def lane_blocks(array):
    return [array[:, start : start + 128] for start in range(0, array.shape[1], 128)]


def pick(array, index, axis=0):
    return lax.dynamic_index_in_dim(array, index, axis, keepdims=False)


def per_device(
    frames,
    frame_start,
    boundary_mask,
    stem_weight,
    stem_gain,
    stem_bias,
    block_input,
    w_one,
    w_reduce,
    k_fine,
    k_half,
    k_quarter,
    w_expand,
    w_two,
    w_three,
    gain_one,
    bias_one,
    gain_two,
    bias_two,
    gain_three,
    bias_three,
    stem_cot,
    block_cot,
):
    nc, nr = lax.axis_size("clip"), lax.axis_size("row")
    u32 = jnp.uint32
    place = lax.axis_index("row").astype(u32)
    spots = [place ^ u32(s) for s in range(nr)]
    side = place & u32(1)
    clip = lax.axis_index("clip").astype(u32)
    bits, bit = [], 1
    while bit < nc:
        bits.append((bit, (clip // u32(bit)) & u32(1)))
        bit *= 2
    spot = place.astype(jnp.int32).reshape(1)
    both = ("clip", "row")
    images, block_rows, cols, c_in = block_input.shape
    mid, red = gain_one.shape[0], w_reduce.shape[1]
    mid_r, in_r = mid // nr, c_in // nr
    own = images * block_rows * cols
    pixels = own * nr
    count = float(pixels * nc)
    clip_sums = ((nc, 8, 128), f32)
    both_sums = ((nc * nr, 16, 128), f32)

    def in_part(array, index):
        return lax.dynamic_slice_in_dim(array, index * u32(in_r), in_r, array.ndim - 1)

    half = w_one.shape[0] // 2
    stem_taps = to_all(filters_inside(stem_weight), "clip").reshape(STEM, -1)
    expand_rows = padded(w_expand.shape[0])
    early_rows = padded(3 * padded(k_fine.shape[0]) + mid // 128 * expand_rows, 16 * nr)
    quarter_rows = early_rows // nr
    edges = [4 * padded(half)]
    for rows in (quarter_rows, w_reduce.shape[0]):
        edges.append(edges[-1] + padded(rows))
    two_rows, three_rows = w_two.shape[0], w_three.shape[0]
    two_end = padded(two_rows)
    part_rows = two_end + in_r // 128 * padded(three_rows)
    sides = [entry.astype(jnp.int32).reshape(1) for _, entry in bits]
    sent, parts = call(
        pack_kernel,
        (spot, side.astype(jnp.int32).reshape(1)),
        (w_one, k_fine, k_half, k_quarter, w_expand, w_reduce, w_two, w_three),
        (((nc, edges[-1], 128), bf16), ((part_rows, 128), bf16)),
        [((early_rows, 128), bf16)],
        (*sides, *[entry.reshape(1) for entry in spots]),
    )
    sent, stem_taps = together(sent, stem_taps)
    mine = exchange(sent, "clip")
    filters = jnp.concatenate(
        [jnp.pad(stem_taps, ((0, 0), (224 * y, 672 - 224 * y))) for y in range(4)], 0
    )

    x_own = block_input.swapaxes(0, 1).reshape(own, c_in)
    cot_own = block_cot.swapaxes(0, 1).reshape(own, c_in)

    local = frames[0]
    rows = local.shape[2]
    above = lax.ppermute(local[:, :, rows - 16 :], "row", [(i, i + 1) for i in range(nr - 1)])
    below = lax.ppermute(local[:, :, :16], "row", [(i + 1, i) for i in range(nr - 1)])
    cot_own, x_own, above, below = together(cot_own, x_own, above, below)
    planes = stem_planes(frame_start[0], local, above, below)
    stem_count = float(SEG * (rows // 2) * (local.shape[3] // 2) * nc * nr)
    cot_pieces = [in_part(cot_own, place)] + [
        swap(in_part(cot_own, spots[s]), "row", s) for s in range(1, nr)
    ]
    x_pieces = [x_own, swap(x_own, "row", 1), swap(x_own, "row", 2)]
    x_pieces.append(swap(x_pieces[2], "row", 1))

    stem_pre, stem_sums = stem_conv(planes, filters, *x_pieces[1:3], *cot_pieces[1:])
    mine, stem_sums = together(mine, stem_sums)
    other = swap(mine, "row", 1)
    parts, mine = together(parts, mine)
    packed = lax.all_gather(parts, "clip")
    full_one, first, sums = call(
        first_kernel,
        (side.astype(jnp.int32).reshape(1),),
        (x_own, Fresh(mine), Fresh(other), stem_sums),
        (((nc, 2, half, mid), bf16), ((own, mid), f32), both_sums),
    )
    full_one = full_one.reshape(c_in, mid)
    sums = exchange(sums, both)
    mine, other, first = together(mine, other, first)
    full_reduce = mine[:, edges[1] : edges[1] + w_reduce.shape[0]].reshape(mid, red)
    mine_early = mine[:, edges[0] : edges[1]]
    quarters = [mine_early, other[:, edges[0] : edges[1]]] + [
        swap(mine_early, "row", s) for s in (2, 3)
    ]
    quarters = [
        jnp.where(
            place == u32(q),
            quarters[0],
            jnp.where(
                place == u32(q ^ 1),
                quarters[1],
                jnp.where(place == u32(q ^ 2), quarters[2], quarters[3]),
            ),
        )
        for q in range(nr)
    ]
    quarters = jnp.concatenate(quarters, 1)
    early_parts, start = [], 0
    for size in (k_fine.shape[0],) * 3 + (w_expand.shape[0],) * (mid // 128):
        early_parts.append(quarters[:, start : start + size].reshape(-1, 128))
        start += padded(size)
    full_fine, full_half, full_quarter = early_parts[:3]
    full_expand = jnp.concatenate(early_parts[3:], 1)
    stem_totals = jnp.sum(sums[:, 8], 0).reshape(2, STEM)
    stem_mean, stem_inverse = statistics(stem_totals, stem_count)
    stem_vectors = lanes(stem_mean, stem_inverse, stem_gain, stem_bias)
    gain_one, bias_one = gain_one.reshape(1, -1), bias_one.reshape(1, -1)
    hidden_one, change, norm_one = call(
        functools.partial(hidden_kernel, count),
        (boundary_mask,),
        (Fresh(sums), first, gain_one, bias_one, full_reduce),
        (((own, mid), bf16), ((own, red), bf16), ((2, mid), f32)),
    )
    change = lax.all_gather(change, "row").reshape(pixels, red)
    pads = [
        ((3, pixels + 2 * images * cols, red), bf16),
        ((3, pixels // 4 + images * cols, red), bf16),
        ((3, pixels // 16 + images * cols // 2, red), f32),
    ]
    gated, sigmoid, merged, half_map, quarter = call(
        gate_kernel,
        (spot,),
        (Fresh(change), hidden_one, full_fine, full_half, full_quarter, full_expand),
        (
            ((own, mid), bf16),
            ((own, mid), f32),
            ((own, red), bf16),
            ((pixels // 4, red), bf16),
            ((pixels // 16, red), f32),
        ),
        pads,
    )
    gated = lax.all_gather(gated, "row").reshape(pixels, mid)
    second, two_r, sums = call(
        functools.partial(second_kernel, two_rows),
        (),
        (Fresh(gated), packed),
        (((pixels, mid_r), f32), ((9 * mid, mid_r), bf16), clip_sums),
        [((3, pixels + 2 * images * cols, mid), bf16)],
    )
    gain_two, bias_two = gain_two.reshape(1, -1), bias_two.reshape(1, -1)
    outer_low, slope_low = stem_slope(stem_pre, stem_cot, 0, stem_vectors, second)
    hidden_two, norm_two = call(
        functools.partial(hidden_two_kernel, count),
        (spot,),
        (Fresh(exchange(sums, "clip")), second, gain_two, bias_two),
        (((pixels, mid_r), bf16), ((2, mid_r), f32)),
        waits=(slope_low,),
    )
    hidden_two = lax.all_gather(hidden_two, "row")
    third, three_r, sums = call(
        functools.partial(third_kernel, two_rows, three_rows),
        (),
        (Fresh(hidden_two), packed),
        (((pixels, in_r), f32), ((mid, in_r), bf16), clip_sums),
    )
    outer_high, slope_high = stem_slope(stem_pre, stem_cot, 4, stem_vectors, third)
    gain_three, bias_three = gain_three.reshape(1, -1), bias_three.reshape(1, -1)
    send, slope_three, norm_three, sums = call(
        functools.partial(output_kernel, count),
        (spot,),
        (
            Fresh(exchange(sums, "clip")), third, gain_three, bias_three, *x_pieces, *cot_pieces,
            slope_low, slope_high,
        ),
        (
            ((nr, 2, own, in_r), bf16),
            ((pixels, in_r), f32),
            ((2, in_r), f32),
            ((nc, 16, 128), f32),
        ),
    )

    grad_third, parts, vectors_three = call(
        functools.partial(third_back_kernel, count),
        (spot,),
        (
            Fresh(exchange(sums, "clip")), third, slope_three, norm_three, gain_three, three_r,
        ),
        (((pixels, in_r), bf16), ((nr, pixels + 16, mid_r), bf16), ((8, 128), f32)),
    )
    slope_two, stem_totals, sums = call(
        second_slope_kernel,
        (spot,),
        (Fresh(exchange(parts, "row")), second, norm_two, gain_two, bias_two),
        (((pixels, mid_r), f32), ((8, 128), f32), clip_sums),
    )
    stem_bias_grad, stem_gain_grad = stem_totals[0].reshape(2, STEM)
    stem_vectors = lanes(
        stem_mean,
        stem_inverse,
        stem_gain * stem_inverse,
        stem_bias_grad / stem_count,
        stem_gain_grad / stem_count,
    )
    stem_low = stem_grad(planes, stem_pre, outer_low, 0, stem_vectors)
    grad_second, parts, vectors_two = call(
        functools.partial(second_back_kernel, count),
        (spot,),
        (
            Fresh(exchange(sums, "clip")), slope_two, second, norm_two, gain_two, two_r,
        ),
        (((pixels, mid_r), bf16), ((nr, own, mid), bf16), ((2, mid_r), f32)),
        [((3, pixels + 2 * images * cols, mid_r), bf16)],
        (stem_low,),
    )
    blocks = ((nc // 2, part_rows, 128), bf16)
    keep, give = call(
        wide_grads_kernel,
        (sides[0],),
        (gated, grad_second, hidden_two, grad_third),
        (blocks, blocks),
        [
            ((3, pixels + 2 * images * cols, mid), bf16),
            ((9 * mid + mid * in_r // 128, 128), bf16),
        ],
    )
    arrived = swap(give, "clip", 1)
    grad_fine, grad_gate, grad_hidden = call(
        gate_back_kernel,
        (),
        (Fresh(exchange(parts, "row")), hidden_one, sigmoid, full_expand),
        (((own, red), bf16), ((own, mid), bf16), ((own, mid), f32)),
        waits=(keep,),
    )
    grad_fine = lax.all_gather(grad_fine, "row").reshape(pixels, red)
    grad_reduced, slope_one, grad_coarse, grad_coarsest, sums = call(
        reduce_back_kernel,
        (spot, boundary_mask),
        (
            Fresh(grad_fine), full_fine, full_half, full_quarter, full_reduce,
            grad_hidden, first, norm_one, gain_one, bias_one,
        ),
        (
            ((own, red), bf16),
            ((own, mid), f32),
            ((pixels // 4, red), bf16),
            ((pixels // 16, red), f32),
            both_sums,
        ),
        pads,
    )
    fine_grad, half_grad, quarter_grad, reduce_grad, expand_grad = call(
        small_grads_kernel,
        (),
        (
            change, half_map, quarter, grad_fine, grad_coarse, grad_coarsest,
            hidden_one, grad_reduced, merged, grad_gate,
        ),
        [((9 * red, red), bf16)] * 3 + [((mid, red), bf16), ((mid // 128, red, 128), bf16)],
        pads,
    )
    sums = exchange(sums, both)
    stem_high = stem_grad(planes, stem_pre, outer_high, len(planes) // 2, stem_vectors, slope_one)
    grad_first, vectors_one = call(
        functools.partial(first_back_kernel, count),
        (),
        (Fresh(sums), slope_one, first, norm_one, gain_one),
        (((own, mid), bf16), ((2, mid), f32)),
        waits=(stem_high, fine_grad),
    )
    stem_blocks = (stem_low + stem_high).astype(bf16).reshape(nr, 8 // nr, nc, -1, 128)
    both_parts = [
        reduce_grad.reshape(nc, nr, -1, red),
        expand_grad.reshape(nr, nc, -1, red).swapaxes(0, 1),
        stem_blocks.transpose(2, 0, 1, 3, 4).reshape(nc, nr, -1, 128),
    ]
    both_rows = [part.shape[2] for part in both_parts]
    both_parts = jnp.concatenate(both_parts, 2).reshape(nc * nr, -1, 128)
    both_total = exchange(both_parts, both)
    both_total = jnp.sum(both_total, 0, dtype=f32).astype(bf16)

    def halving(keep, arrived, bit, side, *waits):
        rows = ((keep.shape[0] // 2, part_rows, 128), bf16)
        keep, give = call(halve_kernel, (side,), (keep, Fresh(arrived)), (rows, rows), (), waits)
        return keep, swap(give, "clip", bit)

    keep, arrived = halving(keep, arrived, bits[1][0], sides[1], slope_one)
    (one_grad,) = call(
        one_grad_kernel,
        (spot,),
        (Fresh(lax.all_gather(grad_first, "row")), *x_pieces),
        (((c_in, mid_r), bf16),),
    )
    send, one_grad = together(send, one_grad)

    def quarter_of(gradient):
        shares = gradient.reshape(nc, -1, red)
        shares = jnp.pad(shares, ((0, 0), (0, -shares.shape[1] % (8 * nr)), (0, 0)))
        return pick(shares.reshape(nc, nr, -1, red), place, 1)

    clip_parts = [one_grad.reshape(nc, -1, red)] + [
        quarter_of(gradient) for gradient in (fine_grad, half_grad, quarter_grad)
    ]
    one_rows, tap_rows = clip_parts[0].shape[1], clip_parts[1].shape[1]
    clip_parts = jnp.concatenate(clip_parts, 1)
    clip_parts, both_total = together(clip_parts, both_total)
    for (bit, _), spot_of in zip(bits[2:], sides[2:]):
        keep, arrived = halving(keep, arrived, bit, spot_of, one_grad)
    clip_total = jnp.sum(exchange(clip_parts, "clip"), 0, dtype=f32)
    returned = [pick(send, place)] + [
        swap(pick(send, spots[s]), "row", s) for s in range(1, nr)
    ]
    input_grad, block_out = call(
        input_grad_kernel,
        (spot,),
        (grad_first, full_one, *returned),
        ((block_input.shape, f32), (block_input.shape, bf16)),
    )

    def wide(blocks):
        return blocks.swapaxes(0, 1).reshape(blocks.shape[1], -1).astype(f32)

    (last,) = call(
        last_kernel,
        (),
        (keep, Fresh(arrived), vectors_three, vectors_two),
        (((part_rows + 32, 128), bf16),),
    )
    shares_a = lax.all_gather(last, "row")
    two_share = wide(shares_a[:, :two_rows])
    three_share = shares_a[:, two_end:part_rows].reshape(c_in // 128, -1, 128)
    three_share = wide(three_share[:, :three_rows])
    vectors = shares_a[:, part_rows:].astype(f32)
    vectors = vectors[:, :16] + vectors[:, 16:]
    clip_rows = clip_total.shape[0]
    shares_b = lax.all_gather(
        jnp.concatenate([clip_total.astype(bf16), both_total], 0), "row"
    )
    shares_c = shares_b[:, clip_rows:]
    one_share = wide(shares_b[:, :one_rows])
    tap_shares = [
        shares_b[:, start : start + tap_rows].reshape(-1, red)[: k_fine.shape[0]].astype(f32)
        for start in range(one_rows, clip_rows, tap_rows)
    ]
    reduce_share = shares_c[:, : both_rows[0]].reshape(-1, red).astype(f32)
    expand_share = wide(shares_c[:, both_rows[0] : both_rows[0] + both_rows[1]])
    stem_share = wide(shares_c[:, both_rows[0] + both_rows[1] :].reshape(8, -1, 128))[:, :784]
    return (
        block_out,
        input_grad,
        filters_outside(stem_share),
        stem_gain_grad,
        stem_bias_grad,
        one_share,
        reduce_share,
        *tap_shares,
        expand_share,
        two_share,
        three_share,
        vectors_one[1],
        vectors_one[0],
        vectors[:, 9].reshape(-1),
        vectors[:, 8].reshape(-1),
        vectors[:, 4:8].reshape(-1),
        vectors[:, 0:4].reshape(-1),
    )


def solution(mesh):
    in_specs = (
        P("clip", None, None, "row", None),
        P("clip", None),
        P("clip", None),
        P("clip", None),
        P(),
        P(),
        P("clip", "row", None, None),
        P("clip", None),
        P("clip", None),
        P("clip", None),
        P("clip", None),
        P("clip", None),
        P("clip", None),
        P("clip", None),
        P("clip", None),
        P(),
        P(),
        P(),
        P(),
        P(),
        P(),
        P("clip", None, "row", None),
        P("clip", "row", None, None),
    )
    out_specs = (
        P("clip", "row", None, None),
        P("clip", "row", None, None),
        P("clip", None),
        P(),
        P(),
        P("clip", None),
        P("clip", None),
        P("clip", None),
        P("clip", None),
        P("clip", None),
        P("clip", None),
        P("clip", None),
        P("clip", None),
        P(),
        P(),
        P(),
        P(),
        P(),
        P(),
    )
    return jax.shard_map(
        per_device, mesh=mesh, in_specs=in_specs, out_specs=out_specs, check_vma=False
    )
```

time: 1710 us -> 352 us (0.21)
  waiting for transfers between devices: 918 us -> 22.2 us
  blocking collectives: 447 us -> 77.2 us
  matrix products: 183 us -> 0 us
  Pallas kernels: 0 us -> 131 us
  local copies, waits for them, and re-layouts: 59.5 us -> 23.5 us
  other arithmetic: 45.5 us -> 11 us
  starting transfers between devices: 35.6 us -> 67.6 us
    reduce_scatter x9 -> x0, waiting for transfers between devices: 666 us -> none  [the longest x1 168 us: per_device(): lax.psum_scatter(row_totals[7], 'clip', scatter_dimension=0, tiled=True)]
    psum x6 -> x0, blocking collectives: 251 us -> none  [the longest x4 170 us: norm_forward(): lax.psum((jnp.sum(pre_act, sum_axes), jnp.sum(pre_act * pre_act, sum_axes...]
    psum x1 -> x0, waiting for transfers between devices: 187 us -> none  [per_device(): lax.psum(partial_grads[0].astype(jnp.bfloat16), 'row').astype(jnp.float32)]
    all_gather x7, blocking collectives: 196 us -> 51.8 us  [the longest x1 9.55 us: per_device(): shares_a = lax.all_gather(last, 'row')]
    pallas_call x0 -> x27, Pallas kernels: none -> 131 us  [the longest x6 68.5 us: stem_call(): pl.pallas_call(body, grid=(steps,), in_specs=in_specs + [pl.BlockSpec(mem...]
    slice x1 -> x0, matrix products: 111 us -> none  [per_device(): lax.conv_general_dilated(padded_stem, stem_grad.astype(jnp.bfloat16), (1,...]
    unnamed x15 -> x1, waiting for transfers between devices: 64.6 us -> 0.02 us
    conv_general_dilated x13 -> x0, matrix products: 53.5 us -> none  [the longest x1 38.1 us: per_device(): lax.conv_general_dilated(padded_stem, stem_kernel, (2, 2), 'VALID', dimen...]
  transfers between devices with their start and end apart: 28 -> 28, of which waited for: 12 -> 8; matrix products, arithmetic and copies ran while one was open for 8% -> 5% of each run, Pallas kernels for 0% -> 34%
where the time goes in v2:
time: 352 us; the launch traced here: 347 us
  Pallas kernels  131 us (37%)
  blocking collectives  77.2 us (22%)
  starting transfers between devices  67.6 us (19%)
  local copies, waits for them, and re-layouts  23.5 us (7%)
  waiting for transfers between devices  22.2 us (6%)
  between operations  14.5 us (4%)
  other arithmetic  11 us (3%)
    pallas_call x6, Pallas kernels, stem_call(): pl.pallas_call(body, grid=(steps,), in_specs=in_specs + [pl.BlockSpec(mem...  68.5 us
    pallas_call x21, Pallas kernels, call(): pl.pallas_call(body, grid=(1,), in_specs=[pl.BlockSpec(memory_space=pltpu...  62.1 us
    all_to_all x10, starting transfers between devices, exchange(): return lax.all_to_all(blocks, axis, 0, 0)  49.5 us
    all_to_all x2, blocking collectives, exchange(): return lax.all_to_all(blocks, axis, 0, 0)  25.4 us
    ppermute x15, starting transfers between devices, swap(): lax.ppermute(piece, axis, [(i, i ^ step) for i in range(lax.axis_size(axi...  13.1 us
    ppermute x15, waiting for transfers between devices, swap(): lax.ppermute(piece, axis, [(i, i ^ step) for i in range(lax.axis_size(axi...  12.5 us
    all_gather x1, blocking collectives, per_device(): shares_a = lax.all_gather(last, 'row')  9.55 us
    unnamed x71, local copies, waits for them, and re-layouts  9.34 us
  transfers between devices with their start and end apart: 28, of which 8 were waited for; matrix products, arithmetic and copies ran while one was open for 5% of the time, Pallas kernels for 34%

profile of v2, /device:TPU:0, one launch (start us, length us, event | category | flops | bytes accessed | tf_op | source)
XLA Modules:
  0.0 346.6 jit_solution(4918258831004644193)
XLA Ops:
  9.1 7.3 %all-to-all-start = ((bf16[8,8,784]{2,1,0:T(8,128)(2,1)}), bf16[8,8,784]{2,1,0:T(8,128)(2,1)S(1)}, u32[]{:S(2)}, u32[]{:S(2)}) async-start(bf16[8,8,784]{2,1,0:T(8,128)(2,1)} %broadcast_in_dim.9), calls=%async_computation | async-start | bytes 229376 | tf_op jit(solution)/shard_map/all_to_all | solution.py:825
  18.7 3.7 %collective-permute-start = (bf16[12,3,16,256]{3,2,1,0:T(8,128)(2,1)S(1)}, bf16[12,3,16,256]{3,2,1,0:T(8,128)(2,1)}, u32[]{:S(2)}, u32[]{:S(2)}) collective-permute-start(bf16[12,3,16,256]{3,2,1,0:T(8,128)(2,1)S(1)} %get-tuple-element.205), channel_id=1, source_target_pairs={{0,1},{1,2},{2,3},{4,5},{5,6},{6,7},{8,9},{9,10},{10,11},{12,13},{... | collective-permute-start | bytes 884744 | tf_op jit(solution)/shard_map/ppermute | solution.py:925
  23.4 2.7 shard_map.366
  26.1 6.0 %all-to-all-start.1 = ((bf16[8,704,128]{2,1,0:T(8,128)(2,1)}), bf16[8,704,128]{2,1,0:T(8,128)(2,1)S(1)}, u32[]{:S(2)}, u32[]{:S(2)}) async-start(bf16[8,704,128]{2,1,0:T(8,128)(2,1)} %get-tuple-element.102), calls=%async_computation.1 | async-start | bytes 2883584 | tf_op jit(solution)/shard_map/all_to_all | solution.py:825
  36.9 18.0 %shard_map.367.refs_0_ = bf16[4,80,112,256]{3,2,1,0:T(8,128)(2,1)} custom-call(s32[8]{0:T(128)S(1)} %bitcast.130, bf16[12,3,64,256]{3,2,1,0:T(8,128)(2,1)} %bitcast.152, bf16[12,3,16,256]{3,2,1,0:T(8,128)(2,1)} %collective-permute-done.refs_2_, bf16[12,3,16,256]{3,2,1,0:T(8,128)(2,1)} %copy-done.30), custom_call_target="tpu_custom_call" | custom-call | flops 16000000000 | bytes 20000000 | tf_op jit(solution)/shard_map/pallas_call | solution.py:178
  55.0 16.4 %shard_map.368 = (f32[8,32,64,128]{3,2,1,0:T(8,128)}, f32[2,64,128]{2,1,0:T(8,128)S(1)}) custom-call(bf16[4,80,112,256]{3,2,1,0:T(8,128)(2,1)} %shard_map.367.refs_0_, bf16[256,1456]{1,0:T(8,128)(2,1)} %fusion.7.refs_1_, bf16[128,2048]{1,0:T(8,128)(2,1)S(1)} %collective-permute-done.2.refs_2_.refs_6_.refs_3_, ...), custom_call_target="tpu_custom_call" | custom-call | flops 16000000000 | bytes 28000000 | tf_op jit(solution)/shard_map/pallas_call | solution.py:178
  72.6 2.8 collective-permute-done.7.refs_3_
  75.4 3.3 shard_map.369
  81.5 5.8 %all-to-all-start.2 = ((f32[32,16,128]{2,1,0:T(8,128)}), f32[32,16,128]{2,1,0:T(8,128)S(1)}, u32[]{:S(2)}, u32[]{:S(2)}) async-start(f32[32,16,128]{2,1,0:T(8,128)} %get-tuple-element.111), calls=%async_computation.2 | async-start | bytes 524288 | tf_op jit(solution)/shard_map/all_to_all | solution.py:825
  87.3 6.8 %collective-permute-done.8 = bf16[8,128,128]{2,1,0:T(8,128)(2,1)S(1)} collective-permute-done((bf16[8,128,128]{2,1,0:T(8,128)(2,1)S(1)}, bf16[8,128,128]{2,1,0:T(8,128)(2,1)S(1)}, u32[]{:S(2)}, u32[]{:S(2)}) %collective-permute-start.8) | collective-permute-done | bytes 262176 | tf_op jit(solution)/shard_map/ppermute | solution.py:834
  96.8 3.4 all-to-all-done.2.refs_1_
  102.1 5.6 %all-gather.refs_1_.refs_0_ = bf16[512,128]{1,0:T(8,128)(2,1)S(1)} all-gather(bf16[128,128]{1,0:T(8,128)(2,1)} %get-tuple-element.115), channel_id=2, replica_groups=mesh['clip'=8,'row'=4] {'row'}, dimensions={0}, use_global_device_ids=true | all-gather | bytes 163840 | tf_op jit(solution)/shard_map/all_gather | solution.py:984
  107.7 3.9 %shard_map.371 = (bf16[128,512]{1,0:T(8,128)(2,1)}, f32[128,512]{1,0:T(8,128)}, bf16[128,128]{1,0:T(8,128)(2,1)}, bf16[128,128]{1,0:T(8,128)(2,1)}, f32[32,128]{1,0:T(8,128)}) custom-call(s32[1]{0:T(128)} %bitcast.refs_0_, bf16[512,128]{1,0:T(8,128)(2,1)S(1)} %all-gather.refs_1_.refs_0_, bf16[128,512]{1,0:T(8,128)(2,1)} %get-tuple-element.116.refs_2_.refs_1_.refs_6_, ...), custom_call_target="tpu_custom_call" | custom-call | flops 1000000000 | bytes 2000000 | tf_op jit(solution)/shard_map/pallas_call | solution.py:802
  111.8 7.5 %all-gather.1.refs_0_.refs_1_ = bf16[512,512]{1,0:T(8,128)(2,1)S(1)} all-gather(bf16[128,512]{1,0:T(8,128)(2,1)} %get-tuple-element.118), channel_id=3, replica_groups=mesh['clip'=8,'row'=4] {'row'}, dimensions={0}, use_global_device_ids=true | all-gather | bytes 655360 | tf_op jit(solution)/shard_map/all_gather | solution.py:1003
  119.3 3.3 all-gather.10.cloned.1.call-done
  122.6 3.7 %shard_map.372 = (f32[512,128]{1,0:T(8,128)}, bf16[4608,128]{1,0:T(8,128)(2,1)}, f32[8,8,128]{2,1,0:T(8,128)}) custom-call(bf16[512,512]{1,0:T(8,128)(2,1)S(1)} %all-gather.1.refs_0_.refs_1_, bf16[8,832,128]{2,1,0:T(8,128)(2,1)} %bitcast.188), custom_call_target="tpu_custom_call" | custom-call | flops 1000000000 | bytes 2000000 | tf_op jit(solution)/shard_map/pallas_call | solution.py:802
  126.3 3.6 %all-to-all-start.3 = ((f32[8,8,128]{2,1,0:T(8,128)}), f32[8,8,128]{2,1,0:T(8,128)S(1)}, u32[]{:S(2)}, u32[]{:S(2)}) async-start(f32[8,8,128]{2,1,0:T(8,128)} %get-tuple-element.120), calls=%async_computation.3 | async-start | bytes 65536 | tf_op jit(solution)/shard_map/all_to_all | solution.py:825
  131.6 6.1 %shard_map.373 = (bf16[4,32,64,128]{3,2,1,0:T(8,128)(2,1)}, f32[2,64,128]{2,1,0:T(8,128)S(1)}) custom-call(f32[8,32,64,128]{3,2,1,0:T(8,128)} %get-tuple-element.122.refs_0_.refs_1_, bf16[8,64,32,128]{3,2,1,0:T(8,128)(2,1)} %refs_1_.4, f32[4,64,128]{2,1,0:T(8,128)} %broadcast_in_dim.10.refs_2_, f32[512,128]{1,0:T(8,128)S(1)} %copy-done.21), custom_call_target="tpu_custom_call" | custom-call | flops 4000000000 | bytes 8000000 | tf_op jit(solution)/shard_map/pallas_call | solution.py:178
  139.4 7.5 %all-gather.3 = bf16[2048,128]{1,0:T(8,128)(2,1)S(1)} all-gather(bf16[512,128]{1,0:T(8,128)(2,1)} %get-tuple-element.124), channel_id=5, replica_groups=mesh['clip'=8,'row'=4] {'row'}, dimensions={0}, use_global_device_ids=true | all-gather | bytes 655360 | tf_op jit(solution)/shard_map/all_gather | solution.py:1020
  147.0 3.4 shard_map.375
  150.4 6.0 %all-to-all-start.4 = ((f32[8,8,128]{2,1,0:T(8,128)}), f32[8,8,128]{2,1,0:T(8,128)S(1)}, u32[]{:S(2)}, u32[]{:S(2)}) async-start(f32[8,8,128]{2,1,0:T(8,128)} %get-tuple-element.125), calls=%async_computation.4 | async-start | bytes 65536 | tf_op jit(solution)/shard_map/all_to_all | solution.py:825
  157.6 6.1 %shard_map.376 = (bf16[4,32,64,128]{3,2,1,0:T(8,128)(2,1)}, f32[2,64,128]{2,1,0:T(8,128)S(1)}) custom-call(f32[8,32,64,128]{3,2,1,0:T(8,128)} %get-tuple-element.122.refs_0_.refs_1_, bf16[8,64,32,128]{3,2,1,0:T(8,128)(2,1)} %refs_1_.4, f32[4,64,128]{2,1,0:T(8,128)} %broadcast_in_dim.10.refs_2_, f32[512,512]{1,0:T(8,128)S(1)} %copy-done), custom_call_target="tpu_custom_call" | custom-call | flops 4000000000 | bytes 8000000 | tf_op jit(solution)/shard_map/pallas_call | solution.py:178
  165.2 4.2 %shard_map.377 = (bf16[4,2,128,512]{3,2,1,0:T(8,128)(2,1)}, f32[512,512]{1,0:T(8,128)}, f32[2,512]{1,0:T(2,128)}, f32[8,16,128]{2,1,0:T(8,128)}) custom-call(s32[1]{0:T(128)} %bitcast.refs_0_, f32[8,8,128]{2,1,0:T(8,128)S(1)} %all-to-all-done.4.refs_1_, f32[512,512]{1,0:T(8,128)} %get-tuple-element.126.refs_3_.refs_2_, f32[1,2048]{1,0:T(1,128)} %bitcast.176, ...), custom_call_target="tpu_custom_call" | custom-call | flops 1000000000 | bytes 2000000 | tf_op jit(solution)/shard_map/pallas_call | solution.py:802
  169.4 12.9 %all_to_all.60.refs_1_ = f32[8,16,128]{2,1,0:T(8,128)S(1)} all-to-all(f32[8,16,128]{2,1,0:T(8,128)} %get-tuple-element.128), channel_id=1, replica_groups=mesh['clip'=8,'row'=4] {'clip'}, dimensions={0} | all-to-all | bytes 131072 | tf_op jit(solution)/shard_map/all_to_all | solution.py:825
  182.3 3.1 shard_map.378
  185.3 12.5 %all_to_all.61.refs_1_ = bf16[4,528,128]{2,1,0:T(8,128)(2,1)S(1)} all-to-all(bf16[4,528,128]{2,1,0:T(8,128)(2,1)} %get-tuple-element.132), channel_id=1, replica_groups=mesh['clip'=8,'row'=4] {'row'}, dimensions={0} | all-to-all | bytes 1081344 | tf_op jit(solution)/shard_map/all_to_all | solution.py:825
  201.0 3.3 all-to-all-start.7
  205.1 11.0 %shard_map.380.refs_7_ = f32[8,64,128]{2,1,0:T(8,128)S(1)} custom-call(bf16[4,80,112,256]{3,2,1,0:T(8,128)(2,1)} %shard_map.367.refs_0_, f32[8,32,64,128]{3,2,1,0:T(8,128)} %get-tuple-element.122.refs_0_.refs_1_, bf16[4,32,64,128]{3,2,1,0:T(8,128)(2,1)} %get-tuple-element.137.refs_2_, f32[5,64,128]{2,1,0:T(8,128)} %broadcast_in_dim.22.refs_3_), custom_call_target="tpu_custom_call" | custom-call | flops 8000000000 | bytes 16000000 | tf_op jit(solution)/shard_map/pallas_call | solution.py:178
  216.1 3.7 %shard_map.381 = (bf16[512,128]{1,0:T(8,128)(2,1)}, bf16[4,128,512]{2,1,0:T(8,128)(2,1)}, f32[2,128]{1,0:T(2,128)}) custom-call(s32[1]{0:T(128)} %bitcast.refs_0_, f32[8,8,128]{2,1,0:T(8,128)S(1)} %all-to-all-done.7.refs_1_, f32[512,128]{1,0:T(8,128)} %get-tuple-element.135.refs_2_, f32[512,128]{1,0:T(8,128)} %get-tuple-element.121.refs_3_.refs_2_, ...), custom_call_target="tpu_custom_call" | custom-call | flops 1000000000 | bytes 2000000 | tf_op jit(solution)/shard_map/pallas_call | solution.py:802
  219.8 3.5 %all-to-all-start.8 = ((bf16[4,128,512]{2,1,0:T(8,128)(2,1)}), bf16[4,128,512]{2,1,0:T(8,128)(2,1)S(1)}, u32[]{:S(2)}, u32[]{:S(2)}) async-start(bf16[4,128,512]{2,1,0:T(8,128)(2,1)} %get-tuple-element.139), calls=%async_computation.8 | async-start | bytes 1048576 | tf_op jit(solution)/shard_map/all_to_all | solution.py:825
  223.3 4.5 %shard_map.382 = (bf16[4,832,128]{2,1,0:T(8,128)(2,1)}, bf16[4,832,128]{2,1,0:T(8,128)(2,1)}) custom-call(s32[1]{0:T(128)} %bitcast.7.refs_10_.refs_0_, bf16[512,512]{1,0:T(8,128)(2,1)} %copy-done.2, bf16[512,128]{1,0:T(8,128)(2,1)} %get-tuple-element.141.refs_2_, bf16[4,512,128]{2,1,0:T(8,128)(2,1)} %bitcast.127, bf16[512,512]{1,0:T(8,128)(2,1)} %get-tuple-element.142.refs_4_), custom_call_target="tpu_custom_call" | custom-call | flops 1000000000 | bytes 2000000 | tf_op jit(solution)/shard_map/pallas_call | solution.py:802
  229.7 2.4 all-to-all-done.8.refs_0_
  233.2 1.9 shard_map.383
  235.2 5.6 %all-gather.4.refs_2_.refs_3_ = bf16[512,128]{1,0:T(8,128)(2,1)S(1)} all-gather(bf16[128,128]{1,0:T(8,128)(2,1)} %get-tuple-element.144), channel_id=6, replica_groups=mesh['clip'=8,'row'=4] {'row'}, dimensions={0}, use_global_device_ids=true | all-gather | bytes 163840 | tf_op jit(solution)/shard_map/all_gather | solution.py:1096
  240.8 4.7 %shard_map.384 = (bf16[128,128]{1,0:T(8,128)(2,1)}, f32[128,512]{1,0:T(8,128)}, bf16[128,128]{1,0:T(8,128)(2,1)}, f32[32,128]{1,0:T(8,128)}, f32[32,16,128]{2,1,0:T(8,128)}) custom-call(s32[1]{0:T(128)} %bitcast.refs_0_, s32[1,8]{1,0:T(1,128)S(1)} %copy-done.16, bf16[512,128]{1,0:T(8,128)(2,1)S(1)} %all-gather.4.refs_2_.refs_3_, ...), custom_call_target="tpu_custom_call" | custom-call | flops 1000000000 | bytes 2000000 | tf_op jit(solution)/shard_map/pallas_call | solution.py:802
  246.4 10.8 %shard_map.385.refs_5_ = f32[8,64,128]{2,1,0:T(8,128)S(1)} custom-call(bf16[4,80,112,256]{3,2,1,0:T(8,128)(2,1)} %shard_map.367.refs_0_, f32[8,32,64,128]{3,2,1,0:T(8,128)} %get-tuple-element.122.refs_0_.refs_1_, bf16[4,32,64,128]{3,2,1,0:T(8,128)(2,1)} %get-tuple-element.149.refs_2_, f32[5,64,128]{2,1,0:T(8,128)} %broadcast_in_dim.22.refs_3_, ...), custom_call_target="tpu_custom_call" | custom-call | flops 8000000000 | bytes 16000000 | tf_op jit(solution)/shard_map/pallas_call | solution.py:178
  257.3 5.2 %all-to-all-start.9 = ((f32[32,16,128]{2,1,0:T(8,128)}), f32[32,16,128]{2,1,0:T(8,128)S(1)}, u32[]{:S(2)}, u32[]{:S(2)}) async-start(f32[32,16,128]{2,1,0:T(8,128)} %get-tuple-element.147), calls=%async_computation.9 | async-start | bytes 524288 | tf_op jit(solution)/shard_map/all_to_all | solution.py:825
  262.5 3.2 shard_map.386
  269.6 2.3 shard_map.390
  273.5 4.6 %all-to-all-start.10 = ((bf16[32,48,128]{2,1,0:T(8,128)(2,1)}), bf16[32,48,128]{2,1,0:T(8,128)(2,1)S(1)}, u32[]{:S(2)}, u32[]{:S(2)}) async-start(bf16[32,48,128]{2,1,0:T(8,128)(2,1)} %pad_maximum_fusion.1), calls=%async_computation.10 | async-start | bytes 786432 | tf_op jit(solution)/shard_map/all_to_all | solution.py:825
  279.9 9.1 %all-gather.5 = bf16[512,512]{1,0:T(8,128)(2,1)S(1)} all-gather(bf16[128,512]{1,0:T(8,128)(2,1)} %get-tuple-element.158.refs_1_), channel_id=7, replica_groups=mesh['clip'=8,'row'=4] {'row'}, dimensions={0}, use_global_device_ids=true | all-gather | bytes 655360 | tf_op jit(solution)/shard_map/all_gather | solution.py:1152
  288.9 3.2 shard_map.388.refs_3_
  297.3 2.0 collective-permute-start.16
  300.4 4.2 %all-to-all-start.11 = ((bf16[8,376,128]{2,1,0:T(8,128)(2,1)}), bf16[8,376,128]{2,1,0:T(8,128)(2,1)S(1)}, u32[]{:S(2)}, u32[]{:S(2)}) async-start(bf16[8,376,128]{2,1,0:T(8,128)(2,1)} %pad_maximum_fusion), calls=%async_computation.11 | async-start | bytes 1540096 | tf_op jit(solution)/shard_map/all_to_all | solution.py:825
  304.6 2.6 collective-permute-done.12.refs_5_
  307.9 3.7 %shard_map.389 = (f32[8,2,8,2048]{3,2,1,0:T(8,128)}, bf16[8,2,8,2048]{3,2,1,0:T(8,128)(2,1)}) custom-call(s32[1]{0:T(128)} %bitcast.refs_0_, bf16[128,512]{1,0:T(8,128)(2,1)} %get-tuple-element.158.refs_1_, bf16[2048,512]{1,0:T(8,128)(2,1)} %bitcast.200, bf16[2,128,512]{2,1,0:T(8,128)(2,1)} %get-tuple-element.209.refs_3_, bf16[2,128,512]{2,1,0:T(8,128)(2,1)} %copy-done.33, ...), custom_call_target="tpu_custom_call" | custom-call | flops 1000000000 | bytes 2000000 | tf_op jit(solution)/shard_map/pallas_call | solution.py:802
  313.7 9.6 %all-gather.7 = bf16[3456,128]{1,0:T(8,128)(2,1)S(1)} all-gather(bf16[864,128]{1,0:T(8,128)(2,1)} %shard_map.392), channel_id=9, replica_groups=mesh['clip'=8,'row'=4] {'row'}, dimensions={0}, use_global_device_ids=true | all-gather | bytes 1105920 | tf_op jit(solution)/shard_map/all_gather | solution.py:1190
  327.4 7.0 %all-gather.6 = bf16[1696,128]{1,0:T(8,128)(2,1)S(1)} all-gather(bf16[424,128]{1,0:T(8,128)(2,1)S(1)} %pad_maximum_fusion.6), channel_id=8, replica_groups=mesh['clip'=8,'row'=4] {'row'}, dimensions={0}, use_global_device_ids=true | all-gather | bytes 542720 | tf_op jit(solution)/shard_map/all_gather | solution.py:1197
  (174 shorter events, 58.6 us)
Async XLA Ops:
  7.2 15.3 %copy-start.23 = (bf16[8,2,8,2048]{3,2,1,0:T(8,128)(2,1)S(1)}, bf16[8,2,8,2048]{3,2,1,0:T(8,128)(2,1)}, u32[]{:S(2)}) copy-start(bf16[8,2,8,2048]{3,2,1,0:T(8,128)(2,1)} %param.29) | copy-start | bytes 1572868
  8.1 15.3 %copy-start.24 = (bf16[8,2,8,2048]{3,2,1,0:T(8,128)(2,1)S(1)}, bf16[8,2,8,2048]{3,2,1,0:T(8,128)(2,1)}, u32[]{:S(2)}) copy-start(bf16[8,2,8,2048]{3,2,1,0:T(8,128)(2,1)} %param.45) | copy-start | bytes 1572868
  9.1 17.0 %all-to-all-start = ((bf16[8,8,784]{2,1,0:T(8,128)(2,1)}), bf16[8,8,784]{2,1,0:T(8,128)(2,1)S(1)}, u32[]{:S(2)}, u32[]{:S(2)}) async-start(bf16[8,8,784]{2,1,0:T(8,128)(2,1)} %broadcast_in_dim.9), calls=%async_computation | async-start | bytes 229376 | tf_op jit(solution)/shard_map/all_to_all | solution.py:825
  17.4 15.7 %collective-permute-start.1 = (bf16[12,3,16,256]{3,2,1,0:T(8,128)(2,1)S(1)}, bf16[12,3,16,256]{3,2,1,0:T(8,128)(2,1)S(1)}, u32[]{:S(2)}, u32[]{:S(2)}) collective-permute-start(bf16[12,3,16,256]{3,2,1,0:T(8,128)(2,1)S(1)} %get-tuple-element.204), channel_id=1, source_target_pairs={{1,0},{2,1},{3,2},{5,4},{6,5},{7,6},{9,8},{10,9},{11,10},{13,12},{... | collective-permute-start | bytes 884744 | tf_op jit(solution)/shard_map/ppermute | solution.py:926
  18.7 14.4 %collective-permute-start = (bf16[12,3,16,256]{3,2,1,0:T(8,128)(2,1)S(1)}, bf16[12,3,16,256]{3,2,1,0:T(8,128)(2,1)}, u32[]{:S(2)}, u32[]{:S(2)}) collective-permute-start(bf16[12,3,16,256]{3,2,1,0:T(8,128)(2,1)S(1)} %get-tuple-element.205), channel_id=1, source_target_pairs={{0,1},{1,2},{2,3},{4,5},{5,6},{6,7},{8,9},{9,10},{10,11},{12,13},{... | collective-permute-start | bytes 884744 | tf_op jit(solution)/shard_map/ppermute | solution.py:925
  26.1 46.0 %all-to-all-start.1 = ((bf16[8,704,128]{2,1,0:T(8,128)(2,1)}), bf16[8,704,128]{2,1,0:T(8,128)(2,1)S(1)}, u32[]{:S(2)}, u32[]{:S(2)}) async-start(bf16[8,704,128]{2,1,0:T(8,128)(2,1)} %get-tuple-element.102), calls=%async_computation.1 | async-start | bytes 2883584 | tf_op jit(solution)/shard_map/all_to_all | solution.py:825
  32.1 4.8 %copy-start.15 = (s32[1,8]{1,0:T(1,128)S(1)}, s32[1,8]{1,0:T(1,128)}, u32[]{:S(2)}) copy-start(s32[1,8]{1,0:T(1,128)} %param.24) | copy-start | bytes 100
  32.1 90.5 %all-gather.10.cloned.1.call-start = ((), (), s32[]{:S(2)}) async-start(), calls=%async_computation.12 | async-start | bytes 1916928 | tf_op jit(solution)/shard_map/all_gather | solution.py:940
  33.2 3.7 %copy-start.30 = (bf16[12,3,16,256]{3,2,1,0:T(8,128)(2,1)}, bf16[12,3,16,256]{3,2,1,0:T(8,128)(2,1)S(1)}, u32[]{:S(2)}) copy-start(bf16[12,3,16,256]{3,2,1,0:T(8,128)(2,1)S(1)} %collective-permute-done.1.refs_3_) | copy-start | bytes 884740
  33.2 21.8 %collective-permute-start.3 = (bf16[128,2048]{1,0:T(8,128)(2,1)}, bf16[128,2048]{1,0:T(8,128)(2,1)S(1)}, u32[]{:S(2)}, u32[]{:S(2)}) collective-permute-start(bf16[128,2048]{1,0:T(8,128)(2,1)} %bitcast.5.refs_1_.refs_5_.refs_2_), channel_id=1, source_target_pairs={{0,2},{1,3},{2,0},{3,1},{4,6},{5,7},{6,4},{7,5},{8,10},{9,11},{10,... | collective-permute-start | bytes 1572872 | tf_op jit(solution)/shard_map/ppermute | solution.py:834
  34.1 20.9 %collective-permute-start.2 = (bf16[128,2048]{1,0:T(8,128)(2,1)}, bf16[128,2048]{1,0:T(8,128)(2,1)S(1)}, u32[]{:S(2)}, u32[]{:S(2)}) collective-permute-start(bf16[128,2048]{1,0:T(8,128)(2,1)} %bitcast.5.refs_1_.refs_5_.refs_2_), channel_id=1, source_target_pairs={{0,1},{1,0},{2,3},{3,2},{4,5},{5,4},{6,7},{7,6},{8,9},{9,8},{10,11... | collective-permute-start | bytes 1572872 | tf_op jit(solution)/shard_map/ppermute | solution.py:834
  34.8 20.2 %collective-permute-start.6 = (bf16[128,512]{1,0:T(8,128)(2,1)S(1)}, bf16[128,512]{1,0:T(8,128)(2,1)S(1)}, u32[]{:S(2)}, u32[]{:S(2)}) collective-permute-start(bf16[128,512]{1,0:T(8,128)(2,1)S(1)} %get-tuple-element.211), channel_id=1, source_target_pairs={{0,3},{1,2},{2,1},{3,0},{4,7},{5,6},{6,5},{7,4},{8,11},{9,10},{10,... | collective-permute-start | bytes 393224 | tf_op jit(solution)/shard_map/ppermute | solution.py:834
  36.1 18.9 %collective-permute-start.5 = (bf16[128,512]{1,0:T(8,128)(2,1)S(1)}, bf16[128,512]{1,0:T(8,128)(2,1)S(1)}, u32[]{:S(2)}, u32[]{:S(2)}) collective-permute-start(bf16[128,512]{1,0:T(8,128)(2,1)S(1)} %get-tuple-element.212), channel_id=1, source_target_pairs={{0,2},{1,3},{2,0},{3,1},{4,6},{5,7},{6,4},{7,5},{8,10},{9,11},{10,... | collective-permute-start | bytes 393224 | tf_op jit(solution)/shard_map/ppermute | solution.py:834
  36.9 18.1 %collective-permute-start.4 = (bf16[128,512]{1,0:T(8,128)(2,1)S(1)}, bf16[128,512]{1,0:T(8,128)(2,1)S(1)}, u32[]{:S(2)}, u32[]{:S(2)}) collective-permute-start(bf16[128,512]{1,0:T(8,128)(2,1)S(1)} %get-tuple-element.213), channel_id=1, source_target_pairs={{0,1},{1,0},{2,3},{3,2},{4,5},{5,4},{6,7},{7,6},{8,9},{9,8},{10,11... | collective-permute-start | bytes 393224 | tf_op jit(solution)/shard_map/ppermute | solution.py:834
  54.9 16.5 %copy-start.7 = (bf16[128,512]{1,0:T(8,128)(2,1)}, bf16[128,512]{1,0:T(8,128)(2,1)S(1)}, u32[]{:S(2)}) copy-start(bf16[128,512]{1,0:T(8,128)(2,1)S(1)} %collective-permute-done.6.refs_6_.refs_12_) | copy-start | bytes 393220
  55.0 16.5 %copy-start.8 = (bf16[128,512]{1,0:T(8,128)(2,1)}, bf16[128,512]{1,0:T(8,128)(2,1)S(1)}, u32[]{:S(2)}) copy-start(bf16[128,512]{1,0:T(8,128)(2,1)S(1)} %collective-permute-done.5.refs_5_.refs_11_) | copy-start | bytes 393220
  55.0 16.5 %copy-start.9 = (bf16[128,512]{1,0:T(8,128)(2,1)}, bf16[128,512]{1,0:T(8,128)(2,1)S(1)}, u32[]{:S(2)}) copy-start(bf16[128,512]{1,0:T(8,128)(2,1)S(1)} %collective-permute-done.4.refs_4_.refs_10_) | copy-start | bytes 393220
  55.0 25.8 %copy-start.4 = (bf16[128,2048]{1,0:T(8,128)(2,1)}, bf16[128,2048]{1,0:T(8,128)(2,1)S(1)}, u32[]{:S(2)}) copy-start(bf16[128,2048]{1,0:T(8,128)(2,1)S(1)} %collective-permute-done.3.refs_3_.refs_7_.refs_4_) | copy-start | bytes 1572868
  55.0 16.4 %copy-start.5 = (bf16[128,2048]{1,0:T(8,128)(2,1)}, bf16[128,2048]{1,0:T(8,128)(2,1)S(1)}, u32[]{:S(2)}) copy-start(bf16[128,2048]{1,0:T(8,128)(2,1)S(1)} %collective-permute-done.2.refs_2_.refs_6_.refs_3_) | copy-start | bytes 1572868
  72.1 3.3 collective-permute-start.7
  75.4 3.3 copy-start.14
  78.7 8.5 %collective-permute-start.9 = (bf16[8,128,128]{2,1,0:T(8,128)(2,1)S(1)}, bf16[8,128,128]{2,1,0:T(8,128)(2,1)S(1)}, u32[]{:S(2)}, u32[]{:S(2)}) collective-permute-start(bf16[8,128,128]{2,1,0:T(8,128)(2,1)S(1)} %slice.133), channel_id=1, source_target_pairs={{0,3},{1,2},{2,1},{3,0},{4,7},{5,6},{6,5},{7,4},{8,11},{9,10},{10,... | collective-permute-start | bytes 786440 | tf_op jit(solution)/shard_map/ppermute | solution.py:834
  80.0 14.1 %collective-permute-start.8 = (bf16[8,128,128]{2,1,0:T(8,128)(2,1)S(1)}, bf16[8,128,128]{2,1,0:T(8,128)(2,1)S(1)}, u32[]{:S(2)}, u32[]{:S(2)}) collective-permute-start(bf16[8,128,128]{2,1,0:T(8,128)(2,1)S(1)} %slice.133), channel_id=1, source_target_pairs={{0,2},{1,3},{2,0},{3,1},{4,6},{5,7},{6,4},{7,5},{8,10},{9,11},{10,... | collective-permute-start | bytes 786440 | tf_op jit(solution)/shard_map/ppermute | solution.py:834
  80.8 83.6 %collective-permute-start.10 = (bf16[128,2048]{1,0:T(8,128)(2,1)S(1)}, bf16[128,2048]{1,0:T(8,128)(2,1)S(1)}, u32[]{:S(2)}, u32[]{:S(2)}) collective-permute-start(bf16[128,2048]{1,0:T(8,128)(2,1)S(1)} %collective-permute-done.3.refs_3_.refs_7_.refs_4_), channel_id=1, source_target_pairs={{0,1},{1,0},{2,3},{3,2},{4,5},{5,4},{6,7},{7,6},{8,9},{9,8},{10,11... | collective-permute-start | bytes 1572872 | tf_op jit(solution)/shard_map/ppermute | solution.py:834
  81.5 18.7 %all-to-all-start.2 = ((f32[32,16,128]{2,1,0:T(8,128)}), f32[32,16,128]{2,1,0:T(8,128)S(1)}, u32[]{:S(2)}, u32[]{:S(2)}) async-start(f32[32,16,128]{2,1,0:T(8,128)} %get-tuple-element.111), calls=%async_computation.2 | async-start | bytes 524288 | tf_op jit(solution)/shard_map/all_to_all | solution.py:825
  95.1 5.0 %copy-start.16 = (s32[1,8]{1,0:T(1,128)S(1)}, s32[1,8]{1,0:T(1,128)}, u32[]{:S(2)}) copy-start(s32[1,8]{1,0:T(1,128)} %refs_1_.5) | copy-start | bytes 100
  107.7 3.9 %copy-start.10 = (bf16[512,128]{1,0:T(8,128)(2,1)}, bf16[512,128]{1,0:T(8,128)(2,1)S(1)}, u32[]{:S(2)}) copy-start(bf16[512,128]{1,0:T(8,128)(2,1)S(1)} %all-gather.refs_1_.refs_0_) | copy-start | bytes 393220
  107.7 4.0 %copy-start.28 = (f32[64]{0:T(128)S(1)}, f32[64]{0:T(128)}, u32[]{:S(2)}) copy-start(f32[64]{0:T(128)} %param.27) | copy-start | bytes 772
  107.7 4.1 %copy-start.29 = (f32[64]{0:T(128)S(1)}, f32[64]{0:T(128)}, u32[]{:S(2)}) copy-start(f32[64]{0:T(128)} %param.28) | copy-start | bytes 772
  119.3 7.0 %copy-start.2 = (bf16[512,512]{1,0:T(8,128)(2,1)}, bf16[512,512]{1,0:T(8,128)(2,1)S(1)}, u32[]{:S(2)}) copy-start(bf16[512,512]{1,0:T(8,128)(2,1)S(1)} %all-gather.1.refs_0_.refs_1_) | copy-start | bytes 1572868
  126.3 11.4 %all-to-all-start.3 = ((f32[8,8,128]{2,1,0:T(8,128)}), f32[8,8,128]{2,1,0:T(8,128)S(1)}, u32[]{:S(2)}, u32[]{:S(2)}) async-start(f32[8,8,128]{2,1,0:T(8,128)} %get-tuple-element.120), calls=%async_computation.3 | async-start | bytes 65536 | tf_op jit(solution)/shard_map/all_to_all | solution.py:825
  147.0 3.4 copy-start.3
  150.4 14.0 %all-to-all-start.4 = ((f32[8,8,128]{2,1,0:T(8,128)}), f32[8,8,128]{2,1,0:T(8,128)S(1)}, u32[]{:S(2)}, u32[]{:S(2)}) async-start(f32[8,8,128]{2,1,0:T(8,128)} %get-tuple-element.125), calls=%async_computation.4 | async-start | bytes 65536 | tf_op jit(solution)/shard_map/all_to_all | solution.py:825
  201.0 15.1 %all-to-all-start.7 = ((f32[8,8,128]{2,1,0:T(8,128)}), f32[8,8,128]{2,1,0:T(8,128)S(1)}, u32[]{:S(2)}, u32[]{:S(2)}) async-start(f32[8,8,128]{2,1,0:T(8,128)} %get-tuple-element.134), calls=%async_computation.7 | async-start | bytes 65536 | tf_op jit(solution)/shard_map/all_to_all | solution.py:825
  219.8 12.3 %all-to-all-start.8 = ((bf16[4,128,512]{2,1,0:T(8,128)(2,1)}), bf16[4,128,512]{2,1,0:T(8,128)(2,1)S(1)}, u32[]{:S(2)}, u32[]{:S(2)}) async-start(bf16[4,128,512]{2,1,0:T(8,128)(2,1)} %get-tuple-element.139), calls=%async_computation.8 | async-start | bytes 1048576 | tf_op jit(solution)/shard_map/all_to_all | solution.py:825
  227.7 41.9 %collective-permute-start.14 = (bf16[4,832,128]{2,1,0:T(8,128)(2,1)}, bf16[4,832,128]{2,1,0:T(8,128)(2,1)S(1)}, u32[]{:S(2)}, u32[]{:S(2)}) collective-permute-start(bf16[4,832,128]{2,1,0:T(8,128)(2,1)} %get-tuple-element.171), channel_id=1, source_target_pairs={{0,4},{4,0},{8,12},{12,8},{16,20},{20,16},{24,28},{28,24},{1,5},{5... | collective-permute-start | bytes 2555912 | tf_op jit(solution)/shard_map/ppermute | solution.py:834
  240.8 4.7 %copy-start.11 = (bf16[512,128]{1,0:T(8,128)(2,1)}, bf16[512,128]{1,0:T(8,128)(2,1)S(1)}, u32[]{:S(2)}) copy-start(bf16[512,128]{1,0:T(8,128)(2,1)S(1)} %all-gather.4.refs_2_.refs_3_) | copy-start | bytes 393220
  257.3 16.2 %all-to-all-start.9 = ((f32[32,16,128]{2,1,0:T(8,128)}), f32[32,16,128]{2,1,0:T(8,128)S(1)}, u32[]{:S(2)}, u32[]{:S(2)}) async-start(f32[32,16,128]{2,1,0:T(8,128)} %get-tuple-element.147), calls=%async_computation.9 | async-start | bytes 524288 | tf_op jit(solution)/shard_map/all_to_all | solution.py:825
  265.7 3.9 %copy-start.18 = (f32[128,512]{1,0:T(8,128)S(1)}, f32[128,512]{1,0:T(8,128)}, u32[]{:S(2)}) copy-start(f32[128,512]{1,0:T(8,128)} %get-tuple-element.148.refs_4_.refs_1_.refs_3_) | copy-start | bytes 786436
  271.9 23.6 %collective-permute-start.15 = (bf16[2,832,128]{2,1,0:T(8,128)(2,1)}, bf16[2,832,128]{2,1,0:T(8,128)(2,1)S(1)}, u32[]{:S(2)}, u32[]{:S(2)}) collective-permute-start(bf16[2,832,128]{2,1,0:T(8,128)(2,1)} %get-tuple-element.173), channel_id=1, source_target_pairs={{0,8},{4,12},{8,0},{12,4},{16,24},{20,28},{24,16},{28,20},{1,9},{5... | collective-permute-start | bytes 1277960 | tf_op jit(solution)/shard_map/ppermute | solution.py:834
  273.5 26.8 %all-to-all-start.10 = ((bf16[32,48,128]{2,1,0:T(8,128)(2,1)}), bf16[32,48,128]{2,1,0:T(8,128)(2,1)S(1)}, u32[]{:S(2)}, u32[]{:S(2)}) async-start(bf16[32,48,128]{2,1,0:T(8,128)(2,1)} %pad_maximum_fusion.1), calls=%async_computation.10 | async-start | bytes 786432 | tf_op jit(solution)/shard_map/all_to_all | solution.py:825
  288.9 3.2 copy-start.22
  292.1 3.4 copy-start.1
  292.9 11.6 %collective-permute-start.13 = (bf16[2,128,512]{2,1,0:T(8,128)(2,1)S(1)}, bf16[2,128,512]{2,1,0:T(8,128)(2,1)S(1)}, u32[]{:S(2)}, u32[]{:S(2)}) collective-permute-start(bf16[2,128,512]{2,1,0:T(8,128)(2,1)S(1)} %get-tuple-element.206), channel_id=1, source_target_pairs={{0,3},{1,2},{2,1},{3,0},{4,7},{5,6},{6,5},{7,4},{8,11},{9,10},{10,... | collective-permute-start | bytes 786440 | tf_op jit(solution)/shard_map/ppermute | solution.py:834
  294.6 12.5 %collective-permute-start.12 = (bf16[2,128,512]{2,1,0:T(8,128)(2,1)S(1)}, bf16[2,128,512]{2,1,0:T(8,128)(2,1)S(1)}, u32[]{:S(2)}, u32[]{:S(2)}) collective-permute-start(bf16[2,128,512]{2,1,0:T(8,128)(2,1)S(1)} %get-tuple-element.207), channel_id=1, source_target_pairs={{0,2},{1,3},{2,0},{3,1},{4,6},{5,7},{6,4},{7,5},{8,10},{9,11},{10,... | collective-permute-start | bytes 786440 | tf_op jit(solution)/shard_map/ppermute | solution.py:834
  294.9 12.3 %collective-permute-start.11 = (bf16[2,128,512]{2,1,0:T(8,128)(2,1)S(1)}, bf16[2,128,512]{2,1,0:T(8,128)(2,1)S(1)}, u32[]{:S(2)}, u32[]{:S(2)}) collective-permute-start(bf16[2,128,512]{2,1,0:T(8,128)(2,1)S(1)} %get-tuple-element.208), channel_id=1, source_target_pairs={{0,1},{1,0},{2,3},{3,2},{4,5},{5,4},{6,7},{7,6},{8,9},{9,8},{10,11... | collective-permute-start | bytes 786440 | tf_op jit(solution)/shard_map/ppermute | solution.py:834
  297.3 14.6 %collective-permute-start.16 = (bf16[1,832,128]{2,1,0:T(8,128)(2,1)}, bf16[1,832,128]{2,1,0:T(8,128)(2,1)S(1)}, u32[]{:S(2)}, u32[]{:S(2)}) collective-permute-start(bf16[1,832,128]{2,1,0:T(8,128)(2,1)} %get-tuple-element.175), channel_id=1, source_target_pairs={{0,16},{4,20},{8,24},{12,28},{16,0},{20,4},{24,8},{28,12},{1,17},{... | collective-permute-start | bytes 638984 | tf_op jit(solution)/shard_map/ppermute | solution.py:834
  300.4 26.8 %all-to-all-start.11 = ((bf16[8,376,128]{2,1,0:T(8,128)(2,1)}), bf16[8,376,128]{2,1,0:T(8,128)(2,1)S(1)}, u32[]{:S(2)}, u32[]{:S(2)}) async-start(bf16[8,376,128]{2,1,0:T(8,128)(2,1)} %pad_maximum_fusion), calls=%async_computation.11 | async-start | bytes 1540096 | tf_op jit(solution)/shard_map/all_to_all | solution.py:825
  (14 other events, 21.1 us)
Sparse Core Ops, SparseCore 0:
  72.7 49.8 all-gather.9

commit v3 on v2

--- a/solution.py
+++ b/solution.py
@@ -52,24 +52,33 @@
     for side in range(2):
         first = start_ref[2 * pair + side]
         lanes = slice(128 * side, 128 * side + 128)
-        for block in range(6):
-            if block == 0:
-                window = above_ref[pl.ds(first, WIN)]
-            elif block == 5:
-                window = below_ref[pl.ds(first, WIN)]
-            else:
-                window = local_ref[pl.ds(first, WIN), :, 16 * block - 16 : 16 * block, :]
-            window = window.reshape(240, 256)
-            stacked = jnp.dot(pick_ref[...], window, preferred_element_type=jnp.float32)
-            shifted = jnp.dot(
-                stacked.astype(jnp.bfloat16), shift_ref[...], preferred_element_type=jnp.float32
-            ).astype(jnp.bfloat16)
-            low, high = (8 if block == 0 else 0), (8 if block == 5 else 16)
-            for kx in range(7):
-                piece = shifted[:, 128 * kx : 128 * kx + 128].reshape(16, 16, 128)
-                planes_ref[
-                    0, 16 * block - 8 + low : 16 * block - 8 + high, 16 * kx : 16 * kx + 16, lanes
-                ] = piece[low:high]
+        for base in (0, 3):
+            parts = []
+            for block in range(base, base + 3):
+                if block == 0:
+                    window = above_ref[pl.ds(first, WIN)]
+                elif block == 5:
+                    window = below_ref[pl.ds(first, WIN)]
+                else:
+                    window = local_ref[pl.ds(first, WIN), :, 16 * block - 16 : 16 * block, :]
+                part = jnp.dot(
+                    pick_ref[...], window.reshape(240, 256), preferred_element_type=jnp.float32
+                )
+                parts.append(part.astype(jnp.bfloat16))
+            stacked = jnp.concatenate(parts, 0)
+            low, high = (8, 48) if base == 0 else (0, 40)
+            at = 16 * base - 8
+            for first_kx in range(0, 7, 2):
+                count = min(2, 7 - first_kx)
+                shifted = jnp.dot(
+                    stacked,
+                    shift_ref[:, 128 * first_kx : 128 * (first_kx + count)],
+                    preferred_element_type=jnp.float32,
+                ).astype(jnp.bfloat16)
+                for k in range(count):
+                    piece = shifted[:, 128 * k : 128 * k + 128].reshape(48, 16, 128)
+                    channels = slice(16 * (first_kx + k), 16 * (first_kx + k) + 16)
+                    planes_ref[0, at + low : at + high, channels, lanes] = piece[low:high]
 
 
 def stem_conv_kernel(planes_ref, weight_ref, pre_ref, sums_ref):
@@ -77,16 +86,20 @@
     def _():
         sums_ref[...] = jnp.zeros_like(sums_ref)
 
-    @pl.loop(0, 8)
-    def _(group):
-        patches = planes_ref[0, pl.ds(5 + 8 * group, 13)].reshape(13 * 112, 256)
-        out = jnp.dot(weight_ref[...], patches, preferred_element_type=jnp.float32)
-        out = out.reshape(4, 64, 256)
-        for side in range(2):
-            half = out[:, :, 128 * side : 128 * side + 128]
-            pre_ref[side, pl.ds(4 * group, 4)] = half
-            sums_ref[0] += jnp.sum(half, 0)
-            sums_ref[1] += jnp.sum(half * half, 0)
+    @pl.loop(0, 2)
+    def _(part):
+        totals = [jnp.zeros((64, 128), jnp.float32)] * 2
+        for step in range(4):
+            group = 4 * part + step
+            patches = planes_ref[0, pl.ds(5 + 8 * group, 13)].reshape(13 * 112, 256)
+            out = jnp.dot(weight_ref[...], patches, preferred_element_type=jnp.float32)
+            out = out.reshape(4, 64, 256)
+            for side in range(2):
+                half = out[:, :, 128 * side : 128 * side + 128]
+                pre_ref[side, pl.ds(4 * group, 4)] = half
+                totals = [totals[0] + jnp.sum(half, 0), totals[1] + jnp.sum(half * half, 0)]
+        sums_ref[0] += totals[0]
+        sums_ref[1] += totals[1]
 
 
 def stem_slope_kernel(pre_ref, cot_ref, vectors_ref, outer_ref, sums_ref, swap_ref):
@@ -125,22 +138,27 @@
     def _():
         acc_ref[...] = jnp.zeros_like(acc_ref)
 
-    @pl.loop(0, 8)
-    def _(group):
-        rows = pl.ds(4 * group, 4)
-        sides = []
-        for side in range(2):
-            normed = (pre_ref[side, rows] - vectors_ref[0]) * vectors_ref[1]
-            outer = outer_ref[side, rows].astype(jnp.float32)
-            grad = vectors_ref[2] * (outer - vectors_ref[3] - normed * vectors_ref[4])
-            sides.append(grad.astype(jnp.bfloat16).reshape(256, 128))
-        patches = planes_ref[0, pl.ds(5 + 8 * group, 13)].reshape(13 * 112, 256)
-        acc_ref[...] += lax.dot_general(
-            jnp.concatenate(sides, 1),
-            patches,
-            (((1,), (1,)), ((), ())),
-            preferred_element_type=jnp.float32,
-        )
+    @pl.loop(0, 2)
+    def _(half):
+        total = None
+        for step in range(4):
+            group = 4 * half + step
+            rows = pl.ds(4 * group, 4)
+            sides = []
+            for side in range(2):
+                normed = (pre_ref[side, rows] - vectors_ref[0]) * vectors_ref[1]
+                outer = outer_ref[side, rows].astype(jnp.float32)
+                grad = vectors_ref[2] * (outer - vectors_ref[3] - normed * vectors_ref[4])
+                sides.append(grad.astype(jnp.bfloat16).reshape(256, 128))
+            patches = planes_ref[0, pl.ds(5 + 8 * group, 13)].reshape(13 * 112, 256)
+            term = lax.dot_general(
+                jnp.concatenate(sides, 1),
+                patches,
+                (((1,), (1,)), ((), ())),
+                preferred_element_type=jnp.float32,
+            )
+            total = term if total is None else total + term
+        acc_ref[...] += total
 
     @pl.when(pair == last)
     def _():
@@ -170,6 +188,7 @@
 
 
 def stem_call(kernel, steps, in_specs, out_specs, outs, scratch, flops, moved, args, waits=()):
+    flops = 10**6 if len(waits) == 1 and args[-1].shape[0] == 5 else flops
     used = len(args)
 
     def body(*refs):
@@ -395,7 +414,7 @@
                 reduce_ref, two_ref, three_ref, sent_ref, parts_ref, early_ref):
     place, side = place_ref[0], side_ref[0]
     half = one_ref.shape[0] // 2
-    quarter = early_ref.shape[0] // 4
+    part = early_ref.shape[0] // 2
     start = 0
     for part_ref in (fine_ref, half_w_ref, quarter_w_ref):
         early_ref[start : start + part_ref.shape[0]] = part_ref[...]
@@ -414,7 +433,7 @@
     rows = pl.ds(pl.multiple_of(side * half, half), half)
     for block in range(one_ref.shape[1] // 128):
         start = put(start, one_ref[rows, 128 * block : 128 * block + 128])
-    start = put(start, early_ref[pl.ds(pl.multiple_of(place * quarter, quarter), quarter)])
+    start = put(start, early_ref[pl.ds(pl.multiple_of(side * part, part), part)])
     put(start, reduce_ref[...])
     wide = three_ref.shape[1] // 4
     columns = pl.ds(pl.multiple_of(place * 128, 128), 128)
@@ -536,7 +555,8 @@
 
 def output_kernel(count, place_ref, sums_ref, third_ref, gain_ref, bias_ref,
                   x0_ref, x1_ref, x2_ref, x3_ref, c0_ref, c1_ref, c2_ref, c3_ref,
-                  low_ref, high_ref, send_ref, slope_ref, norm_ref, out_sums_ref):
+                  low_ref, high_ref, s0_ref, s1_ref, s2_ref, s3_ref, slope_ref, norm_ref,
+                  out_sums_ref):
     place = place_ref[0]
     mean, inverse = norm_of(sums_ref, 4, count)
     norm_ref[...] = jnp.concatenate([mean, inverse], 0)
@@ -545,17 +565,20 @@
     lanes_r = pl.ds(pl.multiple_of(place * wide, wide), wide)
     total_bias, total_gain = jnp.zeros((1, wide), f32), jnp.zeros((1, wide), f32)
     pieces = zip(
-        sources(place, 4), (x0_ref, x1_ref, x2_ref, x3_ref), (c0_ref, c1_ref, c2_ref, c3_ref)
-    )
-    for source, x_ref, c_ref in pieces:
+        sources(place, 4),
+        (x0_ref, x1_ref, x2_ref, x3_ref),
+        (c0_ref, c1_ref, c2_ref, c3_ref),
+        (s0_ref, s1_ref, s2_ref, s3_ref),
+    )
+    for source, x_ref, c_ref, send_ref in pieces:
         rows = pl.ds(pl.multiple_of(source * own, own), own)
         normed = (third_ref[rows] - mean) * inverse
         summed = normed * gain + bias + x_ref[:, lanes_r].astype(f32)
         sigmoid = jax.nn.sigmoid(summed)
-        send_ref[pl.ds(source, 1), 0] = (summed * sigmoid).astype(bf16)[None]
+        send_ref[0] = (summed * sigmoid).astype(bf16)
         slope = c_ref[...].astype(f32) * (sigmoid * (1.0 + summed * (1.0 - sigmoid)))
         slope_ref[rows] = slope
-        send_ref[pl.ds(source, 1), 1] = slope.astype(bf16)[None]
+        send_ref[1] = slope.astype(bf16)
         total_bias += column_sum(slope)
         total_gain += column_sum(slope * normed)
     put_sums(out_sums_ref, total_bias, total_gain, stem_row(low_ref, high_ref))
@@ -618,24 +641,10 @@
         part_ref[part] = back.astype(bf16)
 
 
-def split_blocks(side, first_ref, second_ref, put):
-    for index in range(2 * first_ref.shape[0]):
-        own, rest = (first_ref, second_ref) if index % 2 == 0 else (second_ref, first_ref)
-
-        @pl.when(side == 0)
-        def _():
-            put(index, own, index // 2)
-
-        @pl.when(side == 1)
-        def _():
-            put(index, rest, index // 2)
-
-
-def wide_grads_kernel(side_ref, gated_ref, grad_ref, hidden_ref, third_ref,
-                      keep_ref, send_ref, pad_ref, all_ref):
+def wide_grads_kernel(gated_ref, grad_ref, hidden_ref, third_ref, out_ref, pad_ref, all_ref):
     band = shift_columns(pad_ref, gated_ref[...], 8)
     rows, channels = gated_ref.shape
-    clips = 2 * keep_ref.shape[0]
+    clips = out_ref.shape[0]
     two_rows = 9 * channels // clips
     for ky, kx in taps:
         tap = 3 * ky + kx
@@ -650,29 +659,18 @@
             all_ref[first : first + 128] = value[:, 128 * block : 128 * block + 128]
     three_rows = channels // clips
 
-    def put(clip, out_ref, index):
-        out_ref[index, 0:two_rows] = all_ref[two_rows * clip : two_rows * clip + two_rows]
+    for clip in range(clips):
+        out_ref[clip, 0:two_rows] = all_ref[two_rows * clip : two_rows * clip + two_rows]
         at = padded(two_rows)
         for block in range(third_ref.shape[1] // 128):
             first = start + channels * block + three_rows * clip
-            out_ref[index, at : at + three_rows] = all_ref[first : first + three_rows]
+            out_ref[clip, at : at + three_rows] = all_ref[first : first + three_rows]
             at += padded(three_rows)
 
-    split_blocks(side_ref[0], keep_ref, send_ref, put)
-
-
-def halve_kernel(side_ref, held_ref, arrived_ref, keep_ref, send_ref):
-    def put(source, out_ref, index):
-        total = held_ref[source].astype(f32) + arrived_ref[source].astype(f32)
-        out_ref[index] = total.astype(bf16)
-
-    split_blocks(side_ref[0], keep_ref, send_ref, put)
-
-
-def last_kernel(held_ref, arrived_ref, three_ref, two_ref, out_ref):
-    rows = held_ref.shape[1]
-    total = held_ref[0].astype(f32) + arrived_ref[0].astype(f32)
-    out_ref[0:rows] = total.astype(bf16)
+
+def last_kernel(sum_ref, three_ref, two_ref, out_ref):
+    rows = sum_ref.shape[0]
+    out_ref[0:rows] = sum_ref[...]
     vectors = jnp.concatenate([three_ref[...], two_ref[...], jnp.zeros((6, 128), f32)], 0)
     upper = vectors.astype(bf16)
     out_ref[rows : rows + 16] = upper
@@ -739,8 +737,7 @@
 
 def one_grad_kernel(place_ref, grad_ref, x0_ref, x1_ref, x2_ref, x3_ref, out_ref):
     place = place_ref[0]
-    wide = out_ref.shape[1]
-    lanes_r = pl.ds(pl.multiple_of(place * wide, wide), wide)
+    lanes_r = pl.ds(pl.multiple_of(place * 128, 128), 128)
     total = None
     for source, x_ref in zip(sources(place, 4), (x0_ref, x1_ref, x2_ref, x3_ref)):
         grad = grad_ref[pl.ds(source, 1), :, lanes_r][0]
@@ -749,27 +746,44 @@
     out_ref[...] = total.astype(bf16)
 
 
-def small_grads_kernel(change_ref, half_ref, quarter_ref, grad_ref, coarse_ref, coarsest_ref,
-                       hidden_ref, reduced_ref, merged_ref, gate_ref,
-                       fine_ref, half_w_ref, quarter_w_ref, reduce_ref, expand_ref,
-                       pad_ref, pad_half_ref, pad_quarter_ref):
+def small_grads_kernel(place_ref, change_ref, half_ref, quarter_ref, grad_ref, coarse_ref,
+                       coarsest_ref, hidden_ref, reduced_ref, merged_ref, gate_ref,
+                       stem_low_ref, stem_high_ref, out_ref,
+                       pad_ref, pad_half_ref, pad_quarter_ref, grads_ref, shares_ref):
+    place = place_ref[0]
+    clips, part = out_ref.shape[0], shares_ref.shape[1] // 4
     scales = (
-        (change_ref, grad_ref, fine_ref, pad_ref, 8, None),
-        (half_ref, coarse_ref, half_w_ref, pad_half_ref, 4, None),
-        (quarter_ref, coarsest_ref, quarter_w_ref, pad_quarter_ref, 2, lax.Precision.HIGHEST),
-    )
-    for map_ref, cot_ref, out_ref, padded_ref, width, precision in scales:
+        (change_ref, grad_ref, pad_ref, 8, None),
+        (half_ref, coarse_ref, pad_half_ref, 4, None),
+        (quarter_ref, coarsest_ref, pad_quarter_ref, 2, lax.Precision.HIGHEST),
+    )
+    at = 0
+    for map_ref, cot_ref, padded_ref, width, precision in scales:
         rows, channels = map_ref.shape
         band = shift_columns(padded_ref, map_ref[...], width)
         for ky, kx in taps:
             tap = 3 * ky + kx
-            out_ref[tap * channels : (tap + 1) * channels, :] = dot(
+            grads_ref[tap * channels : (tap + 1) * channels, :] = dot(
                 padded_ref[kx, ky * band : ky * band + rows], cot_ref[...], "TN", precision
             ).astype(bf16)
-    reduce_ref[...] = dot(hidden_ref[...], reduced_ref[...], "TN").astype(bf16)
-    value = dot(merged_ref[...], gate_ref[...], "TN").astype(bf16)
-    for block in range(expand_ref.shape[0]):
-        expand_ref[block] = value[:, 128 * block : 128 * block + 128]
+        share = 9 * channels // clips
+        for clip in range(clips):
+            shares_ref[clip, :share] = grads_ref[share * clip : share * clip + share]
+        out_ref[:, at : at + part] = shares_ref[:, pl.ds(pl.multiple_of(place * part, part), part)]
+        at += part
+    value = dot(hidden_ref[...], reduced_ref[...], "TN").astype(bf16)
+    expand = dot(merged_ref[...], gate_ref[...], "TN").astype(bf16)
+    blocks = [value] + [
+        expand[:, first : first + 128] for first in range(0, expand.shape[1], 128)
+    ]
+    blocks += [
+        (stem_low_ref[k] + stem_high_ref[k]).astype(bf16) for k in range(stem_low_ref.shape[0])
+    ]
+    for block in blocks:
+        share = block.shape[0] // clips
+        for clip in range(clips):
+            out_ref[clip, at : at + share] = block[share * clip : share * clip + share]
+        at += padded(share)
 
 
 def input_grad_kernel(place_ref, grad_ref, weight_ref, r0_ref, r1_ref, r2_ref, r3_ref,
@@ -785,6 +799,58 @@
         for row in range(shape[0]):
             input_ref[:, row, :, lanes_r] = value[row]
             out_ref[:, row, :, lanes_r] = result[row].astype(bf16)
+
+
+def by_source(place, refs):
+    pieces = [ref[...].astype(f32) for ref in refs]
+    low, high = (place & 1) == 0, (place & 2) == 0
+    pairs = []
+    for first, second in ((pieces[0], pieces[1]), (pieces[2], pieces[3])):
+        pairs.append((jnp.where(low, first, second), jnp.where(low, second, first)))
+    near, far = pairs
+    return [jnp.where(high, near[k], far[k]) for k in range(2)] + [
+        jnp.where(high, far[k], near[k]) for k in range(2)
+    ]
+
+
+def wide_shares_kernel(place_ref, *refs):
+    pieces = by_source(place_ref[0], refs[:4])
+    two_ref, three_ref, gain_two_ref, bias_two_ref, gain_three_ref, bias_three_ref = refs[4:]
+    two_rows, three_rows = two_ref.shape[0], three_ref.shape[0]
+    blocks = three_ref.shape[1] // 512
+    vectors_at = padded(two_rows) + blocks * padded(three_rows)
+    for source, piece in enumerate(pieces):
+        lanes_of = slice(128 * source, 128 * source + 128)
+        two_ref[:, lanes_of] = piece[:two_rows]
+        vectors = piece[vectors_at : vectors_at + 16] + piece[vectors_at + 16 : vectors_at + 32]
+        bias_two_ref[:, lanes_of], gain_two_ref[:, lanes_of] = vectors[8:9], vectors[9:10]
+        for block in range(blocks):
+            start = padded(two_rows) + block * padded(three_rows)
+            first = 128 * (blocks * source + block)
+            three_ref[:, first : first + 128] = piece[start : start + three_rows]
+            bias_three_ref[:, first : first + 128] = vectors[block : block + 1]
+            gain_three_ref[:, first : first + 128] = vectors[4 + block : 5 + block]
+
+
+def one_share_kernel(place_ref, *refs):
+    for source, piece in enumerate(by_source(place_ref[0], refs[:4])):
+        refs[4][:, 128 * source : 128 * source + 128] = piece
+
+
+def rest_shares_kernel(tap_rows, place_ref, *refs):
+    pieces = by_source(place_ref[0], refs[:4])
+    fine_ref, half_w_ref, quarter_w_ref, reduce_ref, expand_ref, stem_ref = refs[4:]
+    start = 0
+    for out_ref in (fine_ref, half_w_ref, quarter_w_ref):
+        rows = [piece[start : start + tap_rows] for piece in pieces]
+        out_ref[...] = jnp.concatenate(rows, 0)[: out_ref.shape[0]]
+        start += tap_rows
+    total = pieces[0] + pieces[1] + pieces[2] + pieces[3]
+    for out_ref in (reduce_ref, expand_ref, stem_ref):
+        rows = out_ref.shape[0]
+        for first in range(0, out_ref.shape[1], 128):
+            out_ref[:, first : first + 128] = total[start : start + rows]
+            start += padded(rows)
 
 
 class Fresh:
@@ -872,11 +938,6 @@
     place = lax.axis_index("row").astype(u32)
     spots = [place ^ u32(s) for s in range(nr)]
     side = place & u32(1)
-    clip = lax.axis_index("clip").astype(u32)
-    bits, bit = [], 1
-    while bit < nc:
-        bits.append((bit, (clip // u32(bit)) & u32(1)))
-        bit *= 2
     spot = place.astype(jnp.int32).reshape(1)
     both = ("clip", "row")
     images, block_rows, cols, c_in = block_input.shape
@@ -892,25 +953,24 @@
         return lax.dynamic_slice_in_dim(array, index * u32(in_r), in_r, array.ndim - 1)
 
     half = w_one.shape[0] // 2
-    stem_taps = to_all(filters_inside(stem_weight), "clip").reshape(STEM, -1)
     expand_rows = padded(w_expand.shape[0])
-    early_rows = padded(3 * padded(k_fine.shape[0]) + mid // 128 * expand_rows, 16 * nr)
-    quarter_rows = early_rows // nr
+    early_rows = padded(3 * padded(k_fine.shape[0]) + mid // 128 * expand_rows, 32)
     edges = [4 * padded(half)]
-    for rows in (quarter_rows, w_reduce.shape[0]):
+    for rows in (early_rows // 2, w_reduce.shape[0]):
         edges.append(edges[-1] + padded(rows))
     two_rows, three_rows = w_two.shape[0], w_three.shape[0]
     two_end = padded(two_rows)
     part_rows = two_end + in_r // 128 * padded(three_rows)
-    sides = [entry.astype(jnp.int32).reshape(1) for _, entry in bits]
     sent, parts = call(
         pack_kernel,
         (spot, side.astype(jnp.int32).reshape(1)),
         (w_one, k_fine, k_half, k_quarter, w_expand, w_reduce, w_two, w_three),
         (((nc, edges[-1], 128), bf16), ((part_rows, 128), bf16)),
         [((early_rows, 128), bf16)],
-        (*sides, *[entry.reshape(1) for entry in spots]),
-    )
+        [entry.reshape(1) for entry in spots],
+    )
+    taps_own, sent = together(filters_inside(stem_weight), sent)
+    stem_taps = to_all(taps_own, "clip").reshape(STEM, -1)
     sent, stem_taps = together(sent, stem_taps)
     mine = exchange(sent, "clip")
     filters = jnp.concatenate(
@@ -936,7 +996,6 @@
     stem_pre, stem_sums = stem_conv(planes, filters, *x_pieces[1:3], *cot_pieces[1:])
     mine, stem_sums = together(mine, stem_sums)
     other = swap(mine, "row", 1)
-    parts, mine = together(parts, mine)
     packed = lax.all_gather(parts, "clip")
     full_one, first, sums = call(
         first_kernel,
@@ -948,23 +1007,14 @@
     sums = exchange(sums, both)
     mine, other, first = together(mine, other, first)
     full_reduce = mine[:, edges[1] : edges[1] + w_reduce.shape[0]].reshape(mid, red)
-    mine_early = mine[:, edges[0] : edges[1]]
-    quarters = [mine_early, other[:, edges[0] : edges[1]]] + [
-        swap(mine_early, "row", s) for s in (2, 3)
-    ]
-    quarters = [
-        jnp.where(
-            place == u32(q),
-            quarters[0],
-            jnp.where(
-                place == u32(q ^ 1),
-                quarters[1],
-                jnp.where(place == u32(q ^ 2), quarters[2], quarters[3]),
-            ),
-        )
-        for q in range(nr)
-    ]
-    quarters = jnp.concatenate(quarters, 1)
+    halves = [entry[:, edges[0] : edges[1]] for entry in (mine, other)]
+    quarters = jnp.concatenate(
+        [
+            jnp.where(side == u32(0), halves[0], halves[1]),
+            jnp.where(side == u32(0), halves[1], halves[0]),
+        ],
+        1,
+    )
     early_parts, start = [], 0
     for size in (k_fine.shape[0],) * 3 + (w_expand.shape[0],) * (mid // 128):
         early_parts.append(quarters[:, start : start + size].reshape(-1, 128))
@@ -1026,7 +1076,7 @@
     )
     outer_high, slope_high = stem_slope(stem_pre, stem_cot, 4, stem_vectors, third)
     gain_three, bias_three = gain_three.reshape(1, -1), bias_three.reshape(1, -1)
-    send, slope_three, norm_three, sums = call(
+    *send, slope_three, norm_three, sums = call(
         functools.partial(output_kernel, count),
         (spot,),
         (
@@ -1034,13 +1084,14 @@
             slope_low, slope_high,
         ),
         (
-            ((nr, 2, own, in_r), bf16),
+            *[((2, own, in_r), bf16)] * nr,
             ((pixels, in_r), f32),
             ((2, in_r), f32),
             ((nc, 16, 128), f32),
         ),
     )
 
+    returned = [send[0]] + [swap(send[s], "row", s) for s in range(1, nr)]
     grad_third, parts, vectors_three = call(
         functools.partial(third_back_kernel, count),
         (spot,),
@@ -1048,6 +1099,7 @@
             Fresh(exchange(sums, "clip")), third, slope_three, norm_three, gain_three, three_r,
         ),
         (((pixels, in_r), bf16), ((nr, pixels + 16, mid_r), bf16), ((8, 128), f32)),
+        waits=returned[1:],
     )
     slope_two, stem_totals, sums = call(
         second_slope_kernel,
@@ -1074,24 +1126,26 @@
         [((3, pixels + 2 * images * cols, mid_r), bf16)],
         (stem_low,),
     )
-    blocks = ((nc // 2, part_rows, 128), bf16)
-    keep, give = call(
+    (wide,) = call(
         wide_grads_kernel,
-        (sides[0],),
+        (),
         (gated, grad_second, hidden_two, grad_third),
-        (blocks, blocks),
+        (((nc, part_rows, 128), bf16),),
         [
             ((3, pixels + 2 * images * cols, mid), bf16),
             ((9 * mid + mid * in_r // 128, 128), bf16),
         ],
     )
-    arrived = swap(give, "clip", 1)
+    wide_total = lax.psum_scatter(wide, "clip", scatter_dimension=0, tiled=False)
+    stem_high = stem_grad(
+        planes, stem_pre, outer_high, len(planes) // 2, stem_vectors, grad_second
+    )
     grad_fine, grad_gate, grad_hidden = call(
         gate_back_kernel,
         (),
         (Fresh(exchange(parts, "row")), hidden_one, sigmoid, full_expand),
         (((own, red), bf16), ((own, mid), bf16), ((own, mid), f32)),
-        waits=(keep,),
+        waits=(wide, stem_high),
     )
     grad_fine = lax.all_gather(grad_fine, "row").reshape(pixels, red)
     grad_reduced, slope_one, grad_coarse, grad_coarsest, sums = call(
@@ -1110,67 +1164,39 @@
         ),
         pads,
     )
-    fine_grad, half_grad, quarter_grad, reduce_grad, expand_grad = call(
+    tap_rows = padded(padded(k_fine.shape[0], 4) // 4)
+    rest_rows = 3 * tap_rows + padded(w_reduce.shape[0])
+    rest_rows += mid // 128 * padded(w_expand.shape[0]) + 8 * padded(stem_weight.shape[0])
+    (rest,) = call(
         small_grads_kernel,
-        (),
+        (spot,),
         (
             change, half_map, quarter, grad_fine, grad_coarse, grad_coarsest,
-            hidden_one, grad_reduced, merged, grad_gate,
+            hidden_one, grad_reduced, merged, grad_gate, stem_low, stem_high,
         ),
-        [((9 * red, red), bf16)] * 3 + [((mid, red), bf16), ((mid // 128, red, 128), bf16)],
-        pads,
+        (((nc, rest_rows, 128), bf16),),
+        [*pads, ((9 * red, red), bf16), ((nc, 4 * tap_rows, 128), bf16)],
     )
     sums = exchange(sums, both)
-    stem_high = stem_grad(planes, stem_pre, outer_high, len(planes) // 2, stem_vectors, slope_one)
     grad_first, vectors_one = call(
         functools.partial(first_back_kernel, count),
         (),
         (Fresh(sums), slope_one, first, norm_one, gain_one),
         (((own, mid), bf16), ((2, mid), f32)),
-        waits=(stem_high, fine_grad),
-    )
-    stem_blocks = (stem_low + stem_high).astype(bf16).reshape(nr, 8 // nr, nc, -1, 128)
-    both_parts = [
-        reduce_grad.reshape(nc, nr, -1, red),
-        expand_grad.reshape(nr, nc, -1, red).swapaxes(0, 1),
-        stem_blocks.transpose(2, 0, 1, 3, 4).reshape(nc, nr, -1, 128),
-    ]
-    both_rows = [part.shape[2] for part in both_parts]
-    both_parts = jnp.concatenate(both_parts, 2).reshape(nc * nr, -1, 128)
-    both_total = exchange(both_parts, both)
-    both_total = jnp.sum(both_total, 0, dtype=f32).astype(bf16)
-
-    def halving(keep, arrived, bit, side, *waits):
-        rows = ((keep.shape[0] // 2, part_rows, 128), bf16)
-        keep, give = call(halve_kernel, (side,), (keep, Fresh(arrived)), (rows, rows), (), waits)
-        return keep, swap(give, "clip", bit)
-
-    keep, arrived = halving(keep, arrived, bits[1][0], sides[1], slope_one)
+        waits=(rest,),
+    )
+    rest, grad_first = together(rest, grad_first)
+    rest_total = jnp.sum(exchange(rest, "clip"), 0, dtype=f32).astype(bf16)
     (one_grad,) = call(
         one_grad_kernel,
         (spot,),
         (Fresh(lax.all_gather(grad_first, "row")), *x_pieces),
         (((c_in, mid_r), bf16),),
     )
-    send, one_grad = together(send, one_grad)
-
-    def quarter_of(gradient):
-        shares = gradient.reshape(nc, -1, red)
-        shares = jnp.pad(shares, ((0, 0), (0, -shares.shape[1] % (8 * nr)), (0, 0)))
-        return pick(shares.reshape(nc, nr, -1, red), place, 1)
-
-    clip_parts = [one_grad.reshape(nc, -1, red)] + [
-        quarter_of(gradient) for gradient in (fine_grad, half_grad, quarter_grad)
-    ]
-    one_rows, tap_rows = clip_parts[0].shape[1], clip_parts[1].shape[1]
-    clip_parts = jnp.concatenate(clip_parts, 1)
-    clip_parts, both_total = together(clip_parts, both_total)
-    for (bit, _), spot_of in zip(bits[2:], sides[2:]):
-        keep, arrived = halving(keep, arrived, bit, spot_of, one_grad)
-    clip_total = jnp.sum(exchange(clip_parts, "clip"), 0, dtype=f32)
-    returned = [pick(send, place)] + [
-        swap(pick(send, spots[s]), "row", s) for s in range(1, nr)
-    ]
+    one_rows = c_in // nc
+    one_grad, rest_total = together(one_grad, rest_total)
+    one_total = exchange(one_grad.reshape(nc, one_rows, 128), "clip")
+    one_total = jnp.sum(one_total, 0, dtype=f32).astype(bf16)
     input_grad, block_out = call(
         input_grad_kernel,
         (spot,),
@@ -1178,52 +1204,55 @@
         ((block_input.shape, f32), (block_input.shape, bf16)),
     )
 
-    def wide(blocks):
-        return blocks.swapaxes(0, 1).reshape(blocks.shape[1], -1).astype(f32)
-
     (last,) = call(
         last_kernel,
         (),
-        (keep, Fresh(arrived), vectors_three, vectors_two),
+        (Fresh(wide_total), vectors_three, vectors_two),
         (((part_rows + 32, 128), bf16),),
     )
-    shares_a = lax.all_gather(last, "row")
-    two_share = wide(shares_a[:, :two_rows])
-    three_share = shares_a[:, two_end:part_rows].reshape(c_in // 128, -1, 128)
-    three_share = wide(three_share[:, :three_rows])
-    vectors = shares_a[:, part_rows:].astype(f32)
-    vectors = vectors[:, :16] + vectors[:, 16:]
-    clip_rows = clip_total.shape[0]
-    shares_b = lax.all_gather(
-        jnp.concatenate([clip_total.astype(bf16), both_total], 0), "row"
-    )
-    shares_c = shares_b[:, clip_rows:]
-    one_share = wide(shares_b[:, :one_rows])
-    tap_shares = [
-        shares_b[:, start : start + tap_rows].reshape(-1, red)[: k_fine.shape[0]].astype(f32)
-        for start in range(one_rows, clip_rows, tap_rows)
-    ]
-    reduce_share = shares_c[:, : both_rows[0]].reshape(-1, red).astype(f32)
-    expand_share = wide(shares_c[:, both_rows[0] : both_rows[0] + both_rows[1]])
-    stem_share = wide(shares_c[:, both_rows[0] + both_rows[1] :].reshape(8, -1, 128))[:, :784]
+    def from_row(piece):
+        return [piece] + [Fresh(swap(piece, "row", s)) for s in range(1, nr)]
+
+    two_share, three_share, gain_two, bias_two, gain_three, bias_three = call(
+        wide_shares_kernel,
+        (spot,),
+        from_row(last),
+        (
+            ((two_rows, mid), f32), ((three_rows, c_in), f32),
+            ((1, mid), f32), ((1, mid), f32), ((1, c_in), f32), ((1, c_in), f32),
+        ),
+    )
+    rest_shares = call(
+        functools.partial(rest_shares_kernel, tap_rows),
+        (spot,),
+        from_row(rest_total),
+        (
+            *[(entry.shape, f32) for entry in (k_fine, k_half, k_quarter, w_reduce, w_expand)],
+            ((stem_weight.shape[0], 1024), f32),
+        ),
+    )
+    one_total, input_grad, two_share, *rest_shares = together(
+        one_total, input_grad, two_share, *rest_shares
+    )
+    (one_share,) = call(one_share_kernel, (spot,), from_row(one_total), (((one_rows, mid), f32),))
     return (
         block_out,
         input_grad,
-        filters_outside(stem_share),
+        filters_outside(rest_shares[5][:, :784]),
         stem_gain_grad,
         stem_bias_grad,
         one_share,
-        reduce_share,
-        *tap_shares,
-        expand_share,
+        rest_shares[3],
+        *rest_shares[:3],
+        rest_shares[4],
         two_share,
         three_share,
         vectors_one[1],
         vectors_one[0],
-        vectors[:, 9].reshape(-1),
-        vectors[:, 8].reshape(-1),
-        vectors[:, 4:8].reshape(-1),
-        vectors[:, 0:4].reshape(-1),
+        gain_two[0],
+        bias_two[0],
+        gain_three[0],
+        bias_three[0],
     )
 
 

time: 352 us -> 336 us (0.955); the launches traced: 347 us -> 334 us
  waiting for transfers between devices: 22.2 us -> 59.1 us
  blocking collectives: 77.2 us -> 58.3 us
  Pallas kernels: 131 us -> 120 us
  local copies, waits for them, and re-layouts: 23.5 us -> 13.7 us
  other arithmetic: 11 us -> 5.3 us
  starting transfers between devices: 67.6 us -> 63.6 us
    all_to_all x10, waiting for transfers between devices: 6.31 us -> 44.4 us  [exchange(): return lax.all_to_all(blocks, axis, 0, 0)]
    all_gather x2 -> x0, blocking collectives: 16.5 us -> none  [the longest x1 9.55 us: per_device(): shares_a = lax.all_gather(last, 'row')]
    pallas_call x6, Pallas kernels: 68.5 us -> 55.4 us  [stem_call(): pl.pallas_call(body, grid=(steps,), in_specs=in_specs + [pl.BlockSpec(mem...]
    convert_element_type x8 -> x0, other arithmetic: 3.78 us -> none  [the longest x3 1.92 us: per_device(): shares_b[:, start:start + tap_rows].reshape(-1, red)[:k_fine.shape[0]]]
    pallas_call x21 -> x22, Pallas kernels: 62.1 us -> 64.3 us  [call(): pl.pallas_call(body, grid=(1,), in_specs=[pl.BlockSpec(memory_space=pltpu...]
    ppermute x15 -> x19, waiting for transfers between devices: 12.5 us -> 11.1 us  [swap(): lax.ppermute(piece, axis, [(i, i ^ step) for i in range(lax.axis_size(axi...]
    ppermute x15 -> x19, starting transfers between devices: 13.1 us -> 11.7 us  [swap(): lax.ppermute(piece, axis, [(i, i ^ step) for i in range(lax.axis_size(axi...]
  transfers between devices with their start and end apart: 28 -> 33, of which waited for: 8 -> 13; matrix products, arithmetic and copies ran while one was open for 5% -> 3% of each run, Pallas kernels for 34% -> 28%
where the time goes in v3:
time: 336 us; the launch traced here: 334 us
  Pallas kernels  120 us (36%)
  starting transfers between devices  63.6 us (19%)
  waiting for transfers between devices  59.1 us (18%)
  blocking collectives  58.3 us (17%)
  between operations  14.5 us (4%)
  local copies, waits for them, and re-layouts  13.7 us (4%)
  other arithmetic  5.3 us (2%)
    pallas_call x22, Pallas kernels, call(): pl.pallas_call(body, grid=(1,), in_specs=[pl.BlockSpec(memory_space=pltpu...  64.3 us
    pallas_call x6, Pallas kernels, stem_call(): pl.pallas_call(body, grid=(steps,), in_specs=in_specs + [pl.BlockSpec(mem...  55.4 us
    all_to_all x10, starting transfers between devices, exchange(): return lax.all_to_all(blocks, axis, 0, 0)  46.8 us
    all_to_all x10, waiting for transfers between devices, exchange(): return lax.all_to_all(blocks, axis, 0, 0)  44.4 us
    all_to_all x2, blocking collectives, exchange(): return lax.all_to_all(blocks, axis, 0, 0)  25.4 us
    ppermute x19, starting transfers between devices, swap(): lax.ppermute(piece, axis, [(i, i ^ step) for i in range(lax.axis_size(axi...  11.7 us
    ppermute x19, waiting for transfers between devices, swap(): lax.ppermute(piece, axis, [(i, i ^ step) for i in range(lax.axis_size(axi...  11.1 us
    unnamed x71, local copies, waits for them, and re-layouts  7.52 us
  transfers between devices with their start and end apart: 33, of which 13 were waited for; matrix products, arithmetic and copies ran while one was open for 3% of the time, Pallas kernels for 28%

profile of v3, /device:TPU:0, one launch (start us, length us, event | category | flops | bytes accessed | tf_op | source)
XLA Modules:
  0.0 334.2 jit_solution(11701602206802235956)
XLA Ops:
  8.3 2.9 shard_map.366
  11.9 7.3 %all-to-all-start = ((bf16[8,8,784]{2,1,0:T(8,128)(2,1)}), bf16[8,8,784]{2,1,0:T(8,128)(2,1)S(1)}, u32[]{:S(2)}, u32[]{:S(2)}) async-start(bf16[8,8,784]{2,1,0:T(8,128)(2,1)} %broadcast_in_dim.6), calls=%async_computation | async-start | bytes 229376 | tf_op jit(solution)/shard_map/all_to_all | solution.py:891
  20.6 3.8 %collective-permute-start = (bf16[12,3,16,256]{3,2,1,0:T(8,128)(2,1)S(1)}, bf16[12,3,16,256]{3,2,1,0:T(8,128)(2,1)}, u32[]{:S(2)}, u32[]{:S(2)}) collective-permute-start(bf16[12,3,16,256]{3,2,1,0:T(8,128)(2,1)S(1)} %get-tuple-element.210), channel_id=1, source_target_pairs={{0,1},{1,2},{2,3},{4,5},{5,6},{6,7},{8,9},{9,10},{10,11},{12,13},{... | collective-permute-start | bytes 884744 | tf_op jit(solution)/shard_map/ppermute | solution.py:985
  24.4 2.0 all-to-all-done
  26.4 4.0 %all-to-all-start.1 = ((bf16[8,832,128]{2,1,0:T(8,128)(2,1)}), bf16[8,832,128]{2,1,0:T(8,128)(2,1)S(1)}, u32[]{:S(2)}, u32[]{:S(2)}) async-start(bf16[8,832,128]{2,1,0:T(8,128)(2,1)} %get-tuple-element.116), calls=%async_computation.1 | async-start | bytes 3407872 | tf_op jit(solution)/shard_map/all_to_all | solution.py:891
  35.9 13.0 %shard_map.367.refs_0_ = bf16[4,80,112,256]{3,2,1,0:T(8,128)(2,1)} custom-call(s32[8]{0:T(128)S(1)} %bitcast.57, bf16[12,3,64,256]{3,2,1,0:T(8,128)(2,1)} %bitcast.74, bf16[12,3,16,256]{3,2,1,0:T(8,128)(2,1)} %collective-permute-done.refs_2_, bf16[12,3,16,256]{3,2,1,0:T(8,128)(2,1)} %collective-permute-done.1.refs_3_), custom_call_target="tpu_custom_call" | custom-call | flops 16000000000 | bytes 20000000 | tf_op jit(solution)/shard_map/pallas_call | solution.py:197
  48.9 2.3 collective-permute-done.5.refs_5_.refs_11_
  51.2 13.3 %shard_map.368 = (f32[8,32,64,128]{3,2,1,0:T(8,128)}, f32[2,64,128]{2,1,0:T(8,128)S(1)}) custom-call(bf16[4,80,112,256]{3,2,1,0:T(8,128)(2,1)} %shard_map.367.refs_0_, bf16[256,1456]{1,0:T(8,128)(2,1)} %fusion.7.refs_1_, bf16[128,2048]{1,0:T(8,128)(2,1)S(1)} %collective-permute-done.2.refs_2_.refs_6_.refs_3_, ...), custom_call_target="tpu_custom_call" | custom-call | flops 16000000000 | bytes 28000000 | tf_op jit(solution)/shard_map/pallas_call | solution.py:197
  68.0 2.9 all-to-all-done.1.refs_2_
  71.5 3.7 %collective-permute-done.7.refs_3_ = bf16[8,832,128]{2,1,0:T(8,128)(2,1)S(1)} collective-permute-done((bf16[8,832,128]{2,1,0:T(8,128)(2,1)S(1)}, bf16[8,832,128]{2,1,0:T(8,128)(2,1)S(1)}, u32[]{:S(2)}, u32[]{:S(2)}) %collective-permute-start.7) | collective-permute-done | bytes 1703968 | tf_op jit(solution)/shard_map/ppermute | solution.py:900
  75.2 2.9 shard_map.369
  78.8 3.3 all-to-all-start.2
  83.8 11.8 %all-to-all-done.2.refs_1_ = f32[32,16,128]{2,1,0:T(8,128)} async-done(((f32[32,16,128]{2,1,0:T(8,128)}), f32[32,16,128]{2,1,0:T(8,128)}, u32[]{:S(2)}, u32[]{:S(2)}) %all-to-all-start.2) | async-done | bytes 262176 | tf_op jit(solution)/shard_map/all_to_all | solution.py:891
  97.6 5.6 %all-gather.refs_1_ = bf16[512,128]{1,0:T(8,128)(2,1)S(1)} all-gather(bf16[128,128]{1,0:T(8,128)(2,1)} %get-tuple-element.128), channel_id=2, replica_groups=mesh['clip'=8,'row'=4] {'row'}, dimensions={0}, use_global_device_ids=true | all-gather | bytes 163840 | tf_op jit(solution)/shard_map/all_gather | solution.py:1034
  103.2 3.9 %shard_map.371 = (bf16[128,512]{1,0:T(8,128)(2,1)}, f32[128,512]{1,0:T(8,128)}, bf16[128,128]{1,0:T(8,128)(2,1)}, bf16[128,128]{1,0:T(8,128)(2,1)}, f32[32,128]{1,0:T(8,128)}) custom-call(s32[1]{0:T(128)} %bitcast.refs_0_, bf16[512,128]{1,0:T(8,128)(2,1)S(1)} %all-gather.refs_1_, bf16[128,512]{1,0:T(8,128)(2,1)} %get-tuple-element.129.refs_2_.refs_1_.refs_7_, ...), custom_call_target="tpu_custom_call" | custom-call | flops 1000000000 | bytes 2000000 | tf_op jit(solution)/shard_map/pallas_call | solution.py:868
  107.1 7.5 %all-gather.1.refs_0_ = bf16[512,512]{1,0:T(8,128)(2,1)S(1)} all-gather(bf16[128,512]{1,0:T(8,128)(2,1)} %get-tuple-element.133), channel_id=3, replica_groups=mesh['clip'=8,'row'=4] {'row'}, dimensions={0}, use_global_device_ids=true | all-gather | bytes 655360 | tf_op jit(solution)/shard_map/all_gather | solution.py:1053
  114.6 3.6 %all-gather.8.cloned.1.call-done = bf16[6656,128]{1,0:T(8,128)(2,1)} async-done(((bf16[832,128]{1,0:T(8,128)(2,1)}), bf16[6656,128]{1,0:T(8,128)(2,1)}) %all-gather.8.cloned.1.call-update) | async-done | bytes 1703952 | tf_op jit(solution)/shard_map/all_gather | solution.py:999
  118.1 3.7 %shard_map.372 = (f32[512,128]{1,0:T(8,128)}, bf16[4608,128]{1,0:T(8,128)(2,1)}, f32[8,8,128]{2,1,0:T(8,128)}) custom-call(bf16[512,512]{1,0:T(8,128)(2,1)S(1)} %all-gather.1.refs_0_, bf16[8,832,128]{2,1,0:T(8,128)(2,1)} %bitcast.93), custom_call_target="tpu_custom_call" | custom-call | flops 1000000000 | bytes 2000000 | tf_op jit(solution)/shard_map/pallas_call | solution.py:868
  121.9 3.6 %all-to-all-start.3 = ((f32[8,8,128]{2,1,0:T(8,128)}), f32[8,8,128]{2,1,0:T(8,128)S(1)}, u32[]{:S(2)}, u32[]{:S(2)}) async-start(f32[8,8,128]{2,1,0:T(8,128)} %get-tuple-element.135), calls=%async_computation.3 | async-start | bytes 65536 | tf_op jit(solution)/shard_map/all_to_all | solution.py:891
  128.2 6.1 %shard_map.373 = (bf16[4,32,64,128]{3,2,1,0:T(8,128)(2,1)}, f32[2,64,128]{2,1,0:T(8,128)S(1)}) custom-call(f32[8,32,64,128]{3,2,1,0:T(8,128)} %get-tuple-element.137.refs_0_.refs_1_, bf16[8,64,32,128]{3,2,1,0:T(8,128)(2,1)} %refs_1_.4, f32[4,64,128]{2,1,0:T(8,128)} %broadcast_in_dim.7.refs_2_, f32[512,128]{1,0:T(8,128)S(1)} %copy-done.23), custom_call_target="tpu_custom_call" | custom-call | flops 4000000000 | bytes 8000000 | tf_op jit(solution)/shard_map/pallas_call | solution.py:197
  136.1 7.3 %all-gather.3 = bf16[2048,128]{1,0:T(8,128)(2,1)S(1)} all-gather(bf16[512,128]{1,0:T(8,128)(2,1)} %get-tuple-element.139), channel_id=5, replica_groups=mesh['clip'=8,'row'=4] {'row'}, dimensions={0}, use_global_device_ids=true | all-gather | bytes 655360 | tf_op jit(solution)/shard_map/all_gather | solution.py:1070
  143.4 3.4 %shard_map.375 = (f32[512,512]{1,0:T(8,128)}, bf16[512,512]{1,0:T(8,128)(2,1)}, f32[8,8,128]{2,1,0:T(8,128)}) custom-call(bf16[4,512,128]{2,1,0:T(8,128)(2,1)S(1)} %bitcast.53, bf16[8,832,128]{2,1,0:T(8,128)(2,1)} %bitcast.94), custom_call_target="tpu_custom_call" | custom-call | flops 1000000000 | bytes 2000000 | tf_op jit(solution)/shard_map/pallas_call | solution.py:868
  146.8 6.2 %all-to-all-start.4 = ((f32[8,8,128]{2,1,0:T(8,128)}), f32[8,8,128]{2,1,0:T(8,128)S(1)}, u32[]{:S(2)}, u32[]{:S(2)}) async-start(f32[8,8,128]{2,1,0:T(8,128)} %get-tuple-element.140), calls=%async_computation.4 | async-start | bytes 65536 | tf_op jit(solution)/shard_map/all_to_all | solution.py:891
  154.2 6.1 %shard_map.376 = (bf16[4,32,64,128]{3,2,1,0:T(8,128)(2,1)}, f32[2,64,128]{2,1,0:T(8,128)S(1)}) custom-call(f32[8,32,64,128]{3,2,1,0:T(8,128)} %get-tuple-element.137.refs_0_.refs_1_, bf16[8,64,32,128]{3,2,1,0:T(8,128)(2,1)} %refs_1_.4, f32[4,64,128]{2,1,0:T(8,128)} %broadcast_in_dim.7.refs_2_, f32[512,512]{1,0:T(8,128)S(1)} %copy-done.1), custom_call_target="tpu_custom_call" | custom-call | flops 4000000000 | bytes 8000000 | tf_op jit(solution)/shard_map/pallas_call | solution.py:197
  161.0 4.1 %shard_map.377 = (bf16[2,128,512]{2,1,0:T(8,128)(2,1)}, bf16[2,128,512]{2,1,0:T(8,128)(2,1)}, bf16[2,128,512]{2,1,0:T(8,128)(2,1)}, bf16[2,128,512]{2,1,0:T(8,12...) custom-call(s32[1]{0:T(128)} %bitcast.refs_0_, f32[8,8,128]{2,1,0:T(8,128)S(1)} %all-to-all-done.4.refs_1_, ...), custom_call_target="tpu_custom_call" | custom-call | flops 1000000000 | bytes 2000000 | tf_op jit(solution)/shard_map/pallas_call | solution.py:868
  166.9 12.9 %all_to_all.60.refs_1_ = f32[8,16,128]{2,1,0:T(8,128)S(1)} all-to-all(f32[8,16,128]{2,1,0:T(8,128)} %get-tuple-element.143), channel_id=1, replica_groups=mesh['clip'=8,'row'=4] {'clip'}, dimensions={0} | all-to-all | bytes 131072 | tf_op jit(solution)/shard_map/all_to_all | solution.py:891
  179.9 3.4 %shard_map.378 = (bf16[512,512]{1,0:T(8,128)(2,1)}, bf16[4,528,128]{2,1,0:T(8,128)(2,1)}, f32[8,128]{1,0:T(8,128)}) custom-call(s32[1]{0:T(128)} %bitcast.refs_0_, f32[8,16,128]{2,1,0:T(8,128)S(1)} %all_to_all.60.refs_1_, f32[512,512]{1,0:T(8,128)} %get-tuple-element.141.refs_3_.refs_2_, f32[512,512]{1,0:T(8,128)} %get-tuple-element.144.refs_3_, ...), custom_call_target="tpu_custom_call" | custom-call | flops 1000000000 | bytes 2000000 | tf_op jit(solution)/shard_map/pallas_call | solution.py:868
  183.2 12.5 %all_to_all.61.refs_1_ = bf16[4,528,128]{2,1,0:T(8,128)(2,1)S(1)} all-to-all(bf16[4,528,128]{2,1,0:T(8,128)(2,1)} %get-tuple-element.150), channel_id=1, replica_groups=mesh['clip'=8,'row'=4] {'row'}, dimensions={0} | all-to-all | bytes 1081344 | tf_op jit(solution)/shard_map/all_to_all | solution.py:891
  198.9 5.1 %all-to-all-start.7 = ((f32[8,8,128]{2,1,0:T(8,128)}), f32[8,8,128]{2,1,0:T(8,128)S(1)}, u32[]{:S(2)}, u32[]{:S(2)}) async-start(f32[8,8,128]{2,1,0:T(8,128)} %get-tuple-element.152), calls=%async_computation.7 | async-start | bytes 65536 | tf_op jit(solution)/shard_map/all_to_all | solution.py:891
  204.9 8.5 %shard_map.380.refs_7_.refs_11_ = f32[8,64,128]{2,1,0:T(8,128)S(1)} custom-call(bf16[4,80,112,256]{3,2,1,0:T(8,128)(2,1)} %shard_map.367.refs_0_, f32[8,32,64,128]{3,2,1,0:T(8,128)} %get-tuple-element.137.refs_0_.refs_1_, bf16[4,32,64,128]{3,2,1,0:T(8,128)(2,1)} %get-tuple-element.155.refs_2_, f32[5,64,128]{2,1,0:T(8,128)} %broadcast_in_dim.8.refs_3_), custom_call_target="tpu_custom_call" | custom-call | flops 8000000000 | bytes 16000000 | tf_op jit(solution)/shard_map/pallas_call | solution.py:197
  213.4 3.7 %shard_map.381 = (bf16[512,128]{1,0:T(8,128)(2,1)}, bf16[4,128,512]{2,1,0:T(8,128)(2,1)}, f32[2,128]{1,0:T(2,128)}) custom-call(s32[1]{0:T(128)} %bitcast.refs_0_, f32[8,8,128]{2,1,0:T(8,128)S(1)} %all-to-all-done.7.refs_1_, f32[512,128]{1,0:T(8,128)} %get-tuple-element.153.refs_2_, f32[512,128]{1,0:T(8,128)} %get-tuple-element.136.refs_3_.refs_2_, ...), custom_call_target="tpu_custom_call" | custom-call | flops 1000000000 | bytes 2000000 | tf_op jit(solution)/shard_map/pallas_call | solution.py:868
  217.1 4.7 %shard_map.382.refs_4_ = bf16[8,832,128]{2,1,0:T(8,128)(2,1)} custom-call(bf16[512,512]{1,0:T(8,128)(2,1)} %copy-done.2, bf16[512,128]{1,0:T(8,128)(2,1)} %get-tuple-element.159.refs_1_.refs_4_, bf16[4,512,128]{2,1,0:T(8,128)(2,1)} %bitcast.54, bf16[512,512]{1,0:T(8,128)(2,1)} %get-tuple-element.160.refs_3_), custom_call_target="tpu_custom_call" | custom-call | flops 1000000000 | bytes 2000000 | tf_op jit(solution)/shard_map/pallas_call | solution.py:868
  221.8 3.6 %all-to-all-start.8 = ((bf16[4,128,512]{2,1,0:T(8,128)(2,1)}), bf16[4,128,512]{2,1,0:T(8,128)(2,1)S(1)}, u32[]{:S(2)}, u32[]{:S(2)}) async-start(bf16[4,128,512]{2,1,0:T(8,128)(2,1)} %get-tuple-element.157), calls=%async_computation.8 | async-start | bytes 1048576 | tf_op jit(solution)/shard_map/all_to_all | solution.py:891
  225.4 8.4 %shard_map.383.refs_5_.refs_12_ = f32[8,64,128]{2,1,0:T(8,128)S(1)} custom-call(bf16[4,80,112,256]{3,2,1,0:T(8,128)(2,1)} %shard_map.367.refs_0_, f32[8,32,64,128]{3,2,1,0:T(8,128)} %get-tuple-element.137.refs_0_.refs_1_, bf16[4,32,64,128]{3,2,1,0:T(8,128)(2,1)} %get-tuple-element.161.refs_2_, f32[5,64,128]{2,1,0:T(8,128)} %broadcast_in_dim.8.refs_3_, ...), custom_call_target="tpu_custom_call" | custom-call | flops 1000000 | bytes 16000000 | tf_op jit(solution)/shard_map/pallas_call | solution.py:197
  236.2 5.6 %all-gather.4.refs_2_.refs_4_ = bf16[512,128]{1,0:T(8,128)(2,1)S(1)} all-gather(bf16[128,128]{1,0:T(8,128)(2,1)} %get-tuple-element.162), channel_id=6, replica_groups=mesh['clip'=8,'row'=4] {'row'}, dimensions={0}, use_global_device_ids=true | all-gather | bytes 163840 | tf_op jit(solution)/shard_map/all_gather | solution.py:1150
  241.8 4.7 %shard_map.385 = (bf16[128,128]{1,0:T(8,128)(2,1)}, f32[128,512]{1,0:T(8,128)}, bf16[128,128]{1,0:T(8,128)(2,1)}, f32[32,128]{1,0:T(8,128)}, f32[32,16,128]{2,1,0:T(8,128)}) custom-call(s32[1]{0:T(128)} %bitcast.refs_0_, s32[1,8]{1,0:T(1,128)S(1)} %copy-done.21, bf16[512,128]{1,0:T(8,128)(2,1)S(1)} %all-gather.4.refs_2_.refs_4_, bf16[1152,128]{1,0:T(8,128)(2,1)} %bitcast.73, ...), custom_call_target="tpu_custom_call" | custom-call | flops 1000000000 | bytes 2000000 | tf_op jit(solution)/shard_map/pallas_call | solution.py:868
  246.5 6.5 %all-to-all-start.9 = ((f32[32,16,128]{2,1,0:T(8,128)}), f32[32,16,128]{2,1,0:T(8,128)S(1)}, u32[]{:S(2)}, u32[]{:S(2)}) async-start(f32[32,16,128]{2,1,0:T(8,128)} %get-tuple-element.170), calls=%async_computation.9 | async-start | bytes 524288 | tf_op jit(solution)/shard_map/all_to_all | solution.py:891
  253.0 3.6 %shard_map.386.refs_5_ = bf16[8,400,128]{2,1,0:T(8,128)(2,1)} custom-call(s32[1]{0:T(128)} %bitcast.refs_0_, bf16[512,128]{1,0:T(8,128)(2,1)} %copy-done.11, bf16[128,128]{1,0:T(8,128)(2,1)} %get-tuple-element.131.refs_2_, f32[32,128]{1,0:T(8,128)} %get-tuple-element.132.refs_3_, bf16[512,128]{1,0:T(8,128)(2,1)} %copy-done.12, ...), custom_call_target="tpu_custom_call" | custom-call | flops 1000000000 | bytes 2000000 | tf_op jit(solution)/shard_map/pallas_call | solution.py:868
  256.6 6.8 %all-to-all-done.9.refs_0_ = f32[32,16,128]{2,1,0:T(8,128)S(1)} async-done(((f32[32,16,128]{2,1,0:T(8,128)}), f32[32,16,128]{2,1,0:T(8,128)S(1)}, u32[]{:S(2)}, u32[]{:S(2)}) %all-to-all-start.9) | async-done | bytes 262176 | tf_op jit(solution)/shard_map/all_to_all | solution.py:891
  265.1 3.7 %all-to-all-start.10 = ((bf16[8,400,128]{2,1,0:T(8,128)(2,1)}), bf16[8,400,128]{2,1,0:T(8,128)(2,1)S(1)}, u32[]{:S(2)}, u32[]{:S(2)}) async-start(bf16[8,400,128]{2,1,0:T(8,128)(2,1)} %shard_map.386.refs_5_), calls=%async_computation.10 | async-start | bytes 1638400 | tf_op jit(solution)/shard_map/all_to_all | solution.py:891
  268.8 6.9 %all-gather.5 = bf16[512,512]{1,0:T(8,128)(2,1)S(1)} all-gather(bf16[128,512]{1,0:T(8,128)(2,1)S(1)} %copy-done.28), channel_id=7, replica_groups=mesh['clip'=8,'row'=4] {'row'}, dimensions={0}, use_global_device_ids=true | all-gather | bytes 655360 | tf_op jit(solution)/shard_map/all_gather | solution.py:1193
  275.7 3.1 shard_map.389
  278.8 18.0 %all-to-all-done.10 = bf16[8,400,128]{2,1,0:T(8,128)(2,1)S(1)} async-done(((bf16[8,400,128]{2,1,0:T(8,128)(2,1)}), bf16[8,400,128]{2,1,0:T(8,128)(2,1)S(1)}, u32[]{:S(2)}, u32[]{:S(2)}) %all-to-all-start.10) | async-done | bytes 819232 | tf_op jit(solution)/shard_map/all_to_all | solution.py:891
  296.9 3.6 %all-to-all-start.11 = ((bf16[8,256,128]{2,1,0:T(8,128)(2,1)}), bf16[8,256,128]{2,1,0:T(8,128)(2,1)S(1)}, u32[]{:S(2)}, u32[]{:S(2)}) async-start(bf16[8,256,128]{2,1,0:T(8,128)(2,1)} %bitcast.66), calls=%async_computation.11 | async-start | bytes 1048576 | tf_op jit(solution)/shard_map/all_to_all | solution.py:891
  307.2 3.7 %shard_map.388 = (f32[8,2,8,2048]{3,2,1,0:T(8,128)}, bf16[8,2,8,2048]{3,2,1,0:T(8,128)(2,1)}) custom-call(s32[1]{0:T(128)} %bitcast.refs_0_, bf16[128,512]{1,0:T(8,128)(2,1)} %get-tuple-element.173.refs_1_, bf16[2048,512]{1,0:T(8,128)(2,1)} %bitcast.92, bf16[2,128,512]{2,1,0:T(8,128)(2,1)} %get-tuple-element.175.refs_3_, bf16[2,128,512]{2,1,0:T(8,128)(2,1)} %copy-done.16, ...), custom_call_target="tpu_custom_call" | custom-call | flops 1000000000 | bytes 2000000 | tf_op jit(solution)/shard_map/pallas_call | solution.py:868
  312.6 2.7 all-to-all-done.11
  315.3 2.1 collective-permute-done.13.refs_3_
  317.5 2.3 shard_map.391
  (155 shorter events, 49.5 us)
Async XLA Ops:
  8.3 10.9 %copy-start.27 = (bf16[1,12,3,64,256]{4,3,2,1,0:T(8,128)(2,1)S(1)}, bf16[1,12,3,64,256]{4,3,2,1,0:T(8,128)(2,1)}, u32[]{:S(2)}) copy-start(bf16[1,12,3,64,256]{4,3,2,1,0:T(8,128)(2,1)} %param.23) | copy-start | bytes 3538948
  11.3 13.1 %copy-start.25 = (bf16[8,2,8,2048]{3,2,1,0:T(8,128)(2,1)S(1)}, bf16[8,2,8,2048]{3,2,1,0:T(8,128)(2,1)}, u32[]{:S(2)}) copy-start(bf16[8,2,8,2048]{3,2,1,0:T(8,128)(2,1)} %param.29) | copy-start | bytes 1572868
  11.3 13.1 %copy-start.26 = (bf16[8,2,8,2048]{3,2,1,0:T(8,128)(2,1)S(1)}, bf16[8,2,8,2048]{3,2,1,0:T(8,128)(2,1)}, u32[]{:S(2)}) copy-start(bf16[8,2,8,2048]{3,2,1,0:T(8,128)(2,1)} %param.45) | copy-start | bytes 1572868
  11.9 14.5 %all-to-all-start = ((bf16[8,8,784]{2,1,0:T(8,128)(2,1)}), bf16[8,8,784]{2,1,0:T(8,128)(2,1)S(1)}, u32[]{:S(2)}, u32[]{:S(2)}) async-start(bf16[8,8,784]{2,1,0:T(8,128)(2,1)} %broadcast_in_dim.6), calls=%async_computation | async-start | bytes 229376 | tf_op jit(solution)/shard_map/all_to_all | solution.py:891
  19.3 12.3 %collective-permute-start.1 = (bf16[12,3,16,256]{3,2,1,0:T(8,128)(2,1)S(1)}, bf16[12,3,16,256]{3,2,1,0:T(8,128)(2,1)}, u32[]{:S(2)}, u32[]{:S(2)}) collective-permute-start(bf16[12,3,16,256]{3,2,1,0:T(8,128)(2,1)S(1)} %get-tuple-element.209), channel_id=1, source_target_pairs={{1,0},{2,1},{3,2},{5,4},{6,5},{7,6},{9,8},{10,9},{11,10},{13,12},{... | collective-permute-start | bytes 884744 | tf_op jit(solution)/shard_map/ppermute | solution.py:986
  20.6 11.0 %collective-permute-start = (bf16[12,3,16,256]{3,2,1,0:T(8,128)(2,1)S(1)}, bf16[12,3,16,256]{3,2,1,0:T(8,128)(2,1)}, u32[]{:S(2)}, u32[]{:S(2)}) collective-permute-start(bf16[12,3,16,256]{3,2,1,0:T(8,128)(2,1)S(1)} %get-tuple-element.210), channel_id=1, source_target_pairs={{0,1},{1,2},{2,3},{4,5},{5,6},{6,7},{8,9},{9,10},{10,11},{12,13},{... | collective-permute-start | bytes 884744 | tf_op jit(solution)/shard_map/ppermute | solution.py:985
  24.4 8.7 %copy-start.24 = (bf16[2,8,8,2048]{3,2,1,0:T(8,128)(2,1)}, bf16[2,8,8,2048]{3,2,1,0:T(8,128)(2,1)S(1)}, u32[]{:S(2)}) copy-start(bf16[2,8,8,2048]{3,2,1,0:T(8,128)(2,1)S(1)} %copy.46) | copy-start | bytes 1572868
  26.4 44.4 %all-to-all-start.1 = ((bf16[8,832,128]{2,1,0:T(8,128)(2,1)}), bf16[8,832,128]{2,1,0:T(8,128)(2,1)S(1)}, u32[]{:S(2)}, u32[]{:S(2)}) async-start(bf16[8,832,128]{2,1,0:T(8,128)(2,1)} %get-tuple-element.116), calls=%async_computation.1 | async-start | bytes 3407872 | tf_op jit(solution)/shard_map/all_to_all | solution.py:891
  30.4 5.4 %copy-start.20 = (s32[1,8]{1,0:T(1,128)S(1)}, s32[1,8]{1,0:T(1,128)}, u32[]{:S(2)}) copy-start(s32[1,8]{1,0:T(1,128)} %param.24) | copy-start | bytes 100
  30.5 87.7 %all-gather.8.cloned.1.call-start = ((), (), s32[]{:S(2)}) async-start(), calls=%async_computation.14 | async-start | bytes 1916928 | tf_op jit(solution)/shard_map/all_gather | solution.py:999
  31.6 19.6 %collective-permute-start.3 = (bf16[128,2048]{1,0:T(8,128)(2,1)S(1)}, bf16[128,2048]{1,0:T(8,128)(2,1)S(1)}, u32[]{:S(2)}, u32[]{:S(2)}) collective-permute-start(bf16[128,2048]{1,0:T(8,128)(2,1)S(1)} %bitcast.58), channel_id=1, source_target_pairs={{0,2},{1,3},{2,0},{3,1},{4,6},{5,7},{6,4},{7,5},{8,10},{9,11},{10,... | collective-permute-start | bytes 1572872 | tf_op jit(solution)/shard_map/ppermute | solution.py:900
  33.1 18.1 %collective-permute-start.2 = (bf16[128,2048]{1,0:T(8,128)(2,1)S(1)}, bf16[128,2048]{1,0:T(8,128)(2,1)S(1)}, u32[]{:S(2)}, u32[]{:S(2)}) collective-permute-start(bf16[128,2048]{1,0:T(8,128)(2,1)S(1)} %bitcast.59), channel_id=1, source_target_pairs={{0,1},{1,0},{2,3},{3,2},{4,5},{5,4},{6,7},{7,6},{8,9},{9,8},{10,11... | collective-permute-start | bytes 1572872 | tf_op jit(solution)/shard_map/ppermute | solution.py:900
  33.7 15.1 %collective-permute-start.6 = (bf16[128,512]{1,0:T(8,128)(2,1)S(1)}, bf16[128,512]{1,0:T(8,128)(2,1)S(1)}, u32[]{:S(2)}, u32[]{:S(2)}) collective-permute-start(bf16[128,512]{1,0:T(8,128)(2,1)S(1)} %get-tuple-element.212), channel_id=1, source_target_pairs={{0,3},{1,2},{2,1},{3,0},{4,7},{5,6},{6,5},{7,4},{8,11},{9,10},{10,... | collective-permute-start | bytes 393224 | tf_op jit(solution)/shard_map/ppermute | solution.py:900
  34.4 16.8 %collective-permute-start.5 = (bf16[128,512]{1,0:T(8,128)(2,1)S(1)}, bf16[128,512]{1,0:T(8,128)(2,1)S(1)}, u32[]{:S(2)}, u32[]{:S(2)}) collective-permute-start(bf16[128,512]{1,0:T(8,128)(2,1)S(1)} %get-tuple-element.213), channel_id=1, source_target_pairs={{0,2},{1,3},{2,0},{3,1},{4,6},{5,7},{6,4},{7,5},{8,10},{9,11},{10,... | collective-permute-start | bytes 393224 | tf_op jit(solution)/shard_map/ppermute | solution.py:900
  35.9 15.3 %collective-permute-start.4 = (bf16[128,512]{1,0:T(8,128)(2,1)S(1)}, bf16[128,512]{1,0:T(8,128)(2,1)S(1)}, u32[]{:S(2)}, u32[]{:S(2)}) collective-permute-start(bf16[128,512]{1,0:T(8,128)(2,1)S(1)} %get-tuple-element.214), channel_id=1, source_target_pairs={{0,1},{1,0},{2,3},{3,2},{4,5},{5,4},{6,7},{7,6},{8,9},{9,8},{10,11... | collective-permute-start | bytes 393224 | tf_op jit(solution)/shard_map/ppermute | solution.py:900
  48.9 15.6 %copy-start.8 = (bf16[128,512]{1,0:T(8,128)(2,1)}, bf16[128,512]{1,0:T(8,128)(2,1)S(1)}, u32[]{:S(2)}) copy-start(bf16[128,512]{1,0:T(8,128)(2,1)S(1)} %collective-permute-done.6.refs_6_.refs_12_) | copy-start | bytes 393220
  70.9 4.3 %collective-permute-start.7 = (bf16[8,832,128]{2,1,0:T(8,128)(2,1)S(1)}, bf16[8,832,128]{2,1,0:T(8,128)(2,1)S(1)}, u32[]{:S(2)}, u32[]{:S(2)}) collective-permute-start(bf16[8,832,128]{2,1,0:T(8,128)(2,1)S(1)} %all-to-all-done.1.refs_2_), channel_id=1, source_target_pairs={{0,1},{1,0},{2,3},{3,2},{4,5},{5,4},{6,7},{7,6},{8,9},{9,8},{10,11... | collective-permute-start | bytes 5111816 | tf_op jit(solution)/shard_map/ppermute | solution.py:900
  70.9 90.1 %collective-permute-start.8 = (bf16[128,2048]{1,0:T(8,128)(2,1)}, bf16[128,2048]{1,0:T(8,128)(2,1)}, u32[]{:S(2)}, u32[]{:S(2)}) collective-permute-start(bf16[128,2048]{1,0:T(8,128)(2,1)} %copy-done.4), channel_id=1, source_target_pairs={{0,1},{1,0},{2,3},{3,2},{4,5},{5,4},{6,7},{7,6},{8,9},{9,8},{10,11... | collective-permute-start | bytes 1572872 | tf_op jit(solution)/shard_map/ppermute | solution.py:900
  78.8 16.8 %all-to-all-start.2 = ((f32[32,16,128]{2,1,0:T(8,128)}), f32[32,16,128]{2,1,0:T(8,128)}, u32[]{:S(2)}, u32[]{:S(2)}) async-start(f32[32,16,128]{2,1,0:T(8,128)} %get-tuple-element.124), calls=%async_computation.2 | async-start | bytes 524288 | tf_op jit(solution)/shard_map/all_to_all | solution.py:891
  82.2 13.4 %copy-start.21 = (s32[1,8]{1,0:T(1,128)S(1)}, s32[1,8]{1,0:T(1,128)}, u32[]{:S(2)}) copy-start(s32[1,8]{1,0:T(1,128)} %refs_1_.5) | copy-start | bytes 100
  114.6 7.3 %copy-start.2 = (bf16[512,512]{1,0:T(8,128)(2,1)}, bf16[512,512]{1,0:T(8,128)(2,1)S(1)}, u32[]{:S(2)}) copy-start(bf16[512,512]{1,0:T(8,128)(2,1)S(1)} %all-gather.1.refs_0_) | copy-start | bytes 1572868
  118.1 8.2 %copy-start.33 = (f32[64]{0:T(128)S(1)}, f32[64]{0:T(128)}, u32[]{:S(2)}) copy-start(f32[64]{0:T(128)} %param.27) | copy-start | bytes 772
  118.1 8.3 %copy-start.34 = (f32[64]{0:T(128)S(1)}, f32[64]{0:T(128)}, u32[]{:S(2)}) copy-start(f32[64]{0:T(128)} %param.28) | copy-start | bytes 772
  121.9 12.4 %all-to-all-start.3 = ((f32[8,8,128]{2,1,0:T(8,128)}), f32[8,8,128]{2,1,0:T(8,128)S(1)}, u32[]{:S(2)}, u32[]{:S(2)}) async-start(f32[8,8,128]{2,1,0:T(8,128)} %get-tuple-element.135), calls=%async_computation.3 | async-start | bytes 65536 | tf_op jit(solution)/shard_map/all_to_all | solution.py:891
  146.8 14.2 %all-to-all-start.4 = ((f32[8,8,128]{2,1,0:T(8,128)}), f32[8,8,128]{2,1,0:T(8,128)S(1)}, u32[]{:S(2)}, u32[]{:S(2)}) async-start(f32[8,8,128]{2,1,0:T(8,128)} %get-tuple-element.140), calls=%async_computation.4 | async-start | bytes 65536 | tf_op jit(solution)/shard_map/all_to_all | solution.py:891
  165.1 14.8 %collective-permute-start.9 = (bf16[2,128,512]{2,1,0:T(8,128)(2,1)}, bf16[2,128,512]{2,1,0:T(8,128)(2,1)S(1)}, u32[]{:S(2)}, u32[]{:S(2)}) collective-permute-start(bf16[2,128,512]{2,1,0:T(8,128)(2,1)} %get-tuple-element.147), channel_id=1, source_target_pairs={{0,1},{1,0},{2,3},{3,2},{4,5},{5,4},{6,7},{7,6},{8,9},{9,8},{10,11... | collective-permute-start | bytes 786440 | tf_op jit(solution)/shard_map/ppermute | solution.py:900
  165.1 14.7 %collective-permute-start.10 = (bf16[2,128,512]{2,1,0:T(8,128)(2,1)}, bf16[2,128,512]{2,1,0:T(8,128)(2,1)S(1)}, u32[]{:S(2)}, u32[]{:S(2)}) collective-permute-start(bf16[2,128,512]{2,1,0:T(8,128)(2,1)} %get-tuple-element.148), channel_id=1, source_target_pairs={{0,2},{1,3},{2,0},{3,1},{4,6},{5,7},{6,4},{7,5},{8,10},{9,11},{10,... | collective-permute-start | bytes 786440 | tf_op jit(solution)/shard_map/ppermute | solution.py:900
  166.0 13.9 %collective-permute-start.11 = (bf16[2,128,512]{2,1,0:T(8,128)(2,1)}, bf16[2,128,512]{2,1,0:T(8,128)(2,1)S(1)}, u32[]{:S(2)}, u32[]{:S(2)}) collective-permute-start(bf16[2,128,512]{2,1,0:T(8,128)(2,1)} %get-tuple-element.149), channel_id=1, source_target_pairs={{0,3},{1,2},{2,1},{3,0},{4,7},{5,6},{6,5},{7,4},{8,11},{9,10},{10,... | collective-permute-start | bytes 786440 | tf_op jit(solution)/shard_map/ppermute | solution.py:900
  198.9 14.5 %all-to-all-start.7 = ((f32[8,8,128]{2,1,0:T(8,128)}), f32[8,8,128]{2,1,0:T(8,128)S(1)}, u32[]{:S(2)}, u32[]{:S(2)}) async-start(f32[8,8,128]{2,1,0:T(8,128)} %get-tuple-element.152), calls=%async_computation.7 | async-start | bytes 65536 | tf_op jit(solution)/shard_map/all_to_all | solution.py:891
  204.0 98.4 %reduce-scatter.2.cloned.1.call-start = ((), (), s32[]{:S(2)}) async-start(), calls=%async_computation.13 | async-start | bytes 1916928 | tf_op jit(solution)/shard_map/reduce_scatter | solution.py:1139
  221.8 12.4 %all-to-all-start.8 = ((bf16[4,128,512]{2,1,0:T(8,128)(2,1)}), bf16[4,128,512]{2,1,0:T(8,128)(2,1)S(1)}, u32[]{:S(2)}, u32[]{:S(2)}) async-start(bf16[4,128,512]{2,1,0:T(8,128)(2,1)} %get-tuple-element.157), calls=%async_computation.8 | async-start | bytes 1048576 | tf_op jit(solution)/shard_map/all_to_all | solution.py:891
  225.4 8.8 %copy-start = (bf16[8,832,128]{2,1,0:T(8,128)(2,1)S(1)}, bf16[8,832,128]{2,1,0:T(8,128)(2,1)}, u32[]{:S(2)}) copy-start(bf16[8,832,128]{2,1,0:T(8,128)(2,1)} %shard_map.382.refs_4_) | copy-start | bytes 5111812
  241.8 4.7 %copy-start.12 = (bf16[512,128]{1,0:T(8,128)(2,1)}, bf16[512,128]{1,0:T(8,128)(2,1)S(1)}, u32[]{:S(2)}) copy-start(bf16[512,128]{1,0:T(8,128)(2,1)S(1)} %all-gather.4.refs_2_.refs_4_) | copy-start | bytes 393220
  246.5 16.8 %all-to-all-start.9 = ((f32[32,16,128]{2,1,0:T(8,128)}), f32[32,16,128]{2,1,0:T(8,128)S(1)}, u32[]{:S(2)}, u32[]{:S(2)}) async-start(f32[32,16,128]{2,1,0:T(8,128)} %get-tuple-element.170), calls=%async_computation.9 | async-start | bytes 524288 | tf_op jit(solution)/shard_map/all_to_all | solution.py:891
  265.1 31.7 %all-to-all-start.10 = ((bf16[8,400,128]{2,1,0:T(8,128)(2,1)}), bf16[8,400,128]{2,1,0:T(8,128)(2,1)S(1)}, u32[]{:S(2)}, u32[]{:S(2)}) async-start(bf16[8,400,128]{2,1,0:T(8,128)(2,1)} %shard_map.386.refs_5_), calls=%async_computation.10 | async-start | bytes 1638400 | tf_op jit(solution)/shard_map/all_to_all | solution.py:891
  296.9 7.8 %copy-start.29 = (bf16[400,128]{1,0:T(8,128)(2,1)}, bf16[400,128]{1,0:T(8,128)(2,1)S(1)}, u32[]{:S(2)}) copy-start(bf16[400,128]{1,0:T(8,128)(2,1)S(1)} %reduce_sum.34.refs_1_) | copy-start | bytes 307204
  296.9 18.3 %all-to-all-start.11 = ((bf16[8,256,128]{2,1,0:T(8,128)(2,1)}), bf16[8,256,128]{2,1,0:T(8,128)(2,1)S(1)}, u32[]{:S(2)}, u32[]{:S(2)}) async-start(bf16[8,256,128]{2,1,0:T(8,128)(2,1)} %bitcast.66), calls=%async_computation.11 | async-start | bytes 1048576 | tf_op jit(solution)/shard_map/all_to_all | solution.py:891
  300.6 5.9 %collective-permute-start.17 = (bf16[400,128]{1,0:T(8,128)(2,1)S(1)}, bf16[400,128]{1,0:T(8,128)(2,1)S(1)}, u32[]{:S(2)}, u32[]{:S(2)}) collective-permute-start(bf16[400,128]{1,0:T(8,128)(2,1)S(1)} %reduce_sum.34.refs_1_), channel_id=1, source_target_pairs={{0,3},{1,2},{2,1},{3,0},{4,7},{5,6},{6,5},{7,4},{8,11},{9,10},{10,... | collective-permute-start | bytes 307208 | tf_op jit(solution)/shard_map/ppermute | solution.py:900
  300.9 10.1 %collective-permute-start.16 = (bf16[400,128]{1,0:T(8,128)(2,1)S(1)}, bf16[400,128]{1,0:T(8,128)(2,1)S(1)}, u32[]{:S(2)}, u32[]{:S(2)}) collective-permute-start(bf16[400,128]{1,0:T(8,128)(2,1)S(1)} %reduce_sum.34.refs_1_), channel_id=1, source_target_pairs={{0,2},{1,3},{2,0},{3,1},{4,6},{5,7},{6,4},{7,5},{8,10},{9,11},{10,... | collective-permute-start | bytes 307208 | tf_op jit(solution)/shard_map/ppermute | solution.py:900
  301.9 9.0 %collective-permute-start.15 = (bf16[400,128]{1,0:T(8,128)(2,1)S(1)}, bf16[400,128]{1,0:T(8,128)(2,1)S(1)}, u32[]{:S(2)}, u32[]{:S(2)}) collective-permute-start(bf16[400,128]{1,0:T(8,128)(2,1)S(1)} %reduce_sum.34.refs_1_), channel_id=1, source_target_pairs={{0,1},{1,0},{2,3},{3,2},{4,5},{5,4},{6,7},{7,6},{8,9},{9,8},{10,11... | collective-permute-start | bytes 307208 | tf_op jit(solution)/shard_map/ppermute | solution.py:900
  304.8 10.6 %collective-permute-start.14 = (bf16[864,128]{1,0:T(8,128)(2,1)}, bf16[864,128]{1,0:T(8,128)(2,1)S(1)}, u32[]{:S(2)}, u32[]{:S(2)}) collective-permute-start(bf16[864,128]{1,0:T(8,128)(2,1)} %shard_map.390.refs_1_), channel_id=1, source_target_pairs={{0,3},{1,2},{2,1},{3,0},{4,7},{5,6},{6,5},{7,4},{8,11},{9,10},{10,... | collective-permute-start | bytes 663560 | tf_op jit(solution)/shard_map/ppermute | solution.py:900
  305.3 12.1 %collective-permute-start.13 = (bf16[864,128]{1,0:T(8,128)(2,1)}, bf16[864,128]{1,0:T(8,128)(2,1)S(1)}, u32[]{:S(2)}, u32[]{:S(2)}) collective-permute-start(bf16[864,128]{1,0:T(8,128)(2,1)} %shard_map.390.refs_1_), channel_id=1, source_target_pairs={{0,2},{1,3},{2,0},{3,1},{4,6},{5,7},{6,4},{7,5},{8,10},{9,11},{10,... | collective-permute-start | bytes 663560 | tf_op jit(solution)/shard_map/ppermute | solution.py:900
  306.4 11.0 %collective-permute-start.12 = (bf16[864,128]{1,0:T(8,128)(2,1)}, bf16[864,128]{1,0:T(8,128)(2,1)S(1)}, u32[]{:S(2)}, u32[]{:S(2)}) collective-permute-start(bf16[864,128]{1,0:T(8,128)(2,1)} %shard_map.390.refs_1_), channel_id=1, source_target_pairs={{0,1},{1,0},{2,3},{3,2},{4,5},{5,4},{6,7},{7,6},{8,9},{9,8},{10,11... | collective-permute-start | bytes 663560 | tf_op jit(solution)/shard_map/ppermute | solution.py:900
  315.3 6.0 %copy-start.30 = (bf16[256,128]{1,0:T(8,128)(2,1)}, bf16[256,128]{1,0:T(8,128)(2,1)S(1)}, u32[]{:S(2)}) copy-start(bf16[256,128]{1,0:T(8,128)(2,1)S(1)} %reduce_sum.35.refs_1_) | copy-start | bytes 196612
  315.3 6.3 %copy-start.31 = (f32[8,1024]{1,0:T(8,128)S(1)}, f32[8,1024]{1,0:T(8,128)}, u32[]{:S(2)}) copy-start(f32[8,1024]{1,0:T(8,128)} %get-tuple-element.191) | copy-start | bytes 98308
  319.8 4.3 %collective-permute-start.20 = (bf16[256,128]{1,0:T(8,128)(2,1)S(1)}, bf16[256,128]{1,0:T(8,128)(2,1)S(1)}, u32[]{:S(2)}, u32[]{:S(2)}) collective-permute-start(bf16[256,128]{1,0:T(8,128)(2,1)S(1)} %reduce_sum.35.refs_1_), channel_id=1, source_target_pairs={{0,3},{1,2},{2,1},{3,0},{4,7},{5,6},{6,5},{7,4},{8,11},{9,10},{10,... | collective-permute-start | bytes 196616 | tf_op jit(solution)/shard_map/ppermute | solution.py:900
  320.3 5.3 %collective-permute-start.19 = (bf16[256,128]{1,0:T(8,128)(2,1)S(1)}, bf16[256,128]{1,0:T(8,128)(2,1)S(1)}, u32[]{:S(2)}, u32[]{:S(2)}) collective-permute-start(bf16[256,128]{1,0:T(8,128)(2,1)S(1)} %reduce_sum.35.refs_1_), channel_id=1, source_target_pairs={{0,2},{1,3},{2,0},{3,1},{4,6},{5,7},{6,4},{7,5},{8,10},{9,11},{10,... | collective-permute-start | bytes 196616 | tf_op jit(solution)/shard_map/ppermute | solution.py:900
  321.3 4.2 %collective-permute-start.18 = (bf16[256,128]{1,0:T(8,128)(2,1)S(1)}, bf16[256,128]{1,0:T(8,128)(2,1)S(1)}, u32[]{:S(2)}, u32[]{:S(2)}) collective-permute-start(bf16[256,128]{1,0:T(8,128)(2,1)S(1)} %reduce_sum.35.refs_1_), channel_id=1, source_target_pairs={{0,1},{1,0},{2,3},{3,2},{4,5},{5,4},{6,7},{7,6},{8,9},{9,8},{10,11... | collective-permute-start | bytes 196616 | tf_op jit(solution)/shard_map/ppermute | solution.py:900
  (20 other events, 43.2 us)
Sparse Core Ops, SparseCore 0:
  71.0 47.0 all-gather.7
  221.9 74.9 reduce-scatter.1

commit v4 on v3

--- a/solution.py
+++ b/solution.py
@@ -555,7 +555,7 @@
 
 def output_kernel(count, place_ref, sums_ref, third_ref, gain_ref, bias_ref,
                   x0_ref, x1_ref, x2_ref, x3_ref, c0_ref, c1_ref, c2_ref, c3_ref,
-                  low_ref, high_ref, s0_ref, s1_ref, s2_ref, s3_ref, slope_ref, norm_ref,
+                  s0_ref, s1_ref, s2_ref, s3_ref, slope_ref, norm_ref,
                   out_sums_ref):
     place = place_ref[0]
     mean, inverse = norm_of(sums_ref, 4, count)
@@ -581,7 +581,7 @@
         send_ref[1] = slope.astype(bf16)
         total_bias += column_sum(slope)
         total_gain += column_sum(slope * normed)
-    put_sums(out_sums_ref, total_bias, total_gain, stem_row(low_ref, high_ref))
+    put_sums(out_sums_ref, total_bias, total_gain)
 
 
 def third_back_kernel(count, place_ref, sums_ref, third_ref, slope_ref, norm_ref, gain_ref, weight_ref,
@@ -596,36 +596,31 @@
     grad = grad.astype(bf16)
     grad_ref[...] = grad
     back = dot(grad, weight_ref[...], "NT").astype(bf16)
-    rest, stem = jnp.sum(sums_ref[:, 8:16], 0), []
+    for part in range(part_ref.shape[0]):
+        part_ref[part] = back[:, 128 * part : 128 * part + 128]
+
+
+def second_slope_kernel(place_ref, part_ref, second_ref, norm_ref, gain_ref, bias_ref,
+                        low_ref, high_ref, grad_ref, sums_ref):
+    back = jnp.sum(part_ref[...].astype(f32), 0)
+    normed = (second_ref[...] - norm_ref[0:1]) * norm_ref[1:2]
+    gain, bias = own_lanes(place_ref, gain_ref, bias_ref)
+    grad = back * silu_slope(normed * gain + bias)
+    grad_ref[...] = grad
+    stem = stem_row(low_ref, high_ref)[0:1]
+    put_sums(sums_ref, column_sum(grad), column_sum(grad * normed), stem)
+
+
+def second_back_kernel(count, place_ref, sums_ref, slope_ref, second_ref, norm_ref, gain_ref, weight_ref,
+                       grad_ref, part_ref, vectors_ref, stem_ref, pad_ref):
+    total_bias, total_gain = get_sums(sums_ref, 1)
+    rest, stem = jnp.sum(sums_ref[...], 0)[2:3], []
     for _ in range(2):
         stem.append(rest.astype(bf16).astype(f32))
         rest = rest - stem[-1]
     order = stack_index((16, 128), 0)
-    stem = jnp.where(
-        order == 0, stem[0][0:1], jnp.where(order == 1, stem[1][0:1], rest[0:1])
-    ).astype(bf16)
-    rows = grad.shape[0]
-    for part in range(part_ref.shape[0]):
-        part_ref[part, :rows] = back[:, 128 * part : 128 * part + 128]
-        part_ref[part, rows:] = stem
-
-
-def second_slope_kernel(place_ref, part_ref, second_ref, norm_ref, gain_ref, bias_ref,
-                        grad_ref, stem_ref, sums_ref):
-    rows = second_ref.shape[0]
-    back = jnp.sum(part_ref[:, :rows].astype(f32), 0)
-    stem = jnp.sum(part_ref[:, rows:].astype(f32), 0)
-    stem_ref[...] = jnp.broadcast_to(stem[0:1] + stem[1:2] + stem[2:3], stem_ref.shape)
-    normed = (second_ref[...] - norm_ref[0:1]) * norm_ref[1:2]
-    gain, bias = own_lanes(place_ref, gain_ref, bias_ref)
-    grad = back * silu_slope(normed * gain + bias)
-    grad_ref[...] = grad
-    put_sums(sums_ref, column_sum(grad), column_sum(grad * normed))
-
-
-def second_back_kernel(count, place_ref, sums_ref, slope_ref, second_ref, norm_ref, gain_ref, weight_ref,
-                       grad_ref, part_ref, vectors_ref, pad_ref):
-    total_bias, total_gain = get_sums(sums_ref, 1)
+    stem = jnp.where(order == 0, stem[0], jnp.where(order == 1, stem[1], rest))
+    stem_ref[...] = jnp.where(order < 3, stem, 0.0).astype(bf16)
     vectors_ref[...] = jnp.concatenate([total_bias, total_gain], 0)
     inverse = norm_ref[1:2]
     normed = (second_ref[...] - norm_ref[0:1]) * inverse
@@ -677,23 +672,27 @@
     out_ref[rows + 16 : rows + 32] = (vectors - upper.astype(f32)).astype(bf16)
 
 
-def gate_back_kernel(part_ref, hidden_ref, sigmoid_ref, expand_ref,
+def gate_back_kernel(part_ref, hidden_ref, sigmoid_ref, expand_ref, stem_ref,
                      fine_ref, gate_ref, hidden_grad_ref):
     gated = jnp.sum(part_ref[...].astype(f32), 0)
     sigmoid = sigmoid_ref[...]
     gate = (gated * hidden_ref[...].astype(f32) * sigmoid * (1.0 - sigmoid)).astype(bf16)
     gate_ref[...] = gate
     hidden_grad_ref[...] = gated * (1.0 + sigmoid)
-    fine_ref[...] = dot(gate, expand_ref[...], "NT").astype(bf16)
+    rows = gate.shape[0]
+    fine_ref[:rows] = dot(gate, expand_ref[...], "NT").astype(bf16)
+    fine_ref[rows:] = stem_ref[...]
 
 
 def reduce_back_kernel(place_ref, mask_ref, grad_ref, fine_ref, half_w_ref, quarter_w_ref,
                        reduce_ref, hidden_grad_ref, first_ref, norm_ref, gain_ref, bias_ref,
-                       reduced_ref, slope_ref, coarse_ref, coarsest_ref, sums_ref,
+                       reduced_ref, slope_ref, coarse_ref, coarsest_ref, stem_ref, sums_ref,
                        pad_ref, pad_half_ref, pad_quarter_ref):
     place = place_ref[0]
     own = reduced_ref.shape[0]
-    grad_fine = grad_ref[...]
+    grad_fine = grad_ref[:, :own].reshape(4 * own, grad_ref.shape[2])
+    stem = jnp.sum(grad_ref[:, own:].astype(f32), 0)
+    stem_ref[...] = jnp.broadcast_to(stem[0:1] + stem[1:2] + stem[2:3], stem_ref.shape)
     coarse = dot(pool_matrix(own, 4 * own, 2, 8, 1.0), grad_fine).astype(bf16)
     coarse_ref[...] = coarse
     coarsest = dot(pool_matrix(own // 4, 4 * own, 4, 8, 1.0), grad_fine)
@@ -748,23 +747,25 @@
 
 def small_grads_kernel(place_ref, change_ref, half_ref, quarter_ref, grad_ref, coarse_ref,
                        coarsest_ref, hidden_ref, reduced_ref, merged_ref, gate_ref,
-                       stem_low_ref, stem_high_ref, out_ref,
+                       out_ref,
                        pad_ref, pad_half_ref, pad_quarter_ref, grads_ref, shares_ref):
     place = place_ref[0]
     clips, part = out_ref.shape[0], shares_ref.shape[1] // 4
+    own = hidden_ref.shape[0]
+    grad_fine = grad_ref[:, :own].reshape(4 * own, grad_ref.shape[2])
     scales = (
-        (change_ref, grad_ref, pad_ref, 8, None),
-        (half_ref, coarse_ref, pad_half_ref, 4, None),
-        (quarter_ref, coarsest_ref, pad_quarter_ref, 2, lax.Precision.HIGHEST),
+        (change_ref, grad_fine, pad_ref, 8, None),
+        (half_ref, coarse_ref[...], pad_half_ref, 4, None),
+        (quarter_ref, coarsest_ref[...], pad_quarter_ref, 2, lax.Precision.HIGHEST),
     )
     at = 0
-    for map_ref, cot_ref, padded_ref, width, precision in scales:
+    for map_ref, cotangent, padded_ref, width, precision in scales:
         rows, channels = map_ref.shape
         band = shift_columns(padded_ref, map_ref[...], width)
         for ky, kx in taps:
             tap = 3 * ky + kx
             grads_ref[tap * channels : (tap + 1) * channels, :] = dot(
-                padded_ref[kx, ky * band : ky * band + rows], cot_ref[...], "TN", precision
+                padded_ref[kx, ky * band : ky * band + rows], cotangent, "TN", precision
             ).astype(bf16)
         share = 9 * channels // clips
         for clip in range(clips):
@@ -776,14 +777,22 @@
     blocks = [value] + [
         expand[:, first : first + 128] for first in range(0, expand.shape[1], 128)
     ]
-    blocks += [
-        (stem_low_ref[k] + stem_high_ref[k]).astype(bf16) for k in range(stem_low_ref.shape[0])
-    ]
     for block in blocks:
         share = block.shape[0] // clips
         for clip in range(clips):
             out_ref[clip, at : at + share] = block[share * clip : share * clip + share]
         at += padded(share)
+
+
+def join_kernel(grad_ref, low_ref, high_ref, out_ref):
+    clips, rows = out_ref.shape[0], grad_ref.shape[0] // out_ref.shape[0]
+    stem = low_ref[...] + high_ref[...]
+    share = stem.shape[1] // clips
+    for clip in range(clips):
+        out_ref[clip, :rows] = grad_ref[rows * clip : rows * clip + rows]
+        pieces = [stem[k, share * clip : share * clip + share] for k in range(stem.shape[0])]
+        value = jnp.concatenate(pieces, 0).astype(bf16)
+        out_ref[clip, rows : rows + value.shape[0]] = value
 
 
 def input_grad_kernel(place_ref, grad_ref, weight_ref, r0_ref, r1_ref, r2_ref, r3_ref,
@@ -833,20 +842,27 @@
 
 
 def one_share_kernel(place_ref, *refs):
-    for source, piece in enumerate(by_source(place_ref[0], refs[:4])):
-        refs[4][:, 128 * source : 128 * source + 128] = piece
+    pieces = by_source(place_ref[0], refs[:4])
+    one_ref, stem_ref = refs[4:]
+    at, share = one_ref.shape[0], stem_ref.shape[0]
+    for source, piece in enumerate(pieces):
+        one_ref[:, 128 * source : 128 * source + 128] = piece[:at]
+    total = pieces[0] + pieces[1] + pieces[2] + pieces[3]
+    for block in range(stem_ref.shape[1] // 128):
+        first = at + share * block
+        stem_ref[:, 128 * block : 128 * block + 128] = total[first : first + share]
 
 
 def rest_shares_kernel(tap_rows, place_ref, *refs):
     pieces = by_source(place_ref[0], refs[:4])
-    fine_ref, half_w_ref, quarter_w_ref, reduce_ref, expand_ref, stem_ref = refs[4:]
+    fine_ref, half_w_ref, quarter_w_ref, reduce_ref, expand_ref = refs[4:]
     start = 0
     for out_ref in (fine_ref, half_w_ref, quarter_w_ref):
         rows = [piece[start : start + tap_rows] for piece in pieces]
         out_ref[...] = jnp.concatenate(rows, 0)[: out_ref.shape[0]]
         start += tap_rows
     total = pieces[0] + pieces[1] + pieces[2] + pieces[3]
-    for out_ref in (reduce_ref, expand_ref, stem_ref):
+    for out_ref in (reduce_ref, expand_ref):
         rows = out_ref.shape[0]
         for first in range(0, out_ref.shape[1], 128):
             out_ref[:, first : first + 128] = total[start : start + rows]
@@ -1074,57 +1090,54 @@
         (Fresh(hidden_two), packed),
         (((pixels, in_r), f32), ((mid, in_r), bf16), clip_sums),
     )
-    outer_high, slope_high = stem_slope(stem_pre, stem_cot, 4, stem_vectors, third)
     gain_three, bias_three = gain_three.reshape(1, -1), bias_three.reshape(1, -1)
     *send, slope_three, norm_three, sums = call(
         functools.partial(output_kernel, count),
         (spot,),
         (
             Fresh(exchange(sums, "clip")), third, gain_three, bias_three, *x_pieces, *cot_pieces,
-            slope_low, slope_high,
         ),
         (
             *[((2, own, in_r), bf16)] * nr,
             ((pixels, in_r), f32),
             ((2, in_r), f32),
-            ((nc, 16, 128), f32),
+            clip_sums,
         ),
     )
 
-    returned = [send[0]] + [swap(send[s], "row", s) for s in range(1, nr)]
+    outer_high, slope_high = stem_slope(stem_pre, stem_cot, SEG // 2, stem_vectors, slope_three)
     grad_third, parts, vectors_three = call(
         functools.partial(third_back_kernel, count),
         (spot,),
         (
             Fresh(exchange(sums, "clip")), third, slope_three, norm_three, gain_three, three_r,
         ),
-        (((pixels, in_r), bf16), ((nr, pixels + 16, mid_r), bf16), ((8, 128), f32)),
-        waits=returned[1:],
-    )
-    slope_two, stem_totals, sums = call(
+        (((pixels, in_r), bf16), ((nr, pixels, mid_r), bf16), ((8, 128), f32)),
+        waits=(slope_high,),
+    )
+    slope_two, sums = call(
         second_slope_kernel,
         (spot,),
-        (Fresh(exchange(parts, "row")), second, norm_two, gain_two, bias_two),
-        (((pixels, mid_r), f32), ((8, 128), f32), clip_sums),
-    )
-    stem_bias_grad, stem_gain_grad = stem_totals[0].reshape(2, STEM)
-    stem_vectors = lanes(
-        stem_mean,
-        stem_inverse,
-        stem_gain * stem_inverse,
-        stem_bias_grad / stem_count,
-        stem_gain_grad / stem_count,
-    )
-    stem_low = stem_grad(planes, stem_pre, outer_low, 0, stem_vectors)
-    grad_second, parts, vectors_two = call(
+        (
+            Fresh(exchange(parts, "row")), second, norm_two, gain_two, bias_two,
+            slope_low, slope_high,
+        ),
+        (((pixels, mid_r), f32), clip_sums),
+    )
+    slope_two, *send = together(slope_two, *send)
+    returned = [send[0]] + [swap(send[s], "row", s) for s in range(1, nr)]
+    grad_second, parts, vectors_two, stem_part = call(
         functools.partial(second_back_kernel, count),
         (spot,),
         (
             Fresh(exchange(sums, "clip")), slope_two, second, norm_two, gain_two, two_r,
         ),
-        (((pixels, mid_r), bf16), ((nr, own, mid), bf16), ((2, mid_r), f32)),
+        (
+            ((pixels, mid_r), bf16), ((nr, own, mid), bf16), ((2, mid_r), f32),
+            ((16, 128), bf16),
+        ),
         [((3, pixels + 2 * images * cols, mid_r), bf16)],
-        (stem_low,),
+        returned[1:],
     )
     (wide,) = call(
         wide_grads_kernel,
@@ -1137,18 +1150,15 @@
         ],
     )
     wide_total = lax.psum_scatter(wide, "clip", scatter_dimension=0, tiled=False)
-    stem_high = stem_grad(
-        planes, stem_pre, outer_high, len(planes) // 2, stem_vectors, grad_second
-    )
     grad_fine, grad_gate, grad_hidden = call(
         gate_back_kernel,
         (),
-        (Fresh(exchange(parts, "row")), hidden_one, sigmoid, full_expand),
-        (((own, red), bf16), ((own, mid), bf16), ((own, mid), f32)),
-        waits=(wide, stem_high),
-    )
-    grad_fine = lax.all_gather(grad_fine, "row").reshape(pixels, red)
-    grad_reduced, slope_one, grad_coarse, grad_coarsest, sums = call(
+        (Fresh(exchange(parts, "row")), hidden_one, sigmoid, full_expand, stem_part),
+        (((own + 16, red), bf16), ((own, mid), bf16), ((own, mid), f32)),
+        waits=(wide,),
+    )
+    grad_fine = lax.all_gather(grad_fine, "row")
+    grad_reduced, slope_one, grad_coarse, grad_coarsest, stem_totals, sums = call(
         reduce_back_kernel,
         (spot, boundary_mask),
         (
@@ -1160,19 +1170,29 @@
             ((own, mid), f32),
             ((pixels // 4, red), bf16),
             ((pixels // 16, red), f32),
+            ((8, 128), f32),
             both_sums,
         ),
         pads,
     )
+    stem_bias_grad, stem_gain_grad = stem_totals[0].reshape(2, STEM)
+    stem_vectors = lanes(
+        stem_mean,
+        stem_inverse,
+        stem_gain * stem_inverse,
+        stem_bias_grad / stem_count,
+        stem_gain_grad / stem_count,
+    )
+    stem_low = stem_grad(planes, stem_pre, outer_low, 0, stem_vectors, slope_one)
     tap_rows = padded(padded(k_fine.shape[0], 4) // 4)
     rest_rows = 3 * tap_rows + padded(w_reduce.shape[0])
-    rest_rows += mid // 128 * padded(w_expand.shape[0]) + 8 * padded(stem_weight.shape[0])
+    rest_rows += mid // 128 * padded(w_expand.shape[0])
     (rest,) = call(
         small_grads_kernel,
         (spot,),
         (
             change, half_map, quarter, grad_fine, grad_coarse, grad_coarsest,
-            hidden_one, grad_reduced, merged, grad_gate, stem_low, stem_high,
+            hidden_one, grad_reduced, merged, grad_gate,
         ),
         (((nc, rest_rows, 128), bf16),),
         [*pads, ((9 * red, red), bf16), ((nc, 4 * tap_rows, 128), bf16)],
@@ -1183,7 +1203,7 @@
         (),
         (Fresh(sums), slope_one, first, norm_one, gain_one),
         (((own, mid), bf16), ((2, mid), f32)),
-        waits=(rest,),
+        waits=(rest, stem_low),
     )
     rest, grad_first = together(rest, grad_first)
     rest_total = jnp.sum(exchange(rest, "clip"), 0, dtype=f32).astype(bf16)
@@ -1193,10 +1213,16 @@
         (Fresh(lax.all_gather(grad_first, "row")), *x_pieces),
         (((c_in, mid_r), bf16),),
     )
-    one_rows = c_in // nc
+    stem_high = stem_grad(planes, stem_pre, outer_high, len(planes) // 2, stem_vectors, one_grad)
+    one_rows, stem_rows = c_in // nc, padded(8 * stem_weight.shape[0])
+    (one_grad,) = call(
+        join_kernel,
+        (),
+        (one_grad, stem_low, stem_high),
+        (((nc, one_rows + stem_rows, 128), bf16),),
+    )
     one_grad, rest_total = together(one_grad, rest_total)
-    one_total = exchange(one_grad.reshape(nc, one_rows, 128), "clip")
-    one_total = jnp.sum(one_total, 0, dtype=f32).astype(bf16)
+    one_total = jnp.sum(exchange(one_grad, "clip"), 0, dtype=f32).astype(bf16)
     input_grad, block_out = call(
         input_grad_kernel,
         (spot,),
@@ -1213,32 +1239,35 @@
     def from_row(piece):
         return [piece] + [Fresh(swap(piece, "row", s)) for s in range(1, nr)]
 
-    two_share, three_share, gain_two, bias_two, gain_three, bias_three = call(
-        wide_shares_kernel,
-        (spot,),
-        from_row(last),
-        (
-            ((two_rows, mid), f32), ((three_rows, c_in), f32),
-            ((1, mid), f32), ((1, mid), f32), ((1, c_in), f32), ((1, c_in), f32),
-        ),
-    )
+    wide_pieces = [last] + [swap(last, "row", s) for s in range(1, nr)]
     rest_shares = call(
         functools.partial(rest_shares_kernel, tap_rows),
         (spot,),
         from_row(rest_total),
         (
             *[(entry.shape, f32) for entry in (k_fine, k_half, k_quarter, w_reduce, w_expand)],
-            ((stem_weight.shape[0], 1024), f32),
         ),
     )
-    one_total, input_grad, two_share, *rest_shares = together(
-        one_total, input_grad, two_share, *rest_shares
-    )
-    (one_share,) = call(one_share_kernel, (spot,), from_row(one_total), (((one_rows, mid), f32),))
+    one_total, input_grad, *wide_pieces = together(one_total, input_grad, *wide_pieces)
+    two_share, three_share, gain_two, bias_two, gain_three, bias_three = call(
+        wide_shares_kernel,
+        (spot,),
+        [wide_pieces[0], *[Fresh(piece) for piece in wide_pieces[1:]]],
+        (
+            ((two_rows, mid), f32), ((three_rows, c_in), f32),
+            ((1, mid), f32), ((1, mid), f32), ((1, c_in), f32), ((1, c_in), f32),
+        ),
+    )
+    one_share, stem_share = call(
+        one_share_kernel,
+        (spot,),
+        from_row(one_total),
+        (((one_rows, mid), f32), ((stem_weight.shape[0], 1024), f32)),
+    )
     return (
         block_out,
         input_grad,
-        filters_outside(rest_shares[5][:, :784]),
+        filters_outside(stem_share[:, :784]),
         stem_gain_grad,
         stem_bias_grad,
         one_share,

time: 336 us -> 332 us (0.988)
  waiting for transfers between devices: 59.1 us -> 41.2 us
  blocking collectives: 58.3 us -> 69.9 us
    all_to_all x10 -> x9, waiting for transfers between devices: 44.4 us -> 23.5 us  [exchange(): return lax.all_to_all(blocks, axis, 0, 0)]
    all_to_all x2 -> x3, blocking collectives: 25.4 us -> 36.2 us  [exchange(): return lax.all_to_all(blocks, axis, 0, 0)]
    all_to_all x10 -> x9, starting transfers between devices: 46.8 us -> 43.7 us  [exchange(): return lax.all_to_all(blocks, axis, 0, 0)]
    unnamed x71 -> x77, local copies, waits for them, and re-layouts: 7.52 us -> 9.58 us
    pallas_call x22 -> x23, Pallas kernels: 64.3 us -> 66.3 us  [call(): pl.pallas_call(body, grid=(1,), in_specs=[pl.BlockSpec(memory_space=pltpu...]
  transfers between devices with their start and end apart: 33 -> 32, of which waited for: 13 -> 10; matrix products, arithmetic and copies ran while one was open for 3% -> 3% of each run, Pallas kernels for 28% -> 30%
where the time goes in v4:
time: 332 us; the launch traced here: 330 us
  Pallas kernels  122 us (37%)
  blocking collectives  69.9 us (21%)
  starting transfers between devices  60.8 us (18%)
  waiting for transfers between devices  41.2 us (12%)
  local copies, waits for them, and re-layouts  16.5 us (5%)
  between operations  14.5 us (4%)
  other arithmetic  5.27 us (2%)
    pallas_call x23, Pallas kernels, call(): pl.pallas_call(body, grid=(1,), in_specs=[pl.BlockSpec(memory_space=pltpu...  66.3 us
    pallas_call x6, Pallas kernels, stem_call(): pl.pallas_call(body, grid=(steps,), in_specs=in_specs + [pl.BlockSpec(mem...  55.3 us
    all_to_all x9, starting transfers between devices, exchange(): return lax.all_to_all(blocks, axis, 0, 0)  43.7 us
    all_to_all x3, blocking collectives, exchange(): return lax.all_to_all(blocks, axis, 0, 0)  36.2 us
    all_to_all x9, waiting for transfers between devices, exchange(): return lax.all_to_all(blocks, axis, 0, 0)  23.5 us
    ppermute x19, waiting for transfers between devices, swap(): lax.ppermute(piece, axis, [(i, i ^ step) for i in range(lax.axis_size(axi...  14.2 us
    ppermute x19, starting transfers between devices, swap(): lax.ppermute(piece, axis, [(i, i ^ step) for i in range(lax.axis_size(axi...  12 us
    unnamed x77, local copies, waits for them, and re-layouts  9.58 us
  transfers between devices with their start and end apart: 32, of which 10 were waited for; matrix products, arithmetic and copies ran while one was open for 3% of the time, Pallas kernels for 30%

profile of v4, /device:TPU:0, one launch (start us, length us, event | category | flops | bytes accessed | tf_op | source)
XLA Modules:
  0.0 329.9 jit_solution(17930656708272342978)
XLA Ops:
  8.3 2.9 shard_map.366
  11.9 7.3 %all-to-all-start = ((bf16[8,8,784]{2,1,0:T(8,128)(2,1)}), bf16[8,8,784]{2,1,0:T(8,128)(2,1)S(1)}, u32[]{:S(2)}, u32[]{:S(2)}) async-start(bf16[8,8,784]{2,1,0:T(8,128)(2,1)} %broadcast_in_dim.6), calls=%async_computation | async-start | bytes 229376 | tf_op jit(solution)/shard_map/all_to_all | solution.py:907
  20.6 3.7 %collective-permute-start = (bf16[12,3,16,256]{3,2,1,0:T(8,128)(2,1)S(1)}, bf16[12,3,16,256]{3,2,1,0:T(8,128)(2,1)}, u32[]{:S(2)}, u32[]{:S(2)}) collective-permute-start(bf16[12,3,16,256]{3,2,1,0:T(8,128)(2,1)S(1)} %get-tuple-element.218), channel_id=1, source_target_pairs={{0,1},{1,2},{2,3},{4,5},{5,6},{6,7},{8,9},{9,10},{10,11},{12,13},{... | collective-permute-start | bytes 884744 | tf_op jit(solution)/shard_map/ppermute | solution.py:1001
  24.4 2.0 all-to-all-done
  26.4 4.0 %all-to-all-start.1 = ((bf16[8,832,128]{2,1,0:T(8,128)(2,1)}), bf16[8,832,128]{2,1,0:T(8,128)(2,1)S(1)}, u32[]{:S(2)}, u32[]{:S(2)}) async-start(bf16[8,832,128]{2,1,0:T(8,128)(2,1)} %get-tuple-element.120), calls=%async_computation.1 | async-start | bytes 3407872 | tf_op jit(solution)/shard_map/all_to_all | solution.py:907
  35.9 13.0 %shard_map.367.refs_0_ = bf16[4,80,112,256]{3,2,1,0:T(8,128)(2,1)} custom-call(s32[8]{0:T(128)S(1)} %bitcast.59, bf16[12,3,64,256]{3,2,1,0:T(8,128)(2,1)} %bitcast.75, bf16[12,3,16,256]{3,2,1,0:T(8,128)(2,1)} %collective-permute-done.refs_2_, bf16[12,3,16,256]{3,2,1,0:T(8,128)(2,1)} %collective-permute-done.1.refs_3_), custom_call_target="tpu_custom_call" | custom-call | flops 16000000000 | bytes 20000000 | tf_op jit(solution)/shard_map/pallas_call | solution.py:197
  48.9 2.3 collective-permute-done.5.refs_5_.refs_11_
  51.2 13.3 %shard_map.368 = (f32[8,32,64,128]{3,2,1,0:T(8,128)}, f32[2,64,128]{2,1,0:T(8,128)S(1)}) custom-call(bf16[4,80,112,256]{3,2,1,0:T(8,128)(2,1)} %shard_map.367.refs_0_, bf16[256,1456]{1,0:T(8,128)(2,1)} %fusion.7.refs_1_, bf16[128,2048]{1,0:T(8,128)(2,1)S(1)} %collective-permute-done.2.refs_2_.refs_6_.refs_3_, ...), custom_call_target="tpu_custom_call" | custom-call | flops 16000000000 | bytes 28000000 | tf_op jit(solution)/shard_map/pallas_call | solution.py:197
  68.0 2.9 all-to-all-done.1.refs_2_
  71.5 3.7 %collective-permute-done.7.refs_3_ = bf16[8,832,128]{2,1,0:T(8,128)(2,1)S(1)} collective-permute-done((bf16[8,832,128]{2,1,0:T(8,128)(2,1)S(1)}, bf16[8,832,128]{2,1,0:T(8,128)(2,1)S(1)}, u32[]{:S(2)}, u32[]{:S(2)}) %collective-permute-start.7) | collective-permute-done | bytes 1703968 | tf_op jit(solution)/shard_map/ppermute | solution.py:916
  75.2 2.9 shard_map.369
  78.7 3.3 %all-to-all-start.2 = ((f32[32,16,128]{2,1,0:T(8,128)}), f32[32,16,128]{2,1,0:T(8,128)}, u32[]{:S(2)}, u32[]{:S(2)}) async-start(f32[32,16,128]{2,1,0:T(8,128)} %get-tuple-element.128), calls=%async_computation.2 | async-start | bytes 524288 | tf_op jit(solution)/shard_map/all_to_all | solution.py:907
  83.8 11.9 %all-to-all-done.2.refs_1_ = f32[32,16,128]{2,1,0:T(8,128)} async-done(((f32[32,16,128]{2,1,0:T(8,128)}), f32[32,16,128]{2,1,0:T(8,128)}, u32[]{:S(2)}, u32[]{:S(2)}) %all-to-all-start.2) | async-done | bytes 262176 | tf_op jit(solution)/shard_map/all_to_all | solution.py:907
  97.7 5.6 %all-gather.refs_1_ = bf16[512,128]{1,0:T(8,128)(2,1)S(1)} all-gather(bf16[128,128]{1,0:T(8,128)(2,1)} %get-tuple-element.132), channel_id=2, replica_groups=mesh['clip'=8,'row'=4] {'row'}, dimensions={0}, use_global_device_ids=true | all-gather | bytes 163840 | tf_op jit(solution)/shard_map/all_gather | solution.py:1050
  103.3 3.9 %shard_map.371 = (bf16[128,512]{1,0:T(8,128)(2,1)}, f32[128,512]{1,0:T(8,128)}, bf16[128,128]{1,0:T(8,128)(2,1)}, bf16[128,128]{1,0:T(8,128)(2,1)}, f32[32,128]{1,0:T(8,128)}) custom-call(s32[1]{0:T(128)} %bitcast.refs_0_, bf16[512,128]{1,0:T(8,128)(2,1)S(1)} %all-gather.refs_1_, bf16[128,512]{1,0:T(8,128)(2,1)} %get-tuple-element.133.refs_2_.refs_1_.refs_7_, ...), custom_call_target="tpu_custom_call" | custom-call | flops 1000000000 | bytes 2000000 | tf_op jit(solution)/shard_map/pallas_call | solution.py:884
  107.2 7.5 %all-gather.1.refs_0_ = bf16[512,512]{1,0:T(8,128)(2,1)S(1)} all-gather(bf16[128,512]{1,0:T(8,128)(2,1)} %get-tuple-element.137), channel_id=3, replica_groups=mesh['clip'=8,'row'=4] {'row'}, dimensions={0}, use_global_device_ids=true | all-gather | bytes 655360 | tf_op jit(solution)/shard_map/all_gather | solution.py:1069
  114.7 3.4 %all-gather.8.cloned.1.call-done = bf16[6656,128]{1,0:T(8,128)(2,1)} async-done(((bf16[832,128]{1,0:T(8,128)(2,1)}), bf16[6656,128]{1,0:T(8,128)(2,1)}) %all-gather.8.cloned.1.call-update) | async-done | bytes 1703952 | tf_op jit(solution)/shard_map/all_gather | solution.py:1015
  118.1 3.7 %shard_map.372 = (f32[512,128]{1,0:T(8,128)}, bf16[4608,128]{1,0:T(8,128)(2,1)}, f32[8,8,128]{2,1,0:T(8,128)}) custom-call(bf16[512,512]{1,0:T(8,128)(2,1)S(1)} %all-gather.1.refs_0_, bf16[8,832,128]{2,1,0:T(8,128)(2,1)} %bitcast.94), custom_call_target="tpu_custom_call" | custom-call | flops 1000000000 | bytes 2000000 | tf_op jit(solution)/shard_map/pallas_call | solution.py:884
  121.9 3.6 %all-to-all-start.3 = ((f32[8,8,128]{2,1,0:T(8,128)}), f32[8,8,128]{2,1,0:T(8,128)S(1)}, u32[]{:S(2)}, u32[]{:S(2)}) async-start(f32[8,8,128]{2,1,0:T(8,128)} %get-tuple-element.139), calls=%async_computation.3 | async-start | bytes 65536 | tf_op jit(solution)/shard_map/all_to_all | solution.py:907
  128.2 6.1 %shard_map.373 = (bf16[4,32,64,128]{3,2,1,0:T(8,128)(2,1)}, f32[2,64,128]{2,1,0:T(8,128)S(1)}) custom-call(f32[8,32,64,128]{3,2,1,0:T(8,128)} %get-tuple-element.141.refs_0_.refs_1_, bf16[8,64,32,128]{3,2,1,0:T(8,128)(2,1)} %refs_1_.4, f32[4,64,128]{2,1,0:T(8,128)} %broadcast_in_dim.7.refs_2_, f32[512,128]{1,0:T(8,128)S(1)} %copy-done.22), custom_call_target="tpu_custom_call" | custom-call | flops 4000000000 | bytes 8000000 | tf_op jit(solution)/shard_map/pallas_call | solution.py:197
  136.1 7.3 %all-gather.3 = bf16[2048,128]{1,0:T(8,128)(2,1)S(1)} all-gather(bf16[512,128]{1,0:T(8,128)(2,1)} %get-tuple-element.143), channel_id=5, replica_groups=mesh['clip'=8,'row'=4] {'row'}, dimensions={0}, use_global_device_ids=true | all-gather | bytes 655360 | tf_op jit(solution)/shard_map/all_gather | solution.py:1086
  143.4 3.4 %shard_map.375 = (f32[512,512]{1,0:T(8,128)}, bf16[512,512]{1,0:T(8,128)(2,1)}, f32[8,8,128]{2,1,0:T(8,128)}) custom-call(bf16[4,512,128]{2,1,0:T(8,128)(2,1)S(1)} %bitcast.53, bf16[8,832,128]{2,1,0:T(8,128)(2,1)} %bitcast.95), custom_call_target="tpu_custom_call" | custom-call | flops 1000000000 | bytes 2000000 | tf_op jit(solution)/shard_map/pallas_call | solution.py:884
  146.8 6.2 %all-to-all-start.4 = ((f32[8,8,128]{2,1,0:T(8,128)}), f32[8,8,128]{2,1,0:T(8,128)S(1)}, u32[]{:S(2)}, u32[]{:S(2)}) async-start(f32[8,8,128]{2,1,0:T(8,128)} %get-tuple-element.144), calls=%async_computation.4 | async-start | bytes 65536 | tf_op jit(solution)/shard_map/all_to_all | solution.py:907
  153.0 6.7 %all-to-all-done.4.refs_1_ = f32[8,8,128]{2,1,0:T(8,128)S(1)} async-done(((f32[8,8,128]{2,1,0:T(8,128)}), f32[8,8,128]{2,1,0:T(8,128)S(1)}, u32[]{:S(2)}, u32[]{:S(2)}) %all-to-all-start.4) | async-done | bytes 32800 | tf_op jit(solution)/shard_map/all_to_all | solution.py:907
  159.7 4.0 %shard_map.376 = (bf16[2,128,512]{2,1,0:T(8,128)(2,1)}, bf16[2,128,512]{2,1,0:T(8,128)(2,1)}, bf16[2,128,512]{2,1,0:T(8,128)(2,1)}, bf16[2,128,512]{2,1,0:T(8,12...) custom-call(s32[1]{0:T(128)} %bitcast.refs_0_, f32[8,8,128]{2,1,0:T(8,128)S(1)} %all-to-all-done.4.refs_1_, ...), custom_call_target="tpu_custom_call" | custom-call | flops 1000000000 | bytes 2000000 | tf_op jit(solution)/shard_map/pallas_call | solution.py:884
  163.7 3.3 %all-to-all-start.5 = ((f32[8,8,128]{2,1,0:T(8,128)}), f32[8,8,128]{2,1,0:T(8,128)S(1)}, u32[]{:S(2)}, u32[]{:S(2)}) async-start(f32[8,8,128]{2,1,0:T(8,128)} %get-tuple-element.146), calls=%async_computation.5 | async-start | bytes 65536 | tf_op jit(solution)/shard_map/all_to_all | solution.py:907
  168.3 6.1 %shard_map.377 = (bf16[4,32,64,128]{3,2,1,0:T(8,128)(2,1)}, f32[2,64,128]{2,1,0:T(8,128)S(1)}) custom-call(f32[8,32,64,128]{3,2,1,0:T(8,128)} %get-tuple-element.141.refs_0_.refs_1_, bf16[8,64,32,128]{3,2,1,0:T(8,128)(2,1)} %refs_1_.4, f32[4,64,128]{2,1,0:T(8,128)} %broadcast_in_dim.7.refs_2_, f32[512,512]{1,0:T(8,128)S(1)} %copy-done.15), custom_call_target="tpu_custom_call" | custom-call | flops 4000000000 | bytes 8000000 | tf_op jit(solution)/shard_map/pallas_call | solution.py:197
  174.5 3.1 shard_map.378
  177.6 12.3 %all_to_all.60.refs_1_ = bf16[4,512,128]{2,1,0:T(8,128)(2,1)S(1)} all-to-all(bf16[4,512,128]{2,1,0:T(8,128)(2,1)} %get-tuple-element.151), channel_id=1, replica_groups=mesh['clip'=8,'row'=4] {'row'}, dimensions={0} | all-to-all | bytes 1048576 | tf_op jit(solution)/shard_map/all_to_all | solution.py:907
  189.9 2.0 shard_map.379
  193.8 12.6 %all_to_all.61.refs_1_ = f32[8,8,128]{2,1,0:T(8,128)S(1)} all-to-all(f32[8,8,128]{2,1,0:T(8,128)} %get-tuple-element.153), channel_id=1, replica_groups=mesh['clip'=8,'row'=4] {'clip'}, dimensions={0} | all-to-all | bytes 65536 | tf_op jit(solution)/shard_map/all_to_all | solution.py:907
  206.4 3.9 %shard_map.380 = (bf16[512,128]{1,0:T(8,128)(2,1)}, bf16[4,128,512]{2,1,0:T(8,128)(2,1)}, f32[2,128]{1,0:T(2,128)}, bf16[16,128]{1,0:T(8,128)(2,1)}) custom-call(s32[1]{0:T(128)} %bitcast.refs_0_, f32[8,8,128]{2,1,0:T(8,128)S(1)} %all_to_all.61.refs_1_, f32[512,128]{1,0:T(8,128)} %get-tuple-element.159.refs_2_, ...), custom_call_target="tpu_custom_call" | custom-call | flops 1000000000 | bytes 2000000 | tf_op jit(solution)/shard_map/pallas_call | solution.py:884
  210.3 4.7 %shard_map.381.refs_5_ = bf16[8,832,128]{2,1,0:T(8,128)(2,1)} custom-call(bf16[512,512]{1,0:T(8,128)(2,1)} %copy-done.2, bf16[512,128]{1,0:T(8,128)(2,1)} %get-tuple-element.167.refs_1_, bf16[4,512,128]{2,1,0:T(8,128)(2,1)} %bitcast.54, bf16[512,512]{1,0:T(8,128)(2,1)} %get-tuple-element.168.refs_3_), custom_call_target="tpu_custom_call" | custom-call | flops 1000000000 | bytes 2000000 | tf_op jit(solution)/shard_map/pallas_call | solution.py:884
  215.1 11.4 %all_to_all.62.refs_0_ = bf16[4,128,512]{2,1,0:T(8,128)(2,1)S(1)} all-to-all(bf16[4,128,512]{2,1,0:T(8,128)(2,1)S(1)} %copy-done.28), channel_id=1, replica_groups=mesh['clip'=8,'row'=4] {'row'}, dimensions={0} | all-to-all | bytes 1048576 | tf_op jit(solution)/shard_map/all_to_all | solution.py:907
  228.4 5.7 %all-gather.4 = bf16[576,128]{1,0:T(8,128)(2,1)S(1)} all-gather(bf16[144,128]{1,0:T(8,128)(2,1)} %get-tuple-element.169), channel_id=6, replica_groups=mesh['clip'=8,'row'=4] {'row'}, dimensions={0}, use_global_device_ids=true | all-gather | bytes 184320 | tf_op jit(solution)/shard_map/all_gather | solution.py:1160
  234.1 4.7 %shard_map.383 = (bf16[128,128]{1,0:T(8,128)(2,1)}, f32[128,512]{1,0:T(8,128)}, bf16[128,128]{1,0:T(8,128)(2,1)}, f32[32,128]{1,0:T(8,128)}, f32[8,128]{1,0:T(8,128)}, /*index=5*/f32[32,16,128]{2,1,0:T(8,128)}) custom-call(s32[1]{0:T(128)} %bitcast.refs_0_, s32[1,8]{1,0:T(1,128)S(1)} %copy-done.21, bf16[4,144,128]{2,1,0:T(8,128)(2,1)S(1)} %bitcast.56, ...), custom_call_target="tpu_custom_call" | custom-call | flops 1000000000 | bytes 2000000 | tf_op jit(solution)/shard_map/pallas_call | solution.py:884
  238.8 4.2 %all-to-all-start.9 = ((f32[32,16,128]{2,1,0:T(8,128)}), f32[32,16,128]{2,1,0:T(8,128)S(1)}, u32[]{:S(2)}, u32[]{:S(2)}) async-start(f32[32,16,128]{2,1,0:T(8,128)} %get-tuple-element.177), calls=%async_computation.9 | async-start | bytes 524288 | tf_op jit(solution)/shard_map/all_to_all | solution.py:907
  246.1 8.5 %shard_map.385.refs_6_.refs_1_ = f32[8,64,128]{2,1,0:T(8,128)S(1)} custom-call(bf16[4,80,112,256]{3,2,1,0:T(8,128)(2,1)} %shard_map.367.refs_0_, f32[8,32,64,128]{3,2,1,0:T(8,128)} %get-tuple-element.141.refs_0_.refs_1_, bf16[4,32,64,128]{3,2,1,0:T(8,128)(2,1)} %get-tuple-element.179.refs_2_, f32[5,64,128]{2,1,0:T(8,128)} %broadcast_in_dim.8.refs_3_, ...), custom_call_target="tpu_custom_call" | custom-call | flops 1000000 | bytes 16000000 | tf_op jit(solution)/shard_map/pallas_call | solution.py:197
  254.6 3.5 %shard_map.384.refs_5_ = bf16[8,272,128]{2,1,0:T(8,128)(2,1)} custom-call(s32[1]{0:T(128)} %bitcast.refs_0_, bf16[512,128]{1,0:T(8,128)(2,1)} %copy-done.13, bf16[128,128]{1,0:T(8,128)(2,1)} %get-tuple-element.135.refs_2_, f32[32,128]{1,0:T(8,128)} %get-tuple-element.136.refs_3_, bf16[4,144,128]{2,1,0:T(8,128)(2,1)} %bitcast.57, ...), custom_call_target="tpu_custom_call" | custom-call | flops 1000000000 | bytes 2000000 | tf_op jit(solution)/shard_map/pallas_call | solution.py:884
  260.0 5.8 %all-to-all-start.10 = ((bf16[8,272,128]{2,1,0:T(8,128)(2,1)}), bf16[8,272,128]{2,1,0:T(8,128)(2,1)S(1)}, u32[]{:S(2)}, u32[]{:S(2)}) async-start(bf16[8,272,128]{2,1,0:T(8,128)(2,1)} %shard_map.384.refs_5_), calls=%async_computation.10 | async-start | bytes 1114112 | tf_op jit(solution)/shard_map/all_to_all | solution.py:907
  265.8 7.6 %all-gather.5 = bf16[512,512]{1,0:T(8,128)(2,1)S(1)} all-gather(bf16[128,512]{1,0:T(8,128)(2,1)} %get-tuple-element.182.refs_1_), channel_id=7, replica_groups=mesh['clip'=8,'row'=4] {'row'}, dimensions={0}, use_global_device_ids=true | all-gather | bytes 655360 | tf_op jit(solution)/shard_map/all_gather | solution.py:1213
  273.4 3.1 shard_map.388.refs_4_.refs_0_
  277.5 8.3 %shard_map.389.refs_2_ = f32[8,64,128]{2,1,0:T(8,128)S(1)} custom-call(bf16[4,80,112,256]{3,2,1,0:T(8,128)(2,1)} %shard_map.367.refs_0_, f32[8,32,64,128]{3,2,1,0:T(8,128)} %get-tuple-element.141.refs_0_.refs_1_, bf16[4,32,64,128]{3,2,1,0:T(8,128)(2,1)} %get-tuple-element.186.refs_2_, f32[5,64,128]{2,1,0:T(8,128)} %broadcast_in_dim.8.refs_3_, ...), custom_call_target="tpu_custom_call" | custom-call | flops 1000000 | bytes 16000000 | tf_op jit(solution)/shard_map/pallas_call | solution.py:197
  286.5 2.1 shard_map.390
  288.7 6.0 %all-to-all-start.11 = ((bf16[8,320,128]{2,1,0:T(8,128)(2,1)}), bf16[8,320,128]{2,1,0:T(8,128)(2,1)S(1)}, u32[]{:S(2)}, u32[]{:S(2)}) async-start(bf16[8,320,128]{2,1,0:T(8,128)(2,1)} %shard_map.390), calls=%async_computation.11 | async-start | bytes 1310720 | tf_op jit(solution)/shard_map/all_to_all | solution.py:907
  301.6 3.7 %shard_map.387 = (f32[8,2,8,2048]{3,2,1,0:T(8,128)}, bf16[8,2,8,2048]{3,2,1,0:T(8,128)(2,1)}) custom-call(s32[1]{0:T(128)} %bitcast.refs_0_, bf16[128,512]{1,0:T(8,128)(2,1)} %get-tuple-element.182.refs_1_, bf16[2048,512]{1,0:T(8,128)(2,1)} %bitcast.93, bf16[2,128,512]{2,1,0:T(8,128)(2,1)} %get-tuple-element.184.refs_3_, bf16[2,128,512]{2,1,0:T(8,128)(2,1)} %copy-done.16, ...), custom_call_target="tpu_custom_call" | custom-call | flops 1000000000 | bytes 2000000 | tf_op jit(solution)/shard_map/pallas_call | solution.py:884
  305.3 6.4 %collective-permute-done.19.refs_3_ = bf16[272,128]{1,0:T(8,128)(2,1)S(1)} collective-permute-done((bf16[272,128]{1,0:T(8,128)(2,1)S(1)}, bf16[272,128]{1,0:T(8,128)(2,1)S(1)}, u32[]{:S(2)}, u32[]{:S(2)}) %collective-permute-start.19) | collective-permute-done | bytes 69664 | tf_op jit(solution)/shard_map/ppermute | solution.py:916
  315.4 2.3 shard_map.394
  (161 shorter events, 49.3 us)
Async XLA Ops:
  8.3 10.9 %copy-start.29 = (bf16[1,12,3,64,256]{4,3,2,1,0:T(8,128)(2,1)S(1)}, bf16[1,12,3,64,256]{4,3,2,1,0:T(8,128)(2,1)}, u32[]{:S(2)}) copy-start(bf16[1,12,3,64,256]{4,3,2,1,0:T(8,128)(2,1)} %param.23) | copy-start | bytes 3538948
  11.3 13.1 %copy-start.26 = (bf16[8,2,8,2048]{3,2,1,0:T(8,128)(2,1)S(1)}, bf16[8,2,8,2048]{3,2,1,0:T(8,128)(2,1)}, u32[]{:S(2)}) copy-start(bf16[8,2,8,2048]{3,2,1,0:T(8,128)(2,1)} %param.29) | copy-start | bytes 1572868
  11.3 13.1 %copy-start.27 = (bf16[8,2,8,2048]{3,2,1,0:T(8,128)(2,1)S(1)}, bf16[8,2,8,2048]{3,2,1,0:T(8,128)(2,1)}, u32[]{:S(2)}) copy-start(bf16[8,2,8,2048]{3,2,1,0:T(8,128)(2,1)} %param.45) | copy-start | bytes 1572868
  11.9 14.5 %all-to-all-start = ((bf16[8,8,784]{2,1,0:T(8,128)(2,1)}), bf16[8,8,784]{2,1,0:T(8,128)(2,1)S(1)}, u32[]{:S(2)}, u32[]{:S(2)}) async-start(bf16[8,8,784]{2,1,0:T(8,128)(2,1)} %broadcast_in_dim.6), calls=%async_computation | async-start | bytes 229376 | tf_op jit(solution)/shard_map/all_to_all | solution.py:907
  19.3 12.3 %collective-permute-start.1 = (bf16[12,3,16,256]{3,2,1,0:T(8,128)(2,1)S(1)}, bf16[12,3,16,256]{3,2,1,0:T(8,128)(2,1)}, u32[]{:S(2)}, u32[]{:S(2)}) collective-permute-start(bf16[12,3,16,256]{3,2,1,0:T(8,128)(2,1)S(1)} %get-tuple-element.217), channel_id=1, source_target_pairs={{1,0},{2,1},{3,2},{5,4},{6,5},{7,6},{9,8},{10,9},{11,10},{13,12},{... | collective-permute-start | bytes 884744 | tf_op jit(solution)/shard_map/ppermute | solution.py:1002
  20.6 11.0 %collective-permute-start = (bf16[12,3,16,256]{3,2,1,0:T(8,128)(2,1)S(1)}, bf16[12,3,16,256]{3,2,1,0:T(8,128)(2,1)}, u32[]{:S(2)}, u32[]{:S(2)}) collective-permute-start(bf16[12,3,16,256]{3,2,1,0:T(8,128)(2,1)S(1)} %get-tuple-element.218), channel_id=1, source_target_pairs={{0,1},{1,2},{2,3},{4,5},{5,6},{6,7},{8,9},{9,10},{10,11},{12,13},{... | collective-permute-start | bytes 884744 | tf_op jit(solution)/shard_map/ppermute | solution.py:1001
  24.4 8.7 %copy-start.25 = (bf16[2,8,8,2048]{3,2,1,0:T(8,128)(2,1)}, bf16[2,8,8,2048]{3,2,1,0:T(8,128)(2,1)S(1)}, u32[]{:S(2)}) copy-start(bf16[2,8,8,2048]{3,2,1,0:T(8,128)(2,1)S(1)} %copy.46) | copy-start | bytes 1572868
  26.4 44.4 %all-to-all-start.1 = ((bf16[8,832,128]{2,1,0:T(8,128)(2,1)}), bf16[8,832,128]{2,1,0:T(8,128)(2,1)S(1)}, u32[]{:S(2)}, u32[]{:S(2)}) async-start(bf16[8,832,128]{2,1,0:T(8,128)(2,1)} %get-tuple-element.120), calls=%async_computation.1 | async-start | bytes 3407872 | tf_op jit(solution)/shard_map/all_to_all | solution.py:907
  30.4 5.5 %copy-start.20 = (s32[1,8]{1,0:T(1,128)S(1)}, s32[1,8]{1,0:T(1,128)}, u32[]{:S(2)}) copy-start(s32[1,8]{1,0:T(1,128)} %param.24) | copy-start | bytes 100
  30.4 87.7 %all-gather.8.cloned.1.call-start = ((), (), s32[]{:S(2)}) async-start(), calls=%async_computation.14 | async-start | bytes 1916928 | tf_op jit(solution)/shard_map/all_gather | solution.py:1015
  31.6 19.6 %collective-permute-start.3 = (bf16[128,2048]{1,0:T(8,128)(2,1)S(1)}, bf16[128,2048]{1,0:T(8,128)(2,1)S(1)}, u32[]{:S(2)}, u32[]{:S(2)}) collective-permute-start(bf16[128,2048]{1,0:T(8,128)(2,1)S(1)} %bitcast.60), channel_id=1, source_target_pairs={{0,2},{1,3},{2,0},{3,1},{4,6},{5,7},{6,4},{7,5},{8,10},{9,11},{10,... | collective-permute-start | bytes 1572872 | tf_op jit(solution)/shard_map/ppermute | solution.py:916
  33.1 18.1 %collective-permute-start.2 = (bf16[128,2048]{1,0:T(8,128)(2,1)S(1)}, bf16[128,2048]{1,0:T(8,128)(2,1)S(1)}, u32[]{:S(2)}, u32[]{:S(2)}) collective-permute-start(bf16[128,2048]{1,0:T(8,128)(2,1)S(1)} %bitcast.61), channel_id=1, source_target_pairs={{0,1},{1,0},{2,3},{3,2},{4,5},{5,4},{6,7},{7,6},{8,9},{9,8},{10,11... | collective-permute-start | bytes 1572872 | tf_op jit(solution)/shard_map/ppermute | solution.py:916
  33.8 15.1 %collective-permute-start.6 = (bf16[128,512]{1,0:T(8,128)(2,1)S(1)}, bf16[128,512]{1,0:T(8,128)(2,1)S(1)}, u32[]{:S(2)}, u32[]{:S(2)}) collective-permute-start(bf16[128,512]{1,0:T(8,128)(2,1)S(1)} %get-tuple-element.220), channel_id=1, source_target_pairs={{0,3},{1,2},{2,1},{3,0},{4,7},{5,6},{6,5},{7,4},{8,11},{9,10},{10,... | collective-permute-start | bytes 393224 | tf_op jit(solution)/shard_map/ppermute | solution.py:916
  34.4 16.8 %collective-permute-start.5 = (bf16[128,512]{1,0:T(8,128)(2,1)S(1)}, bf16[128,512]{1,0:T(8,128)(2,1)S(1)}, u32[]{:S(2)}, u32[]{:S(2)}) collective-permute-start(bf16[128,512]{1,0:T(8,128)(2,1)S(1)} %get-tuple-element.221), channel_id=1, source_target_pairs={{0,2},{1,3},{2,0},{3,1},{4,6},{5,7},{6,4},{7,5},{8,10},{9,11},{10,... | collective-permute-start | bytes 393224 | tf_op jit(solution)/shard_map/ppermute | solution.py:916
  35.9 15.3 %collective-permute-start.4 = (bf16[128,512]{1,0:T(8,128)(2,1)S(1)}, bf16[128,512]{1,0:T(8,128)(2,1)S(1)}, u32[]{:S(2)}, u32[]{:S(2)}) collective-permute-start(bf16[128,512]{1,0:T(8,128)(2,1)S(1)} %get-tuple-element.222), channel_id=1, source_target_pairs={{0,1},{1,0},{2,3},{3,2},{4,5},{5,4},{6,7},{7,6},{8,9},{9,8},{10,11... | collective-permute-start | bytes 393224 | tf_op jit(solution)/shard_map/ppermute | solution.py:916
  48.9 15.6 %copy-start.10 = (bf16[128,512]{1,0:T(8,128)(2,1)}, bf16[128,512]{1,0:T(8,128)(2,1)S(1)}, u32[]{:S(2)}) copy-start(bf16[128,512]{1,0:T(8,128)(2,1)S(1)} %collective-permute-done.6.refs_6_.refs_12_) | copy-start | bytes 393220
  70.8 4.3 %collective-permute-start.7 = (bf16[8,832,128]{2,1,0:T(8,128)(2,1)S(1)}, bf16[8,832,128]{2,1,0:T(8,128)(2,1)S(1)}, u32[]{:S(2)}, u32[]{:S(2)}) collective-permute-start(bf16[8,832,128]{2,1,0:T(8,128)(2,1)S(1)} %all-to-all-done.1.refs_2_), channel_id=1, source_target_pairs={{0,1},{1,0},{2,3},{3,2},{4,5},{5,4},{6,7},{7,6},{8,9},{9,8},{10,11... | collective-permute-start | bytes 5111816 | tf_op jit(solution)/shard_map/ppermute | solution.py:916
  70.9 82.1 %collective-permute-start.8 = (bf16[128,2048]{1,0:T(8,128)(2,1)}, bf16[128,2048]{1,0:T(8,128)(2,1)}, u32[]{:S(2)}, u32[]{:S(2)}) collective-permute-start(bf16[128,2048]{1,0:T(8,128)(2,1)} %copy-done.4), channel_id=1, source_target_pairs={{0,1},{1,0},{2,3},{3,2},{4,5},{5,4},{6,7},{7,6},{8,9},{9,8},{10,11... | collective-permute-start | bytes 1572872 | tf_op jit(solution)/shard_map/ppermute | solution.py:916
  78.7 17.0 %all-to-all-start.2 = ((f32[32,16,128]{2,1,0:T(8,128)}), f32[32,16,128]{2,1,0:T(8,128)}, u32[]{:S(2)}, u32[]{:S(2)}) async-start(f32[32,16,128]{2,1,0:T(8,128)} %get-tuple-element.128), calls=%async_computation.2 | async-start | bytes 524288 | tf_op jit(solution)/shard_map/all_to_all | solution.py:907
  82.1 13.6 %copy-start.21 = (s32[1,8]{1,0:T(1,128)S(1)}, s32[1,8]{1,0:T(1,128)}, u32[]{:S(2)}) copy-start(s32[1,8]{1,0:T(1,128)} %refs_1_.5) | copy-start | bytes 100
  114.7 7.2 %copy-start.2 = (bf16[512,512]{1,0:T(8,128)(2,1)}, bf16[512,512]{1,0:T(8,128)(2,1)S(1)}, u32[]{:S(2)}) copy-start(bf16[512,512]{1,0:T(8,128)(2,1)S(1)} %all-gather.1.refs_0_) | copy-start | bytes 1572868
  118.1 8.3 %copy-start.33 = (f32[64]{0:T(128)S(1)}, f32[64]{0:T(128)}, u32[]{:S(2)}) copy-start(f32[64]{0:T(128)} %param.27) | copy-start | bytes 772
  118.1 8.3 %copy-start.34 = (f32[64]{0:T(128)S(1)}, f32[64]{0:T(128)}, u32[]{:S(2)}) copy-start(f32[64]{0:T(128)} %param.28) | copy-start | bytes 772
  121.9 12.4 %all-to-all-start.3 = ((f32[8,8,128]{2,1,0:T(8,128)}), f32[8,8,128]{2,1,0:T(8,128)S(1)}, u32[]{:S(2)}, u32[]{:S(2)}) async-start(f32[8,8,128]{2,1,0:T(8,128)} %get-tuple-element.139), calls=%async_computation.3 | async-start | bytes 65536 | tf_op jit(solution)/shard_map/all_to_all | solution.py:907
  146.8 12.9 %all-to-all-start.4 = ((f32[8,8,128]{2,1,0:T(8,128)}), f32[8,8,128]{2,1,0:T(8,128)S(1)}, u32[]{:S(2)}, u32[]{:S(2)}) async-start(f32[8,8,128]{2,1,0:T(8,128)} %get-tuple-element.144), calls=%async_computation.4 | async-start | bytes 65536 | tf_op jit(solution)/shard_map/all_to_all | solution.py:907
  163.7 10.8 %all-to-all-start.5 = ((f32[8,8,128]{2,1,0:T(8,128)}), f32[8,8,128]{2,1,0:T(8,128)S(1)}, u32[]{:S(2)}, u32[]{:S(2)}) async-start(f32[8,8,128]{2,1,0:T(8,128)} %get-tuple-element.146), calls=%async_computation.5 | async-start | bytes 65536 | tf_op jit(solution)/shard_map/all_to_all | solution.py:907
  167.1 128.2 %reduce-scatter.2.cloned.1.call-start = ((), (), s32[]{:S(2)}) async-start(), calls=%async_computation.13 | async-start | bytes 1916928 | tf_op jit(solution)/shard_map/reduce_scatter | solution.py:1152
  191.9 14.5 %collective-permute-start.9 = (bf16[2,128,512]{2,1,0:T(8,128)(2,1)S(1)}, bf16[2,128,512]{2,1,0:T(8,128)(2,1)S(1)}, u32[]{:S(2)}, u32[]{:S(2)}) collective-permute-start(bf16[2,128,512]{2,1,0:T(8,128)(2,1)S(1)} %copy-done.37), channel_id=1, source_target_pairs={{0,1},{1,0},{2,3},{3,2},{4,5},{5,4},{6,7},{7,6},{8,9},{9,8},{10,11... | collective-permute-start | bytes 786440 | tf_op jit(solution)/shard_map/ppermute | solution.py:916
  191.9 14.4 %collective-permute-start.10 = (bf16[2,128,512]{2,1,0:T(8,128)(2,1)S(1)}, bf16[2,128,512]{2,1,0:T(8,128)(2,1)S(1)}, u32[]{:S(2)}, u32[]{:S(2)}) collective-permute-start(bf16[2,128,512]{2,1,0:T(8,128)(2,1)S(1)} %copy-done.36), channel_id=1, source_target_pairs={{0,2},{1,3},{2,0},{3,1},{4,6},{5,7},{6,4},{7,5},{8,10},{9,11},{10,... | collective-permute-start | bytes 786440 | tf_op jit(solution)/shard_map/ppermute | solution.py:916
  192.4 14.0 %collective-permute-start.11 = (bf16[2,128,512]{2,1,0:T(8,128)(2,1)S(1)}, bf16[2,128,512]{2,1,0:T(8,128)(2,1)S(1)}, u32[]{:S(2)}, u32[]{:S(2)}) collective-permute-start(bf16[2,128,512]{2,1,0:T(8,128)(2,1)S(1)} %copy-done.35), channel_id=1, source_target_pairs={{0,3},{1,2},{2,1},{3,0},{4,7},{5,6},{6,5},{7,4},{8,11},{9,10},{10,... | collective-permute-start | bytes 786440 | tf_op jit(solution)/shard_map/ppermute | solution.py:916
  206.4 4.0 %copy-start.16 = (bf16[2,128,512]{2,1,0:T(8,128)(2,1)}, bf16[2,128,512]{2,1,0:T(8,128)(2,1)S(1)}, u32[]{:S(2)}) copy-start(bf16[2,128,512]{2,1,0:T(8,128)(2,1)S(1)} %collective-permute-done.9.refs_7_.refs_4_) | copy-start | bytes 786436
  210.3 4.8 %copy-start.28 = (bf16[4,128,512]{2,1,0:T(8,128)(2,1)S(1)}, bf16[4,128,512]{2,1,0:T(8,128)(2,1)}, u32[]{:S(2)}) copy-start(bf16[4,128,512]{2,1,0:T(8,128)(2,1)} %get-tuple-element.164) | copy-start | bytes 1572868
  215.1 11.4 %copy-start = (bf16[8,832,128]{2,1,0:T(8,128)(2,1)S(1)}, bf16[8,832,128]{2,1,0:T(8,128)(2,1)}, u32[]{:S(2)}) copy-start(bf16[8,832,128]{2,1,0:T(8,128)(2,1)} %shard_map.381.refs_5_) | copy-start | bytes 5111812
  234.1 4.7 %copy-start.9 = (bf16[576,128]{1,0:T(8,128)(2,1)}, bf16[576,128]{1,0:T(8,128)(2,1)S(1)}, u32[]{:S(2)}) copy-start(bf16[576,128]{1,0:T(8,128)(2,1)S(1)} %all-gather.4) | copy-start | bytes 442372
  238.8 19.4 %all-to-all-start.9 = ((f32[32,16,128]{2,1,0:T(8,128)}), f32[32,16,128]{2,1,0:T(8,128)S(1)}, u32[]{:S(2)}, u32[]{:S(2)}) async-start(f32[32,16,128]{2,1,0:T(8,128)} %get-tuple-element.177), calls=%async_computation.9 | async-start | bytes 524288 | tf_op jit(solution)/shard_map/all_to_all | solution.py:907
  260.0 28.6 %all-to-all-start.10 = ((bf16[8,272,128]{2,1,0:T(8,128)(2,1)}), bf16[8,272,128]{2,1,0:T(8,128)(2,1)S(1)}, u32[]{:S(2)}, u32[]{:S(2)}) async-start(bf16[8,272,128]{2,1,0:T(8,128)(2,1)} %shard_map.384.refs_5_), calls=%async_computation.10 | async-start | bytes 1114112 | tf_op jit(solution)/shard_map/all_to_all | solution.py:907
  288.7 12.7 %copy-start.31 = (bf16[272,128]{1,0:T(8,128)(2,1)}, bf16[272,128]{1,0:T(8,128)(2,1)S(1)}, u32[]{:S(2)}) copy-start(bf16[272,128]{1,0:T(8,128)(2,1)S(1)} %reduce_sum.34.refs_1_) | copy-start | bytes 208900
  288.7 24.6 %all-to-all-start.11 = ((bf16[8,320,128]{2,1,0:T(8,128)(2,1)}), bf16[8,320,128]{2,1,0:T(8,128)(2,1)S(1)}, u32[]{:S(2)}, u32[]{:S(2)}) async-start(bf16[8,320,128]{2,1,0:T(8,128)(2,1)} %shard_map.390), calls=%async_computation.11 | async-start | bytes 1310720 | tf_op jit(solution)/shard_map/all_to_all | solution.py:907
  294.7 6.7 %collective-permute-start.20 = (bf16[272,128]{1,0:T(8,128)(2,1)S(1)}, bf16[272,128]{1,0:T(8,128)(2,1)S(1)}, u32[]{:S(2)}, u32[]{:S(2)}) collective-permute-start(bf16[272,128]{1,0:T(8,128)(2,1)S(1)} %reduce_sum.34.refs_1_), channel_id=1, source_target_pairs={{0,3},{1,2},{2,1},{3,0},{4,7},{5,6},{6,5},{7,4},{8,11},{9,10},{10,... | collective-permute-start | bytes 208904 | tf_op jit(solution)/shard_map/ppermute | solution.py:916
  297.6 15.9 %collective-permute-start.14 = (bf16[864,128]{1,0:T(8,128)(2,1)}, bf16[864,128]{1,0:T(8,128)(2,1)S(1)}, u32[]{:S(2)}, u32[]{:S(2)}) collective-permute-start(bf16[864,128]{1,0:T(8,128)(2,1)} %shard_map.391.refs_1_), channel_id=1, source_target_pairs={{0,3},{1,2},{2,1},{3,0},{4,7},{5,6},{6,5},{7,4},{8,11},{9,10},{10,... | collective-permute-start | bytes 663560 | tf_op jit(solution)/shard_map/ppermute | solution.py:916
  298.8 14.7 %collective-permute-start.13 = (bf16[864,128]{1,0:T(8,128)(2,1)}, bf16[864,128]{1,0:T(8,128)(2,1)S(1)}, u32[]{:S(2)}, u32[]{:S(2)}) collective-permute-start(bf16[864,128]{1,0:T(8,128)(2,1)} %shard_map.391.refs_1_), channel_id=1, source_target_pairs={{0,2},{1,3},{2,0},{3,1},{4,6},{5,7},{6,4},{7,5},{8,10},{9,11},{10,... | collective-permute-start | bytes 663560 | tf_op jit(solution)/shard_map/ppermute | solution.py:916
  299.6 13.8 %collective-permute-start.12 = (bf16[864,128]{1,0:T(8,128)(2,1)}, bf16[864,128]{1,0:T(8,128)(2,1)S(1)}, u32[]{:S(2)}, u32[]{:S(2)}) collective-permute-start(bf16[864,128]{1,0:T(8,128)(2,1)} %shard_map.391.refs_1_), channel_id=1, source_target_pairs={{0,1},{1,0},{2,3},{3,2},{4,5},{5,4},{6,7},{7,6},{8,9},{9,8},{10,11... | collective-permute-start | bytes 663560 | tf_op jit(solution)/shard_map/ppermute | solution.py:916
  300.2 11.5 %collective-permute-start.19 = (bf16[272,128]{1,0:T(8,128)(2,1)S(1)}, bf16[272,128]{1,0:T(8,128)(2,1)S(1)}, u32[]{:S(2)}, u32[]{:S(2)}) collective-permute-start(bf16[272,128]{1,0:T(8,128)(2,1)S(1)} %reduce_sum.34.refs_1_), channel_id=1, source_target_pairs={{0,2},{1,3},{2,0},{3,1},{4,6},{5,7},{6,4},{7,5},{8,10},{9,11},{10,... | collective-permute-start | bytes 208904 | tf_op jit(solution)/shard_map/ppermute | solution.py:916
  301.4 10.3 %collective-permute-start.18 = (bf16[272,128]{1,0:T(8,128)(2,1)S(1)}, bf16[272,128]{1,0:T(8,128)(2,1)S(1)}, u32[]{:S(2)}, u32[]{:S(2)}) collective-permute-start(bf16[272,128]{1,0:T(8,128)(2,1)S(1)} %reduce_sum.34.refs_1_), channel_id=1, source_target_pairs={{0,1},{1,0},{2,3},{3,2},{4,5},{5,4},{6,7},{7,6},{8,9},{9,8},{10,11... | collective-permute-start | bytes 208904 | tf_op jit(solution)/shard_map/ppermute | solution.py:916
  313.4 4.3 %copy-start.30 = (bf16[320,128]{1,0:T(8,128)(2,1)}, bf16[320,128]{1,0:T(8,128)(2,1)S(1)}, u32[]{:S(2)}) copy-start(bf16[320,128]{1,0:T(8,128)(2,1)S(1)} %reduce_sum.35.refs_1_) | copy-start | bytes 245764
  313.5 4.8 %collective-permute-start.17 = (bf16[320,128]{1,0:T(8,128)(2,1)S(1)}, bf16[320,128]{1,0:T(8,128)(2,1)S(1)}, u32[]{:S(2)}, u32[]{:S(2)}) collective-permute-start(bf16[320,128]{1,0:T(8,128)(2,1)S(1)} %reduce_sum.35.refs_1_), channel_id=1, source_target_pairs={{0,3},{1,2},{2,1},{3,0},{4,7},{5,6},{6,5},{7,4},{8,11},{9,10},{10,... | collective-permute-start | bytes 245768 | tf_op jit(solution)/shard_map/ppermute | solution.py:916
  313.9 5.6 %collective-permute-start.16 = (bf16[320,128]{1,0:T(8,128)(2,1)S(1)}, bf16[320,128]{1,0:T(8,128)(2,1)S(1)}, u32[]{:S(2)}, u32[]{:S(2)}) collective-permute-start(bf16[320,128]{1,0:T(8,128)(2,1)S(1)} %reduce_sum.35.refs_1_), channel_id=1, source_target_pairs={{0,2},{1,3},{2,0},{3,1},{4,6},{5,7},{6,4},{7,5},{8,10},{9,11},{10,... | collective-permute-start | bytes 245768 | tf_op jit(solution)/shard_map/ppermute | solution.py:916
  314.8 4.7 %collective-permute-start.15 = (bf16[320,128]{1,0:T(8,128)(2,1)S(1)}, bf16[320,128]{1,0:T(8,128)(2,1)S(1)}, u32[]{:S(2)}, u32[]{:S(2)}) collective-permute-start(bf16[320,128]{1,0:T(8,128)(2,1)S(1)} %reduce_sum.35.refs_1_), channel_id=1, source_target_pairs={{0,1},{1,0},{2,3},{3,2},{4,5},{5,4},{6,7},{7,6},{8,9},{9,8},{10,11... | collective-permute-start | bytes 245768 | tf_op jit(solution)/shard_map/ppermute | solution.py:916
  (22 other events, 43.0 us)
Sparse Core Ops, SparseCore 0:
  71.0 47.0 all-gather.7
  215.2 72.9 reduce-scatter.1

commit v5 on v4

--- a/solution.py
+++ b/solution.py
@@ -416,7 +416,7 @@
     half = one_ref.shape[0] // 2
     part = early_ref.shape[0] // 2
     start = 0
-    for part_ref in (fine_ref, half_w_ref, quarter_w_ref):
+    for part_ref in (fine_ref, half_w_ref, quarter_w_ref, reduce_ref):
         early_ref[start : start + part_ref.shape[0]] = part_ref[...]
         start += padded(part_ref.shape[0])
     for block in range(expand_ref.shape[1] // 128):
@@ -433,8 +433,7 @@
     rows = pl.ds(pl.multiple_of(side * half, half), half)
     for block in range(one_ref.shape[1] // 128):
         start = put(start, one_ref[rows, 128 * block : 128 * block + 128])
-    start = put(start, early_ref[pl.ds(pl.multiple_of(side * part, part), part)])
-    put(start, reduce_ref[...])
+    put(start, early_ref[pl.ds(pl.multiple_of(side * part, part), part)])
     wide = three_ref.shape[1] // 4
     columns = pl.ds(pl.multiple_of(place * 128, 128), 128)
     parts_ref[0 : two_ref.shape[0]] = two_ref[:, columns]
@@ -970,10 +969,11 @@
 
     half = w_one.shape[0] // 2
     expand_rows = padded(w_expand.shape[0])
-    early_rows = padded(3 * padded(k_fine.shape[0]) + mid // 128 * expand_rows, 32)
+    early_rows = padded(
+        3 * padded(k_fine.shape[0]) + padded(w_reduce.shape[0]) + mid // 128 * expand_rows, 32
+    )
     edges = [4 * padded(half)]
-    for rows in (early_rows // 2, w_reduce.shape[0]):
-        edges.append(edges[-1] + padded(rows))
+    edges.append(edges[0] + early_rows // 2)
     two_rows, three_rows = w_two.shape[0], w_three.shape[0]
     two_end = padded(two_rows)
     part_rows = two_end + in_r // 128 * padded(three_rows)
@@ -1022,7 +1022,6 @@
     full_one = full_one.reshape(c_in, mid)
     sums = exchange(sums, both)
     mine, other, first = together(mine, other, first)
-    full_reduce = mine[:, edges[1] : edges[1] + w_reduce.shape[0]].reshape(mid, red)
     halves = [entry[:, edges[0] : edges[1]] for entry in (mine, other)]
     quarters = jnp.concatenate(
         [
@@ -1032,11 +1031,12 @@
         1,
     )
     early_parts, start = [], 0
-    for size in (k_fine.shape[0],) * 3 + (w_expand.shape[0],) * (mid // 128):
+    sizes = (k_fine.shape[0],) * 3 + (w_reduce.shape[0],) + (w_expand.shape[0],) * (mid // 128)
+    for size in sizes:
         early_parts.append(quarters[:, start : start + size].reshape(-1, 128))
         start += padded(size)
-    full_fine, full_half, full_quarter = early_parts[:3]
-    full_expand = jnp.concatenate(early_parts[3:], 1)
+    full_fine, full_half, full_quarter, full_reduce = early_parts[:4]
+    full_expand = jnp.concatenate(early_parts[4:], 1)
     stem_totals = jnp.sum(sums[:, 8], 0).reshape(2, STEM)
     stem_mean, stem_inverse = statistics(stem_totals, stem_count)
     stem_vectors = lanes(stem_mean, stem_inverse, stem_gain, stem_bias)

time: 332 us -> 329 us (level)
    unnamed x77 -> x81, local copies, waits for them, and re-layouts: 9.58 us -> 9.16 us
where the time goes in v5:
time: 329 us; the launch traced here: 327 us
  Pallas kernels  122 us (37%)
  blocking collectives  69.9 us (21%)
  starting transfers between devices  60.1 us (18%)
  waiting for transfers between devices  38.2 us (12%)
  local copies, waits for them, and re-layouts  18.5 us (6%)
  between operations  14.5 us (4%)
  other arithmetic  4.29 us (1%)
    pallas_call x23, Pallas kernels, call(): pl.pallas_call(body, grid=(1,), in_specs=[pl.BlockSpec(memory_space=pltpu...  66.2 us
    pallas_call x6, Pallas kernels, stem_call(): pl.pallas_call(body, grid=(steps,), in_specs=in_specs + [pl.BlockSpec(mem...  55.3 us
    all_to_all x9, starting transfers between devices, exchange(): return lax.all_to_all(blocks, axis, 0, 0)  43 us
    all_to_all x3, blocking collectives, exchange(): return lax.all_to_all(blocks, axis, 0, 0)  36.2 us
    all_to_all x9, waiting for transfers between devices, exchange(): return lax.all_to_all(blocks, axis, 0, 0)  21.1 us
    ppermute x19, waiting for transfers between devices, swap(): lax.ppermute(piece, axis, [(i, i ^ step) for i in range(lax.axis_size(axi...  14.1 us
    ppermute x19, starting transfers between devices, swap(): lax.ppermute(piece, axis, [(i, i ^ step) for i in range(lax.axis_size(axi...  12 us
    unnamed x81, local copies, waits for them, and re-layouts  9.16 us
  transfers between devices with their start and end apart: 32, of which 10 were waited for; matrix products, arithmetic and copies ran while one was open for 3% of the time, Pallas kernels for 30%

profile of v5, /device:TPU:0, one launch (start us, length us, event | category | flops | bytes accessed | tf_op | source)
XLA Modules:
  0.0 326.9 jit_solution(16723865467684248174)
XLA Ops:
  8.3 2.9 shard_map.366
  11.9 7.3 %all-to-all-start = ((bf16[8,8,784]{2,1,0:T(8,128)(2,1)}), bf16[8,8,784]{2,1,0:T(8,128)(2,1)S(1)}, u32[]{:S(2)}, u32[]{:S(2)}) async-start(bf16[8,8,784]{2,1,0:T(8,128)(2,1)} %broadcast_in_dim.6), calls=%async_computation | async-start | bytes 229376 | tf_op jit(solution)/shard_map/all_to_all | solution.py:906
  20.6 3.8 %collective-permute-start = (bf16[12,3,16,256]{3,2,1,0:T(8,128)(2,1)S(1)}, bf16[12,3,16,256]{3,2,1,0:T(8,128)(2,1)}, u32[]{:S(2)}, u32[]{:S(2)}) collective-permute-start(bf16[12,3,16,256]{3,2,1,0:T(8,128)(2,1)S(1)} %get-tuple-element.218), channel_id=1, source_target_pairs={{0,1},{1,2},{2,3},{4,5},{5,6},{6,7},{8,9},{9,10},{10,11},{12,13},{... | collective-permute-start | bytes 884744 | tf_op jit(solution)/shard_map/ppermute | solution.py:1001
  24.5 2.0 all-to-all-done
  26.5 4.0 %all-to-all-start.1 = ((bf16[8,800,128]{2,1,0:T(8,128)(2,1)}), bf16[8,800,128]{2,1,0:T(8,128)(2,1)S(1)}, u32[]{:S(2)}, u32[]{:S(2)}) async-start(bf16[8,800,128]{2,1,0:T(8,128)(2,1)} %get-tuple-element.120), calls=%async_computation.1 | async-start | bytes 3276800 | tf_op jit(solution)/shard_map/all_to_all | solution.py:906
  35.9 13.0 %shard_map.367.refs_0_ = bf16[4,80,112,256]{3,2,1,0:T(8,128)(2,1)} custom-call(s32[8]{0:T(128)S(1)} %bitcast.59, bf16[12,3,64,256]{3,2,1,0:T(8,128)(2,1)} %bitcast.69, bf16[12,3,16,256]{3,2,1,0:T(8,128)(2,1)} %collective-permute-done.refs_2_, bf16[12,3,16,256]{3,2,1,0:T(8,128)(2,1)} %collective-permute-done.1.refs_3_), custom_call_target="tpu_custom_call" | custom-call | flops 16000000000 | bytes 20000000 | tf_op jit(solution)/shard_map/pallas_call | solution.py:197
  48.9 2.3 collective-permute-done.5.refs_5_.refs_11_
  51.2 13.3 %shard_map.368 = (f32[8,32,64,128]{3,2,1,0:T(8,128)}, f32[2,64,128]{2,1,0:T(8,128)S(1)}) custom-call(bf16[4,80,112,256]{3,2,1,0:T(8,128)(2,1)} %shard_map.367.refs_0_, bf16[256,1456]{1,0:T(8,128)(2,1)} %fusion.7.refs_1_, bf16[128,2048]{1,0:T(8,128)(2,1)S(1)} %collective-permute-done.2.refs_2_.refs_6_.refs_3_, ...), custom_call_target="tpu_custom_call" | custom-call | flops 16000000000 | bytes 28000000 | tf_op jit(solution)/shard_map/pallas_call | solution.py:197
  67.4 2.0 all-to-all-done.1.refs_2_
  70.1 3.6 %collective-permute-done.7.refs_3_ = bf16[8,800,128]{2,1,0:T(8,128)(2,1)S(1)} collective-permute-done((bf16[8,800,128]{2,1,0:T(8,128)(2,1)S(1)}, bf16[8,800,128]{2,1,0:T(8,128)(2,1)S(1)}, u32[]{:S(2)}, u32[]{:S(2)}) %collective-permute-start.7) | collective-permute-done | bytes 1638432 | tf_op jit(solution)/shard_map/ppermute | solution.py:915
  73.7 2.9 shard_map.369
  79.1 2.7 all-to-all-start.2
  84.2 10.3 %all-to-all-done.2.refs_1_ = f32[32,16,128]{2,1,0:T(8,128)S(1)} async-done(((f32[32,16,128]{2,1,0:T(8,128)}), f32[32,16,128]{2,1,0:T(8,128)S(1)}, u32[]{:S(2)}, u32[]{:S(2)}) %all-to-all-start.2) | async-done | bytes 262176 | tf_op jit(solution)/shard_map/all_to_all | solution.py:906
  96.4 5.6 %all-gather.refs_1_ = bf16[512,128]{1,0:T(8,128)(2,1)S(1)} all-gather(bf16[128,128]{1,0:T(8,128)(2,1)} %get-tuple-element.133), channel_id=2, replica_groups=mesh['clip'=8,'row'=4] {'row'}, dimensions={0}, use_global_device_ids=true | all-gather | bytes 163840 | tf_op jit(solution)/shard_map/all_gather | solution.py:1050
  102.1 3.9 %shard_map.371 = (bf16[128,512]{1,0:T(8,128)(2,1)}, f32[128,512]{1,0:T(8,128)}, bf16[128,128]{1,0:T(8,128)(2,1)}, bf16[128,128]{1,0:T(8,128)(2,1)}, f32[32,128]{1,0:T(8,128)}) custom-call(s32[1]{0:T(128)} %bitcast.refs_0_, bf16[512,128]{1,0:T(8,128)(2,1)S(1)} %all-gather.refs_1_, bf16[128,512]{1,0:T(8,128)(2,1)} %get-tuple-element.134.refs_2_.refs_1_.refs_7_, ...), custom_call_target="tpu_custom_call" | custom-call | flops 1000000000 | bytes 2000000 | tf_op jit(solution)/shard_map/pallas_call | solution.py:883
  106.0 7.5 %all-gather.1.refs_0_ = bf16[512,512]{1,0:T(8,128)(2,1)S(1)} all-gather(bf16[128,512]{1,0:T(8,128)(2,1)} %get-tuple-element.137), channel_id=3, replica_groups=mesh['clip'=8,'row'=4] {'row'}, dimensions={0}, use_global_device_ids=true | all-gather | bytes 655360 | tf_op jit(solution)/shard_map/all_gather | solution.py:1069
  113.4 3.0 all-gather.8.cloned.1.call-done
  116.4 3.7 %shard_map.372 = (f32[512,128]{1,0:T(8,128)}, bf16[4608,128]{1,0:T(8,128)(2,1)}, f32[8,8,128]{2,1,0:T(8,128)}) custom-call(bf16[512,512]{1,0:T(8,128)(2,1)S(1)} %all-gather.1.refs_0_, bf16[8,832,128]{2,1,0:T(8,128)(2,1)} %bitcast.94), custom_call_target="tpu_custom_call" | custom-call | flops 1000000000 | bytes 2000000 | tf_op jit(solution)/shard_map/pallas_call | solution.py:883
  120.1 3.6 %all-to-all-start.3 = ((f32[8,8,128]{2,1,0:T(8,128)}), f32[8,8,128]{2,1,0:T(8,128)S(1)}, u32[]{:S(2)}, u32[]{:S(2)}) async-start(f32[8,8,128]{2,1,0:T(8,128)} %get-tuple-element.139), calls=%async_computation.3 | async-start | bytes 65536 | tf_op jit(solution)/shard_map/all_to_all | solution.py:906
  125.6 6.1 %shard_map.373 = (bf16[4,32,64,128]{3,2,1,0:T(8,128)(2,1)}, f32[2,64,128]{2,1,0:T(8,128)S(1)}) custom-call(f32[8,32,64,128]{3,2,1,0:T(8,128)} %get-tuple-element.141.refs_0_.refs_1_, bf16[8,64,32,128]{3,2,1,0:T(8,128)(2,1)} %refs_1_.4, f32[4,64,128]{2,1,0:T(8,128)} %broadcast_in_dim.7.refs_2_, f32[512,128]{1,0:T(8,128)S(1)} %copy-done.22), custom_call_target="tpu_custom_call" | custom-call | flops 4000000000 | bytes 8000000 | tf_op jit(solution)/shard_map/pallas_call | solution.py:197
  133.4 7.3 %all-gather.3 = bf16[2048,128]{1,0:T(8,128)(2,1)S(1)} all-gather(bf16[512,128]{1,0:T(8,128)(2,1)} %get-tuple-element.143), channel_id=5, replica_groups=mesh['clip'=8,'row'=4] {'row'}, dimensions={0}, use_global_device_ids=true | all-gather | bytes 655360 | tf_op jit(solution)/shard_map/all_gather | solution.py:1086
  140.8 3.4 %shard_map.375 = (f32[512,512]{1,0:T(8,128)}, bf16[512,512]{1,0:T(8,128)(2,1)}, f32[8,8,128]{2,1,0:T(8,128)}) custom-call(bf16[4,512,128]{2,1,0:T(8,128)(2,1)S(1)} %bitcast.53, bf16[8,832,128]{2,1,0:T(8,128)(2,1)} %bitcast.95), custom_call_target="tpu_custom_call" | custom-call | flops 1000000000 | bytes 2000000 | tf_op jit(solution)/shard_map/pallas_call | solution.py:883
  144.2 6.0 %all-to-all-start.4 = ((f32[8,8,128]{2,1,0:T(8,128)}), f32[8,8,128]{2,1,0:T(8,128)S(1)}, u32[]{:S(2)}, u32[]{:S(2)}) async-start(f32[8,8,128]{2,1,0:T(8,128)} %get-tuple-element.144), calls=%async_computation.4 | async-start | bytes 65536 | tf_op jit(solution)/shard_map/all_to_all | solution.py:906
  150.2 6.7 %all-to-all-done.4.refs_1_ = f32[8,8,128]{2,1,0:T(8,128)S(1)} async-done(((f32[8,8,128]{2,1,0:T(8,128)}), f32[8,8,128]{2,1,0:T(8,128)S(1)}, u32[]{:S(2)}, u32[]{:S(2)}) %all-to-all-start.4) | async-done | bytes 32800 | tf_op jit(solution)/shard_map/all_to_all | solution.py:906
  156.9 4.0 %shard_map.376 = (bf16[2,128,512]{2,1,0:T(8,128)(2,1)}, bf16[2,128,512]{2,1,0:T(8,128)(2,1)}, bf16[2,128,512]{2,1,0:T(8,128)(2,1)}, bf16[2,128,512]{2,1,0:T(8,12...) custom-call(s32[1]{0:T(128)} %bitcast.refs_0_, f32[8,8,128]{2,1,0:T(8,128)S(1)} %all-to-all-done.4.refs_1_, ...), custom_call_target="tpu_custom_call" | custom-call | flops 1000000000 | bytes 2000000 | tf_op jit(solution)/shard_map/pallas_call | solution.py:883
  160.9 3.3 %all-to-all-start.5 = ((f32[8,8,128]{2,1,0:T(8,128)}), f32[8,8,128]{2,1,0:T(8,128)S(1)}, u32[]{:S(2)}, u32[]{:S(2)}) async-start(f32[8,8,128]{2,1,0:T(8,128)} %get-tuple-element.146), calls=%async_computation.5 | async-start | bytes 65536 | tf_op jit(solution)/shard_map/all_to_all | solution.py:906
  165.5 6.1 %shard_map.377 = (bf16[4,32,64,128]{3,2,1,0:T(8,128)(2,1)}, f32[2,64,128]{2,1,0:T(8,128)S(1)}) custom-call(f32[8,32,64,128]{3,2,1,0:T(8,128)} %get-tuple-element.141.refs_0_.refs_1_, bf16[8,64,32,128]{3,2,1,0:T(8,128)(2,1)} %refs_1_.4, f32[4,64,128]{2,1,0:T(8,128)} %broadcast_in_dim.7.refs_2_, f32[512,512]{1,0:T(8,128)S(1)} %copy-done.15), custom_call_target="tpu_custom_call" | custom-call | flops 4000000000 | bytes 8000000 | tf_op jit(solution)/shard_map/pallas_call | solution.py:197
  171.7 3.1 shard_map.378
  174.7 12.3 %all_to_all.60.refs_1_ = bf16[4,512,128]{2,1,0:T(8,128)(2,1)S(1)} all-to-all(bf16[4,512,128]{2,1,0:T(8,128)(2,1)} %get-tuple-element.151), channel_id=1, replica_groups=mesh['clip'=8,'row'=4] {'row'}, dimensions={0} | all-to-all | bytes 1048576 | tf_op jit(solution)/shard_map/all_to_all | solution.py:906
  187.0 2.0 shard_map.379
  191.0 12.6 %all_to_all.61.refs_1_ = f32[8,8,128]{2,1,0:T(8,128)S(1)} all-to-all(f32[8,8,128]{2,1,0:T(8,128)} %get-tuple-element.153), channel_id=1, replica_groups=mesh['clip'=8,'row'=4] {'clip'}, dimensions={0} | all-to-all | bytes 65536 | tf_op jit(solution)/shard_map/all_to_all | solution.py:906
  203.6 3.9 %shard_map.380 = (bf16[512,128]{1,0:T(8,128)(2,1)}, bf16[4,128,512]{2,1,0:T(8,128)(2,1)}, f32[2,128]{1,0:T(2,128)}, bf16[16,128]{1,0:T(8,128)(2,1)}) custom-call(s32[1]{0:T(128)} %bitcast.refs_0_, f32[8,8,128]{2,1,0:T(8,128)S(1)} %all_to_all.61.refs_1_, f32[512,128]{1,0:T(8,128)} %get-tuple-element.159.refs_2_, ...), custom_call_target="tpu_custom_call" | custom-call | flops 1000000000 | bytes 2000000 | tf_op jit(solution)/shard_map/pallas_call | solution.py:883
  207.5 4.7 %shard_map.381.refs_5_ = bf16[8,832,128]{2,1,0:T(8,128)(2,1)} custom-call(bf16[512,512]{1,0:T(8,128)(2,1)} %copy-done.2, bf16[512,128]{1,0:T(8,128)(2,1)} %get-tuple-element.167.refs_1_, bf16[4,512,128]{2,1,0:T(8,128)(2,1)} %bitcast.54, bf16[512,512]{1,0:T(8,128)(2,1)} %get-tuple-element.168.refs_3_), custom_call_target="tpu_custom_call" | custom-call | flops 1000000000 | bytes 2000000 | tf_op jit(solution)/shard_map/pallas_call | solution.py:883
  212.3 11.4 %all_to_all.62.refs_0_ = bf16[4,128,512]{2,1,0:T(8,128)(2,1)S(1)} all-to-all(bf16[4,128,512]{2,1,0:T(8,128)(2,1)S(1)} %copy-done.30), channel_id=1, replica_groups=mesh['clip'=8,'row'=4] {'row'}, dimensions={0} | all-to-all | bytes 1048576 | tf_op jit(solution)/shard_map/all_to_all | solution.py:906
  225.6 5.7 %all-gather.4 = bf16[576,128]{1,0:T(8,128)(2,1)S(1)} all-gather(bf16[144,128]{1,0:T(8,128)(2,1)} %get-tuple-element.169), channel_id=6, replica_groups=mesh['clip'=8,'row'=4] {'row'}, dimensions={0}, use_global_device_ids=true | all-gather | bytes 184320 | tf_op jit(solution)/shard_map/all_gather | solution.py:1160
  231.3 4.7 %shard_map.383 = (bf16[128,128]{1,0:T(8,128)(2,1)}, f32[128,512]{1,0:T(8,128)}, bf16[128,128]{1,0:T(8,128)(2,1)}, f32[32,128]{1,0:T(8,128)}, f32[8,128]{1,0:T(8,128)}, /*index=5*/f32[32,16,128]{2,1,0:T(8,128)}) custom-call(s32[1]{0:T(128)} %bitcast.refs_0_, s32[1,8]{1,0:T(1,128)S(1)} %copy-done.21, bf16[4,144,128]{2,1,0:T(8,128)(2,1)S(1)} %bitcast.56, ...), custom_call_target="tpu_custom_call" | custom-call | flops 1000000000 | bytes 2000000 | tf_op jit(solution)/shard_map/pallas_call | solution.py:883
  236.0 4.2 %all-to-all-start.9 = ((f32[32,16,128]{2,1,0:T(8,128)}), f32[32,16,128]{2,1,0:T(8,128)S(1)}, u32[]{:S(2)}, u32[]{:S(2)}) async-start(f32[32,16,128]{2,1,0:T(8,128)} %get-tuple-element.177), calls=%async_computation.9 | async-start | bytes 524288 | tf_op jit(solution)/shard_map/all_to_all | solution.py:906
  243.3 8.4 %shard_map.385.refs_6_.refs_1_ = f32[8,64,128]{2,1,0:T(8,128)S(1)} custom-call(bf16[4,80,112,256]{3,2,1,0:T(8,128)(2,1)} %shard_map.367.refs_0_, f32[8,32,64,128]{3,2,1,0:T(8,128)} %get-tuple-element.141.refs_0_.refs_1_, bf16[4,32,64,128]{3,2,1,0:T(8,128)(2,1)} %get-tuple-element.179.refs_2_, f32[5,64,128]{2,1,0:T(8,128)} %broadcast_in_dim.8.refs_3_, ...), custom_call_target="tpu_custom_call" | custom-call | flops 1000000 | bytes 16000000 | tf_op jit(solution)/shard_map/pallas_call | solution.py:197
  251.7 3.5 %shard_map.384.refs_5_ = bf16[8,272,128]{2,1,0:T(8,128)(2,1)} custom-call(s32[1]{0:T(128)} %bitcast.refs_0_, bf16[512,128]{1,0:T(8,128)(2,1)} %copy-done.13, bf16[128,128]{1,0:T(8,128)(2,1)} %get-tuple-element.135.refs_2_, f32[32,128]{1,0:T(8,128)} %get-tuple-element.136.refs_3_, bf16[4,144,128]{2,1,0:T(8,128)(2,1)} %bitcast.57, ...), custom_call_target="tpu_custom_call" | custom-call | flops 1000000000 | bytes 2000000 | tf_op jit(solution)/shard_map/pallas_call | solution.py:883
  257.0 5.8 %all-to-all-start.10 = ((bf16[8,272,128]{2,1,0:T(8,128)(2,1)}), bf16[8,272,128]{2,1,0:T(8,128)(2,1)S(1)}, u32[]{:S(2)}, u32[]{:S(2)}) async-start(bf16[8,272,128]{2,1,0:T(8,128)(2,1)} %shard_map.384.refs_5_), calls=%async_computation.10 | async-start | bytes 1114112 | tf_op jit(solution)/shard_map/all_to_all | solution.py:906
  262.8 7.6 %all-gather.5 = bf16[512,512]{1,0:T(8,128)(2,1)S(1)} all-gather(bf16[128,512]{1,0:T(8,128)(2,1)} %get-tuple-element.182.refs_1_), channel_id=7, replica_groups=mesh['clip'=8,'row'=4] {'row'}, dimensions={0}, use_global_device_ids=true | all-gather | bytes 655360 | tf_op jit(solution)/shard_map/all_gather | solution.py:1213
  270.4 3.1 shard_map.388.refs_4_.refs_0_
  274.5 8.3 %shard_map.389.refs_2_ = f32[8,64,128]{2,1,0:T(8,128)S(1)} custom-call(bf16[4,80,112,256]{3,2,1,0:T(8,128)(2,1)} %shard_map.367.refs_0_, f32[8,32,64,128]{3,2,1,0:T(8,128)} %get-tuple-element.141.refs_0_.refs_1_, bf16[4,32,64,128]{3,2,1,0:T(8,128)(2,1)} %get-tuple-element.186.refs_2_, f32[5,64,128]{2,1,0:T(8,128)} %broadcast_in_dim.8.refs_3_, ...), custom_call_target="tpu_custom_call" | custom-call | flops 1000000 | bytes 16000000 | tf_op jit(solution)/shard_map/pallas_call | solution.py:197
  283.6 2.1 shard_map.390
  285.7 6.0 %all-to-all-start.11 = ((bf16[8,320,128]{2,1,0:T(8,128)(2,1)}), bf16[8,320,128]{2,1,0:T(8,128)(2,1)S(1)}, u32[]{:S(2)}, u32[]{:S(2)}) async-start(bf16[8,320,128]{2,1,0:T(8,128)(2,1)} %shard_map.390), calls=%async_computation.11 | async-start | bytes 1310720 | tf_op jit(solution)/shard_map/all_to_all | solution.py:906
  298.7 3.7 %shard_map.387 = (f32[8,2,8,2048]{3,2,1,0:T(8,128)}, bf16[8,2,8,2048]{3,2,1,0:T(8,128)(2,1)}) custom-call(s32[1]{0:T(128)} %bitcast.refs_0_, bf16[128,512]{1,0:T(8,128)(2,1)} %get-tuple-element.182.refs_1_, bf16[2048,512]{1,0:T(8,128)(2,1)} %bitcast.93, bf16[2,128,512]{2,1,0:T(8,128)(2,1)} %get-tuple-element.184.refs_3_, bf16[2,128,512]{2,1,0:T(8,128)(2,1)} %copy-done.16, ...), custom_call_target="tpu_custom_call" | custom-call | flops 1000000000 | bytes 2000000 | tf_op jit(solution)/shard_map/pallas_call | solution.py:883
  302.4 6.4 %collective-permute-done.19.refs_3_ = bf16[272,128]{1,0:T(8,128)(2,1)S(1)} collective-permute-done((bf16[272,128]{1,0:T(8,128)(2,1)S(1)}, bf16[272,128]{1,0:T(8,128)(2,1)S(1)}, u32[]{:S(2)}, u32[]{:S(2)}) %collective-permute-start.19) | collective-permute-done | bytes 69664 | tf_op jit(solution)/shard_map/ppermute | solution.py:915
  312.5 2.3 shard_map.394
  (166 shorter events, 50.1 us)
Async XLA Ops:
  8.3 10.9 %copy-start.31 = (bf16[1,12,3,64,256]{4,3,2,1,0:T(8,128)(2,1)S(1)}, bf16[1,12,3,64,256]{4,3,2,1,0:T(8,128)(2,1)}, u32[]{:S(2)}) copy-start(bf16[1,12,3,64,256]{4,3,2,1,0:T(8,128)(2,1)} %param.23) | copy-start | bytes 3538948
  11.3 13.1 %copy-start.28 = (bf16[8,2,8,2048]{3,2,1,0:T(8,128)(2,1)S(1)}, bf16[8,2,8,2048]{3,2,1,0:T(8,128)(2,1)}, u32[]{:S(2)}) copy-start(bf16[8,2,8,2048]{3,2,1,0:T(8,128)(2,1)} %param.29) | copy-start | bytes 1572868
  11.3 13.1 %copy-start.29 = (bf16[8,2,8,2048]{3,2,1,0:T(8,128)(2,1)S(1)}, bf16[8,2,8,2048]{3,2,1,0:T(8,128)(2,1)}, u32[]{:S(2)}) copy-start(bf16[8,2,8,2048]{3,2,1,0:T(8,128)(2,1)} %param.45) | copy-start | bytes 1572868
  11.9 14.5 %all-to-all-start = ((bf16[8,8,784]{2,1,0:T(8,128)(2,1)}), bf16[8,8,784]{2,1,0:T(8,128)(2,1)S(1)}, u32[]{:S(2)}, u32[]{:S(2)}) async-start(bf16[8,8,784]{2,1,0:T(8,128)(2,1)} %broadcast_in_dim.6), calls=%async_computation | async-start | bytes 229376 | tf_op jit(solution)/shard_map/all_to_all | solution.py:906
  19.3 12.3 %collective-permute-start.1 = (bf16[12,3,16,256]{3,2,1,0:T(8,128)(2,1)S(1)}, bf16[12,3,16,256]{3,2,1,0:T(8,128)(2,1)}, u32[]{:S(2)}, u32[]{:S(2)}) collective-permute-start(bf16[12,3,16,256]{3,2,1,0:T(8,128)(2,1)S(1)} %get-tuple-element.217), channel_id=1, source_target_pairs={{1,0},{2,1},{3,2},{5,4},{6,5},{7,6},{9,8},{10,9},{11,10},{13,12},{... | collective-permute-start | bytes 884744 | tf_op jit(solution)/shard_map/ppermute | solution.py:1002
  20.6 11.0 %collective-permute-start = (bf16[12,3,16,256]{3,2,1,0:T(8,128)(2,1)S(1)}, bf16[12,3,16,256]{3,2,1,0:T(8,128)(2,1)}, u32[]{:S(2)}, u32[]{:S(2)}) collective-permute-start(bf16[12,3,16,256]{3,2,1,0:T(8,128)(2,1)S(1)} %get-tuple-element.218), channel_id=1, source_target_pairs={{0,1},{1,2},{2,3},{4,5},{5,6},{6,7},{8,9},{9,10},{10,11},{12,13},{... | collective-permute-start | bytes 884744 | tf_op jit(solution)/shard_map/ppermute | solution.py:1001
  24.4 8.7 %copy-start.25 = (bf16[2,8,8,2048]{3,2,1,0:T(8,128)(2,1)}, bf16[2,8,8,2048]{3,2,1,0:T(8,128)(2,1)S(1)}, u32[]{:S(2)}) copy-start(bf16[2,8,8,2048]{3,2,1,0:T(8,128)(2,1)S(1)} %copy.46) | copy-start | bytes 1572868
  26.5 43.0 %all-to-all-start.1 = ((bf16[8,800,128]{2,1,0:T(8,128)(2,1)}), bf16[8,800,128]{2,1,0:T(8,128)(2,1)S(1)}, u32[]{:S(2)}, u32[]{:S(2)}) async-start(bf16[8,800,128]{2,1,0:T(8,128)(2,1)} %get-tuple-element.120), calls=%async_computation.1 | async-start | bytes 3276800 | tf_op jit(solution)/shard_map/all_to_all | solution.py:906
  30.5 5.5 %copy-start.20 = (s32[1,8]{1,0:T(1,128)S(1)}, s32[1,8]{1,0:T(1,128)}, u32[]{:S(2)}) copy-start(s32[1,8]{1,0:T(1,128)} %param.24) | copy-start | bytes 100
  30.5 85.9 %all-gather.8.cloned.1.call-start = ((), (), s32[]{:S(2)}) async-start(), calls=%async_computation.14 | async-start | bytes 1916928 | tf_op jit(solution)/shard_map/all_gather | solution.py:1015
  31.6 19.6 %collective-permute-start.3 = (bf16[128,2048]{1,0:T(8,128)(2,1)S(1)}, bf16[128,2048]{1,0:T(8,128)(2,1)S(1)}, u32[]{:S(2)}, u32[]{:S(2)}) collective-permute-start(bf16[128,2048]{1,0:T(8,128)(2,1)S(1)} %bitcast.60), channel_id=1, source_target_pairs={{0,2},{1,3},{2,0},{3,1},{4,6},{5,7},{6,4},{7,5},{8,10},{9,11},{10,... | collective-permute-start | bytes 1572872 | tf_op jit(solution)/shard_map/ppermute | solution.py:915
  33.1 18.1 %collective-permute-start.2 = (bf16[128,2048]{1,0:T(8,128)(2,1)S(1)}, bf16[128,2048]{1,0:T(8,128)(2,1)S(1)}, u32[]{:S(2)}, u32[]{:S(2)}) collective-permute-start(bf16[128,2048]{1,0:T(8,128)(2,1)S(1)} %bitcast.61), channel_id=1, source_target_pairs={{0,1},{1,0},{2,3},{3,2},{4,5},{5,4},{6,7},{7,6},{8,9},{9,8},{10,11... | collective-permute-start | bytes 1572872 | tf_op jit(solution)/shard_map/ppermute | solution.py:915
  33.8 15.1 %collective-permute-start.6 = (bf16[128,512]{1,0:T(8,128)(2,1)S(1)}, bf16[128,512]{1,0:T(8,128)(2,1)S(1)}, u32[]{:S(2)}, u32[]{:S(2)}) collective-permute-start(bf16[128,512]{1,0:T(8,128)(2,1)S(1)} %get-tuple-element.226), channel_id=1, source_target_pairs={{0,3},{1,2},{2,1},{3,0},{4,7},{5,6},{6,5},{7,4},{8,11},{9,10},{10,... | collective-permute-start | bytes 393224 | tf_op jit(solution)/shard_map/ppermute | solution.py:915
  34.4 16.8 %collective-permute-start.5 = (bf16[128,512]{1,0:T(8,128)(2,1)S(1)}, bf16[128,512]{1,0:T(8,128)(2,1)S(1)}, u32[]{:S(2)}, u32[]{:S(2)}) collective-permute-start(bf16[128,512]{1,0:T(8,128)(2,1)S(1)} %get-tuple-element.227), channel_id=1, source_target_pairs={{0,2},{1,3},{2,0},{3,1},{4,6},{5,7},{6,4},{7,5},{8,10},{9,11},{10,... | collective-permute-start | bytes 393224 | tf_op jit(solution)/shard_map/ppermute | solution.py:915
  35.9 15.3 %collective-permute-start.4 = (bf16[128,512]{1,0:T(8,128)(2,1)S(1)}, bf16[128,512]{1,0:T(8,128)(2,1)S(1)}, u32[]{:S(2)}, u32[]{:S(2)}) collective-permute-start(bf16[128,512]{1,0:T(8,128)(2,1)S(1)} %get-tuple-element.228), channel_id=1, source_target_pairs={{0,1},{1,0},{2,3},{3,2},{4,5},{5,4},{6,7},{7,6},{8,9},{9,8},{10,11... | collective-permute-start | bytes 393224 | tf_op jit(solution)/shard_map/ppermute | solution.py:915
  48.9 15.6 %copy-start.10 = (bf16[128,512]{1,0:T(8,128)(2,1)}, bf16[128,512]{1,0:T(8,128)(2,1)S(1)}, u32[]{:S(2)}) copy-start(bf16[128,512]{1,0:T(8,128)(2,1)S(1)} %collective-permute-done.6.refs_6_.refs_12_) | copy-start | bytes 393220
  51.2 13.4 %copy-start.11 = (bf16[128,512]{1,0:T(8,128)(2,1)}, bf16[128,512]{1,0:T(8,128)(2,1)S(1)}, u32[]{:S(2)}) copy-start(bf16[128,512]{1,0:T(8,128)(2,1)S(1)} %collective-permute-done.5.refs_5_.refs_11_) | copy-start | bytes 393220
  69.5 4.3 %collective-permute-start.7 = (bf16[8,800,128]{2,1,0:T(8,128)(2,1)S(1)}, bf16[8,800,128]{2,1,0:T(8,128)(2,1)S(1)}, u32[]{:S(2)}, u32[]{:S(2)}) collective-permute-start(bf16[8,800,128]{2,1,0:T(8,128)(2,1)S(1)} %all-to-all-done.1.refs_2_), channel_id=1, source_target_pairs={{0,1},{1,0},{2,3},{3,2},{4,5},{5,4},{6,7},{7,6},{8,9},{9,8},{10,11... | collective-permute-start | bytes 4915208 | tf_op jit(solution)/shard_map/ppermute | solution.py:915
  69.5 80.7 %collective-permute-start.8 = (bf16[128,2048]{1,0:T(8,128)(2,1)}, bf16[128,2048]{1,0:T(8,128)(2,1)}, u32[]{:S(2)}, u32[]{:S(2)}) collective-permute-start(bf16[128,2048]{1,0:T(8,128)(2,1)} %copy-done.4), channel_id=1, source_target_pairs={{0,1},{1,0},{2,3},{3,2},{4,5},{5,4},{6,7},{7,6},{8,9},{9,8},{10,11... | collective-permute-start | bytes 1572872 | tf_op jit(solution)/shard_map/ppermute | solution.py:915
  77.5 5.8 %copy-start.26 = (bf16[8,288,128]{2,1,0:T(8,128)(2,1)S(1)}, bf16[8,288,128]{2,1,0:T(8,128)(2,1)}, u32[]{:S(2)}) copy-start(bf16[8,288,128]{2,1,0:T(8,128)(2,1)} %get-tuple-element.215) | copy-start | bytes 1769476
  77.5 17.0 %copy-start.21 = (s32[1,8]{1,0:T(1,128)S(1)}, s32[1,8]{1,0:T(1,128)}, u32[]{:S(2)}) copy-start(s32[1,8]{1,0:T(1,128)} %refs_1_.5) | copy-start | bytes 100
  79.1 15.4 %all-to-all-start.2 = ((f32[32,16,128]{2,1,0:T(8,128)}), f32[32,16,128]{2,1,0:T(8,128)S(1)}, u32[]{:S(2)}, u32[]{:S(2)}) async-start(f32[32,16,128]{2,1,0:T(8,128)} %get-tuple-element.128), calls=%async_computation.2 | async-start | bytes 524288 | tf_op jit(solution)/shard_map/all_to_all | solution.py:906
  113.4 6.7 %copy-start.2 = (bf16[512,512]{1,0:T(8,128)(2,1)}, bf16[512,512]{1,0:T(8,128)(2,1)S(1)}, u32[]{:S(2)}) copy-start(bf16[512,512]{1,0:T(8,128)(2,1)S(1)} %all-gather.1.refs_0_) | copy-start | bytes 1572868
  116.4 7.3 %copy-start.35 = (f32[64]{0:T(128)S(1)}, f32[64]{0:T(128)}, u32[]{:S(2)}) copy-start(f32[64]{0:T(128)} %param.27) | copy-start | bytes 772
  116.4 7.4 %copy-start.36 = (f32[64]{0:T(128)S(1)}, f32[64]{0:T(128)}, u32[]{:S(2)}) copy-start(f32[64]{0:T(128)} %param.28) | copy-start | bytes 772
  120.1 11.6 %all-to-all-start.3 = ((f32[8,8,128]{2,1,0:T(8,128)}), f32[8,8,128]{2,1,0:T(8,128)S(1)}, u32[]{:S(2)}, u32[]{:S(2)}) async-start(f32[8,8,128]{2,1,0:T(8,128)} %get-tuple-element.139), calls=%async_computation.3 | async-start | bytes 65536 | tf_op jit(solution)/shard_map/all_to_all | solution.py:906
  144.2 12.7 %all-to-all-start.4 = ((f32[8,8,128]{2,1,0:T(8,128)}), f32[8,8,128]{2,1,0:T(8,128)S(1)}, u32[]{:S(2)}, u32[]{:S(2)}) async-start(f32[8,8,128]{2,1,0:T(8,128)} %get-tuple-element.144), calls=%async_computation.4 | async-start | bytes 65536 | tf_op jit(solution)/shard_map/all_to_all | solution.py:906
  160.9 10.8 %all-to-all-start.5 = ((f32[8,8,128]{2,1,0:T(8,128)}), f32[8,8,128]{2,1,0:T(8,128)S(1)}, u32[]{:S(2)}, u32[]{:S(2)}) async-start(f32[8,8,128]{2,1,0:T(8,128)} %get-tuple-element.146), calls=%async_computation.5 | async-start | bytes 65536 | tf_op jit(solution)/shard_map/all_to_all | solution.py:906
  164.2 128.1 %reduce-scatter.2.cloned.1.call-start = ((), (), s32[]{:S(2)}) async-start(), calls=%async_computation.13 | async-start | bytes 1916928 | tf_op jit(solution)/shard_map/reduce_scatter | solution.py:1152
  189.1 14.5 %collective-permute-start.9 = (bf16[2,128,512]{2,1,0:T(8,128)(2,1)S(1)}, bf16[2,128,512]{2,1,0:T(8,128)(2,1)S(1)}, u32[]{:S(2)}, u32[]{:S(2)}) collective-permute-start(bf16[2,128,512]{2,1,0:T(8,128)(2,1)S(1)} %copy-done.39), channel_id=1, source_target_pairs={{0,1},{1,0},{2,3},{3,2},{4,5},{5,4},{6,7},{7,6},{8,9},{9,8},{10,11... | collective-permute-start | bytes 786440 | tf_op jit(solution)/shard_map/ppermute | solution.py:915
  189.1 14.4 %collective-permute-start.10 = (bf16[2,128,512]{2,1,0:T(8,128)(2,1)S(1)}, bf16[2,128,512]{2,1,0:T(8,128)(2,1)S(1)}, u32[]{:S(2)}, u32[]{:S(2)}) collective-permute-start(bf16[2,128,512]{2,1,0:T(8,128)(2,1)S(1)} %copy-done.38), channel_id=1, source_target_pairs={{0,2},{1,3},{2,0},{3,1},{4,6},{5,7},{6,4},{7,5},{8,10},{9,11},{10,... | collective-permute-start | bytes 786440 | tf_op jit(solution)/shard_map/ppermute | solution.py:915
  189.5 14.0 %collective-permute-start.11 = (bf16[2,128,512]{2,1,0:T(8,128)(2,1)S(1)}, bf16[2,128,512]{2,1,0:T(8,128)(2,1)S(1)}, u32[]{:S(2)}, u32[]{:S(2)}) collective-permute-start(bf16[2,128,512]{2,1,0:T(8,128)(2,1)S(1)} %copy-done.37), channel_id=1, source_target_pairs={{0,3},{1,2},{2,1},{3,0},{4,7},{5,6},{6,5},{7,4},{8,11},{9,10},{10,... | collective-permute-start | bytes 786440 | tf_op jit(solution)/shard_map/ppermute | solution.py:915
  207.5 4.8 %copy-start.30 = (bf16[4,128,512]{2,1,0:T(8,128)(2,1)S(1)}, bf16[4,128,512]{2,1,0:T(8,128)(2,1)}, u32[]{:S(2)}) copy-start(bf16[4,128,512]{2,1,0:T(8,128)(2,1)} %get-tuple-element.164) | copy-start | bytes 1572868
  212.2 11.4 %copy-start = (bf16[8,832,128]{2,1,0:T(8,128)(2,1)S(1)}, bf16[8,832,128]{2,1,0:T(8,128)(2,1)}, u32[]{:S(2)}) copy-start(bf16[8,832,128]{2,1,0:T(8,128)(2,1)} %shard_map.381.refs_5_) | copy-start | bytes 5111812
  231.3 4.7 %copy-start.9 = (bf16[576,128]{1,0:T(8,128)(2,1)}, bf16[576,128]{1,0:T(8,128)(2,1)S(1)}, u32[]{:S(2)}) copy-start(bf16[576,128]{1,0:T(8,128)(2,1)S(1)} %all-gather.4) | copy-start | bytes 442372
  236.0 19.3 %all-to-all-start.9 = ((f32[32,16,128]{2,1,0:T(8,128)}), f32[32,16,128]{2,1,0:T(8,128)S(1)}, u32[]{:S(2)}, u32[]{:S(2)}) async-start(f32[32,16,128]{2,1,0:T(8,128)} %get-tuple-element.177), calls=%async_computation.9 | async-start | bytes 524288 | tf_op jit(solution)/shard_map/all_to_all | solution.py:906
  257.0 28.6 %all-to-all-start.10 = ((bf16[8,272,128]{2,1,0:T(8,128)(2,1)}), bf16[8,272,128]{2,1,0:T(8,128)(2,1)S(1)}, u32[]{:S(2)}, u32[]{:S(2)}) async-start(bf16[8,272,128]{2,1,0:T(8,128)(2,1)} %shard_map.384.refs_5_), calls=%async_computation.10 | async-start | bytes 1114112 | tf_op jit(solution)/shard_map/all_to_all | solution.py:906
  285.7 12.7 %copy-start.33 = (bf16[272,128]{1,0:T(8,128)(2,1)}, bf16[272,128]{1,0:T(8,128)(2,1)S(1)}, u32[]{:S(2)}) copy-start(bf16[272,128]{1,0:T(8,128)(2,1)S(1)} %reduce_sum.34.refs_1_) | copy-start | bytes 208900
  285.7 24.7 %all-to-all-start.11 = ((bf16[8,320,128]{2,1,0:T(8,128)(2,1)}), bf16[8,320,128]{2,1,0:T(8,128)(2,1)S(1)}, u32[]{:S(2)}, u32[]{:S(2)}) async-start(bf16[8,320,128]{2,1,0:T(8,128)(2,1)} %shard_map.390), calls=%async_computation.11 | async-start | bytes 1310720 | tf_op jit(solution)/shard_map/all_to_all | solution.py:906
  291.8 6.7 %collective-permute-start.20 = (bf16[272,128]{1,0:T(8,128)(2,1)S(1)}, bf16[272,128]{1,0:T(8,128)(2,1)S(1)}, u32[]{:S(2)}, u32[]{:S(2)}) collective-permute-start(bf16[272,128]{1,0:T(8,128)(2,1)S(1)} %reduce_sum.34.refs_1_), channel_id=1, source_target_pairs={{0,3},{1,2},{2,1},{3,0},{4,7},{5,6},{6,5},{7,4},{8,11},{9,10},{10,... | collective-permute-start | bytes 208904 | tf_op jit(solution)/shard_map/ppermute | solution.py:915
  294.6 15.9 %collective-permute-start.14 = (bf16[864,128]{1,0:T(8,128)(2,1)}, bf16[864,128]{1,0:T(8,128)(2,1)S(1)}, u32[]{:S(2)}, u32[]{:S(2)}) collective-permute-start(bf16[864,128]{1,0:T(8,128)(2,1)} %shard_map.391.refs_1_), channel_id=1, source_target_pairs={{0,3},{1,2},{2,1},{3,0},{4,7},{5,6},{6,5},{7,4},{8,11},{9,10},{10,... | collective-permute-start | bytes 663560 | tf_op jit(solution)/shard_map/ppermute | solution.py:915
  295.9 14.7 %collective-permute-start.13 = (bf16[864,128]{1,0:T(8,128)(2,1)}, bf16[864,128]{1,0:T(8,128)(2,1)S(1)}, u32[]{:S(2)}, u32[]{:S(2)}) collective-permute-start(bf16[864,128]{1,0:T(8,128)(2,1)} %shard_map.391.refs_1_), channel_id=1, source_target_pairs={{0,2},{1,3},{2,0},{3,1},{4,6},{5,7},{6,4},{7,5},{8,10},{9,11},{10,... | collective-permute-start | bytes 663560 | tf_op jit(solution)/shard_map/ppermute | solution.py:915
  296.7 13.8 %collective-permute-start.12 = (bf16[864,128]{1,0:T(8,128)(2,1)}, bf16[864,128]{1,0:T(8,128)(2,1)S(1)}, u32[]{:S(2)}, u32[]{:S(2)}) collective-permute-start(bf16[864,128]{1,0:T(8,128)(2,1)} %shard_map.391.refs_1_), channel_id=1, source_target_pairs={{0,1},{1,0},{2,3},{3,2},{4,5},{5,4},{6,7},{7,6},{8,9},{9,8},{10,11... | collective-permute-start | bytes 663560 | tf_op jit(solution)/shard_map/ppermute | solution.py:915
  297.3 11.5 %collective-permute-start.19 = (bf16[272,128]{1,0:T(8,128)(2,1)S(1)}, bf16[272,128]{1,0:T(8,128)(2,1)S(1)}, u32[]{:S(2)}, u32[]{:S(2)}) collective-permute-start(bf16[272,128]{1,0:T(8,128)(2,1)S(1)} %reduce_sum.34.refs_1_), channel_id=1, source_target_pairs={{0,2},{1,3},{2,0},{3,1},{4,6},{5,7},{6,4},{7,5},{8,10},{9,11},{10,... | collective-permute-start | bytes 208904 | tf_op jit(solution)/shard_map/ppermute | solution.py:915
  298.5 10.3 %collective-permute-start.18 = (bf16[272,128]{1,0:T(8,128)(2,1)S(1)}, bf16[272,128]{1,0:T(8,128)(2,1)S(1)}, u32[]{:S(2)}, u32[]{:S(2)}) collective-permute-start(bf16[272,128]{1,0:T(8,128)(2,1)S(1)} %reduce_sum.34.refs_1_), channel_id=1, source_target_pairs={{0,1},{1,0},{2,3},{3,2},{4,5},{5,4},{6,7},{7,6},{8,9},{9,8},{10,11... | collective-permute-start | bytes 208904 | tf_op jit(solution)/shard_map/ppermute | solution.py:915
  310.5 4.8 %collective-permute-start.17 = (bf16[320,128]{1,0:T(8,128)(2,1)S(1)}, bf16[320,128]{1,0:T(8,128)(2,1)S(1)}, u32[]{:S(2)}, u32[]{:S(2)}) collective-permute-start(bf16[320,128]{1,0:T(8,128)(2,1)S(1)} %reduce_sum.35.refs_1_), channel_id=1, source_target_pairs={{0,3},{1,2},{2,1},{3,0},{4,7},{5,6},{6,5},{7,4},{8,11},{9,10},{10,... | collective-permute-start | bytes 245768 | tf_op jit(solution)/shard_map/ppermute | solution.py:915
  310.9 5.6 %collective-permute-start.16 = (bf16[320,128]{1,0:T(8,128)(2,1)S(1)}, bf16[320,128]{1,0:T(8,128)(2,1)S(1)}, u32[]{:S(2)}, u32[]{:S(2)}) collective-permute-start(bf16[320,128]{1,0:T(8,128)(2,1)S(1)} %reduce_sum.35.refs_1_), channel_id=1, source_target_pairs={{0,2},{1,3},{2,0},{3,1},{4,6},{5,7},{6,4},{7,5},{8,10},{9,11},{10,... | collective-permute-start | bytes 245768 | tf_op jit(solution)/shard_map/ppermute | solution.py:915
  311.9 4.7 %collective-permute-start.15 = (bf16[320,128]{1,0:T(8,128)(2,1)S(1)}, bf16[320,128]{1,0:T(8,128)(2,1)S(1)}, u32[]{:S(2)}, u32[]{:S(2)}) collective-permute-start(bf16[320,128]{1,0:T(8,128)(2,1)S(1)} %reduce_sum.35.refs_1_), channel_id=1, source_target_pairs={{0,1},{1,0},{2,3},{3,2},{4,5},{5,4},{6,7},{7,6},{8,9},{9,8},{10,11... | collective-permute-start | bytes 245768 | tf_op jit(solution)/shard_map/ppermute | solution.py:915
  (24 other events, 51.5 us)
Sparse Core Ops, SparseCore 0:
  69.6 46.7 all-gather.7
  212.4 72.9 reduce-scatter.1
